TPU v7x, 32 devices: a whole 2x2x4 slice. The times are simulated.
32 devices in a mesh: depth: 4 (over z), tile: 8 (over y, x, core).
Axes of the slice: x: 2, y: 2, z: 4, core: 2. Of those that a mesh axis runs over, the one named last changes fastest.
Arguments:
- field: bfloat16 [192, 1152, 1152], P(('depth', 'tile')), may hold values from -6 to 6
- transfer: float32 [4, 16], replicated, may hold values from 0 to 1
- bin_order: int32 [16], replicated, may hold values from 0 to 15, each once
- light_angles: float32 [2], replicated, may hold values from -0.6 to 1.4, as said below
Outputs:
- image: float32 [4, 1152, 1152], P(None, 'tile', 'depth')
Inputs may be any that keep to these rules, and one draw needn't show every extreme that they name: `bin_order`: a permutation of 0 .. 15. `light_angles`: azimuth first, then polar angle, in radians.
All inputs are finite; a program needn't handle non-finite values.
Results may differ from a plain program's by a relative error of at most 0.0003.
Values may be sent and summed in bfloat16 or wider, within the bound.
No kernel may reach another device: no remote copies, remote signals or barrier semaphores. Data moves between devices by JAX's collectives and lax.ppermute only.
A program may use at most 320 MiB of HBM per device.

v0:
```python
import jax
import jax.numpy as jnp
from jax import lax
from jax.sharding import PartitionSpec as P


def with_halo(array, sides, width):
    for axis, dim in sides:
        devices, length = (lax.axis_size(axis), array.shape[dim])
        up = [(i, (i + 1) % devices) for i in range(devices - 1)]
        down = [(j, i) for i, j in up]
        last = lax.slice_in_dim(array, length - width, length, axis=dim)
        first = lax.slice_in_dim(array, 0, width, axis=dim)
        before = lax.ppermute(last, axis, up)
        after = lax.ppermute(first, axis, down)
        array = jnp.concatenate([before, array, after], axis=dim)
    return array


def classify(padded, transfer, bin_order, light_angles):
    table = jnp.take(transfer, bin_order, axis=1)
    centre = padded[1:-1, 1:-1, :]
    grad_x = (padded[2:, 1:-1, :] - padded[:-2, 1:-1, :]) * 0.5
    grad_y = (padded[1:-1, 2:, :] - padded[1:-1, :-2, :]) * 0.5
    zpadded = jnp.pad(centre, ((0, 0), (0, 0), (1, 1)))
    grad_z = (zpadded[:, :, 2:] - zpadded[:, :, :-2]) * 0.5
    azimuth = light_angles[0]
    polar = light_angles[1]
    light_x = jnp.cos(azimuth) * jnp.sin(polar)
    light_y = jnp.sin(azimuth) * jnp.sin(polar)
    light_z = jnp.cos(polar)
    length = jnp.sqrt(grad_x * grad_x + grad_y * grad_y + grad_z * grad_z)
    facing = jnp.abs(grad_x * light_x + grad_y * light_y + grad_z * light_z)
    shade = 0.3 + 0.7 * facing / jnp.maximum(length, 1.0)
    bins = table.shape[1]
    position = jnp.clip((centre + 3.0) / 6.0, 0.0, 1.0) * (bins - 1)
    red = jnp.zeros_like(centre)
    green = jnp.zeros_like(centre)
    blue = jnp.zeros_like(centre)
    opacity = jnp.zeros_like(centre)
    for level in range(bins):
        weight = jnp.maximum(0.0, 1.0 - jnp.abs(position - level))
        red = red + weight * table[0, level]
        green = green + weight * table[1, level]
        blue = blue + weight * table[2, level]
        opacity = opacity + weight * table[3, level]
    alpha = 0.01 * opacity
    scaled = 0.15 * shade
    return (jnp.stack([red * scaled, green * scaled, blue * scaled]), alpha)


def march(emission, alpha):
    through = jnp.cumprod(1.0 - alpha, axis=0)
    before = jnp.concatenate([jnp.ones_like(through[:1]), through[:-1]], axis=0)
    colour = jnp.sum(emission * before[None], axis=1)
    return jnp.concatenate([colour, through[-1][None]], axis=0)


def over_layers(front, back):
    colour = front[:3] + front[3:] * back[:3]
    return jnp.concatenate([colour, front[3:] * back[3:]], axis=0)


def composite_stack(stacked):

    def step(carry, layer):
        return (over_layers(carry, layer), None)

    start = jnp.concatenate([jnp.zeros_like(stacked[0, :3]), jnp.ones_like(stacked[0, 3:])], axis=0)
    result, unused = lax.scan(step, start, stacked)
    return jnp.concatenate([result[:3], 1.0 - result[3:]], axis=0)


def per_device(field, transfer, bin_order, light_angles):
    brick = lax.all_to_all(field, "tile", split_axis=1, concat_axis=0, tiled=True)
    padded = with_halo(brick, (("depth", 0), ("tile", 1)), 1)
    emission, alpha = classify(padded.astype(jnp.float32), transfer, bin_order, light_angles)
    partial_image = march(emission, alpha)
    return composite_stack(
        lax.all_to_all(partial_image[None], "depth", split_axis=3, concat_axis=0, tiled=True)
    )


def solution(mesh):
    in_specs = (P(("depth", "tile"), None, None), P(), P(), P())
    out_specs = P(None, "tile", "depth")
    return jax.shard_map(
        per_device, mesh=mesh, in_specs=in_specs, out_specs=out_specs, check_vma=False
    )
```

profile of v0, /device:TPU:0, one launch (start us, length us, event | category | flops | bytes accessed | tf_op | source)
XLA Modules:
  0.0 1061.6 jit_solution(15854346152551481643)
XLA Ops:
  0.0 43.6 %copy.16 = bf16[6,1152,1152]{2,0,1:T(8,128)(2,1)} copy(bf16[6,1152,1152]{2,1,0:T(8,128)(2,1)} %param.6) | data formatting | bytes 31850496 | tf_op args[0]
  43.6 6.1 all-to-all-start
  50.5 231.6 %all-to-all-done = bf16[6,1152,1152]{2,0,1:T(8,128)(2,1)} async-done(((bf16[6,1152,1152]{2,0,1:T(8,128)(2,1)}), bf16[6,1152,1152]{2,0,1:T(8,128)(2,1)}, u32[]{:S(2)}, u32[]{:S(2)}) %all-to-all-start) | async-done | bytes 15925280 | tf_op jit(solution)/shard_map/all_to_all | solution.py:75
  282.1 11.0 %copy.17 = bf16[8,6,144,1152]{3,2,1,0:T(8,128)(2,1)S(1)} copy(bf16[8,6,144,1152]{3,1,2,0:T(8,128)(2,1)} %bitcast.4) | data formatting | bytes 31850496 | tf_op jit(solution)/shard_map/all_to_all | solution.py:75
  293.1 4.3 collective-permute-start
  302.1 4.4 collective-permute-done.1
  306.8 1.3 collective-permute-start.2
  308.2 1.3 collective-permute-start.3
  314.6 12.3 %maximum_convert_fusion = f32[50,146,1152]{2,1,0:T(8,128)S(1)} fusion(bf16[50,1,1152]{2,1,0:T(2,128)(2,1)S(1)} %collective-permute-done.3, bf16[1,144,1152]{2,1,0:T(8,128)(2,1)S(1)} %collective-permute-done.1, bf16[48,144,1152]{2,1,0:T(8,128)(2,1)} %bitcast.104, bf16[1,144,1152]{2,1,0:T(8,128)(2,1)S(1)} %collective-permute-done, ...), kind=kLoop, calls=%fused_computation.70 | loop fusion | flops 84096000 | bytes 50457600 | tf_op jit(solution)/shard_map/convert_element_type | solution.py:77
  327.0 12.9 %slice.347 = f32[48,144,1152]{2,1,0:T(8,128)} slice(f32[50,146,1152]{2,1,0:T(8,128)S(1)} %maximum_convert_fusion), slice={[1:49], [1:145], [0:1152]} | slice | bytes 63700992 | tf_op jit(solution)/shard_map/slice | solution.py:22
  339.9 8.2 copy-done
  348.1 119.9 %fusion.5 = f32[48,144,1152]{2,1,0:T(8,128)} fusion(f32[]{:T(128)} %bitcast.76, f32[]{:T(128)} %bitcast.75, f32[]{:T(128)} %bitcast.74, f32[]{:T(128)} %bitcast.73, f32[]{:T(128)} %bitcast.72, f32[]{:T(128)} %bitcast.71, f32[]{:T(128)} %bitcast.70, f32[]{:T(128)} %bitcast.69, f32[]{:T(128)} %bitcast.68, f32[]{:T(128)} %bitcast.67, f32[]{:T(128)} %bitcast.66, ...), kind=kOutput, calls=%fused_computation.15 | output fusion | flops 1170505728 | bytes 63709184 | tf_op jit(solution)/shard_map/jit(cumprod)/reduce_window | solution.py:53
  468.0 9.9 slice-done
  477.9 10.6 %concatenate.27 = f32[48,144,1152]{2,1,0:T(8,128)} pad(f32[47,144,1152]{2,1,0:T(8,128)S(1)} %slice-done, f32[]{:T(128)} %constant.41.clone.1), padding=1_0x0_0x0_0 | pad | bytes 63037444 | tf_op jit(solution)/shard_map/concatenate | solution.py:54
  488.5 164.5 %multiply_bitcast_fusion.2 = (f32[1,48,144,1152]{3,2,1,0:T(8,128)}, f32[48,144,1152]{2,1,0:T(8,128)}) fusion(f32[]{:T(128)} %bitcast.22, f32[]{:T(128)} %bitcast.21, f32[]{:T(128)} %bitcast.20, f32[]{:T(128)} %bitcast.19, f32[]{:T(128)} %bitcast.18, f32[]{:T(128)} %bitcast.17, f32[]{:T(128)} %bitcast.16, f32[]{:T(128)} %bitcast.15, f32[]{:T(128)} %bitcast.14, ...), kind=kLoop, calls=%fused_computation.51 | loop fusion | flops 963477504 | bytes 254804048 | tf_op jit(solution)/shard_map/stack | solution.py:49
  653.0 120.0 %multiply_bitcast_fusion.1 = f32[1,48,144,1152]{3,2,1,0:T(8,128)} fusion(f32[48,144,1152]{2,1,0:T(8,128)} %get-tuple-element.39, f32[]{:T(128)} %bitcast.42, f32[]{:T(128)} %bitcast.41, f32[]{:T(128)} %bitcast.40, f32[]{:T(128)} %bitcast.39, f32[]{:T(128)} %bitcast.38, f32[]{:T(128)} %bitcast.37, f32[]{:T(128)} %bitcast.36, f32[]{:T(128)} %bitcast.35, ...), kind=kLoop, calls=%fused_computation.50 | loop fusion | flops 788299776 | bytes 95551552 | tf_op jit(solution)/shard_map/stack | solution.py:49
  773.0 116.5 %multiply_bitcast_fusion = f32[1,48,144,1152]{3,2,1,0:T(8,128)} fusion(f32[48,144,1152]{2,1,0:T(8,128)S(1)} %copy-done.1, f32[]{:T(128)} %bitcast.59, f32[]{:T(128)} %bitcast.58, f32[]{:T(128)} %bitcast.57, f32[]{:T(128)} %bitcast.56, f32[]{:T(128)} %bitcast.55, f32[]{:T(128)} %bitcast.54, f32[]{:T(128)} %bitcast.53, f32[]{:T(128)} %bitcast.52, f32[]{:T(128)} %bitcast.51, ...), kind=kLoop, calls=%fused_computation.49 | loop fusion | flops 788299776 | bytes 95551552 | tf_op jit(solution)/shard_map/stack | solution.py:49
  889.5 39.9 %fusion.3 = f32[3,144,1152]{2,1,0:T(8,128)} fusion(f32[1,48,144,1152]{3,2,1,0:T(8,128)} %multiply_bitcast_fusion, f32[1,48,144,1152]{3,2,1,0:T(8,128)} %multiply_bitcast_fusion.1, f32[1,48,144,1152]{3,2,1,0:T(8,128)} %get-tuple-element.38, f32[48,144,1152]{2,1,0:T(8,128)} %concatenate.27), kind=kLoop, calls=%fused_computation.9 | loop fusion | flops 95053824 | bytes 129392640 | tf_op jit(solution)/shard_map/reduce_sum | solution.py:55
  929.5 1.7 maximum_bitcast_fusion
  931.2 4.0 copy.19
  935.2 5.0 all-to-all-start.1
  940.2 104.8 %all-to-all-done.1 = f32[1,4,144,1152]{2,1,0,3:T(4,128)} async-done(((f32[1,4,144,1152]{2,1,0,3:T(4,128)}), f32[1,4,144,1152]{2,1,0,3:T(4,128)}, u32[]{:S(2)}, u32[]{:S(2)}) %all-to-all-start.1) | async-done | bytes 2654240 | tf_op jit(solution)/shard_map/all_to_all | solution.py:80
  1044.9 6.4 copy.21
  1051.5 9.0 while.10
  (49 shorter events, 18.3 us)
Async XLA Ops:
  0.0 49.7 %copy-start.3 = (f32[4,16]{1,0:T(4,128)S(1)}, f32[4,16]{1,0:T(4,128)}, u32[]{:S(2)}) copy-start(f32[4,16]{1,0:T(4,128)} %param.7) | copy-start | bytes 772
  0.0 49.8 %copy-start.5 = (s32[16]{0:T(128)S(1)}, s32[16]{0:T(128)}, u32[]{:S(2)}) copy-start(s32[16]{0:T(128)} %param.8) | copy-start | bytes 196
  43.6 238.5 %all-to-all-start = ((bf16[6,1152,1152]{2,0,1:T(8,128)(2,1)}), bf16[6,1152,1152]{2,0,1:T(8,128)(2,1)}, u32[]{:S(2)}, u32[]{:S(2)}) async-start(bf16[6,1152,1152]{2,0,1:T(8,128)(2,1)} %copy.16), calls=%async_computation | async-start | bytes 42467328 | tf_op jit(solution)/shard_map/all_to_all | solution.py:75
  49.7 259.7 %copy-start.4 = (f32[2]{0:T(128)S(1)}, f32[2]{0:T(128)}, u32[]{:S(2)}) copy-start(f32[2]{0:T(128)} %param.9) | copy-start | bytes 28
  293.1 20.4 %copy-start.2 = (bf16[8,6,144,1152]{3,2,1,0:T(8,128)(2,1)}, bf16[8,6,144,1152]{3,2,1,0:T(8,128)(2,1)S(1)}, u32[]{:S(2)}) copy-start(bf16[8,6,144,1152]{3,2,1,0:T(8,128)(2,1)S(1)} %copy.17) | copy-start | bytes 47775748
  293.1 8.9 collective-permute-start
  297.5 9.0 collective-permute-start.1
  306.8 6.7 collective-permute-start.2
  308.2 6.5 collective-permute-start.3
  327.0 21.1 %copy-start = (f32[50,146,1152]{2,1,0:T(8,128)}, f32[50,146,1152]{2,1,0:T(8,128)S(1)}, u32[]{:S(2)}) copy-start(f32[50,146,1152]{2,1,0:T(8,128)S(1)} %maximum_convert_fusion) | copy-start | bytes 100915200
  468.0 9.9 slice-start
  653.0 120.0 %copy-start.1 = (f32[48,144,1152]{2,1,0:T(8,128)S(1)}, f32[48,144,1152]{2,1,0:T(8,128)}, u32[]{:S(2)}) copy-start(f32[48,144,1152]{2,1,0:T(8,128)} %get-tuple-element.39) | copy-start | bytes 95551488
  889.5 39.9 %slice-start.1 = ((f32[48,144,1152]{2,1,0:T(8,128)}), f32[1,144,1152]{2,1,0:T(8,128)S(1)}, s32[]{:S(2)}) async-start(f32[48,144,1152]{2,1,0:T(8,128)} %fusion.5), calls=%async_computation.3 | async-start | bytes 1327104 | tf_op jit(solution)/shard_map/slice | solution.py:56
  935.2 109.7 %all-to-all-start.1 = ((f32[1,4,144,1152]{2,1,0,3:T(4,128)}), f32[1,4,144,1152]{2,1,0,3:T(4,128)}, u32[]{:S(2)}, u32[]{:S(2)}) async-start(f32[1,4,144,1152]{2,1,0,3:T(4,128)} %copy.19), calls=%async_computation.1 | async-start | bytes 9437184 | tf_op jit(solution)/shard_map/all_to_all | solution.py:80
where the time goes:
time: 1060 us
  other arithmetic  585 us (55%)
  waiting for transfers between devices  343 us (32%)
  local copies, waits for them, and re-layouts  111 us (10%)
  starting transfers between devices  19.3 us (2%)
    another operation x3, other arithmetic, classify(): return (jnp.stack([red * scaled, green * scaled, blue * scaled]), alpha)  401 us
    all_to_all x1, waiting for transfers between devices, per_device(): lax.all_to_all(field, 'tile', split_axis=1, concat_axis=0, tiled=True)  232 us
    another operation x1, other arithmetic, march(): through = jnp.cumprod(1.0 - alpha, axis=0)  120 us
    all_to_all x1, waiting for transfers between devices, per_device(): lax.all_to_all(partial_image[None], 'depth', split_axis=3, concat_axis=0,...  105 us
    unnamed x14, local copies, waits for them, and re-layouts  51.9 us
    reduce_sum x1, other arithmetic, march(): colour = jnp.sum(emission * before[None], axis=1)  39.9 us
  transfers between devices with their start and end apart: 6, of which 5 were waited for; matrix products, arithmetic and copies ran while one was open for 0% of the time, Pallas kernels for 0%

commit v1 on v0

v1 whole, which is shorter than its diff:
```python
import functools
import math

import jax
import jax.numpy as jnp
from jax import lax
from jax.experimental import pallas as pl
from jax.experimental.pallas import tpu as pltpu
from jax.sharding import PartitionSpec as P

LANES = 128
CODES = 32700.0
VMEM_LIMIT = 56 * 1024 * 1024


def unit_rows(rows):
    return 48 if rows % 48 == 0 else rows


def encode(values):
    top = functools.reduce(jnp.maximum, values)
    top = jnp.max(top, axis=0, keepdims=True)
    exponent = jnp.ceil(jnp.log2(jnp.maximum(top, 1e-30)))
    factor = jnp.exp2(-exponent) * CODES
    codes = [(v * factor + 0.5).astype(jnp.int32).astype(jnp.int16) for v in values]
    row = jnp.broadcast_to(exponent, (16, exponent.shape[1]))
    return codes, row.astype(jnp.int32).astype(jnp.int16)


def decode(codes, row):
    exponent = row.astype(jnp.int32).astype(jnp.float32)[0:1]
    scale = jnp.exp2(exponent) * (1.0 / CODES)
    return [c.astype(jnp.int32).astype(jnp.float32) * scale for c in codes]


def over(front, back):
    clear = 1.0 - front[3]
    return [f + clear * b for f, b in zip(front, back)]


def render_kernel(ctl, light, table, main, above, below, before, after, send, keep, cells, slopes, image, edge, *, groups, units, unit, block, rows, offset, total):
    i = pl.program_id(0)
    half = (groups // 2) * units
    rest = lax.rem(i, half)
    sending = i < half
    parity = jnp.where(sending, 1 - ctl[0], ctl[0])
    group = 2 * (rest // units) + parity
    start = group * rows + offset + lax.rem(rest, units) * unit
    layers = main.shape[0]
    width = main.shape[2]
    if block == unit:
        shift = 0
    else:
        shift = pl.multiple_of(lax.rem(start, block), 8)

    lane = lax.broadcasted_iota(jnp.int32, (8, width), 1)
    first_lane = lane == 0
    last_lane = lane == width - 1

    def load_layer(layer, carry):
        if block != unit:
            edge[...] = main[layer].astype(jnp.float32)
        for r in range(0, unit, 16):
            n = min(16, unit - r)
            if block == unit:
                wide = main[layer, r:r + n, :].astype(jnp.float32)
            else:
                wide = edge[pl.ds(shift + r, n), :]
            for q in range(0, n, 8):
                x = wide[q:q + 8]
                left = jnp.where(first_lane, 0.0, pltpu.roll(x, 1, 1))
                right = jnp.where(last_lane, 0.0, pltpu.roll(x, width - 1, 1))
                cells[layer + 1, 8 + r + q:16 + r + q, :] = x
                slopes[layer, r + q:r + q + 8, :] = right - left
        up = above[layer].astype(jnp.float32)
        down = below[layer].astype(jnp.float32)
        if block == unit:
            up = up[8:16]
            down = down[0:8]
        else:
            up = jnp.where(lax.rem(start, 16) == 0, up[8:16], up[0:8])
            down = jnp.where(lax.rem(start + unit, 16) == 0, down[0:8], down[8:16])
        cells[layer + 1, 0:8, :] = jnp.where(start > 0, up, 0.0)
        cells[layer + 1, 8 + unit:16 + unit, :] = jnp.where(start + unit < total, down, 0.0)
        return carry

    lax.fori_loop(0, layers, load_layer, 0)
    cells[0, 8:8 + unit, :] = before[0].astype(jnp.float32)
    cells[layers + 1, 8:8 + unit, :] = after[0].astype(jnp.float32)

    lx, ly, lz = light[0], light[1], light[2]
    step = 16 if unit % 16 == 0 else 8
    tables = [jnp.broadcast_to(table[k:k + 1, :], (step, LANES)) for k in range(8)]

    def strip(c, carry):
        cols = pl.ds(pl.multiple_of(c * LANES, LANES), LANES)
        for r in range(0, unit, step):
            low = cells[0, 8 + r:8 + r + step, cols]
            here = cells[1, 8 + r:8 + r + step, cols]
            clear = None
            for layer in range(layers):
                high = cells[layer + 2, 8 + r:8 + r + step, cols]
                gx = high - low
                gy = cells[layer + 1, 9 + r:9 + r + step, cols] - cells[layer + 1, 7 + r:7 + r + step, cols]
                gz = slopes[layer, r:r + step, cols]
                facing = jnp.abs(gx * lx + gy * ly + gz * lz)
                square = gx * gx + gy * gy + gz * gz
                shade = 0.045 + facing * lax.rsqrt(jnp.maximum(square, 4.0))
                position = jnp.clip(here * 2.5 + 7.5, 0.0, 15.0)
                index = position.astype(jnp.int32)
                part = position - index.astype(jnp.float32)
                tf = [
                    jnp.take_along_axis(tables[k], index, axis=1, mode="promise_in_bounds")
                    + part * jnp.take_along_axis(tables[4 + k], index, axis=1, mode="promise_in_bounds")
                    for k in range(4)
                ]
                if clear is None:
                    total_colour = [tf[k] * shade for k in range(3)]
                    clear = 1.0 - tf[3]
                else:
                    seen = shade * clear
                    total_colour = [total_colour[k] + tf[k] * seen for k in range(3)]
                    clear = clear - clear * tf[3]
                low, here = here, high
            for k in range(3):
                image[k, r:r + step, cols] = total_colour[k]
            image[3, r:r + step, cols] = 1.0 - clear
        return carry

    lax.fori_loop(0, width // LANES, strip, 0)
    put_unit(image, send, keep, sending, unit, width)


def put_unit(image, send, keep, sending, unit, width):
    @pl.when(sending)
    def _():
        def strip(c, carry):
            cols = pl.ds(pl.multiple_of(c * LANES, LANES), LANES)
            codes, row = encode([image[k, :, cols] for k in range(4)])
            for k in range(4):
                send[0, k * unit:(k + 1) * unit, cols] = codes[k]
            send[0, 4 * unit:4 * unit + 16, cols] = row
            return carry

        lax.fori_loop(0, width // LANES, strip, 0)

    @pl.when(jnp.logical_not(sending))
    def _():
        keep[0] = image[...]


def get_unit(ctl, mine, got, cols, unit):
    theirs = decode(
        [got[0, k * unit:(k + 1) * unit, cols] for k in range(4)],
        got[0, 4 * unit:4 * unit + 16, cols],
    )
    ours = [mine[0, k, :, cols] for k in range(4)]
    behind = ctl[1] == 1
    front = [jnp.where(behind, t, o) for t, o in zip(theirs, ours)]
    back = [jnp.where(behind, o, t) for t, o in zip(theirs, ours)]
    return over(front, back)


def merge_kernel(ctl, mine, got, send, keep, image, *, groups, units, unit):
    i = pl.program_id(0)
    width = mine.shape[3]

    def strip(c, carry):
        cols = pl.ds(pl.multiple_of(c * LANES, LANES), LANES)
        merged = get_unit(ctl, mine, got, cols, unit)
        for k in range(4):
            image[k, :, cols] = merged[k]
        return carry

    lax.fori_loop(0, width // LANES, strip, 0)
    put_unit(image, send, keep, i < (groups // 2) * units, unit, width)


def last_merge_kernel(ctl, mine, got, send, image, *, unit, blocks):
    width = mine.shape[3]

    def strip(c, carry):
        cols = pl.ds(pl.multiple_of(c * LANES, LANES), LANES)
        merged = get_unit(ctl, mine, got, cols, unit)
        for k in range(4):
            image[k, :, cols] = merged[k]
        return carry

    lax.fori_loop(0, width // LANES, strip, 0)
    part = width // blocks
    for b in range(blocks):
        wide = jnp.concatenate([image[k, :, b * part:(b + 1) * part] for k in range(4)], axis=1)
        codes, row = encode([wide])
        send[b, 0, 0:unit, :] = codes[0]
        send[b, 0, unit:unit + 16, :] = row


def compose_kernel(got, out, *, unit, blocks):
    part = out.shape[2]
    total = None
    for b in range(blocks):
        wide = decode([got[b, 0, 0:unit, :]], got[b, 0, unit:unit + 16, :])[0]
        layer = [wide[:, k * part:(k + 1) * part] for k in range(4)]
        total = layer if total is None else over(total, layer)
    for k in range(4):
        out[k] = total[k]


def params():
    return pltpu.CompilerParams(vmem_limit_bytes=VMEM_LIMIT, dimension_semantics=("arbitrary",))


def unit_index(groups, units, bit):
    half = (groups // 2) * units

    def index(i, ctl):
        rest = lax.rem(i, half)
        parity = jnp.where(i < half, 1 - ctl[bit], ctl[bit])
        return (2 * (rest // units) + parity) * units + lax.rem(rest, units)

    return index


def split_outputs(groups, units, unit, width):
    half = (groups // 2) * units
    shapes = [
        jax.ShapeDtypeStruct((half, 4 * unit + 16, width), jnp.int16),
        jax.ShapeDtypeStruct((half, 4, unit, width), jnp.float32),
    ]
    specs = [
        pl.BlockSpec((1, 4 * unit + 16, width), lambda i, ctl: (jnp.minimum(i, half - 1), 0, 0)),
        pl.BlockSpec((1, 4, unit, width), lambda i, ctl: (jnp.maximum(i - half, 0), 0, 0, 0)),
    ]
    return shapes, specs


def render(ctl, light, table, field, before, after, *, groups, units, unit, rows, offset):
    layers, total, width = field.shape
    block = math.lcm(unit, 16)
    half = (groups // 2) * units
    index = unit_index(groups, units, 0)

    def start(i, ctl):
        unit_at = index(i, ctl)
        return (unit_at // units) * rows + offset + lax.rem(unit_at, units) * unit

    def main_at(i, ctl):
        return (0, start(i, ctl) // block, 0)

    def above_at(i, ctl):
        return (0, jnp.maximum(start(i, ctl) - 1, 0) // 16, 0)

    def below_at(i, ctl):
        return (0, jnp.minimum(start(i, ctl) + unit, total - 1) // 16, 0)

    shapes, specs = split_outputs(groups, units, unit, width)
    kernel = functools.partial(
        render_kernel, groups=groups, units=units, unit=unit, block=block, rows=rows, offset=offset, total=total
    )
    cells = layers * 2 * half * unit * width
    return pl.pallas_call(
        kernel,
        grid_spec=pltpu.PrefetchScalarGridSpec(
            num_scalar_prefetch=1,
            grid=(2 * half,),
            in_specs=[
                pl.BlockSpec(memory_space=pltpu.SMEM),
                pl.BlockSpec((8, LANES), lambda i, ctl: (0, 0)),
                pl.BlockSpec((layers, block, width), main_at),
                pl.BlockSpec((layers, 16, width), above_at),
                pl.BlockSpec((layers, 16, width), below_at),
                pl.BlockSpec((1, unit, width), lambda i, ctl: (index(i, ctl), 0, 0)),
                pl.BlockSpec((1, unit, width), lambda i, ctl: (index(i, ctl), 0, 0)),
            ],
            out_specs=specs,
            scratch_shapes=[
                pltpu.VMEM((layers + 2, unit + 16, width), jnp.float32),
                pltpu.VMEM((layers, unit, width), jnp.float32),
                pltpu.VMEM((4, unit, width), jnp.float32),
                pltpu.VMEM((block, width), jnp.float32),
            ],
        ),
        out_shape=shapes,
        compiler_params=params(),
        cost_estimate=pl.CostEstimate(flops=50 * cells, bytes_accessed=6 * cells, transcendentals=cells),
        name="render",
    )(ctl, light, table, field, field, field, before, after)


def merge(ctl, mine, got, *, groups, units, unit):
    width = mine.shape[3]
    half = (groups // 2) * units
    index = unit_index(groups, units, 0)
    shapes, specs = split_outputs(groups, units, unit, width)
    cells = 4 * 2 * half * unit * width
    return pl.pallas_call(
        functools.partial(merge_kernel, groups=groups, units=units, unit=unit),
        grid_spec=pltpu.PrefetchScalarGridSpec(
            num_scalar_prefetch=1,
            grid=(2 * half,),
            in_specs=[
                pl.BlockSpec((1, 4, unit, width), lambda i, ctl: (index(i, ctl), 0, 0, 0)),
                pl.BlockSpec((1, 4 * unit + 16, width), lambda i, ctl: (index(i, ctl), 0, 0)),
            ],
            out_specs=specs,
            scratch_shapes=[pltpu.VMEM((4, unit, width), jnp.float32)],
        ),
        out_shape=shapes,
        compiler_params=params(),
        cost_estimate=pl.CostEstimate(flops=8 * cells, bytes_accessed=9 * cells, transcendentals=0),
        name="merge",
    )(ctl, mine, got)


def last_merge(ctl, mine, got, *, units, unit, blocks):
    width = mine.shape[3]
    cells = 4 * units * unit * width
    return pl.pallas_call(
        functools.partial(last_merge_kernel, unit=unit, blocks=blocks),
        grid_spec=pltpu.PrefetchScalarGridSpec(
            num_scalar_prefetch=1,
            grid=(units,),
            in_specs=[
                pl.BlockSpec((1, 4, unit, width), lambda i, ctl: (i, 0, 0, 0)),
                pl.BlockSpec((1, 4 * unit + 16, width), lambda i, ctl: (i, 0, 0)),
            ],
            out_specs=pl.BlockSpec((blocks, 1, unit + 16, 4 * width // blocks), lambda i, ctl: (0, i, 0, 0)),
            scratch_shapes=[pltpu.VMEM((4, unit, width), jnp.float32)],
        ),
        out_shape=jax.ShapeDtypeStruct((blocks, units, unit + 16, 4 * width // blocks), jnp.int16),
        compiler_params=params(),
        cost_estimate=pl.CostEstimate(flops=8 * cells, bytes_accessed=9 * cells, transcendentals=0),
        name="last_merge",
    )(ctl, mine, got)


def compose(got, *, unit):
    blocks, units = got.shape[:2]
    part = got.shape[3] // 4
    cells = 4 * units * unit * part * blocks
    return pl.pallas_call(
        functools.partial(compose_kernel, unit=unit, blocks=blocks),
        grid=(units,),
        in_specs=[pl.BlockSpec((blocks, 1, unit + 16, 4 * part), lambda i: (0, i, 0, 0))],
        out_specs=pl.BlockSpec((4, unit, part), lambda i: (0, i, 0)),
        out_shape=jax.ShapeDtypeStruct((4, units * unit, part), jnp.float32),
        compiler_params=params(),
        cost_estimate=pl.CostEstimate(flops=8 * cells, bytes_accessed=3 * cells, transcendentals=0),
        name="compose",
    )(got)


def chunk_units(units):
    return [1] * units


def per_device(field, transfer, bin_order, light_angles):
    tiles = lax.axis_size("tile")
    blocks = lax.axis_size("depth")
    devices = tiles * blocks
    layers, total, width = field.shape
    rows = total // tiles
    unit = unit_rows(rows)
    levels = tiles.bit_length() - 1

    table = jnp.take(transfer, bin_order, axis=1)
    table = table * jnp.array([[1.0], [1.0], [1.0], [0.01]], jnp.float32)
    bins = table.shape[1]
    slope = jnp.concatenate([table[:, 1:] - table[:, :-1], jnp.zeros_like(table[:, :1])], axis=1)
    table = jnp.pad(jnp.concatenate([table, slope], axis=0), ((0, 0), (0, LANES - bins)))
    azimuth, polar = light_angles[0], light_angles[1]
    light = 0.105 * jnp.stack(
        [jnp.cos(azimuth) * jnp.sin(polar), jnp.sin(azimuth) * jnp.sin(polar), jnp.cos(polar)]
    )

    tile = lax.axis_index("tile")
    bits = [((tile >> b) & 1).astype(jnp.int32) for b in range(levels)]
    controls = [jnp.stack([bits[min(b, levels - 1)], bits[max(b - 1, 0)]]) for b in range(levels + 1)]
    up = [(i, i + 1) for i in range(devices - 1)]
    down = [(j, i) for i, j in up]
    both = ("depth", "tile")
    first = field[0].reshape(tiles, rows, width)
    last = field[layers - 1].reshape(tiles, rows, width)

    pieces = []
    offset = 0
    for units in chunk_units(rows // unit):
        size = units * unit
        halo = lambda layer: layer[:, offset:offset + size].reshape(tiles * units, unit, width)
        before = lax.ppermute(halo(last), both, up)
        after = lax.ppermute(halo(first), both, down)
        send, keep = render(
            controls[0], light, table, field, before, after,
            groups=tiles, units=units, unit=unit, rows=rows, offset=offset,
        )
        groups = tiles // 2
        for level in range(levels):
            pairs = [(i, i ^ (1 << level)) for i in range(tiles)]
            got = lax.ppermute(send, "tile", pairs)
            if level + 1 < levels:
                send, keep = merge(controls[level + 1], keep, got, groups=groups, units=units, unit=unit)
                groups //= 2
        blocked = last_merge(controls[levels], keep, got, units=units, unit=unit, blocks=blocks)
        blocked = lax.all_to_all(blocked, "depth", split_axis=0, concat_axis=0, tiled=True)
        pieces.append(compose(blocked, unit=unit))
        offset += size
    return jnp.concatenate(pieces, axis=1) if len(pieces) > 1 else pieces[0]


def solution(mesh):
    in_specs = (P(("depth", "tile"), None, None), P(), P(), P())
    out_specs = P(None, "tile", "depth")
    return jax.shard_map(
        per_device, mesh=mesh, in_specs=in_specs, out_specs=out_specs, check_vma=False
    )
```

time: 1060 us -> 398 us (0.38)
  other arithmetic: 585 us -> 7.32 us
  waiting for transfers between devices: 343 us -> 50.9 us
  Pallas kernels: 0 us -> 240 us
  local copies, waits for them, and re-layouts: 111 us -> 15.9 us
  starting transfers between devices: 19.3 us -> 80.2 us
    another operation x4, other arithmetic: 521 us -> 2.49 us  [per_device(): jnp.stack([bits[min(b, levels - 1)], bits[max(b - 1, 0)]])]
    all_to_all x2 -> x3, waiting for transfers between devices: 336 us -> 5.82 us  [per_device(): lax.all_to_all(blocked, 'depth', split_axis=0, concat_axis=0, tiled=True)]
    pallas_call x0 -> x15, Pallas kernels: none -> 240 us  [the longest x3 190 us: render(): pl.pallas_call(kernel, grid_spec=pltpu.PrefetchScalarGridSpec(num_scalar_...]
    ppermute x4 -> x15, starting transfers between devices: 8.21 us -> 66.8 us  [the longest x9 50.7 us: per_device(): got = lax.ppermute(send, 'tile', pairs)]
    unnamed x14 -> x31, local copies, waits for them, and re-layouts: 51.9 us -> 8.47 us
    reduce_sum x1 -> x0, other arithmetic: 39.9 us -> none  [march(): colour = jnp.sum(emission * before[None], axis=1)]
    ppermute x4 -> x15, waiting for transfers between devices: 6.8 us -> 45.1 us  [the longest x9 43.1 us: per_device(): got = lax.ppermute(send, 'tile', pairs)]
    slice x12 -> x4, local copies, waits for them, and re-layouts: 26.2 us -> 6.08 us  [the longest x1 2.96 us: per_device(): first = field[0].reshape(tiles, rows, width)]
  transfers between devices with their start and end apart: 6 -> 18, of which waited for: 5 -> 7; matrix products, arithmetic and copies ran while one was open for 0% -> 2% of each run, Pallas kernels for 0% -> 60%
where the time goes in v1:
time: 398 us; the launch traced here: 397 us
  Pallas kernels  240 us (60%)
  starting transfers between devices  80.2 us (20%)
  waiting for transfers between devices  50.9 us (13%)
  local copies, waits for them, and re-layouts  15.9 us (4%)
  other arithmetic  7.32 us (2%)
    pallas_call x3, Pallas kernels, render(): pl.pallas_call(kernel, grid_spec=pltpu.PrefetchScalarGridSpec(num_scalar_...  190 us
    ppermute x9, starting transfers between devices, per_device(): got = lax.ppermute(send, 'tile', pairs)  50.7 us
    ppermute x9, waiting for transfers between devices, per_device(): got = lax.ppermute(send, 'tile', pairs)  43.1 us
    pallas_call x6, Pallas kernels, merge(): pl.pallas_call(functools.partial(merge_kernel, groups=groups, units=units...  31.6 us
    all_to_all x3, starting transfers between devices, per_device(): lax.all_to_all(blocked, 'depth', split_axis=0, concat_axis=0, tiled=True)  13.4 us
    ppermute x3, starting transfers between devices, per_device(): before = lax.ppermute(halo(last), both, up)  12.2 us
    pallas_call x3, Pallas kernels, last_merge(): pl.pallas_call(functools.partial(last_merge_kernel, unit=unit, blocks=blo...  10.3 us
    unnamed x31, local copies, waits for them, and re-layouts  8.47 us
  transfers between devices with their start and end apart: 18, of which 7 were waited for; matrix products, arithmetic and copies ran while one was open for 2% of the time, Pallas kernels for 60%

profile of v1, /device:TPU:0, one launch (start us, length us, event | category | flops | bytes accessed | tf_op | source)
XLA Modules:
  0.0 397.2 jit_solution(9452313539402464509)
XLA Ops:
  8.1 4.6 %collective-permute-start.10 = (bf16[8,48,1152]{2,1,0:T(8,128)(2,1)}, bf16[8,48,1152]{2,1,0:T(8,128)(2,1)}, u32[]{:S(2)}, u32[]{:S(2)}) collective-permute-start(bf16[8,48,1152]{2,1,0:T(8,128)(2,1)} %get-tuple-element.47), channel_id=1, source_target_pairs={{0,1},{1,2},{2,3},{3,4},{4,5},{5,6},{6,7},{7,8},{8,9},{9,10},{10,1... | collective-permute-start | bytes 2654216 | tf_op jit(solution)/shard_map/ppermute | solution.py:390
  12.7 4.5 %collective-permute-start.5 = (bf16[8,48,1152]{2,1,0:T(8,128)(2,1)}, bf16[8,48,1152]{2,1,0:T(8,128)(2,1)}, u32[]{:S(2)}, u32[]{:S(2)}) collective-permute-start(bf16[8,48,1152]{2,1,0:T(8,128)(2,1)} %get-tuple-element.48), channel_id=1, source_target_pairs={{0,1},{1,2},{2,3},{3,4},{4,5},{5,6},{6,7},{7,8},{8,9},{9,10},{10,1... | collective-permute-start | bytes 2654216 | tf_op jit(solution)/shard_map/ppermute | solution.py:390
  25.3 63.4 %render.4 = (s16[4,208,1152]{2,1,0:T(8,128)(2,1)}, f32[4,4,48,1152]{3,2,1,0:T(8,128)}) custom-call(s32[2]{0:T(128)} %pad_add_fusion.3.ctl, f32[3]{0:T(128)} %maximum_multiply_fusion.light, f32[8,128]{1,0:T(8,128)} %pad.5.table, bf16[6,1152,1152]{2,1,0:T(8,128)(2,1)} %below.5, bf16[6,1152,1152]{2,1,0:T(8,128)(2,1)} %below.5, bf16[6,1152,1152]{2,1,0:T(8,128)(2,1)} %below.5, ...), custom_call_target="tpu_custom_call" | custom-call | flops 132710400 | bytes 15925248 | tf_op jit(solution)/shard_map/render/pallas_call | solution.py:261
  88.7 24.1 %collective-permute-start.7 = (s16[4,208,1152]{2,1,0:T(8,128)(2,1)}, s16[4,208,1152]{2,1,0:T(8,128)(2,1)}, u32[]{:S(2)}, u32[]{:S(2)}) collective-permute-start(s16[4,208,1152]{2,1,0:T(8,128)(2,1)} %get-tuple-element.30), channel_id=1, source_target_pairs={{0,1},{1,0},{2,3},{3,2},{4,5},{5,4},{6,7},{7,6},{8,9},{9,8},{10,11... | collective-permute-start | bytes 5750792 | tf_op jit(solution)/shard_map/ppermute | solution.py:399
  113.8 63.5 %render.5 = (s16[4,208,1152]{2,1,0:T(8,128)(2,1)}, f32[4,4,48,1152]{3,2,1,0:T(8,128)}) custom-call(s32[2]{0:T(128)} %pad_add_fusion.3.ctl, f32[3]{0:T(128)} %maximum_multiply_fusion.light, f32[8,128]{1,0:T(8,128)} %pad.5.table, bf16[6,1152,1152]{2,1,0:T(8,128)(2,1)} %below.5, bf16[6,1152,1152]{2,1,0:T(8,128)(2,1)} %below.5, bf16[6,1152,1152]{2,1,0:T(8,128)(2,1)} %below.5, ...), custom_call_target="tpu_custom_call" | custom-call | flops 132710400 | bytes 15925248 | tf_op jit(solution)/shard_map/render/pallas_call | solution.py:261
  184.5 63.4 %render.3 = (s16[4,208,1152]{2,1,0:T(8,128)(2,1)}, f32[4,4,48,1152]{3,2,1,0:T(8,128)}) custom-call(s32[2]{0:T(128)} %pad_add_fusion.3.ctl, f32[3]{0:T(128)} %maximum_multiply_fusion.light, f32[8,128]{1,0:T(8,128)} %pad.5.table, bf16[6,1152,1152]{2,1,0:T(8,128)(2,1)} %below.5, bf16[6,1152,1152]{2,1,0:T(8,128)(2,1)} %below.5, bf16[6,1152,1152]{2,1,0:T(8,128)(2,1)} %below.5, ...), custom_call_target="tpu_custom_call" | custom-call | flops 132710400 | bytes 15925248 | tf_op jit(solution)/shard_map/render/pallas_call | solution.py:261
  247.9 18.1 %collective-permute-start.2 = (s16[4,208,1152]{2,1,0:T(8,128)(2,1)}, s16[4,208,1152]{2,1,0:T(8,128)(2,1)S(1)}, u32[]{:S(2)}, u32[]{:S(2)}) collective-permute-start(s16[4,208,1152]{2,1,0:T(8,128)(2,1)} %get-tuple-element.24), channel_id=1, source_target_pairs={{0,1},{1,0},{2,3},{3,2},{4,5},{5,4},{6,7},{7,6},{8,9},{9,8},{10,11... | collective-permute-start | bytes 5750792 | tf_op jit(solution)/shard_map/ppermute | solution.py:399
  266.6 6.4 %merge.8 = (s16[2,208,1152]{2,1,0:T(8,128)(2,1)}, f32[2,4,48,1152]{3,2,1,0:T(8,128)}) custom-call(s32[2]{0:T(128)} %pad_add_fusion.2.ctl, f32[4,4,48,1152]{3,2,1,0:T(8,128)} %get-tuple-element.29.mine, s16[4,208,1152]{2,1,0:T(8,128)(2,1)} %collective-permute-done.7.got), custom_call_target="tpu_custom_call" | custom-call | flops 7077888 | bytes 7962624 | tf_op jit(solution)/shard_map/merge/pallas_call | solution.py:296
  273.0 4.0 %collective-permute-start.8 = (s16[2,208,1152]{2,1,0:T(8,128)(2,1)}, s16[2,208,1152]{2,1,0:T(8,128)(2,1)}, u32[]{:S(2)}, u32[]{:S(2)}) collective-permute-start(s16[2,208,1152]{2,1,0:T(8,128)(2,1)} %get-tuple-element.32), channel_id=1, source_target_pairs={{0,2},{1,3},{2,0},{3,1},{4,6},{5,7},{6,4},{7,5},{8,10},{9,11},{10,... | collective-permute-start | bytes 2875400 | tf_op jit(solution)/shard_map/ppermute | solution.py:399
  277.1 6.4 %merge.10 = (s16[2,208,1152]{2,1,0:T(8,128)(2,1)}, f32[2,4,48,1152]{3,2,1,0:T(8,128)}) custom-call(s32[2]{0:T(128)} %pad_add_fusion.2.ctl, f32[4,4,48,1152]{3,2,1,0:T(8,128)} %get-tuple-element.35.mine, s16[4,208,1152]{2,1,0:T(8,128)(2,1)} %collective-permute-done.12.got), custom_call_target="tpu_custom_call" | custom-call | flops 7077888 | bytes 7962624 | tf_op jit(solution)/shard_map/merge/pallas_call | solution.py:296
  284.0 15.4 %collective-permute-done.8.got = s16[2,208,1152]{2,1,0:T(8,128)(2,1)} collective-permute-done((s16[2,208,1152]{2,1,0:T(8,128)(2,1)}, s16[2,208,1152]{2,1,0:T(8,128)(2,1)}, u32[]{:S(2)}, u32[]{:S(2)}) %collective-permute-start.8) | collective-permute-done | bytes 958496 | tf_op jit(solution)/shard_map/ppermute | solution.py:399
  299.4 4.2 %merge.9 = (s16[1,208,1152]{2,1,0:T(8,128)(2,1)}, f32[1,4,48,1152]{3,2,1,0:T(8,128)}) custom-call(s32[2]{0:T(128)} %pad_add_fusion.1.ctl, f32[2,4,48,1152]{3,2,1,0:T(8,128)} %get-tuple-element.31.mine, s16[2,208,1152]{2,1,0:T(8,128)(2,1)} %collective-permute-done.8.got), custom_call_target="tpu_custom_call" | custom-call | flops 3538944 | bytes 3981312 | tf_op jit(solution)/shard_map/merge/pallas_call | solution.py:296
  304.5 11.0 %collective-permute-done.9.got = s16[1,208,1152]{2,1,0:T(8,128)(2,1)S(1)} collective-permute-done((s16[1,208,1152]{2,1,0:T(8,128)(2,1)}, s16[1,208,1152]{2,1,0:T(8,128)(2,1)S(1)}, u32[]{:S(2)}, u32[]{:S(2)}) %collective-permute-start.9) | collective-permute-done | bytes 479264 | tf_op jit(solution)/shard_map/ppermute | solution.py:399
  319.7 3.8 all-to-all-start.1
  324.7 6.3 %merge.6 = (s16[2,208,1152]{2,1,0:T(8,128)(2,1)}, f32[2,4,48,1152]{3,2,1,0:T(8,128)}) custom-call(s32[2]{0:T(128)} %pad_add_fusion.2.ctl, f32[4,4,48,1152]{3,2,1,0:T(8,128)} %get-tuple-element.23.mine, s16[4,208,1152]{2,1,0:T(8,128)(2,1)} %copy-done.3), custom_call_target="tpu_custom_call" | custom-call | flops 7077888 | bytes 7962624 | tf_op jit(solution)/shard_map/merge/pallas_call | solution.py:296
  333.6 4.2 %merge.11 = (s16[1,208,1152]{2,1,0:T(8,128)(2,1)}, f32[1,4,48,1152]{3,2,1,0:T(8,128)}) custom-call(s32[2]{0:T(128)} %pad_add_fusion.1.ctl, f32[2,4,48,1152]{3,2,1,0:T(8,128)} %get-tuple-element.37.mine, s16[2,208,1152]{2,1,0:T(8,128)(2,1)} %copy-done.4), custom_call_target="tpu_custom_call" | custom-call | flops 3538944 | bytes 3981312 | tf_op jit(solution)/shard_map/merge/pallas_call | solution.py:296
  338.8 9.1 %collective-permute-done.14.got = s16[1,208,1152]{2,1,0:T(8,128)(2,1)S(1)} collective-permute-done((s16[1,208,1152]{2,1,0:T(8,128)(2,1)}, s16[1,208,1152]{2,1,0:T(8,128)(2,1)S(1)}, u32[]{:S(2)}, u32[]{:S(2)}) %collective-permute-start.14) | collective-permute-done | bytes 479264 | tf_op jit(solution)/shard_map/ppermute | solution.py:399
  348.7 3.5 last_merge.5
  352.1 4.8 %all-to-all-start.2 = ((s16[4,1,64,1152]{3,2,1,0:T(8,128)(2,1)}), s16[4,1,64,1152]{3,2,1,0:T(8,128)(2,1)S(1)}, u32[]{:S(2)}, u32[]{:S(2)}) async-start(s16[4,1,64,1152]{3,2,1,0:T(8,128)(2,1)} %last_merge.5), calls=%async_computation.2 | async-start | bytes 1179648 | tf_op jit(solution)/shard_map/all_to_all | solution.py:404
  357.9 4.2 %merge.7 = (s16[1,208,1152]{2,1,0:T(8,128)(2,1)}, f32[1,4,48,1152]{3,2,1,0:T(8,128)}) custom-call(s32[2]{0:T(128)} %pad_add_fusion.1.ctl, f32[2,4,48,1152]{3,2,1,0:T(8,128)} %get-tuple-element.25.mine, s16[2,208,1152]{2,1,0:T(8,128)(2,1)} %copy-done.5), custom_call_target="tpu_custom_call" | custom-call | flops 3538944 | bytes 3981312 | tf_op jit(solution)/shard_map/merge/pallas_call | solution.py:296
  363.8 7.6 %collective-permute-done.4.got = s16[1,208,1152]{2,1,0:T(8,128)(2,1)S(1)} collective-permute-done((s16[1,208,1152]{2,1,0:T(8,128)(2,1)}, s16[1,208,1152]{2,1,0:T(8,128)(2,1)S(1)}, u32[]{:S(2)}, u32[]{:S(2)}) %collective-permute-start.4) | collective-permute-done | bytes 479264 | tf_op jit(solution)/shard_map/ppermute | solution.py:399
  372.2 3.4 last_merge.3
  375.7 4.8 %all-to-all-start = ((s16[4,1,64,1152]{3,2,1,0:T(8,128)(2,1)}), s16[4,1,64,1152]{3,2,1,0:T(8,128)(2,1)S(1)}, u32[]{:S(2)}, u32[]{:S(2)}) async-start(s16[4,1,64,1152]{3,2,1,0:T(8,128)(2,1)} %last_merge.3), calls=%async_computation | async-start | bytes 1179648 | tf_op jit(solution)/shard_map/all_to_all | solution.py:404
  385.8 5.8 %all-to-all-done.got = s16[4,1,64,1152]{3,2,1,0:T(8,128)(2,1)S(1)} async-done(((s16[4,1,64,1152]{3,2,1,0:T(8,128)(2,1)}), s16[4,1,64,1152]{3,2,1,0:T(8,128)(2,1)S(1)}, u32[]{:S(2)}, u32[]{:S(2)}) %all-to-all-start) | async-done | bytes 589856 | tf_op jit(solution)/shard_map/all_to_all | solution.py:404
  (77 shorter events, 48.1 us)
Async XLA Ops:
  4.1 108.7 %collective-permute-start.11 = (bf16[8,48,1152]{2,1,0:T(8,128)(2,1)S(1)}, bf16[8,48,1152]{2,1,0:T(8,128)(2,1)S(1)}, u32[]{:S(2)}, u32[]{:S(2)}) collective-permute-start(bf16[8,48,1152]{2,1,0:T(8,128)(2,1)S(1)} %get-tuple-element.44), channel_id=1, source_target_pairs={{1,0},{2,1},{3,2},{4,3},{5,4},{6,5},{7,6},{8,7},{9,8},{10,9},{11,1... | collective-permute-start | bytes 2654216 | tf_op jit(solution)/shard_map/ppermute | solution.py:391
  5.4 19.9 %collective-permute-start.6 = (bf16[8,48,1152]{2,1,0:T(8,128)(2,1)}, bf16[8,48,1152]{2,1,0:T(8,128)(2,1)}, u32[]{:S(2)}, u32[]{:S(2)}) collective-permute-start(bf16[8,48,1152]{2,1,0:T(8,128)(2,1)} %get-tuple-element.45), channel_id=1, source_target_pairs={{1,0},{2,1},{3,2},{4,3},{5,4},{6,5},{7,6},{8,7},{9,8},{10,9},{11,1... | collective-permute-start | bytes 2654216 | tf_op jit(solution)/shard_map/ppermute | solution.py:391
  6.7 10.5 %copy-start.13 = (f32[2]{0:T(128)S(1)}, f32[2]{0:T(128)}, u32[]{:S(2)}) copy-start(f32[2]{0:T(128)} %param.8) | copy-start | bytes 28
  6.7 14.4 %copy-start.14 = (s32[16]{0:T(128)S(1)}, s32[16]{0:T(128)}, u32[]{:S(2)}) copy-start(s32[16]{0:T(128)} %param.7) | copy-start | bytes 196
  6.7 15.0 %copy-start.12 = (f32[4,16]{1,0:T(4,128)S(1)}, f32[4,16]{1,0:T(4,128)}, u32[]{:S(2)}) copy-start(f32[4,16]{1,0:T(4,128)} %param.6) | copy-start | bytes 772
  8.1 104.7 %collective-permute-start.10 = (bf16[8,48,1152]{2,1,0:T(8,128)(2,1)}, bf16[8,48,1152]{2,1,0:T(8,128)(2,1)}, u32[]{:S(2)}, u32[]{:S(2)}) collective-permute-start(bf16[8,48,1152]{2,1,0:T(8,128)(2,1)} %get-tuple-element.47), channel_id=1, source_target_pairs={{0,1},{1,2},{2,3},{3,4},{4,5},{5,6},{6,7},{7,8},{8,9},{9,10},{10,1... | collective-permute-start | bytes 2654216 | tf_op jit(solution)/shard_map/ppermute | solution.py:390
  12.7 12.6 %collective-permute-start.5 = (bf16[8,48,1152]{2,1,0:T(8,128)(2,1)}, bf16[8,48,1152]{2,1,0:T(8,128)(2,1)}, u32[]{:S(2)}, u32[]{:S(2)}) collective-permute-start(bf16[8,48,1152]{2,1,0:T(8,128)(2,1)} %get-tuple-element.48), channel_id=1, source_target_pairs={{0,1},{1,2},{2,3},{3,4},{4,5},{5,6},{6,7},{7,8},{8,9},{9,10},{10,1... | collective-permute-start | bytes 2654216 | tf_op jit(solution)/shard_map/ppermute | solution.py:390
  88.7 178.0 %collective-permute-start.7 = (s16[4,208,1152]{2,1,0:T(8,128)(2,1)}, s16[4,208,1152]{2,1,0:T(8,128)(2,1)}, u32[]{:S(2)}, u32[]{:S(2)}) collective-permute-start(s16[4,208,1152]{2,1,0:T(8,128)(2,1)} %get-tuple-element.30), channel_id=1, source_target_pairs={{0,1},{1,0},{2,3},{3,2},{4,5},{5,4},{6,7},{7,6},{8,9},{9,8},{10,11... | collective-permute-start | bytes 5750792 | tf_op jit(solution)/shard_map/ppermute | solution.py:399
  177.2 99.8 %collective-permute-start.12 = (s16[4,208,1152]{2,1,0:T(8,128)(2,1)}, s16[4,208,1152]{2,1,0:T(8,128)(2,1)}, u32[]{:S(2)}, u32[]{:S(2)}) collective-permute-start(s16[4,208,1152]{2,1,0:T(8,128)(2,1)} %get-tuple-element.36), channel_id=1, source_target_pairs={{0,1},{1,0},{2,3},{3,2},{4,5},{5,4},{6,7},{7,6},{8,9},{9,8},{10,11... | collective-permute-start | bytes 5750792 | tf_op jit(solution)/shard_map/ppermute | solution.py:399
  177.3 5.2 %collective-permute-start.1 = (bf16[8,48,1152]{2,1,0:T(8,128)(2,1)S(1)}, bf16[8,48,1152]{2,1,0:T(8,128)(2,1)S(1)}, u32[]{:S(2)}, u32[]{:S(2)}) collective-permute-start(bf16[8,48,1152]{2,1,0:T(8,128)(2,1)S(1)} %get-tuple-element.43), channel_id=1, source_target_pairs={{1,0},{2,1},{3,2},{4,3},{5,4},{6,5},{7,6},{8,7},{9,8},{10,9},{11,1... | collective-permute-start | bytes 2654216 | tf_op jit(solution)/shard_map/ppermute | solution.py:391
  178.5 5.1 %collective-permute-start = (bf16[8,48,1152]{2,1,0:T(8,128)(2,1)S(1)}, bf16[8,48,1152]{2,1,0:T(8,128)(2,1)S(1)}, u32[]{:S(2)}, u32[]{:S(2)}) collective-permute-start(bf16[8,48,1152]{2,1,0:T(8,128)(2,1)S(1)} %get-tuple-element.46), channel_id=1, source_target_pairs={{0,1},{1,2},{2,3},{3,4},{4,5},{5,6},{6,7},{7,8},{8,9},{9,10},{10,1... | collective-permute-start | bytes 2654216 | tf_op jit(solution)/shard_map/ppermute | solution.py:390
  247.9 75.5 %collective-permute-start.2 = (s16[4,208,1152]{2,1,0:T(8,128)(2,1)}, s16[4,208,1152]{2,1,0:T(8,128)(2,1)S(1)}, u32[]{:S(2)}, u32[]{:S(2)}) collective-permute-start(s16[4,208,1152]{2,1,0:T(8,128)(2,1)} %get-tuple-element.24), channel_id=1, source_target_pairs={{0,1},{1,0},{2,3},{3,2},{4,5},{5,4},{6,7},{7,6},{8,9},{9,8},{10,11... | collective-permute-start | bytes 5750792 | tf_op jit(solution)/shard_map/ppermute | solution.py:399
  273.0 26.3 %collective-permute-start.8 = (s16[2,208,1152]{2,1,0:T(8,128)(2,1)}, s16[2,208,1152]{2,1,0:T(8,128)(2,1)}, u32[]{:S(2)}, u32[]{:S(2)}) collective-permute-start(s16[2,208,1152]{2,1,0:T(8,128)(2,1)} %get-tuple-element.32), channel_id=1, source_target_pairs={{0,2},{1,3},{2,0},{3,1},{4,6},{5,7},{6,4},{7,5},{8,10},{9,11},{10,... | collective-permute-start | bytes 2875400 | tf_op jit(solution)/shard_map/ppermute | solution.py:399
  283.4 49.1 %collective-permute-start.13 = (s16[2,208,1152]{2,1,0:T(8,128)(2,1)}, s16[2,208,1152]{2,1,0:T(8,128)(2,1)S(1)}, u32[]{:S(2)}, u32[]{:S(2)}) collective-permute-start(s16[2,208,1152]{2,1,0:T(8,128)(2,1)} %get-tuple-element.38), channel_id=1, source_target_pairs={{0,2},{1,3},{2,0},{3,1},{4,6},{5,7},{6,4},{7,5},{8,10},{9,11},{10,... | collective-permute-start | bytes 2875400 | tf_op jit(solution)/shard_map/ppermute | solution.py:399
  303.6 11.9 %collective-permute-start.9 = (s16[1,208,1152]{2,1,0:T(8,128)(2,1)}, s16[1,208,1152]{2,1,0:T(8,128)(2,1)S(1)}, u32[]{:S(2)}, u32[]{:S(2)}) collective-permute-start(s16[1,208,1152]{2,1,0:T(8,128)(2,1)} %get-tuple-element.34), channel_id=1, source_target_pairs={{0,4},{1,5},{2,6},{3,7},{4,0},{5,1},{6,2},{7,3},{8,12},{9,13},{10,... | collective-permute-start | bytes 1437704 | tf_op jit(solution)/shard_map/ppermute | solution.py:399
  319.7 32.4 %all-to-all-start.1 = ((s16[4,1,64,1152]{3,2,1,0:T(8,128)(2,1)}), s16[4,1,64,1152]{3,2,1,0:T(8,128)(2,1)S(1)}, u32[]{:S(2)}, u32[]{:S(2)}) async-start(s16[4,1,64,1152]{3,2,1,0:T(8,128)(2,1)} %last_merge.4), calls=%async_computation.1 | async-start | bytes 1179648 | tf_op jit(solution)/shard_map/all_to_all | solution.py:404
  323.5 1.3 copy-start.3
  331.1 25.9 %collective-permute-start.3 = (s16[2,208,1152]{2,1,0:T(8,128)(2,1)}, s16[2,208,1152]{2,1,0:T(8,128)(2,1)S(1)}, u32[]{:S(2)}, u32[]{:S(2)}) collective-permute-start(s16[2,208,1152]{2,1,0:T(8,128)(2,1)} %get-tuple-element.26), channel_id=1, source_target_pairs={{0,2},{1,3},{2,0},{3,1},{4,6},{5,7},{6,4},{7,5},{8,10},{9,11},{10,... | collective-permute-start | bytes 2875400 | tf_op jit(solution)/shard_map/ppermute | solution.py:399
  337.7 10.1 %collective-permute-start.14 = (s16[1,208,1152]{2,1,0:T(8,128)(2,1)}, s16[1,208,1152]{2,1,0:T(8,128)(2,1)S(1)}, u32[]{:S(2)}, u32[]{:S(2)}) collective-permute-start(s16[1,208,1152]{2,1,0:T(8,128)(2,1)} %get-tuple-element.40), channel_id=1, source_target_pairs={{0,4},{1,5},{2,6},{3,7},{4,0},{5,1},{6,2},{7,3},{8,12},{9,13},{10,... | collective-permute-start | bytes 1437704 | tf_op jit(solution)/shard_map/ppermute | solution.py:399
  352.1 23.5 %copy-start = (s16[4,1,64,1152]{3,2,1,0:T(8,128)(2,1)}, s16[4,1,64,1152]{3,2,1,0:T(8,128)(2,1)S(1)}, u32[]{:S(2)}) copy-start(s16[4,1,64,1152]{3,2,1,0:T(8,128)(2,1)S(1)} %all-to-all-done.1.got) | copy-start | bytes 1769476
  352.1 23.5 %all-to-all-start.2 = ((s16[4,1,64,1152]{3,2,1,0:T(8,128)(2,1)}), s16[4,1,64,1152]{3,2,1,0:T(8,128)(2,1)S(1)}, u32[]{:S(2)}, u32[]{:S(2)}) async-start(s16[4,1,64,1152]{3,2,1,0:T(8,128)(2,1)} %last_merge.5), calls=%async_computation.2 | async-start | bytes 1179648 | tf_op jit(solution)/shard_map/all_to_all | solution.py:404
  362.1 9.4 %collective-permute-start.4 = (s16[1,208,1152]{2,1,0:T(8,128)(2,1)}, s16[1,208,1152]{2,1,0:T(8,128)(2,1)S(1)}, u32[]{:S(2)}, u32[]{:S(2)}) collective-permute-start(s16[1,208,1152]{2,1,0:T(8,128)(2,1)} %get-tuple-element.28), channel_id=1, source_target_pairs={{0,4},{1,5},{2,6},{3,7},{4,0},{5,1},{6,2},{7,3},{8,12},{9,13},{10,... | collective-permute-start | bytes 1437704 | tf_op jit(solution)/shard_map/ppermute | solution.py:399
  375.7 7.5 %copy-start.1 = (s16[4,1,64,1152]{3,2,1,0:T(8,128)(2,1)}, s16[4,1,64,1152]{3,2,1,0:T(8,128)(2,1)S(1)}, u32[]{:S(2)}) copy-start(s16[4,1,64,1152]{3,2,1,0:T(8,128)(2,1)S(1)} %all-to-all-done.2.got) | copy-start | bytes 1769476
  375.7 16.0 %all-to-all-start = ((s16[4,1,64,1152]{3,2,1,0:T(8,128)(2,1)}), s16[4,1,64,1152]{3,2,1,0:T(8,128)(2,1)S(1)}, u32[]{:S(2)}, u32[]{:S(2)}) async-start(s16[4,1,64,1152]{3,2,1,0:T(8,128)(2,1)} %last_merge.3), calls=%async_computation | async-start | bytes 1179648 | tf_op jit(solution)/shard_map/all_to_all | solution.py:404
  (9 other events, 8.3 us)

commit v2 on v1

--- a/solution.py
+++ b/solution.py
@@ -38,7 +38,33 @@
     return [f + clear * b for f, b in zip(front, back)]
 
 
-def render_kernel(ctl, light, table, main, above, below, before, after, send, keep, cells, slopes, image, edge, *, groups, units, unit, block, rows, offset, total):
+def lookup(table, index):
+    numbers = lax.GatherDimensionNumbers(
+        offset_dims=(), collapsed_slice_dims=(1,), start_index_map=(1,),
+        operand_batching_dims=(0,), start_indices_batching_dims=(0,),
+    )
+    return lax.gather(
+        table, index[..., None], numbers, slice_sizes=(1, 1), mode=lax.GatherScatterMode.PROMISE_IN_BOUNDS
+    )
+
+
+def padded_rows(unit):
+    return -(-unit // 16) * 16
+
+
+def each_strip(width, body):
+    strips = width // LANES
+    together = 3 if strips % 3 == 0 else 1
+
+    def step(c, carry):
+        for k in range(together):
+            body(pl.multiple_of((c * together + k) * LANES, LANES))
+        return carry
+
+    lax.fori_loop(0, strips // together, step, 0)
+
+
+def render_kernel(ctl, light, table, row_band, column_band, main, above, below, before, after, send, keep, cells, image, stage, ends, *, groups, units, unit, block, rows, offset, total):
     i = pl.program_id(0)
     half = (groups // 2) * units
     rest = lax.rem(i, half)
@@ -48,105 +74,115 @@
     start = group * rows + offset + lax.rem(rest, units) * unit
     layers = main.shape[0]
     width = main.shape[2]
-    if block == unit:
-        shift = 0
-    else:
-        shift = pl.multiple_of(lax.rem(start, block), 8)
-
-    lane = lax.broadcasted_iota(jnp.int32, (8, width), 1)
-    first_lane = lane == 0
-    last_lane = lane == width - 1
+    tall = padded_rows(unit)
+    aligned = block == unit
+    inner = slice(LANES, LANES + width)
+
+    @pl.when(i == 0)
+    def _():
+        cells[:, :, 0:LANES] = jnp.zeros((layers, tall + 32, LANES), jnp.bfloat16)
+        cells[:, :, LANES + width:] = jnp.zeros((layers, tall + 32, LANES), jnp.bfloat16)
 
     def load_layer(layer, carry):
-        if block != unit:
-            edge[...] = main[layer].astype(jnp.float32)
-        for r in range(0, unit, 16):
-            n = min(16, unit - r)
-            if block == unit:
-                wide = main[layer, r:r + n, :].astype(jnp.float32)
-            else:
-                wide = edge[pl.ds(shift + r, n), :]
-            for q in range(0, n, 8):
-                x = wide[q:q + 8]
-                left = jnp.where(first_lane, 0.0, pltpu.roll(x, 1, 1))
-                right = jnp.where(last_lane, 0.0, pltpu.roll(x, width - 1, 1))
-                cells[layer + 1, 8 + r + q:16 + r + q, :] = x
-                slopes[layer, r + q:r + q + 8, :] = right - left
         up = above[layer].astype(jnp.float32)
         down = below[layer].astype(jnp.float32)
-        if block == unit:
-            up = up[8:16]
-            down = down[0:8]
+        up = jnp.where(start > 0, up, 0.0)
+        down = jnp.where(start + unit < total, down, 0.0)
+        if aligned:
+            cells[layer, 0:16, inner] = up.astype(jnp.bfloat16)
+            cells[layer, 16:16 + unit, inner] = main[layer]
+            cells[layer, 16 + unit:32 + unit, inner] = down.astype(jnp.bfloat16)
         else:
+            shift = pl.multiple_of(lax.rem(start, block), 8)
+            stage[0:block, :] = main[layer].astype(jnp.float32)
+            body = stage[pl.ds(shift, unit), :]
             up = jnp.where(lax.rem(start, 16) == 0, up[8:16], up[0:8])
             down = jnp.where(lax.rem(start + unit, 16) == 0, down[0:8], down[8:16])
-        cells[layer + 1, 0:8, :] = jnp.where(start > 0, up, 0.0)
-        cells[layer + 1, 8 + unit:16 + unit, :] = jnp.where(start + unit < total, down, 0.0)
+            stage[0:8, :] = jnp.zeros((8, width), jnp.float32)
+            stage[8:16, :] = up
+            stage[16:16 + unit, :] = body
+            stage[16 + unit:24 + unit, :] = down
+            stage[24 + unit:tall + 32, :] = jnp.zeros((tall + 8 - unit, width), jnp.float32)
+            cells[layer, :, inner] = stage[0:tall + 32, :].astype(jnp.bfloat16)
         return carry
 
     lax.fori_loop(0, layers, load_layer, 0)
-    cells[0, 8:8 + unit, :] = before[0].astype(jnp.float32)
-    cells[layers + 1, 8:8 + unit, :] = after[0].astype(jnp.float32)
+    if not aligned:
+        ends[0, 0:unit, :] = before[0].astype(jnp.float32)
+        ends[1, 0:unit, :] = after[0].astype(jnp.float32)
 
     lx, ly, lz = light[0], light[1], light[2]
-    step = 16 if unit % 16 == 0 else 8
+    step = 16
     tables = [jnp.broadcast_to(table[k:k + 1, :], (step, LANES)) for k in range(8)]
 
     def strip(c, carry):
-        cols = pl.ds(pl.multiple_of(c * LANES, LANES), LANES)
-        for r in range(0, unit, step):
-            low = cells[0, 8 + r:8 + r + step, cols]
-            here = cells[1, 8 + r:8 + r + step, cols]
-            clear = None
-            for layer in range(layers):
-                high = cells[layer + 2, 8 + r:8 + r + step, cols]
-                gx = high - low
-                gy = cells[layer + 1, 9 + r:9 + r + step, cols] - cells[layer + 1, 7 + r:7 + r + step, cols]
-                gz = slopes[layer, r:r + step, cols]
+        at = pl.multiple_of(c * LANES, LANES)
+        cols = pl.ds(at, LANES)
+        shifted = pl.ds(pl.multiple_of(at + LANES, LANES), LANES)
+        window = pl.ds(at, 3 * LANES)
+        spans = [slice(r, r + step) for r in range(0, tall, step)]
+        inside = [slice(16 + r, 16 + r + step) for r in range(0, tall, step)]
+        if aligned:
+            low = [before[0, s, cols].astype(jnp.float32) for s in spans]
+            far = [after[0, s, cols].astype(jnp.float32) for s in spans]
+        else:
+            low = [ends[0, s, cols] for s in spans]
+            far = [ends[1, s, cols] for s in spans]
+        here = [cells[0, s, shifted].astype(jnp.float32) for s in inside]
+        clear = [None] * len(spans)
+        colour = [None] * len(spans)
+        for layer in range(layers):
+            slope_y = jnp.dot(row_band[...], cells[layer, :, shifted], preferred_element_type=jnp.float32)
+            slope_z = jnp.dot(cells[layer, 16:16 + tall, window], column_band[...], preferred_element_type=jnp.float32)
+            for n, s in enumerate(spans):
+                if layer + 1 < layers:
+                    high = cells[layer + 1, inside[n], shifted].astype(jnp.float32)
+                else:
+                    high = far[n]
+                gx = high - low[n]
+                gy = slope_y[s]
+                gz = slope_z[s]
                 facing = jnp.abs(gx * lx + gy * ly + gz * lz)
                 square = gx * gx + gy * gy + gz * gz
                 shade = 0.045 + facing * lax.rsqrt(jnp.maximum(square, 4.0))
-                position = jnp.clip(here * 2.5 + 7.5, 0.0, 15.0)
+                position = jnp.clip(here[n] * 2.5 + 7.5, 0.0, 15.0)
                 index = position.astype(jnp.int32)
                 part = position - index.astype(jnp.float32)
-                tf = [
-                    jnp.take_along_axis(tables[k], index, axis=1, mode="promise_in_bounds")
-                    + part * jnp.take_along_axis(tables[4 + k], index, axis=1, mode="promise_in_bounds")
-                    for k in range(4)
-                ]
-                if clear is None:
-                    total_colour = [tf[k] * shade for k in range(3)]
-                    clear = 1.0 - tf[3]
+                tf = [lookup(tables[k], index) + part * lookup(tables[4 + k], index) for k in range(4)]
+                if layer == 0:
+                    colour[n] = [tf[k] * shade for k in range(3)]
+                    clear[n] = 1.0 - tf[3]
                 else:
-                    seen = shade * clear
-                    total_colour = [total_colour[k] + tf[k] * seen for k in range(3)]
-                    clear = clear - clear * tf[3]
-                low, here = here, high
+                    seen = shade * clear[n]
+                    colour[n] = [colour[n][k] + tf[k] * seen for k in range(3)]
+                    clear[n] = clear[n] - clear[n] * tf[3]
+                low[n], here[n] = here[n], high
+        for n, s in enumerate(spans):
             for k in range(3):
-                image[k, r:r + step, cols] = total_colour[k]
-            image[3, r:r + step, cols] = 1.0 - clear
+                image[k, s, cols] = colour[n][k]
+            image[3, s, cols] = 1.0 - clear[n]
         return carry
 
     lax.fori_loop(0, width // LANES, strip, 0)
-    put_unit(image, send, keep, sending, unit, width)
-
-
-def put_unit(image, send, keep, sending, unit, width):
+
     @pl.when(sending)
     def _():
-        def strip(c, carry):
-            cols = pl.ds(pl.multiple_of(c * LANES, LANES), LANES)
-            codes, row = encode([image[k, :, cols] for k in range(4)])
-            for k in range(4):
-                send[0, k * unit:(k + 1) * unit, cols] = codes[k]
-            send[0, 4 * unit:4 * unit + 16, cols] = row
-            return carry
-
-        lax.fori_loop(0, width // LANES, strip, 0)
+        def put(at):
+            cols = pl.ds(at, LANES)
+            put_codes(send, [image[k, 0:unit, cols] for k in range(4)], cols, unit)
+
+        each_strip(width, put)
 
     @pl.when(jnp.logical_not(sending))
     def _():
-        keep[0] = image[...]
+        keep[0] = image[:, 0:unit, :]
+
+
+def put_codes(send, values, cols, unit):
+    codes, row = encode(values)
+    for k in range(4):
+        send[0, k * unit:(k + 1) * unit, cols] = codes[k]
+    send[0, 4 * unit:4 * unit + 16, cols] = row
 
 
 def get_unit(ctl, mine, got, cols, unit):
@@ -161,32 +197,40 @@
     return over(front, back)
 
 
-def merge_kernel(ctl, mine, got, send, keep, image, *, groups, units, unit):
+def merge_kernel(ctl, mine, got, send, keep, *, groups, units, unit):
     i = pl.program_id(0)
     width = mine.shape[3]
-
-    def strip(c, carry):
-        cols = pl.ds(pl.multiple_of(c * LANES, LANES), LANES)
+    sending = i < (groups // 2) * units
+
+    @pl.when(sending)
+    def _():
+        def put(at):
+            cols = pl.ds(at, LANES)
+            put_codes(send, get_unit(ctl, mine, got, cols, unit), cols, unit)
+
+        each_strip(width, put)
+
+    @pl.when(jnp.logical_not(sending))
+    def _():
+        def put(at):
+            cols = pl.ds(at, LANES)
+            merged = get_unit(ctl, mine, got, cols, unit)
+            for k in range(4):
+                keep[0, k, :, cols] = merged[k]
+
+        each_strip(width, put)
+
+
+def last_merge_kernel(ctl, mine, got, send, image, *, unit, blocks):
+    width = mine.shape[3]
+
+    def put(at):
+        cols = pl.ds(at, LANES)
         merged = get_unit(ctl, mine, got, cols, unit)
         for k in range(4):
             image[k, :, cols] = merged[k]
-        return carry
-
-    lax.fori_loop(0, width // LANES, strip, 0)
-    put_unit(image, send, keep, i < (groups // 2) * units, unit, width)
-
-
-def last_merge_kernel(ctl, mine, got, send, image, *, unit, blocks):
-    width = mine.shape[3]
-
-    def strip(c, carry):
-        cols = pl.ds(pl.multiple_of(c * LANES, LANES), LANES)
-        merged = get_unit(ctl, mine, got, cols, unit)
-        for k in range(4):
-            image[k, :, cols] = merged[k]
-        return carry
-
-    lax.fori_loop(0, width // LANES, strip, 0)
+
+    each_strip(width, put)
     part = width // blocks
     for b in range(blocks):
         wide = jnp.concatenate([image[k, :, b * part:(b + 1) * part] for k in range(4)], axis=1)
@@ -234,9 +278,17 @@
     return shapes, specs
 
 
+def band(shape, dim, offset):
+    place = lax.broadcasted_iota(jnp.int32, shape, dim) - lax.broadcasted_iota(jnp.int32, shape, 1 - dim) - offset
+    return jnp.where(place == 1, 1.0, jnp.where(place == -1, -1.0, 0.0)).astype(jnp.bfloat16)
+
+
 def render(ctl, light, table, field, before, after, *, groups, units, unit, rows, offset):
     layers, total, width = field.shape
     block = math.lcm(unit, 16)
+    tall = padded_rows(unit)
+    row_band = band((tall, tall + 32), 1, 16)
+    column_band = band((3 * LANES, LANES), 0, LANES)
     half = (groups // 2) * units
     index = unit_index(groups, units, 0)
 
@@ -266,6 +318,8 @@
             in_specs=[
                 pl.BlockSpec(memory_space=pltpu.SMEM),
                 pl.BlockSpec((8, LANES), lambda i, ctl: (0, 0)),
+                pl.BlockSpec((tall, tall + 32), lambda i, ctl: (0, 0)),
+                pl.BlockSpec((3 * LANES, LANES), lambda i, ctl: (0, 0)),
                 pl.BlockSpec((layers, block, width), main_at),
                 pl.BlockSpec((layers, 16, width), above_at),
                 pl.BlockSpec((layers, 16, width), below_at),
@@ -274,17 +328,17 @@
             ],
             out_specs=specs,
             scratch_shapes=[
-                pltpu.VMEM((layers + 2, unit + 16, width), jnp.float32),
-                pltpu.VMEM((layers, unit, width), jnp.float32),
-                pltpu.VMEM((4, unit, width), jnp.float32),
-                pltpu.VMEM((block, width), jnp.float32),
+                pltpu.VMEM((layers, tall + 32, width + 2 * LANES), jnp.bfloat16),
+                pltpu.VMEM((4, tall, width), jnp.float32),
+                pltpu.VMEM((max(block, tall + 32), width) if block != unit else (8, LANES), jnp.float32),
+                pltpu.VMEM((2, tall, width) if block != unit else (1, 8, LANES), jnp.float32),
             ],
         ),
         out_shape=shapes,
         compiler_params=params(),
         cost_estimate=pl.CostEstimate(flops=50 * cells, bytes_accessed=6 * cells, transcendentals=cells),
         name="render",
-    )(ctl, light, table, field, field, field, before, after)
+    )(ctl, light, table, row_band, column_band, field, field, field, before, after)
 
 
 def merge(ctl, mine, got, *, groups, units, unit):
@@ -303,7 +357,6 @@
                 pl.BlockSpec((1, 4 * unit + 16, width), lambda i, ctl: (index(i, ctl), 0, 0)),
             ],
             out_specs=specs,
-            scratch_shapes=[pltpu.VMEM((4, unit, width), jnp.float32)],
         ),
         out_shape=shapes,
         compiler_params=params(),
@@ -382,29 +435,46 @@
     first = field[0].reshape(tiles, rows, width)
     last = field[layers - 1].reshape(tiles, rows, width)
 
+    sizes = chunk_units(rows // unit)
+    count = len(sizes)
+    starts = [sum(sizes[:n]) * unit for n in range(count)]
+    halos = []
+    for n, units in enumerate(sizes):
+        def cut(layer):
+            part = layer[:, starts[n]:starts[n] + units * unit]
+            return part.reshape(tiles * units, unit, width)
+
+        ends = (cut(last), cut(first))
+        if n > 0:
+            ends, _ = lax.optimization_barrier((ends, halos[n - 1]))
+        halos.append((lax.ppermute(ends[0], both, up), lax.ppermute(ends[1], both, down)))
+
+    def exchange(send, level):
+        return lax.ppermute(send, "tile", [(i, i ^ (1 << level)) for i in range(tiles)])
+
+    merged = []
     pieces = []
-    offset = 0
-    for units in chunk_units(rows // unit):
-        size = units * unit
-        halo = lambda layer: layer[:, offset:offset + size].reshape(tiles * units, unit, width)
-        before = lax.ppermute(halo(last), both, up)
-        after = lax.ppermute(halo(first), both, down)
+    for n, units in enumerate(sizes):
+        control = controls[0]
+        if n >= 2:
+            control, _ = lax.optimization_barrier((control, merged[n - 2]))
+        before, after = halos[n]
         send, keep = render(
-            controls[0], light, table, field, before, after,
-            groups=tiles, units=units, unit=unit, rows=rows, offset=offset,
+            control, light, table, field, before, after,
+            groups=tiles, units=units, unit=unit, rows=rows, offset=starts[n],
         )
         groups = tiles // 2
-        for level in range(levels):
-            pairs = [(i, i ^ (1 << level)) for i in range(tiles)]
-            got = lax.ppermute(send, "tile", pairs)
-            if level + 1 < levels:
-                send, keep = merge(controls[level + 1], keep, got, groups=groups, units=units, unit=unit)
-                groups //= 2
+        got = exchange(send, 0)
+        for level in range(1, levels):
+            send, keep = merge(controls[level], keep, got, groups=groups, units=units, unit=unit)
+            if level == 1:
+                merged.append(send)
+            groups //= 2
+            got = exchange(send, level)
         blocked = last_merge(controls[levels], keep, got, units=units, unit=unit, blocks=blocks)
         blocked = lax.all_to_all(blocked, "depth", split_axis=0, concat_axis=0, tiled=True)
         pieces.append(compose(blocked, unit=unit))
-        offset += size
-    return jnp.concatenate(pieces, axis=1) if len(pieces) > 1 else pieces[0]
+    return jnp.concatenate(pieces, axis=1) if count > 1 else pieces[0]
 
 
 def solution(mesh):

time: 398 us -> 383 us (0.962)
  Pallas kernels: 240 us -> 227 us
  starting transfers between devices: 80.2 us -> 73.4 us
  waiting for transfers between devices: 50.9 us -> 56.2 us
    pallas_call x3, Pallas kernels: 190 us -> 179 us  [render(): pl.pallas_call(kernel, grid_spec=pltpu.PrefetchScalarGridSpec(num_scalar_...]
    ppermute x15, starting transfers between devices: 66.8 us -> 59.9 us  [the longest x9 47.2 us: exchange(): lax.ppermute(send, 'tile', [(i, i ^ 1 << level) for i in range(tiles)])]
    ppermute x15, waiting for transfers between devices: 45.1 us -> 50.4 us  [the longest x9 45.5 us: exchange(): lax.ppermute(send, 'tile', [(i, i ^ 1 << level) for i in range(tiles)])]
    unnamed x31 -> x33, local copies, waits for them, and re-layouts: 8.47 us -> 8.45 us
  transfers between devices with their start and end apart: 18 -> 18, of which waited for: 7 -> 7; matrix products, arithmetic and copies ran while one was open for 2% -> 2% of each run, Pallas kernels for 60% -> 43%
where the time goes in v2:
time: 383 us; the launch traced here: 382 us
  Pallas kernels  227 us (59%)
  starting transfers between devices  73.4 us (19%)
  waiting for transfers between devices  56.2 us (15%)
  local copies, waits for them, and re-layouts  15.8 us (4%)
  other arithmetic  6.59 us (2%)
    pallas_call x3, Pallas kernels, render(): pl.pallas_call(kernel, grid_spec=pltpu.PrefetchScalarGridSpec(num_scalar_...  179 us
    ppermute x9, starting transfers between devices, exchange(): lax.ppermute(send, 'tile', [(i, i ^ 1 << level) for i in range(tiles)])  47.2 us
    ppermute x9, waiting for transfers between devices, exchange(): lax.ppermute(send, 'tile', [(i, i ^ 1 << level) for i in range(tiles)])  45.5 us
    pallas_call x6, Pallas kernels, merge(): pl.pallas_call(functools.partial(merge_kernel, groups=groups, units=units...  29.8 us
    all_to_all x3, starting transfers between devices, per_device(): lax.all_to_all(blocked, 'depth', split_axis=0, concat_axis=0, tiled=True)  13.5 us
    pallas_call x3, Pallas kernels, last_merge(): pl.pallas_call(functools.partial(last_merge_kernel, unit=unit, blocks=blo...  10.3 us
    ppermute x3, starting transfers between devices, per_device(): lax.ppermute(ends[0], both, up)  8.8 us
    unnamed x33, local copies, waits for them, and re-layouts  8.45 us
  transfers between devices with their start and end apart: 18, of which 7 were waited for; matrix products, arithmetic and copies ran while one was open for 2% of the time, Pallas kernels for 43%

profile of v2, /device:TPU:0, one launch (start us, length us, event | category | flops | bytes accessed | tf_op | source)
XLA Modules:
  0.0 382.2 jit_solution(14021858361947830434)
XLA Ops:
  6.8 4.0 %collective-permute-start = (bf16[8,48,1152]{2,1,0:T(8,128)(2,1)}, bf16[8,48,1152]{2,1,0:T(8,128)(2,1)}, u32[]{:S(2)}, u32[]{:S(2)}) collective-permute-start(bf16[8,48,1152]{2,1,0:T(8,128)(2,1)} %get-tuple-element.58), channel_id=1, source_target_pairs={{0,1},{1,2},{2,3},{3,4},{4,5},{5,6},{6,7},{7,8},{8,9},{9,10},{10,1... | collective-permute-start | bytes 2654216 | tf_op jit(solution)/shard_map/ppermute | solution.py:450
  18.3 59.7 %render.3 = (s16[4,208,1152]{2,1,0:T(8,128)(2,1)}, f32[4,4,48,1152]{3,2,1,0:T(8,128)}) custom-call(s32[2]{0:T(128)} %pad_add_fusion.3.ctl, f32[3]{0:T(128)} %maximum_multiply_fusion.light, f32[8,128]{1,0:T(8,128)} %pad.5.table, bf16[48,80]{1,0:T(8,128)(2,1)} %select_convert_fusion.1.row_band, bf16[384,128]{1,0:T(8,128)(2,1)} %select_convert_fusion.column_band, ...), custom_call_target="tpu_custom_call" | custom-call | flops 132710400 | bytes 15925248 | tf_op jit(solution)/shard_map/render/pallas_call | solution.py:313
  78.0 12.4 %collective-permute-start.2 = (s16[4,208,1152]{2,1,0:T(8,128)(2,1)}, s16[4,208,1152]{2,1,0:T(8,128)(2,1)}, u32[]{:S(2)}, u32[]{:S(2)}) collective-permute-start(s16[4,208,1152]{2,1,0:T(8,128)(2,1)} %get-tuple-element.29), channel_id=1, source_target_pairs={{0,1},{1,0},{2,3},{3,2},{4,5},{5,4},{6,7},{7,6},{8,9},{9,8},{10,11... | collective-permute-start | bytes 5750792 | tf_op jit(solution)/shard_map/ppermute | solution.py:453
  95.2 3.4 collective-permute-done.6.after
  99.6 59.7 %render.4 = (s16[4,208,1152]{2,1,0:T(8,128)(2,1)}, f32[4,4,48,1152]{3,2,1,0:T(8,128)}) custom-call(s32[2]{0:T(128)} %pad_add_fusion.3.ctl, f32[3]{0:T(128)} %maximum_multiply_fusion.light, f32[8,128]{1,0:T(8,128)} %pad.5.table, bf16[48,80]{1,0:T(8,128)(2,1)} %select_convert_fusion.1.row_band, bf16[384,128]{1,0:T(8,128)(2,1)} %select_convert_fusion.column_band, ...), custom_call_target="tpu_custom_call" | custom-call | flops 132710400 | bytes 15925248 | tf_op jit(solution)/shard_map/render/pallas_call | solution.py:313
  159.3 16.5 %collective-permute-start.7 = (s16[4,208,1152]{2,1,0:T(8,128)(2,1)}, s16[4,208,1152]{2,1,0:T(8,128)(2,1)S(1)}, u32[]{:S(2)}, u32[]{:S(2)}) collective-permute-start(s16[4,208,1152]{2,1,0:T(8,128)(2,1)} %get-tuple-element.37), channel_id=1, source_target_pairs={{0,1},{1,0},{2,3},{3,2},{4,5},{5,4},{6,7},{7,6},{8,9},{9,8},{10,11... | collective-permute-start | bytes 5750792 | tf_op jit(solution)/shard_map/ppermute | solution.py:453
  180.6 6.0 %merge.6 = (s16[2,208,1152]{2,1,0:T(8,128)(2,1)}, f32[2,4,48,1152]{3,2,1,0:T(8,128)}) custom-call(s32[2]{0:T(128)} %pad_add_fusion.2.ctl, f32[4,4,48,1152]{3,2,1,0:T(8,128)} %get-tuple-element.28.mine, s16[4,208,1152]{2,1,0:T(8,128)(2,1)} %collective-permute-done.2.got), custom_call_target="tpu_custom_call" | custom-call | flops 7077888 | bytes 7962624 | tf_op jit(solution)/shard_map/merge/pallas_call | solution.py:350
  186.7 59.8 %render.5 = (s16[4,208,1152]{2,1,0:T(8,128)(2,1)}, f32[4,4,48,1152]{3,2,1,0:T(8,128)}) custom-call(s32[2]{0:T(128)} %pad_add_fusion.3.ctl, f32[3]{0:T(128)} %maximum_multiply_fusion.light, f32[8,128]{1,0:T(8,128)} %pad.5.table, bf16[48,80]{1,0:T(8,128)(2,1)} %select_convert_fusion.1.row_band, bf16[384,128]{1,0:T(8,128)(2,1)} %select_convert_fusion.column_band, ...), custom_call_target="tpu_custom_call" | custom-call | flops 132710400 | bytes 15925248 | tf_op jit(solution)/shard_map/render/pallas_call | solution.py:313
  246.5 13.8 %collective-permute-start.12 = (s16[4,208,1152]{2,1,0:T(8,128)(2,1)}, s16[4,208,1152]{2,1,0:T(8,128)(2,1)}, u32[]{:S(2)}, u32[]{:S(2)}) collective-permute-start(s16[4,208,1152]{2,1,0:T(8,128)(2,1)} %get-tuple-element.46), channel_id=1, source_target_pairs={{0,1},{1,0},{2,3},{3,2},{4,5},{5,4},{6,7},{7,6},{8,9},{9,8},{10,11... | collective-permute-start | bytes 5750792 | tf_op jit(solution)/shard_map/ppermute | solution.py:453
  263.6 6.0 %merge.8 = (s16[2,208,1152]{2,1,0:T(8,128)(2,1)}, f32[2,4,48,1152]{3,2,1,0:T(8,128)}) custom-call(s32[2]{0:T(128)} %pad_add_fusion.2.ctl, f32[4,4,48,1152]{3,2,1,0:T(8,128)} %get-tuple-element.36.mine, s16[4,208,1152]{2,1,0:T(8,128)(2,1)} %copy-done.3), custom_call_target="tpu_custom_call" | custom-call | flops 7077888 | bytes 7962624 | tf_op jit(solution)/shard_map/merge/pallas_call | solution.py:350
  270.3 14.2 %collective-permute-done.3.got = s16[2,208,1152]{2,1,0:T(8,128)(2,1)S(1)} collective-permute-done((s16[2,208,1152]{2,1,0:T(8,128)(2,1)}, s16[2,208,1152]{2,1,0:T(8,128)(2,1)S(1)}, u32[]{:S(2)}, u32[]{:S(2)}) %collective-permute-start.3) | collective-permute-done | bytes 958496 | tf_op jit(solution)/shard_map/ppermute | solution.py:453
  285.5 3.9 %merge.7 = (s16[1,208,1152]{2,1,0:T(8,128)(2,1)}, f32[1,4,48,1152]{3,2,1,0:T(8,128)}) custom-call(s32[2]{0:T(128)} %pad_add_fusion.1.ctl, f32[2,4,48,1152]{3,2,1,0:T(8,128)} %get-tuple-element.30.mine, s16[2,208,1152]{2,1,0:T(8,128)(2,1)} %copy-done.6), custom_call_target="tpu_custom_call" | custom-call | flops 3538944 | bytes 3981312 | tf_op jit(solution)/shard_map/merge/pallas_call | solution.py:350
  290.0 12.0 %collective-permute-done.4.got = s16[1,208,1152]{2,1,0:T(8,128)(2,1)S(1)} collective-permute-done((s16[1,208,1152]{2,1,0:T(8,128)(2,1)}, s16[1,208,1152]{2,1,0:T(8,128)(2,1)S(1)}, u32[]{:S(2)}, u32[]{:S(2)}) %collective-permute-start.4) | collective-permute-done | bytes 479264 | tf_op jit(solution)/shard_map/ppermute | solution.py:453
  302.8 3.4 last_merge.3
  306.2 3.9 %all-to-all-start = ((s16[4,1,64,1152]{3,2,1,0:T(8,128)(2,1)}), s16[4,1,64,1152]{3,2,1,0:T(8,128)(2,1)S(1)}, u32[]{:S(2)}, u32[]{:S(2)}) async-start(s16[4,1,64,1152]{3,2,1,0:T(8,128)(2,1)} %last_merge.3), calls=%async_computation | async-start | bytes 1179648 | tf_op jit(solution)/shard_map/all_to_all | solution.py:475
  310.1 6.1 %merge.10 = (s16[2,208,1152]{2,1,0:T(8,128)(2,1)}, f32[2,4,48,1152]{3,2,1,0:T(8,128)}) custom-call(s32[2]{0:T(128)} %pad_add_fusion.2.ctl, f32[4,4,48,1152]{3,2,1,0:T(8,128)} %get-tuple-element.45.mine, s16[4,208,1152]{2,1,0:T(8,128)(2,1)} %collective-permute-done.12.got), custom_call_target="tpu_custom_call" | custom-call | flops 7077888 | bytes 7962624 | tf_op jit(solution)/shard_map/merge/pallas_call | solution.py:350
  318.7 3.9 %merge.9 = (s16[1,208,1152]{2,1,0:T(8,128)(2,1)}, f32[1,4,48,1152]{3,2,1,0:T(8,128)}) custom-call(s32[2]{0:T(128)} %pad_add_fusion.1.ctl, f32[2,4,48,1152]{3,2,1,0:T(8,128)} %get-tuple-element.38.mine, s16[2,208,1152]{2,1,0:T(8,128)(2,1)} %copy-done.4), custom_call_target="tpu_custom_call" | custom-call | flops 3538944 | bytes 3981312 | tf_op jit(solution)/shard_map/merge/pallas_call | solution.py:350
  322.8 10.5 %collective-permute-done.9.got = s16[1,208,1152]{2,1,0:T(8,128)(2,1)S(1)} collective-permute-done((s16[1,208,1152]{2,1,0:T(8,128)(2,1)}, s16[1,208,1152]{2,1,0:T(8,128)(2,1)S(1)}, u32[]{:S(2)}, u32[]{:S(2)}) %collective-permute-start.9) | collective-permute-done | bytes 479264 | tf_op jit(solution)/shard_map/ppermute | solution.py:453
  334.1 3.4 last_merge.4
  337.6 4.8 %all-to-all-start.1 = ((s16[4,1,64,1152]{3,2,1,0:T(8,128)(2,1)}), s16[4,1,64,1152]{3,2,1,0:T(8,128)(2,1)S(1)}, u32[]{:S(2)}, u32[]{:S(2)}) async-start(s16[4,1,64,1152]{3,2,1,0:T(8,128)(2,1)} %last_merge.4), calls=%async_computation.1 | async-start | bytes 1179648 | tf_op jit(solution)/shard_map/all_to_all | solution.py:475
  343.3 3.9 %merge.11 = (s16[1,208,1152]{2,1,0:T(8,128)(2,1)}, f32[1,4,48,1152]{3,2,1,0:T(8,128)}) custom-call(s32[2]{0:T(128)} %pad_add_fusion.1.ctl, f32[2,4,48,1152]{3,2,1,0:T(8,128)} %get-tuple-element.47.mine, s16[2,208,1152]{2,1,0:T(8,128)(2,1)} %copy-done.5), custom_call_target="tpu_custom_call" | custom-call | flops 3538944 | bytes 3981312 | tf_op jit(solution)/shard_map/merge/pallas_call | solution.py:350
  347.8 8.7 %collective-permute-done.14.got = s16[1,208,1152]{2,1,0:T(8,128)(2,1)S(1)} collective-permute-done((s16[1,208,1152]{2,1,0:T(8,128)(2,1)}, s16[1,208,1152]{2,1,0:T(8,128)(2,1)S(1)}, u32[]{:S(2)}, u32[]{:S(2)}) %collective-permute-start.14) | collective-permute-done | bytes 479264 | tf_op jit(solution)/shard_map/ppermute | solution.py:453
  360.7 4.8 %all-to-all-start.2 = ((s16[4,1,64,1152]{3,2,1,0:T(8,128)(2,1)}), s16[4,1,64,1152]{3,2,1,0:T(8,128)(2,1)S(1)}, u32[]{:S(2)}, u32[]{:S(2)}) async-start(s16[4,1,64,1152]{3,2,1,0:T(8,128)(2,1)} %last_merge.5), calls=%async_computation.2 | async-start | bytes 1179648 | tf_op jit(solution)/shard_map/all_to_all | solution.py:475
  370.9 5.8 %all-to-all-done.2.got = s16[4,1,64,1152]{3,2,1,0:T(8,128)(2,1)S(1)} async-done(((s16[4,1,64,1152]{3,2,1,0:T(8,128)(2,1)}), s16[4,1,64,1152]{3,2,1,0:T(8,128)(2,1)S(1)}, u32[]{:S(2)}, u32[]{:S(2)}) %all-to-all-start.2) | async-done | bytes 589856 | tf_op jit(solution)/shard_map/all_to_all | solution.py:475
  (81 shorter events, 48.5 us)
Async XLA Ops:
  4.1 14.2 %collective-permute-start.1 = (bf16[8,48,1152]{2,1,0:T(8,128)(2,1)}, bf16[8,48,1152]{2,1,0:T(8,128)(2,1)}, u32[]{:S(2)}, u32[]{:S(2)}) collective-permute-start(bf16[8,48,1152]{2,1,0:T(8,128)(2,1)} %get-tuple-element.55), channel_id=1, source_target_pairs={{1,0},{2,1},{3,2},{4,3},{5,4},{6,5},{7,6},{8,7},{9,8},{10,9},{11,1... | collective-permute-start | bytes 2654216 | tf_op jit(solution)/shard_map/ppermute | solution.py:450
  5.4 5.4 %copy-start.15 = (s32[16]{0:T(128)S(1)}, s32[16]{0:T(128)}, u32[]{:S(2)}) copy-start(s32[16]{0:T(128)} %param.7) | copy-start | bytes 196
  5.4 5.5 %copy-start.12 = (f32[4,16]{1,0:T(4,128)S(1)}, f32[4,16]{1,0:T(4,128)}, u32[]{:S(2)}) copy-start(f32[4,16]{1,0:T(4,128)} %param.6) | copy-start | bytes 772
  5.4 6.2 %copy-start.14 = (f32[4]{0:T(128)S(1)}, f32[4]{0:T(128)}, u32[]{:S(2)}) copy-start(f32[4]{0:T(128)} %constant.54) | copy-start | bytes 52
  5.4 6.2 %copy-start.13 = (f32[2]{0:T(128)S(1)}, f32[2]{0:T(128)}, u32[]{:S(2)}) copy-start(f32[2]{0:T(128)} %param.8) | copy-start | bytes 28
  6.8 11.4 %collective-permute-start = (bf16[8,48,1152]{2,1,0:T(8,128)(2,1)}, bf16[8,48,1152]{2,1,0:T(8,128)(2,1)}, u32[]{:S(2)}, u32[]{:S(2)}) collective-permute-start(bf16[8,48,1152]{2,1,0:T(8,128)(2,1)} %get-tuple-element.58), channel_id=1, source_target_pairs={{0,1},{1,2},{2,3},{3,4},{4,5},{5,6},{6,7},{7,8},{8,9},{9,10},{10,1... | collective-permute-start | bytes 2654216 | tf_op jit(solution)/shard_map/ppermute | solution.py:450
  78.0 102.6 %collective-permute-start.2 = (s16[4,208,1152]{2,1,0:T(8,128)(2,1)}, s16[4,208,1152]{2,1,0:T(8,128)(2,1)}, u32[]{:S(2)}, u32[]{:S(2)}) collective-permute-start(s16[4,208,1152]{2,1,0:T(8,128)(2,1)} %get-tuple-element.29), channel_id=1, source_target_pairs={{0,1},{1,0},{2,3},{3,2},{4,5},{5,4},{6,7},{7,6},{8,9},{9,8},{10,11... | collective-permute-start | bytes 5750792 | tf_op jit(solution)/shard_map/ppermute | solution.py:453
  90.4 4.8 %collective-permute-start.5 = (bf16[8,48,1152]{2,1,0:T(8,128)(2,1)S(1)}, bf16[8,48,1152]{2,1,0:T(8,128)(2,1)S(1)}, u32[]{:S(2)}, u32[]{:S(2)}) collective-permute-start(bf16[8,48,1152]{2,1,0:T(8,128)(2,1)S(1)} %get-tuple-element.34), channel_id=1, source_target_pairs={{0,1},{1,2},{2,3},{3,4},{4,5},{5,6},{6,7},{7,8},{8,9},{9,10},{10,1... | collective-permute-start | bytes 2654216 | tf_op jit(solution)/shard_map/ppermute | solution.py:450
  92.4 6.2 %collective-permute-start.6 = (bf16[8,48,1152]{2,1,0:T(8,128)(2,1)S(1)}, bf16[8,48,1152]{2,1,0:T(8,128)(2,1)S(1)}, u32[]{:S(2)}, u32[]{:S(2)}) collective-permute-start(bf16[8,48,1152]{2,1,0:T(8,128)(2,1)S(1)} %get-tuple-element.35), channel_id=1, source_target_pairs={{1,0},{2,1},{3,2},{4,3},{5,4},{6,5},{7,6},{8,7},{9,8},{10,9},{11,1... | collective-permute-start | bytes 2654216 | tf_op jit(solution)/shard_map/ppermute | solution.py:450
  159.3 102.9 %collective-permute-start.7 = (s16[4,208,1152]{2,1,0:T(8,128)(2,1)}, s16[4,208,1152]{2,1,0:T(8,128)(2,1)S(1)}, u32[]{:S(2)}, u32[]{:S(2)}) collective-permute-start(s16[4,208,1152]{2,1,0:T(8,128)(2,1)} %get-tuple-element.37), channel_id=1, source_target_pairs={{0,1},{1,0},{2,3},{3,2},{4,5},{5,4},{6,7},{7,6},{8,9},{9,8},{10,11... | collective-permute-start | bytes 5750792 | tf_op jit(solution)/shard_map/ppermute | solution.py:453
  175.8 10.9 %collective-permute-start.10 = (bf16[8,48,1152]{2,1,0:T(8,128)(2,1)}, bf16[8,48,1152]{2,1,0:T(8,128)(2,1)}, u32[]{:S(2)}, u32[]{:S(2)}) collective-permute-start(bf16[8,48,1152]{2,1,0:T(8,128)(2,1)} %get-tuple-element.43), channel_id=1, source_target_pairs={{0,1},{1,2},{2,3},{3,4},{4,5},{5,6},{6,7},{7,8},{8,9},{9,10},{10,1... | collective-permute-start | bytes 2654216 | tf_op jit(solution)/shard_map/ppermute | solution.py:450
  178.7 8.0 %collective-permute-start.11 = (bf16[8,48,1152]{2,1,0:T(8,128)(2,1)S(1)}, bf16[8,48,1152]{2,1,0:T(8,128)(2,1)}, u32[]{:S(2)}, u32[]{:S(2)}) collective-permute-start(bf16[8,48,1152]{2,1,0:T(8,128)(2,1)S(1)} %get-tuple-element.44), channel_id=1, source_target_pairs={{1,0},{2,1},{3,2},{4,3},{5,4},{6,5},{7,6},{8,7},{9,8},{10,9},{11,1... | collective-permute-start | bytes 2654216 | tf_op jit(solution)/shard_map/ppermute | solution.py:450
  246.5 63.6 %collective-permute-start.12 = (s16[4,208,1152]{2,1,0:T(8,128)(2,1)}, s16[4,208,1152]{2,1,0:T(8,128)(2,1)}, u32[]{:S(2)}, u32[]{:S(2)}) collective-permute-start(s16[4,208,1152]{2,1,0:T(8,128)(2,1)} %get-tuple-element.46), channel_id=1, source_target_pairs={{0,1},{1,0},{2,3},{3,2},{4,5},{5,4},{6,7},{7,6},{8,9},{9,8},{10,11... | collective-permute-start | bytes 5750792 | tf_op jit(solution)/shard_map/ppermute | solution.py:453
  260.3 24.2 %collective-permute-start.3 = (s16[2,208,1152]{2,1,0:T(8,128)(2,1)}, s16[2,208,1152]{2,1,0:T(8,128)(2,1)S(1)}, u32[]{:S(2)}, u32[]{:S(2)}) collective-permute-start(s16[2,208,1152]{2,1,0:T(8,128)(2,1)} %get-tuple-element.31), channel_id=1, source_target_pairs={{0,2},{1,3},{2,0},{3,1},{4,6},{5,7},{6,4},{7,5},{8,10},{9,11},{10,... | collective-permute-start | bytes 2875400 | tf_op jit(solution)/shard_map/ppermute | solution.py:453
  269.6 48.1 %collective-permute-start.8 = (s16[2,208,1152]{2,1,0:T(8,128)(2,1)}, s16[2,208,1152]{2,1,0:T(8,128)(2,1)S(1)}, u32[]{:S(2)}, u32[]{:S(2)}) collective-permute-start(s16[2,208,1152]{2,1,0:T(8,128)(2,1)} %get-tuple-element.39), channel_id=1, source_target_pairs={{0,2},{1,3},{2,0},{3,1},{4,6},{5,7},{6,4},{7,5},{8,10},{9,11},{10,... | collective-permute-start | bytes 2875400 | tf_op jit(solution)/shard_map/ppermute | solution.py:453
  289.4 12.6 %collective-permute-start.4 = (s16[1,208,1152]{2,1,0:T(8,128)(2,1)}, s16[1,208,1152]{2,1,0:T(8,128)(2,1)S(1)}, u32[]{:S(2)}, u32[]{:S(2)}) collective-permute-start(s16[1,208,1152]{2,1,0:T(8,128)(2,1)} %get-tuple-element.33), channel_id=1, source_target_pairs={{0,4},{1,5},{2,6},{3,7},{4,0},{5,1},{6,2},{7,3},{8,12},{9,13},{10,... | collective-permute-start | bytes 1437704 | tf_op jit(solution)/shard_map/ppermute | solution.py:453
  306.2 31.3 %all-to-all-start = ((s16[4,1,64,1152]{3,2,1,0:T(8,128)(2,1)}), s16[4,1,64,1152]{3,2,1,0:T(8,128)(2,1)S(1)}, u32[]{:S(2)}, u32[]{:S(2)}) async-start(s16[4,1,64,1152]{3,2,1,0:T(8,128)(2,1)} %last_merge.3), calls=%async_computation | async-start | bytes 1179648 | tf_op jit(solution)/shard_map/all_to_all | solution.py:475
  316.1 26.2 %collective-permute-start.13 = (s16[2,208,1152]{2,1,0:T(8,128)(2,1)}, s16[2,208,1152]{2,1,0:T(8,128)(2,1)S(1)}, u32[]{:S(2)}, u32[]{:S(2)}) collective-permute-start(s16[2,208,1152]{2,1,0:T(8,128)(2,1)} %get-tuple-element.48), channel_id=1, source_target_pairs={{0,2},{1,3},{2,0},{3,1},{4,6},{5,7},{6,4},{7,5},{8,10},{9,11},{10,... | collective-permute-start | bytes 2875400 | tf_op jit(solution)/shard_map/ppermute | solution.py:453
  322.6 10.8 %collective-permute-start.9 = (s16[1,208,1152]{2,1,0:T(8,128)(2,1)}, s16[1,208,1152]{2,1,0:T(8,128)(2,1)S(1)}, u32[]{:S(2)}, u32[]{:S(2)}) collective-permute-start(s16[1,208,1152]{2,1,0:T(8,128)(2,1)} %get-tuple-element.41), channel_id=1, source_target_pairs={{0,4},{1,5},{2,6},{3,7},{4,0},{5,1},{6,2},{7,3},{8,12},{9,13},{10,... | collective-permute-start | bytes 1437704 | tf_op jit(solution)/shard_map/ppermute | solution.py:453
  337.6 23.2 %copy-start = (s16[4,1,64,1152]{3,2,1,0:T(8,128)(2,1)}, s16[4,1,64,1152]{3,2,1,0:T(8,128)(2,1)S(1)}, u32[]{:S(2)}) copy-start(s16[4,1,64,1152]{3,2,1,0:T(8,128)(2,1)S(1)} %all-to-all-done.got) | copy-start | bytes 1769476
  337.6 23.2 %all-to-all-start.1 = ((s16[4,1,64,1152]{3,2,1,0:T(8,128)(2,1)}), s16[4,1,64,1152]{3,2,1,0:T(8,128)(2,1)S(1)}, u32[]{:S(2)}, u32[]{:S(2)}) async-start(s16[4,1,64,1152]{3,2,1,0:T(8,128)(2,1)} %last_merge.4), calls=%async_computation.1 | async-start | bytes 1179648 | tf_op jit(solution)/shard_map/all_to_all | solution.py:475
  347.2 9.3 %collective-permute-start.14 = (s16[1,208,1152]{2,1,0:T(8,128)(2,1)}, s16[1,208,1152]{2,1,0:T(8,128)(2,1)S(1)}, u32[]{:S(2)}, u32[]{:S(2)}) collective-permute-start(s16[1,208,1152]{2,1,0:T(8,128)(2,1)} %get-tuple-element.50), channel_id=1, source_target_pairs={{0,4},{1,5},{2,6},{3,7},{4,0},{5,1},{6,2},{7,3},{8,12},{9,13},{10,... | collective-permute-start | bytes 1437704 | tf_op jit(solution)/shard_map/ppermute | solution.py:453
  360.7 7.5 %copy-start.1 = (s16[4,1,64,1152]{3,2,1,0:T(8,128)(2,1)}, s16[4,1,64,1152]{3,2,1,0:T(8,128)(2,1)S(1)}, u32[]{:S(2)}) copy-start(s16[4,1,64,1152]{3,2,1,0:T(8,128)(2,1)S(1)} %all-to-all-done.1.got) | copy-start | bytes 1769476
  360.7 15.9 %all-to-all-start.2 = ((s16[4,1,64,1152]{3,2,1,0:T(8,128)(2,1)}), s16[4,1,64,1152]{3,2,1,0:T(8,128)(2,1)S(1)}, u32[]{:S(2)}, u32[]{:S(2)}) async-start(s16[4,1,64,1152]{3,2,1,0:T(8,128)(2,1)} %last_merge.5), calls=%async_computation.2 | async-start | bytes 1179648 | tf_op jit(solution)/shard_map/all_to_all | solution.py:475
  (10 other events, 11.8 us)

commit v3 on v2

--- a/solution.py
+++ b/solution.py
@@ -38,14 +38,10 @@
     return [f + clear * b for f, b in zip(front, back)]
 
 
-def lookup(table, index):
-    numbers = lax.GatherDimensionNumbers(
-        offset_dims=(), collapsed_slice_dims=(1,), start_index_map=(1,),
-        operand_batching_dims=(0,), start_indices_batching_dims=(0,),
-    )
-    return lax.gather(
-        table, index[..., None], numbers, slice_sizes=(1, 1), mode=lax.GatherScatterMode.PROMISE_IN_BOUNDS
-    )
+def choose(bins, whole):
+    place = whole.astype(jnp.bfloat16)
+    one, zero = jnp.ones_like(place), jnp.zeros_like(place)
+    return jnp.concatenate([jnp.where(place == k, one, zero) for k in range(bins)], axis=0)
 
 
 def padded_rows(unit):
@@ -113,7 +109,7 @@
 
     lx, ly, lz = light[0], light[1], light[2]
     step = 16
-    tables = [jnp.broadcast_to(table[k:k + 1, :], (step, LANES)) for k in range(8)]
+    bins = table.shape[1] // (2 * step)
 
     def strip(c, carry):
         at = pl.multiple_of(c * LANES, LANES)
@@ -131,32 +127,44 @@
         here = [cells[0, s, shifted].astype(jnp.float32) for s in inside]
         clear = [None] * len(spans)
         colour = [None] * len(spans)
-        for layer in range(layers):
-            slope_y = jnp.dot(row_band[...], cells[layer, :, shifted], preferred_element_type=jnp.float32)
-            slope_z = jnp.dot(cells[layer, 16:16 + tall, window], column_band[...], preferred_element_type=jnp.float32)
+        for first in range(0, layers, 2):
+            pair = range(first, min(first + 2, layers))
+            slope_y = [jnp.dot(row_band[...], cells[l, :, shifted], preferred_element_type=jnp.float32) for l in pair]
+            slope_z = [jnp.dot(cells[l, 16:16 + tall, window], column_band[...], preferred_element_type=jnp.float32) for l in pair]
             for n, s in enumerate(spans):
-                if layer + 1 < layers:
-                    high = cells[layer + 1, inside[n], shifted].astype(jnp.float32)
-                else:
-                    high = far[n]
-                gx = high - low[n]
-                gy = slope_y[s]
-                gz = slope_z[s]
-                facing = jnp.abs(gx * lx + gy * ly + gz * lz)
-                square = gx * gx + gy * gy + gz * gz
-                shade = 0.045 + facing * lax.rsqrt(jnp.maximum(square, 4.0))
-                position = jnp.clip(here[n] * 2.5 + 7.5, 0.0, 15.0)
-                index = position.astype(jnp.int32)
-                part = position - index.astype(jnp.float32)
-                tf = [lookup(tables[k], index) + part * lookup(tables[4 + k], index) for k in range(4)]
-                if layer == 0:
-                    colour[n] = [tf[k] * shade for k in range(3)]
-                    clear[n] = 1.0 - tf[3]
-                else:
-                    seen = shade * clear[n]
-                    colour[n] = [colour[n][k] + tf[k] * seen for k in range(3)]
-                    clear[n] = clear[n] - clear[n] * tf[3]
-                low[n], here[n] = here[n], high
+                parts, picks, shades = [], [], []
+                for m, layer in enumerate(pair):
+                    if layer + 1 < layers:
+                        high = cells[layer + 1, inside[n], shifted].astype(jnp.float32)
+                    else:
+                        high = far[n]
+                    position = jnp.clip(here[n] * 2.5 + 7.5, 0.0, 15.0)
+                    whole = jnp.floor(position)
+                    parts.append(position - whole)
+                    picks.append(choose(bins, whole))
+                    gx = high - low[n]
+                    gy = slope_y[m][s]
+                    gz = slope_z[m][s]
+                    facing = jnp.abs(gx * lx + gy * ly + gz * lz)
+                    square = gx * gx + gy * gy + gz * gz
+                    shades.append(0.045 + facing * lax.rsqrt(jnp.maximum(square, 4.0)))
+                    low[n], here[n] = here[n], high
+                pick = jnp.concatenate(picks, axis=1) if len(picks) > 1 else picks[0]
+                found = jnp.dot(table[...], jnp.concatenate([pick, pick], axis=0), preferred_element_type=jnp.float32)
+                for m, layer in enumerate(pair):
+                    lanes = slice(m * LANES, (m + 1) * LANES)
+                    tf = [
+                        found[k * step:(k + 1) * step, lanes] + parts[m] * found[(4 + k) * step:(5 + k) * step, lanes]
+                        for k in range(4)
+                    ]
+                    shade = shades[m]
+                    if layer == 0:
+                        colour[n] = [tf[k] * shade for k in range(3)]
+                        clear[n] = 1.0 - tf[3]
+                    else:
+                        seen = shade * clear[n]
+                        colour[n] = [colour[n][k] + tf[k] * seen for k in range(3)]
+                        clear[n] = clear[n] - clear[n] * tf[3]
         for n, s in enumerate(spans):
             for k in range(3):
                 image[k, s, cols] = colour[n][k]
@@ -317,7 +325,7 @@
             grid=(2 * half,),
             in_specs=[
                 pl.BlockSpec(memory_space=pltpu.SMEM),
-                pl.BlockSpec((8, LANES), lambda i, ctl: (0, 0)),
+                pl.BlockSpec(table.shape, lambda i, ctl: (0, 0)),
                 pl.BlockSpec((tall, tall + 32), lambda i, ctl: (0, 0)),
                 pl.BlockSpec((3 * LANES, LANES), lambda i, ctl: (0, 0)),
                 pl.BlockSpec((layers, block, width), main_at),
@@ -336,7 +344,7 @@
         ),
         out_shape=shapes,
         compiler_params=params(),
-        cost_estimate=pl.CostEstimate(flops=50 * cells, bytes_accessed=6 * cells, transcendentals=cells),
+        cost_estimate=pl.CostEstimate(flops=16384 * cells, bytes_accessed=6 * cells, transcendentals=cells),
         name="render",
     )(ctl, light, table, row_band, column_band, field, field, field, before, after)
 
@@ -420,7 +428,11 @@
     table = table * jnp.array([[1.0], [1.0], [1.0], [0.01]], jnp.float32)
     bins = table.shape[1]
     slope = jnp.concatenate([table[:, 1:] - table[:, :-1], jnp.zeros_like(table[:, :1])], axis=1)
-    table = jnp.pad(jnp.concatenate([table, slope], axis=0), ((0, 0), (0, LANES - bins)))
+    table = jnp.concatenate([table, slope], axis=0)
+    spread = jnp.eye(16, dtype=jnp.float32)
+    table = (table[:, None, :, None] * spread[None, :, None, :]).reshape(8 * 16, bins * 16)
+    coarse = lax.reduce_precision(table, exponent_bits=8, mantissa_bits=7)
+    table = jnp.concatenate([coarse, table - coarse], axis=1).astype(jnp.bfloat16)
     azimuth, polar = light_angles[0], light_angles[1]
     light = 0.105 * jnp.stack(
         [jnp.cos(azimuth) * jnp.sin(polar), jnp.sin(azimuth) * jnp.sin(polar), jnp.cos(polar)]

time: 383 us -> 351 us (0.916)
  starting transfers between devices: 73.4 us -> 49.9 us
  waiting for transfers between devices: 56.2 us -> 48.8 us
  Pallas kernels: 227 us -> 223 us
    ppermute x9, starting transfers between devices: 47.2 us -> 11.9 us  [exchange(): lax.ppermute(send, 'tile', [(i, i ^ 1 << level) for i in range(tiles)])]
    ppermute x3, starting transfers between devices: 8.8 us -> 19.2 us  [per_device(): lax.ppermute(ends[0], both, up)]
    pallas_call x3, Pallas kernels: 179 us -> 175 us  [render(): pl.pallas_call(kernel, grid_spec=pltpu.PrefetchScalarGridSpec(num_scalar_...]
    unnamed x33 -> x37, local copies, waits for them, and re-layouts: 8.45 us -> 9.75 us
  transfers between devices with their start and end apart: 18 -> 18, of which waited for: 7 -> 5; matrix products, arithmetic and copies ran while one was open for 2% -> 2% of each run, Pallas kernels for 43% -> 63%
where the time goes in v3:
time: 351 us; the launch traced here: 349 us
  Pallas kernels  223 us (64%)
  starting transfers between devices  49.9 us (14%)
  waiting for transfers between devices  48.8 us (14%)
  local copies, waits for them, and re-layouts  17.2 us (5%)
  other arithmetic  7.41 us (2%)
    pallas_call x3, Pallas kernels, render(): pl.pallas_call(kernel, grid_spec=pltpu.PrefetchScalarGridSpec(num_scalar_...  175 us
    ppermute x9, waiting for transfers between devices, exchange(): lax.ppermute(send, 'tile', [(i, i ^ 1 << level) for i in range(tiles)])  43.2 us
    pallas_call x6, Pallas kernels, merge(): pl.pallas_call(functools.partial(merge_kernel, groups=groups, units=units...  29.8 us
    ppermute x3, starting transfers between devices, per_device(): lax.ppermute(ends[0], both, up)  19.2 us
    all_to_all x3, starting transfers between devices, per_device(): lax.all_to_all(blocked, 'depth', split_axis=0, concat_axis=0, tiled=True)  15.1 us
    ppermute x9, starting transfers between devices, exchange(): lax.ppermute(send, 'tile', [(i, i ^ 1 << level) for i in range(tiles)])  11.9 us
    pallas_call x3, Pallas kernels, last_merge(): pl.pallas_call(functools.partial(last_merge_kernel, unit=unit, blocks=blo...  10.3 us
    unnamed x37, local copies, waits for them, and re-layouts  9.75 us
  transfers between devices with their start and end apart: 18, of which 5 were waited for; matrix products, arithmetic and copies ran while one was open for 2% of the time, Pallas kernels for 63%

profile of v3, /device:TPU:0, one launch (start us, length us, event | category | flops | bytes accessed | tf_op | source)
XLA Modules:
  0.0 349.4 jit_solution(11926177446639728834)
XLA Ops:
  0.0 3.0 fusion.6
  7.2 3.9 %collective-permute-start = (bf16[8,48,1152]{2,1,0:T(8,128)(2,1)}, bf16[8,48,1152]{2,1,0:T(8,128)(2,1)}, u32[]{:S(2)}, u32[]{:S(2)}) collective-permute-start(bf16[8,48,1152]{2,1,0:T(8,128)(2,1)} %get-tuple-element.58), channel_id=1, source_target_pairs={{0,1},{1,2},{2,3},{3,4},{4,5},{5,6},{6,7},{7,8},{8,9},{9,10},{10,1... | collective-permute-start | bytes 2654216 | tf_op jit(solution)/shard_map/ppermute | solution.py:462
  19.7 13.2 %collective-permute-start.5 = (bf16[8,48,1152]{2,1,0:T(8,128)(2,1)}, bf16[8,48,1152]{2,1,0:T(8,128)(2,1)S(1)}, u32[]{:S(2)}, u32[]{:S(2)}) collective-permute-start(bf16[8,48,1152]{2,1,0:T(8,128)(2,1)} %get-tuple-element.34), channel_id=1, source_target_pairs={{0,1},{1,2},{2,3},{3,4},{4,5},{5,6},{6,7},{7,8},{8,9},{9,10},{10,1... | collective-permute-start | bytes 2654216 | tf_op jit(solution)/shard_map/ppermute | solution.py:462
  34.3 58.4 %render.3 = (s16[4,208,1152]{2,1,0:T(8,128)(2,1)}, f32[4,4,48,1152]{3,2,1,0:T(8,128)}) custom-call(s32[2]{0:T(128)} %pad_add_fusion.3.ctl, f32[3]{0:T(128)} %maximum_multiply_fusion.light, bf16[128,512]{1,0:T(8,128)(2,1)} %pad_maximum_fusion.1.table, bf16[48,80]{1,0:T(8,128)(2,1)} %select_convert_fusion.1.row_band, ...), custom_call_target="tpu_custom_call" | custom-call | flops 43486543872 | bytes 15925248 | tf_op jit(solution)/shard_map/render/pallas_call | solution.py:321
  92.7 3.1 collective-permute-start.2
  99.1 58.2 %render.4 = (s16[4,208,1152]{2,1,0:T(8,128)(2,1)}, f32[4,4,48,1152]{3,2,1,0:T(8,128)}) custom-call(s32[2]{0:T(128)} %pad_add_fusion.3.ctl, f32[3]{0:T(128)} %maximum_multiply_fusion.light, bf16[128,512]{1,0:T(8,128)(2,1)} %pad_maximum_fusion.1.table, bf16[48,80]{1,0:T(8,128)(2,1)} %select_convert_fusion.1.row_band, ...), custom_call_target="tpu_custom_call" | custom-call | flops 43486543872 | bytes 15925248 | tf_op jit(solution)/shard_map/render/pallas_call | solution.py:321
  161.0 6.0 %merge.6 = (s16[2,208,1152]{2,1,0:T(8,128)(2,1)}, f32[2,4,48,1152]{3,2,1,0:T(8,128)}) custom-call(s32[2]{0:T(128)} %pad_add_fusion.2.ctl, f32[4,4,48,1152]{3,2,1,0:T(8,128)} %get-tuple-element.28.mine, s16[4,208,1152]{2,1,0:T(8,128)(2,1)} %copy-done.4), custom_call_target="tpu_custom_call" | custom-call | flops 7077888 | bytes 7962624 | tf_op jit(solution)/shard_map/merge/pallas_call | solution.py:358
  168.9 58.3 %render.5 = (s16[4,208,1152]{2,1,0:T(8,128)(2,1)}, f32[4,4,48,1152]{3,2,1,0:T(8,128)}) custom-call(s32[2]{0:T(128)} %pad_add_fusion.3.ctl, f32[3]{0:T(128)} %maximum_multiply_fusion.light, bf16[128,512]{1,0:T(8,128)(2,1)} %pad_maximum_fusion.1.table, bf16[48,80]{1,0:T(8,128)(2,1)} %select_convert_fusion.1.row_band, ...), custom_call_target="tpu_custom_call" | custom-call | flops 43486543872 | bytes 15925248 | tf_op jit(solution)/shard_map/render/pallas_call | solution.py:321
  229.3 6.1 %merge.8 = (s16[2,208,1152]{2,1,0:T(8,128)(2,1)}, f32[2,4,48,1152]{3,2,1,0:T(8,128)}) custom-call(s32[2]{0:T(128)} %pad_add_fusion.2.ctl, f32[4,4,48,1152]{3,2,1,0:T(8,128)} %get-tuple-element.36.mine, s16[4,208,1152]{2,1,0:T(8,128)(2,1)} %collective-permute-done.7.got), custom_call_target="tpu_custom_call" | custom-call | flops 7077888 | bytes 7962624 | tf_op jit(solution)/shard_map/merge/pallas_call | solution.py:358
  236.0 15.6 %collective-permute-done.3.got = s16[2,208,1152]{2,1,0:T(8,128)(2,1)} collective-permute-done((s16[2,208,1152]{2,1,0:T(8,128)(2,1)}, s16[2,208,1152]{2,1,0:T(8,128)(2,1)}, u32[]{:S(2)}, u32[]{:S(2)}) %collective-permute-start.3) | collective-permute-done | bytes 958496 | tf_op jit(solution)/shard_map/ppermute | solution.py:465
  251.6 3.9 %merge.7 = (s16[1,208,1152]{2,1,0:T(8,128)(2,1)}, f32[1,4,48,1152]{3,2,1,0:T(8,128)}) custom-call(s32[2]{0:T(128)} %pad_add_fusion.1.ctl, f32[2,4,48,1152]{3,2,1,0:T(8,128)} %get-tuple-element.30.mine, s16[2,208,1152]{2,1,0:T(8,128)(2,1)} %collective-permute-done.3.got), custom_call_target="tpu_custom_call" | custom-call | flops 3538944 | bytes 3981312 | tf_op jit(solution)/shard_map/merge/pallas_call | solution.py:358
  258.2 9.5 %collective-permute-done.4.got = s16[1,208,1152]{2,1,0:T(8,128)(2,1)S(1)} collective-permute-done((s16[1,208,1152]{2,1,0:T(8,128)(2,1)}, s16[1,208,1152]{2,1,0:T(8,128)(2,1)S(1)}, u32[]{:S(2)}, u32[]{:S(2)}) %collective-permute-start.4) | collective-permute-done | bytes 479264 | tf_op jit(solution)/shard_map/ppermute | solution.py:465
  268.4 3.4 last_merge.3
  271.9 5.3 %all-to-all-start = ((s16[4,1,64,1152]{3,2,1,0:T(8,128)(2,1)}), s16[4,1,64,1152]{3,2,1,0:T(8,128)(2,1)S(1)}, u32[]{:S(2)}, u32[]{:S(2)}) async-start(s16[4,1,64,1152]{3,2,1,0:T(8,128)(2,1)} %last_merge.3), calls=%async_computation | async-start | bytes 1179648 | tf_op jit(solution)/shard_map/all_to_all | solution.py:487
  278.5 6.0 %merge.10 = (s16[2,208,1152]{2,1,0:T(8,128)(2,1)}, f32[2,4,48,1152]{3,2,1,0:T(8,128)}) custom-call(s32[2]{0:T(128)} %pad_add_fusion.2.ctl, f32[4,4,48,1152]{3,2,1,0:T(8,128)} %get-tuple-element.45.mine, s16[4,208,1152]{2,1,0:T(8,128)(2,1)} %copy-done.3), custom_call_target="tpu_custom_call" | custom-call | flops 7077888 | bytes 7962624 | tf_op jit(solution)/shard_map/merge/pallas_call | solution.py:358
  286.1 3.9 %merge.9 = (s16[1,208,1152]{2,1,0:T(8,128)(2,1)}, f32[1,4,48,1152]{3,2,1,0:T(8,128)}) custom-call(s32[2]{0:T(128)} %pad_add_fusion.1.ctl, f32[2,4,48,1152]{3,2,1,0:T(8,128)} %get-tuple-element.38.mine, s16[2,208,1152]{2,1,0:T(8,128)(2,1)} %copy-done.5), custom_call_target="tpu_custom_call" | custom-call | flops 3538944 | bytes 3981312 | tf_op jit(solution)/shard_map/merge/pallas_call | solution.py:358
  290.9 9.8 %collective-permute-done.9.got = s16[1,208,1152]{2,1,0:T(8,128)(2,1)S(1)} collective-permute-done((s16[1,208,1152]{2,1,0:T(8,128)(2,1)}, s16[1,208,1152]{2,1,0:T(8,128)(2,1)S(1)}, u32[]{:S(2)}, u32[]{:S(2)}) %collective-permute-start.9) | collective-permute-done | bytes 479264 | tf_op jit(solution)/shard_map/ppermute | solution.py:465
  301.4 3.5 last_merge.4
  304.9 4.8 %all-to-all-start.1 = ((s16[4,1,64,1152]{3,2,1,0:T(8,128)(2,1)}), s16[4,1,64,1152]{3,2,1,0:T(8,128)(2,1)S(1)}, u32[]{:S(2)}, u32[]{:S(2)}) async-start(s16[4,1,64,1152]{3,2,1,0:T(8,128)(2,1)} %last_merge.4), calls=%async_computation.1 | async-start | bytes 1179648 | tf_op jit(solution)/shard_map/all_to_all | solution.py:487
  310.7 3.9 %merge.11 = (s16[1,208,1152]{2,1,0:T(8,128)(2,1)}, f32[1,4,48,1152]{3,2,1,0:T(8,128)}) custom-call(s32[2]{0:T(128)} %pad_add_fusion.1.ctl, f32[2,4,48,1152]{3,2,1,0:T(8,128)} %get-tuple-element.47.mine, s16[2,208,1152]{2,1,0:T(8,128)(2,1)} %copy-done.6), custom_call_target="tpu_custom_call" | custom-call | flops 3538944 | bytes 3981312 | tf_op jit(solution)/shard_map/merge/pallas_call | solution.py:358
  315.4 8.3 %collective-permute-done.14.got = s16[1,208,1152]{2,1,0:T(8,128)(2,1)S(1)} collective-permute-done((s16[1,208,1152]{2,1,0:T(8,128)(2,1)}, s16[1,208,1152]{2,1,0:T(8,128)(2,1)S(1)}, u32[]{:S(2)}, u32[]{:S(2)}) %collective-permute-start.14) | collective-permute-done | bytes 479264 | tf_op jit(solution)/shard_map/ppermute | solution.py:465
  324.5 3.4 last_merge.5
  327.9 4.9 %all-to-all-start.2 = ((s16[4,1,64,1152]{3,2,1,0:T(8,128)(2,1)}), s16[4,1,64,1152]{3,2,1,0:T(8,128)(2,1)S(1)}, u32[]{:S(2)}, u32[]{:S(2)}) async-start(s16[4,1,64,1152]{3,2,1,0:T(8,128)(2,1)} %last_merge.5), calls=%async_computation.2 | async-start | bytes 1179648 | tf_op jit(solution)/shard_map/all_to_all | solution.py:487
  338.2 5.6 %all-to-all-done.2.got = s16[4,1,64,1152]{3,2,1,0:T(8,128)(2,1)S(1)} async-done(((s16[4,1,64,1152]{3,2,1,0:T(8,128)(2,1)}), s16[4,1,64,1152]{3,2,1,0:T(8,128)(2,1)S(1)}, u32[]{:S(2)}, u32[]{:S(2)}) %all-to-all-start.2) | async-done | bytes 589856 | tf_op jit(solution)/shard_map/all_to_all | solution.py:487
  (89 shorter events, 44.4 us)
Async XLA Ops:
  4.4 15.3 %collective-permute-start.1 = (bf16[8,48,1152]{2,1,0:T(8,128)(2,1)}, bf16[8,48,1152]{2,1,0:T(8,128)(2,1)}, u32[]{:S(2)}, u32[]{:S(2)}) collective-permute-start(bf16[8,48,1152]{2,1,0:T(8,128)(2,1)} %get-tuple-element.55), channel_id=1, source_target_pairs={{1,0},{2,1},{3,2},{4,3},{5,4},{6,5},{7,6},{8,7},{9,8},{10,9},{11,1... | collective-permute-start | bytes 2654216 | tf_op jit(solution)/shard_map/ppermute | solution.py:462
  5.7 5.4 %copy-start.17 = (s32[16]{0:T(128)S(1)}, s32[16]{0:T(128)}, u32[]{:S(2)}) copy-start(s32[16]{0:T(128)} %param.7) | copy-start | bytes 196
  5.7 5.4 %copy-start.11 = (f32[2]{0:T(128)S(1)}, f32[2]{0:T(128)}, u32[]{:S(2)}) copy-start(f32[2]{0:T(128)} %param.8) | copy-start | bytes 28
  5.7 8.7 %copy-start.10 = (f32[4,16]{1,0:T(4,128)S(1)}, f32[4,16]{1,0:T(4,128)}, u32[]{:S(2)}) copy-start(f32[4,16]{1,0:T(4,128)} %param.6) | copy-start | bytes 772
  5.7 9.4 %copy-start.12 = (f32[4]{0:T(128)S(1)}, f32[4]{0:T(128)}, u32[]{:S(2)}) copy-start(f32[4]{0:T(128)} %constant.51) | copy-start | bytes 52
  7.2 12.6 %collective-permute-start = (bf16[8,48,1152]{2,1,0:T(8,128)(2,1)}, bf16[8,48,1152]{2,1,0:T(8,128)(2,1)}, u32[]{:S(2)}, u32[]{:S(2)}) collective-permute-start(bf16[8,48,1152]{2,1,0:T(8,128)(2,1)} %get-tuple-element.58), channel_id=1, source_target_pairs={{0,1},{1,2},{2,3},{3,4},{4,5},{5,6},{6,7},{7,8},{8,9},{9,10},{10,1... | collective-permute-start | bytes 2654216 | tf_op jit(solution)/shard_map/ppermute | solution.py:462
  19.7 76.1 %collective-permute-start.5 = (bf16[8,48,1152]{2,1,0:T(8,128)(2,1)}, bf16[8,48,1152]{2,1,0:T(8,128)(2,1)S(1)}, u32[]{:S(2)}, u32[]{:S(2)}) collective-permute-start(bf16[8,48,1152]{2,1,0:T(8,128)(2,1)} %get-tuple-element.34), channel_id=1, source_target_pairs={{0,1},{1,2},{2,3},{3,4},{4,5},{5,6},{6,7},{7,8},{8,9},{9,10},{10,1... | collective-permute-start | bytes 2654216 | tf_op jit(solution)/shard_map/ppermute | solution.py:462
  33.0 62.8 %collective-permute-start.6 = (bf16[8,48,1152]{2,1,0:T(8,128)(2,1)}, bf16[8,48,1152]{2,1,0:T(8,128)(2,1)S(1)}, u32[]{:S(2)}, u32[]{:S(2)}) collective-permute-start(bf16[8,48,1152]{2,1,0:T(8,128)(2,1)} %get-tuple-element.35), channel_id=1, source_target_pairs={{1,0},{2,1},{3,2},{4,3},{5,4},{6,5},{7,6},{8,7},{9,8},{10,9},{11,1... | collective-permute-start | bytes 2654216 | tf_op jit(solution)/shard_map/ppermute | solution.py:462
  92.7 67.0 %collective-permute-start.2 = (s16[4,208,1152]{2,1,0:T(8,128)(2,1)}, s16[4,208,1152]{2,1,0:T(8,128)(2,1)S(1)}, u32[]{:S(2)}, u32[]{:S(2)}) collective-permute-start(s16[4,208,1152]{2,1,0:T(8,128)(2,1)} %get-tuple-element.29), channel_id=1, source_target_pairs={{0,1},{1,0},{2,3},{3,2},{4,5},{5,4},{6,7},{7,6},{8,9},{9,8},{10,11... | collective-permute-start | bytes 5750792 | tf_op jit(solution)/shard_map/ppermute | solution.py:465
  95.8 71.3 %collective-permute-start.10 = (bf16[8,48,1152]{2,1,0:T(8,128)(2,1)S(1)}, bf16[8,48,1152]{2,1,0:T(8,128)(2,1)S(1)}, u32[]{:S(2)}, u32[]{:S(2)}) collective-permute-start(bf16[8,48,1152]{2,1,0:T(8,128)(2,1)S(1)} %get-tuple-element.43), channel_id=1, source_target_pairs={{0,1},{1,2},{2,3},{3,4},{4,5},{5,6},{6,7},{7,8},{8,9},{9,10},{10,1... | collective-permute-start | bytes 2654216 | tf_op jit(solution)/shard_map/ppermute | solution.py:462
  97.8 69.3 %collective-permute-start.11 = (bf16[8,48,1152]{2,1,0:T(8,128)(2,1)S(1)}, bf16[8,48,1152]{2,1,0:T(8,128)(2,1)S(1)}, u32[]{:S(2)}, u32[]{:S(2)}) collective-permute-start(bf16[8,48,1152]{2,1,0:T(8,128)(2,1)S(1)} %get-tuple-element.44), channel_id=1, source_target_pairs={{1,0},{2,1},{3,2},{4,3},{5,4},{6,5},{7,6},{8,7},{9,8},{10,9},{11,1... | collective-permute-start | bytes 2654216 | tf_op jit(solution)/shard_map/ppermute | solution.py:462
  157.4 71.9 %collective-permute-start.7 = (s16[4,208,1152]{2,1,0:T(8,128)(2,1)}, s16[4,208,1152]{2,1,0:T(8,128)(2,1)}, u32[]{:S(2)}, u32[]{:S(2)}) collective-permute-start(s16[4,208,1152]{2,1,0:T(8,128)(2,1)} %get-tuple-element.37), channel_id=1, source_target_pairs={{0,1},{1,0},{2,3},{3,2},{4,5},{5,4},{6,7},{7,6},{8,9},{9,8},{10,11... | collective-permute-start | bytes 5750792 | tf_op jit(solution)/shard_map/ppermute | solution.py:465
  227.1 50.1 %collective-permute-start.12 = (s16[4,208,1152]{2,1,0:T(8,128)(2,1)}, s16[4,208,1152]{2,1,0:T(8,128)(2,1)S(1)}, u32[]{:S(2)}, u32[]{:S(2)}) collective-permute-start(s16[4,208,1152]{2,1,0:T(8,128)(2,1)} %get-tuple-element.46), channel_id=1, source_target_pairs={{0,1},{1,0},{2,3},{3,2},{4,5},{5,4},{6,7},{7,6},{8,9},{9,8},{10,11... | collective-permute-start | bytes 5750792 | tf_op jit(solution)/shard_map/ppermute | solution.py:465
  227.2 24.4 %collective-permute-start.3 = (s16[2,208,1152]{2,1,0:T(8,128)(2,1)}, s16[2,208,1152]{2,1,0:T(8,128)(2,1)}, u32[]{:S(2)}, u32[]{:S(2)}) collective-permute-start(s16[2,208,1152]{2,1,0:T(8,128)(2,1)} %get-tuple-element.31), channel_id=1, source_target_pairs={{0,2},{1,3},{2,0},{3,1},{4,6},{5,7},{6,4},{7,5},{8,10},{9,11},{10,... | collective-permute-start | bytes 2875400 | tf_op jit(solution)/shard_map/ppermute | solution.py:465
  235.4 49.7 %collective-permute-start.8 = (s16[2,208,1152]{2,1,0:T(8,128)(2,1)}, s16[2,208,1152]{2,1,0:T(8,128)(2,1)S(1)}, u32[]{:S(2)}, u32[]{:S(2)}) collective-permute-start(s16[2,208,1152]{2,1,0:T(8,128)(2,1)} %get-tuple-element.39), channel_id=1, source_target_pairs={{0,2},{1,3},{2,0},{3,1},{4,6},{5,7},{6,4},{7,5},{8,10},{9,11},{10,... | collective-permute-start | bytes 2875400 | tf_op jit(solution)/shard_map/ppermute | solution.py:465
  255.5 12.1 %collective-permute-start.4 = (s16[1,208,1152]{2,1,0:T(8,128)(2,1)}, s16[1,208,1152]{2,1,0:T(8,128)(2,1)S(1)}, u32[]{:S(2)}, u32[]{:S(2)}) collective-permute-start(s16[1,208,1152]{2,1,0:T(8,128)(2,1)} %get-tuple-element.33), channel_id=1, source_target_pairs={{0,4},{1,5},{2,6},{3,7},{4,0},{5,1},{6,2},{7,3},{8,12},{9,13},{10,... | collective-permute-start | bytes 1437704 | tf_op jit(solution)/shard_map/ppermute | solution.py:465
  271.9 33.0 %all-to-all-start = ((s16[4,1,64,1152]{3,2,1,0:T(8,128)(2,1)}), s16[4,1,64,1152]{3,2,1,0:T(8,128)(2,1)S(1)}, u32[]{:S(2)}, u32[]{:S(2)}) async-start(s16[4,1,64,1152]{3,2,1,0:T(8,128)(2,1)} %last_merge.3), calls=%async_computation | async-start | bytes 1179648 | tf_op jit(solution)/shard_map/all_to_all | solution.py:487
  284.5 25.2 %collective-permute-start.13 = (s16[2,208,1152]{2,1,0:T(8,128)(2,1)}, s16[2,208,1152]{2,1,0:T(8,128)(2,1)S(1)}, u32[]{:S(2)}, u32[]{:S(2)}) collective-permute-start(s16[2,208,1152]{2,1,0:T(8,128)(2,1)} %get-tuple-element.48), channel_id=1, source_target_pairs={{0,2},{1,3},{2,0},{3,1},{4,6},{5,7},{6,4},{7,5},{8,10},{9,11},{10,... | collective-permute-start | bytes 2875400 | tf_op jit(solution)/shard_map/ppermute | solution.py:465
  290.0 10.6 %collective-permute-start.9 = (s16[1,208,1152]{2,1,0:T(8,128)(2,1)}, s16[1,208,1152]{2,1,0:T(8,128)(2,1)S(1)}, u32[]{:S(2)}, u32[]{:S(2)}) collective-permute-start(s16[1,208,1152]{2,1,0:T(8,128)(2,1)} %get-tuple-element.41), channel_id=1, source_target_pairs={{0,4},{1,5},{2,6},{3,7},{4,0},{5,1},{6,2},{7,3},{8,12},{9,13},{10,... | collective-permute-start | bytes 1437704 | tf_op jit(solution)/shard_map/ppermute | solution.py:465
  304.9 23.0 %copy-start = (s16[4,1,64,1152]{3,2,1,0:T(8,128)(2,1)}, s16[4,1,64,1152]{3,2,1,0:T(8,128)(2,1)S(1)}, u32[]{:S(2)}) copy-start(s16[4,1,64,1152]{3,2,1,0:T(8,128)(2,1)S(1)} %all-to-all-done.got) | copy-start | bytes 1769476
  304.9 23.0 %all-to-all-start.1 = ((s16[4,1,64,1152]{3,2,1,0:T(8,128)(2,1)}), s16[4,1,64,1152]{3,2,1,0:T(8,128)(2,1)S(1)}, u32[]{:S(2)}, u32[]{:S(2)}) async-start(s16[4,1,64,1152]{3,2,1,0:T(8,128)(2,1)} %last_merge.4), calls=%async_computation.1 | async-start | bytes 1179648 | tf_op jit(solution)/shard_map/all_to_all | solution.py:487
  314.6 9.1 %collective-permute-start.14 = (s16[1,208,1152]{2,1,0:T(8,128)(2,1)}, s16[1,208,1152]{2,1,0:T(8,128)(2,1)S(1)}, u32[]{:S(2)}, u32[]{:S(2)}) collective-permute-start(s16[1,208,1152]{2,1,0:T(8,128)(2,1)} %get-tuple-element.50), channel_id=1, source_target_pairs={{0,4},{1,5},{2,6},{3,7},{4,0},{5,1},{6,2},{7,3},{8,12},{9,13},{10,... | collective-permute-start | bytes 1437704 | tf_op jit(solution)/shard_map/ppermute | solution.py:465
  327.9 7.6 %copy-start.1 = (s16[4,1,64,1152]{3,2,1,0:T(8,128)(2,1)}, s16[4,1,64,1152]{3,2,1,0:T(8,128)(2,1)S(1)}, u32[]{:S(2)}) copy-start(s16[4,1,64,1152]{3,2,1,0:T(8,128)(2,1)S(1)} %all-to-all-done.1.got) | copy-start | bytes 1769476
  327.9 15.9 %all-to-all-start.2 = ((s16[4,1,64,1152]{3,2,1,0:T(8,128)(2,1)}), s16[4,1,64,1152]{3,2,1,0:T(8,128)(2,1)S(1)}, u32[]{:S(2)}, u32[]{:S(2)}) async-start(s16[4,1,64,1152]{3,2,1,0:T(8,128)(2,1)} %last_merge.5), calls=%async_computation.2 | async-start | bytes 1179648 | tf_op jit(solution)/shard_map/all_to_all | solution.py:487
  (12 other events, 16.3 us)

commit v4 on v3

--- a/solution.py
+++ b/solution.py
@@ -38,6 +38,16 @@
     return [f + clear * b for f, b in zip(front, back)]
 
 
+def lookup(table, index):
+    numbers = lax.GatherDimensionNumbers(
+        offset_dims=(), collapsed_slice_dims=(1,), start_index_map=(1,),
+        operand_batching_dims=(0,), start_indices_batching_dims=(0,),
+    )
+    return lax.gather(
+        table, index[..., None], numbers, slice_sizes=(1, 1), mode=lax.GatherScatterMode.PROMISE_IN_BOUNDS
+    )
+
+
 def choose(bins, whole):
     place = whole.astype(jnp.bfloat16)
     one, zero = jnp.ones_like(place), jnp.zeros_like(place)
@@ -60,7 +70,7 @@
     lax.fori_loop(0, strips // together, step, 0)
 
 
-def render_kernel(ctl, light, table, row_band, column_band, main, above, below, before, after, send, keep, cells, image, stage, ends, *, groups, units, unit, block, rows, offset, total):
+def render_kernel(ctl, light, table, slope, row_band, column_band, main, above, below, before, after, send, keep, cells, image, stage, ends, *, groups, units, unit, block, rows, offset, total):
     i = pl.program_id(0)
     half = (groups // 2) * units
     rest = lax.rem(i, half)
@@ -109,7 +119,8 @@
 
     lx, ly, lz = light[0], light[1], light[2]
     step = 16
-    bins = table.shape[1] // (2 * step)
+    bins = table.shape[1] // step
+    slopes = [jnp.broadcast_to(slope[k:k + 1, :], (step, LANES)) for k in range(4)]
 
     def strip(c, carry):
         at = pl.multiple_of(c * LANES, LANES)
@@ -132,15 +143,17 @@
             slope_y = [jnp.dot(row_band[...], cells[l, :, shifted], preferred_element_type=jnp.float32) for l in pair]
             slope_z = [jnp.dot(cells[l, 16:16 + tall, window], column_band[...], preferred_element_type=jnp.float32) for l in pair]
             for n, s in enumerate(spans):
-                parts, picks, shades = [], [], []
+                parts, picks, shades, tilts = [], [], [], []
                 for m, layer in enumerate(pair):
                     if layer + 1 < layers:
                         high = cells[layer + 1, inside[n], shifted].astype(jnp.float32)
                     else:
                         high = far[n]
                     position = jnp.clip(here[n] * 2.5 + 7.5, 0.0, 15.0)
-                    whole = jnp.floor(position)
+                    index = position.astype(jnp.int32)
+                    whole = index.astype(jnp.float32)
                     parts.append(position - whole)
+                    tilts.append([lookup(slopes[k], index) for k in range(4)])
                     picks.append(choose(bins, whole))
                     gx = high - low[n]
                     gy = slope_y[m][s]
@@ -150,11 +163,13 @@
                     shades.append(0.045 + facing * lax.rsqrt(jnp.maximum(square, 4.0)))
                     low[n], here[n] = here[n], high
                 pick = jnp.concatenate(picks, axis=1) if len(picks) > 1 else picks[0]
-                found = jnp.dot(table[...], jnp.concatenate([pick, pick], axis=0), preferred_element_type=jnp.float32)
+                found = jnp.dot(table[...], pick, preferred_element_type=jnp.float32)
                 for m, layer in enumerate(pair):
                     lanes = slice(m * LANES, (m + 1) * LANES)
                     tf = [
-                        found[k * step:(k + 1) * step, lanes] + parts[m] * found[(4 + k) * step:(5 + k) * step, lanes]
+                        found[k * step:(k + 1) * step, lanes]
+                        + found[(4 + k) * step:(5 + k) * step, lanes]
+                        + parts[m] * tilts[m][k]
                         for k in range(4)
                     ]
                     shade = shades[m]
@@ -247,7 +262,8 @@
         send[b, 0, unit:unit + 16, :] = row
 
 
-def compose_kernel(got, out, *, unit, blocks):
+def compose_kernel(got, *refs, unit, blocks):
+    out = refs[-1]
     part = out.shape[2]
     total = None
     for b in range(blocks):
@@ -291,7 +307,7 @@
     return jnp.where(place == 1, 1.0, jnp.where(place == -1, -1.0, 0.0)).astype(jnp.bfloat16)
 
 
-def render(ctl, light, table, field, before, after, *, groups, units, unit, rows, offset):
+def render(ctl, light, table, slope, field, before, after, *, groups, units, unit, rows, offset):
     layers, total, width = field.shape
     block = math.lcm(unit, 16)
     tall = padded_rows(unit)
@@ -326,6 +342,7 @@
             in_specs=[
                 pl.BlockSpec(memory_space=pltpu.SMEM),
                 pl.BlockSpec(table.shape, lambda i, ctl: (0, 0)),
+                pl.BlockSpec(slope.shape, lambda i, ctl: (0, 0)),
                 pl.BlockSpec((tall, tall + 32), lambda i, ctl: (0, 0)),
                 pl.BlockSpec((3 * LANES, LANES), lambda i, ctl: (0, 0)),
                 pl.BlockSpec((layers, block, width), main_at),
@@ -346,7 +363,7 @@
         compiler_params=params(),
         cost_estimate=pl.CostEstimate(flops=16384 * cells, bytes_accessed=6 * cells, transcendentals=cells),
         name="render",
-    )(ctl, light, table, row_band, column_band, field, field, field, before, after)
+    )(ctl, light, table, slope, row_band, column_band, field, field, field, before, after)
 
 
 def merge(ctl, mine, got, *, groups, units, unit):
@@ -368,7 +385,7 @@
         ),
         out_shape=shapes,
         compiler_params=params(),
-        cost_estimate=pl.CostEstimate(flops=8 * cells, bytes_accessed=9 * cells, transcendentals=0),
+        cost_estimate=pl.CostEstimate(flops=32768 * cells, bytes_accessed=cells, transcendentals=0),
         name="merge",
     )(ctl, mine, got)
 
@@ -390,25 +407,31 @@
         ),
         out_shape=jax.ShapeDtypeStruct((blocks, units, unit + 16, 4 * width // blocks), jnp.int16),
         compiler_params=params(),
-        cost_estimate=pl.CostEstimate(flops=8 * cells, bytes_accessed=9 * cells, transcendentals=0),
+        cost_estimate=pl.CostEstimate(flops=32768 * cells, bytes_accessed=cells, transcendentals=0),
         name="last_merge",
     )(ctl, mine, got)
 
 
-def compose(got, *, unit):
+def compose(got, so_far, *, unit, first, rows):
     blocks, units = got.shape[:2]
     part = got.shape[3] // 4
     cells = 4 * units * unit * part * blocks
+    operands = [got]
+    in_specs = [pl.BlockSpec((blocks, 1, unit + 16, 4 * part), lambda i: (0, i, 0, 0))]
+    if so_far is not None:
+        operands.append(so_far)
+        in_specs.append(pl.BlockSpec(memory_space=pl.ANY))
     return pl.pallas_call(
         functools.partial(compose_kernel, unit=unit, blocks=blocks),
         grid=(units,),
-        in_specs=[pl.BlockSpec((blocks, 1, unit + 16, 4 * part), lambda i: (0, i, 0, 0))],
-        out_specs=pl.BlockSpec((4, unit, part), lambda i: (0, i, 0)),
-        out_shape=jax.ShapeDtypeStruct((4, units * unit, part), jnp.float32),
+        in_specs=in_specs,
+        out_specs=pl.BlockSpec((4, unit, part), lambda i: (0, first + i, 0)),
+        out_shape=jax.ShapeDtypeStruct((4, rows, part), jnp.float32),
+        input_output_aliases={1: 0} if so_far is not None else {},
         compiler_params=params(),
-        cost_estimate=pl.CostEstimate(flops=8 * cells, bytes_accessed=3 * cells, transcendentals=0),
+        cost_estimate=pl.CostEstimate(flops=32768 * cells, bytes_accessed=cells, transcendentals=0),
         name="compose",
-    )(got)
+    )(*operands)
 
 
 def chunk_units(units):
@@ -428,11 +451,11 @@
     table = table * jnp.array([[1.0], [1.0], [1.0], [0.01]], jnp.float32)
     bins = table.shape[1]
     slope = jnp.concatenate([table[:, 1:] - table[:, :-1], jnp.zeros_like(table[:, :1])], axis=1)
-    table = jnp.concatenate([table, slope], axis=0)
+    slope = jnp.pad(slope, ((0, 4), (0, LANES - bins)))
+    coarse = lax.reduce_precision(table, exponent_bits=8, mantissa_bits=7)
+    table = jnp.concatenate([coarse, table - coarse], axis=0)
     spread = jnp.eye(16, dtype=jnp.float32)
-    table = (table[:, None, :, None] * spread[None, :, None, :]).reshape(8 * 16, bins * 16)
-    coarse = lax.reduce_precision(table, exponent_bits=8, mantissa_bits=7)
-    table = jnp.concatenate([coarse, table - coarse], axis=1).astype(jnp.bfloat16)
+    table = (table[:, None, :, None] * spread[None, :, None, :]).reshape(8 * 16, bins * 16).astype(jnp.bfloat16)
     azimuth, polar = light_angles[0], light_angles[1]
     light = 0.105 * jnp.stack(
         [jnp.cos(azimuth) * jnp.sin(polar), jnp.sin(azimuth) * jnp.sin(polar), jnp.cos(polar)]
@@ -444,8 +467,8 @@
     up = [(i, i + 1) for i in range(devices - 1)]
     down = [(j, i) for i, j in up]
     both = ("depth", "tile")
-    first = field[0].reshape(tiles, rows, width)
-    last = field[layers - 1].reshape(tiles, rows, width)
+    front = field[0].reshape(tiles, rows, width)
+    back = field[layers - 1].reshape(tiles, rows, width)
 
     sizes = chunk_units(rows // unit)
     count = len(sizes)
@@ -456,7 +479,7 @@
             part = layer[:, starts[n]:starts[n] + units * unit]
             return part.reshape(tiles * units, unit, width)
 
-        ends = (cut(last), cut(first))
+        ends = (cut(back), cut(front))
         if n > 0:
             ends, _ = lax.optimization_barrier((ends, halos[n - 1]))
         halos.append((lax.ppermute(ends[0], both, up), lax.ppermute(ends[1], both, down)))
@@ -464,29 +487,60 @@
     def exchange(send, level):
         return lax.ppermute(send, "tile", [(i, i ^ (1 << level)) for i in range(tiles)])
 
-    merged = []
-    pieces = []
-    for n, units in enumerate(sizes):
-        control = controls[0]
-        if n >= 2:
-            control, _ = lax.optimization_barrier((control, merged[n - 2]))
+    chain = []
+    waits = []
+
+    def after_last(control):
+        if chain:
+            control, _, _ = lax.optimization_barrier((control, chain[-1], list(waits)))
+            waits.clear()
+        return control
+
+    state = [None] * count
+
+    def start_chunk(n):
         before, after = halos[n]
         send, keep = render(
-            control, light, table, field, before, after,
-            groups=tiles, units=units, unit=unit, rows=rows, offset=starts[n],
+            after_last(controls[0]), light, table, slope, field, before, after,
+            groups=tiles, units=sizes[n], unit=unit, rows=rows, offset=starts[n],
         )
-        groups = tiles // 2
-        got = exchange(send, 0)
-        for level in range(1, levels):
-            send, keep = merge(controls[level], keep, got, groups=groups, units=units, unit=unit)
-            if level == 1:
-                merged.append(send)
-            groups //= 2
-            got = exchange(send, level)
-        blocked = last_merge(controls[levels], keep, got, units=units, unit=unit, blocks=blocks)
-        blocked = lax.all_to_all(blocked, "depth", split_axis=0, concat_axis=0, tiled=True)
-        pieces.append(compose(blocked, unit=unit))
-    return jnp.concatenate(pieces, axis=1) if count > 1 else pieces[0]
+        chain.append(send)
+        state[n] = (keep, exchange(send, 0))
+
+    def merge_chunk(n, level):
+        keep, got = state[n]
+        send, keep = merge(
+            after_last(controls[level]), keep, got, groups=tiles >> level, units=sizes[n], unit=unit
+        )
+        chain.append(send)
+        state[n] = (keep, exchange(send, level))
+
+    def block_chunk(n):
+        keep, got = state[n]
+        send = last_merge(after_last(controls[levels]), keep, got, units=sizes[n], unit=unit, blocks=blocks)
+        chain.append(send)
+        state[n] = lax.all_to_all(send, "depth", split_axis=0, concat_axis=0, tiled=True)
+
+    def turn(step):
+        n, level = step
+        return (level + 1.5 if n == count - 1 else level, n)
+
+    last = count - 1
+    for n, level in sorted([(n, level) for n in range(count) for level in range(levels + 1)], key=turn):
+        if n == 0 and level == 1 and count > 1:
+            waits.extend(halos[last])
+        if n == 0 and level == 2:
+            waits.extend(state[k][1] for k in range(last))
+        if level == 0:
+            start_chunk(n)
+        elif level < levels:
+            merge_chunk(n, level)
+        else:
+            block_chunk(n)
+    final = None
+    for n in range(count):
+        final = compose(state[n], final, unit=unit, first=starts[n] // unit, rows=rows)
+    return final
 
 
 def solution(mesh):

time: 351 us -> 304 us (0.87)
  Pallas kernels: 223 us -> 188 us
  waiting for transfers between devices: 48.8 us -> 44.1 us
  starting transfers between devices: 49.9 us -> 45.3 us
    pallas_call x3, Pallas kernels: 175 us -> 140 us  [render(): pl.pallas_call(kernel, grid_spec=pltpu.PrefetchScalarGridSpec(num_scalar_...]
    ppermute x9, waiting for transfers between devices: 43.2 us -> 12.9 us  [exchange(): lax.ppermute(send, 'tile', [(i, i ^ 1 << level) for i in range(tiles)])]
    all_to_all x3, waiting for transfers between devices: 5.65 us -> 31.3 us  [block_chunk(): lax.all_to_all(send, 'depth', split_axis=0, concat_axis=0, tiled=True)]
    unnamed x37 -> x43, local copies, waits for them, and re-layouts: 9.75 us -> 9.02 us
  transfers between devices with their start and end apart: 18 -> 18, of which waited for: 5 -> 4; matrix products, arithmetic and copies ran while one was open for 2% -> 3% of each run, Pallas kernels for 63% -> 61%
where the time goes in v4:
time: 304 us; the launch traced here: 303 us
  Pallas kernels  188 us (62%)
  starting transfers between devices  45.3 us (15%)
  waiting for transfers between devices  44.1 us (15%)
  local copies, waits for them, and re-layouts  17.5 us (6%)
  other arithmetic  4.61 us (2%)
  between operations  3.37 us (1%)
    pallas_call x3, Pallas kernels, render(): pl.pallas_call(kernel, grid_spec=pltpu.PrefetchScalarGridSpec(num_scalar_...  140 us
    all_to_all x3, waiting for transfers between devices, block_chunk(): lax.all_to_all(send, 'depth', split_axis=0, concat_axis=0, tiled=True)  31.3 us
    pallas_call x6, Pallas kernels, merge(): pl.pallas_call(functools.partial(merge_kernel, groups=groups, units=units...  30.1 us
    ppermute x3, starting transfers between devices, per_device(): lax.ppermute(ends[0], both, up)  16.9 us
    ppermute x9, waiting for transfers between devices, exchange(): lax.ppermute(send, 'tile', [(i, i ^ 1 << level) for i in range(tiles)])  12.9 us
    all_to_all x3, starting transfers between devices, block_chunk(): lax.all_to_all(send, 'depth', split_axis=0, concat_axis=0, tiled=True)  12.6 us
    ppermute x9, starting transfers between devices, exchange(): lax.ppermute(send, 'tile', [(i, i ^ 1 << level) for i in range(tiles)])  11.9 us
    pallas_call x3, Pallas kernels, last_merge(): pl.pallas_call(functools.partial(last_merge_kernel, unit=unit, blocks=blo...  10.4 us
  transfers between devices with their start and end apart: 18, of which 4 were waited for; matrix products, arithmetic and copies ran while one was open for 3% of the time, Pallas kernels for 61%

profile of v4, /device:TPU:0, one launch (start us, length us, event | category | flops | bytes accessed | tf_op | source)
XLA Modules:
  0.0 303.0 jit_solution(15363914327417726303)
XLA Ops:
  0.0 3.0 fusion.6
  6.9 4.0 %collective-permute-start = (bf16[8,48,1152]{2,1,0:T(8,128)(2,1)}, bf16[8,48,1152]{2,1,0:T(8,128)(2,1)}, u32[]{:S(2)}, u32[]{:S(2)}) collective-permute-start(bf16[8,48,1152]{2,1,0:T(8,128)(2,1)} %get-tuple-element.80), channel_id=1, source_target_pairs={{0,1},{1,2},{2,3},{3,4},{4,5},{5,6},{6,7},{7,8},{8,9},{9,10},{10,1... | collective-permute-start | bytes 2654216 | tf_op jit(solution)/shard_map/ppermute | solution.py:485
  21.7 10.9 %collective-permute-start.2 = (bf16[8,48,1152]{2,1,0:T(8,128)(2,1)}, bf16[8,48,1152]{2,1,0:T(8,128)(2,1)S(1)}, u32[]{:S(2)}, u32[]{:S(2)}) collective-permute-start(bf16[8,48,1152]{2,1,0:T(8,128)(2,1)} %get-tuple-element.40), channel_id=1, source_target_pairs={{0,1},{1,2},{2,3},{3,4},{4,5},{5,6},{6,7},{7,8},{8,9},{9,10},{10,1... | collective-permute-start | bytes 2654216 | tf_op jit(solution)/shard_map/ppermute | solution.py:485
  34.0 46.5 %render.3 = (s16[4,208,1152]{2,1,0:T(8,128)(2,1)}, f32[4,4,48,1152]{3,2,1,0:T(8,128)}) custom-call(s32[2]{0:T(128)} %pad_add_fusion.3.ctl, f32[3]{0:T(128)} %maximum_multiply_fusion.light, bf16[128,256]{1,0:T(8,128)(2,1)} %convert_element_type.34.table, f32[8,128]{1,0:T(8,128)} %pad.20.slope, bf16[48,80]{1,0:T(8,128)(2,1)} %select_convert_fusion.1.row_band, ...), custom_call_target="tpu_custom_call" | custom-call | flops 43486543872 | bytes 15925248 | tf_op jit(solution)/shard_map/render/pallas_call | solution.py:337
  80.5 3.1 %collective-permute-start.6 = (s16[4,208,1152]{2,1,0:T(8,128)(2,1)}, s16[4,208,1152]{2,1,0:T(8,128)(2,1)S(1)}, u32[]{:S(2)}, u32[]{:S(2)}) collective-permute-start(s16[4,208,1152]{2,1,0:T(8,128)(2,1)} %get-tuple-element.38), channel_id=1, source_target_pairs={{0,1},{1,0},{2,3},{3,2},{4,5},{5,4},{6,7},{7,6},{8,9},{9,8},{10,11... | collective-permute-start | bytes 5750792 | tf_op jit(solution)/shard_map/ppermute | solution.py:488
  86.9 46.6 %render.4 = (s16[4,208,1152]{2,1,0:T(8,128)(2,1)}, f32[4,4,48,1152]{3,2,1,0:T(8,128)}) custom-call(s32[2]{0:T(128)} %pad_add_fusion.3.ctl, f32[3]{0:T(128)} %maximum_multiply_fusion.light, bf16[128,256]{1,0:T(8,128)(2,1)} %convert_element_type.34.table, f32[8,128]{1,0:T(8,128)} %pad.20.slope, bf16[48,80]{1,0:T(8,128)(2,1)} %select_convert_fusion.1.row_band, ...), custom_call_target="tpu_custom_call" | custom-call | flops 43486543872 | bytes 15925248 | tf_op jit(solution)/shard_map/render/pallas_call | solution.py:337
  137.1 6.1 %merge.6 = (s16[2,208,1152]{2,1,0:T(8,128)(2,1)}, f32[2,4,48,1152]{3,2,1,0:T(8,128)}) custom-call(s32[2]{0:T(128)} %pad_add_fusion.2.ctl, f32[4,4,48,1152]{3,2,1,0:T(8,128)} %get-tuple-element.46.mine, s16[4,208,1152]{2,1,0:T(8,128)(2,1)} %copy-done.6), custom_call_target="tpu_custom_call" | custom-call | flops 28991029248 | bytes 884736 | tf_op jit(solution)/shard_map/merge/pallas_call | solution.py:375
  146.2 6.1 %merge.7 = (s16[2,208,1152]{2,1,0:T(8,128)(2,1)}, f32[2,4,48,1152]{3,2,1,0:T(8,128)}) custom-call(s32[2]{0:T(128)} %pad_add_fusion.2.ctl, f32[4,4,48,1152]{3,2,1,0:T(8,128)} %get-tuple-element.49.mine, s16[4,208,1152]{2,1,0:T(8,128)(2,1)} %copy-done.8), custom_call_target="tpu_custom_call" | custom-call | flops 28991029248 | bytes 884736 | tf_op jit(solution)/shard_map/merge/pallas_call | solution.py:375
  152.6 46.5 %render.5 = (s16[4,208,1152]{2,1,0:T(8,128)(2,1)}, f32[4,4,48,1152]{3,2,1,0:T(8,128)}) custom-call(s32[2]{0:T(128)} %pad_add_fusion.3.ctl, f32[3]{0:T(128)} %maximum_multiply_fusion.light, bf16[128,256]{1,0:T(8,128)(2,1)} %convert_element_type.34.table, f32[8,128]{1,0:T(8,128)} %pad.20.slope, bf16[48,80]{1,0:T(8,128)(2,1)} %select_convert_fusion.1.row_band, ...), custom_call_target="tpu_custom_call" | custom-call | flops 43486543872 | bytes 15925248 | tf_op jit(solution)/shard_map/render/pallas_call | solution.py:337
  200.1 4.0 %merge.8 = (s16[1,208,1152]{2,1,0:T(8,128)(2,1)}, f32[1,4,48,1152]{3,2,1,0:T(8,128)}) custom-call(s32[2]{0:T(128)} %pad_add_fusion.1.ctl, f32[2,4,48,1152]{3,2,1,0:T(8,128)} %get-tuple-element.54.mine, s16[2,208,1152]{2,1,0:T(8,128)(2,1)} %copy-done.9), custom_call_target="tpu_custom_call" | custom-call | flops 14495514624 | bytes 442368 | tf_op jit(solution)/shard_map/merge/pallas_call | solution.py:375
  204.1 4.0 %merge.9 = (s16[1,208,1152]{2,1,0:T(8,128)(2,1)}, f32[1,4,48,1152]{3,2,1,0:T(8,128)}) custom-call(s32[2]{0:T(128)} %pad_add_fusion.1.ctl, f32[2,4,48,1152]{3,2,1,0:T(8,128)} %get-tuple-element.57.mine, s16[2,208,1152]{2,1,0:T(8,128)(2,1)} %copy-done.10), custom_call_target="tpu_custom_call" | custom-call | flops 14495514624 | bytes 442368 | tf_op jit(solution)/shard_map/merge/pallas_call | solution.py:375
  211.4 6.1 %merge.10 = (s16[2,208,1152]{2,1,0:T(8,128)(2,1)}, f32[2,4,48,1152]{3,2,1,0:T(8,128)}) custom-call(s32[2]{0:T(128)} %pad_add_fusion.2.ctl, f32[4,4,48,1152]{3,2,1,0:T(8,128)} %get-tuple-element.60.mine, s16[4,208,1152]{2,1,0:T(8,128)(2,1)} %copy-done.7), custom_call_target="tpu_custom_call" | custom-call | flops 28991029248 | bytes 884736 | tf_op jit(solution)/shard_map/merge/pallas_call | solution.py:375
  219.1 12.8 %collective-permute-done.11.got = s16[1,208,1152]{2,1,0:T(8,128)(2,1)S(1)} collective-permute-done((s16[1,208,1152]{2,1,0:T(8,128)(2,1)S(1)}, s16[1,208,1152]{2,1,0:T(8,128)(2,1)S(1)}, u32[]{:S(2)}, u32[]{:S(2)}) %collective-permute-start.11) | collective-permute-done | bytes 479264 | tf_op jit(solution)/shard_map/ppermute | solution.py:488
  232.7 3.5 %last_merge.3 = s16[4,1,64,1152]{3,2,1,0:T(8,128)(2,1)} custom-call(s32[2]{0:T(128)} %pad_add_fusion.ctl, f32[1,4,48,1152]{3,2,1,0:T(8,128)} %get-tuple-element.63.mine, s16[1,208,1152]{2,1,0:T(8,128)(2,1)} %copy-done.18), custom_call_target="tpu_custom_call" | custom-call | flops 7247757312 | bytes 221184 | tf_op jit(solution)/shard_map/last_merge/pallas_call | solution.py:396
  237.0 3.4 %last_merge.4 = s16[4,1,64,1152]{3,2,1,0:T(8,128)(2,1)} custom-call(s32[2]{0:T(128)} %pad_add_fusion.ctl, f32[1,4,48,1152]{3,2,1,0:T(8,128)} %get-tuple-element.65.mine, s16[1,208,1152]{2,1,0:T(8,128)(2,1)} %copy-done.16), custom_call_target="tpu_custom_call" | custom-call | flops 7247757312 | bytes 221184 | tf_op jit(solution)/shard_map/last_merge/pallas_call | solution.py:396
  240.4 5.7 %all-to-all-start.1 = ((s16[4,1,64,1152]{3,2,1,0:T(8,128)(2,1)}), s16[4,1,64,1152]{3,2,1,0:T(8,128)(2,1)S(1)}, u32[]{:S(2)}, u32[]{:S(2)}) async-start(s16[4,1,64,1152]{3,2,1,0:T(8,128)(2,1)} %last_merge.4), calls=%async_computation.1 | async-start | bytes 1179648 | tf_op jit(solution)/shard_map/all_to_all | solution.py:522
  247.1 3.9 %merge.11 = (s16[1,208,1152]{2,1,0:T(8,128)(2,1)}, f32[1,4,48,1152]{3,2,1,0:T(8,128)}) custom-call(s32[2]{0:T(128)} %pad_add_fusion.1.ctl, f32[2,4,48,1152]{3,2,1,0:T(8,128)} %get-tuple-element.67.mine, s16[2,208,1152]{2,1,0:T(8,128)(2,1)} %copy-done.11), custom_call_target="tpu_custom_call" | custom-call | flops 14495514624 | bytes 442368 | tf_op jit(solution)/shard_map/merge/pallas_call | solution.py:375
  251.7 10.1 %all-to-all-done.1.got = s16[4,1,64,1152]{3,2,1,0:T(8,128)(2,1)S(1)} async-done(((s16[4,1,64,1152]{3,2,1,0:T(8,128)(2,1)}), s16[4,1,64,1152]{3,2,1,0:T(8,128)(2,1)S(1)}, u32[]{:S(2)}, u32[]{:S(2)}) %all-to-all-start.1) | async-done | bytes 589856 | tf_op jit(solution)/shard_map/all_to_all | solution.py:522
  261.9 3.5 %all-to-all-start.2 = ((s16[4,1,64,1152]{3,2,1,0:T(8,128)(2,1)}), s16[4,1,64,1152]{3,2,1,0:T(8,128)(2,1)S(1)}, u32[]{:S(2)}, u32[]{:S(2)}) async-start(s16[4,1,64,1152]{3,2,1,0:T(8,128)(2,1)} %last_merge.3), calls=%async_computation.2 | async-start | bytes 1179648 | tf_op jit(solution)/shard_map/all_to_all | solution.py:522
  266.1 3.5 %last_merge.5 = s16[4,1,64,1152]{3,2,1,0:T(8,128)(2,1)} custom-call(s32[2]{0:T(128)} %pad_add_fusion.ctl, f32[1,4,48,1152]{3,2,1,0:T(8,128)} %get-tuple-element.70.mine, s16[1,208,1152]{2,1,0:T(8,128)(2,1)} %copy-done.19), custom_call_target="tpu_custom_call" | custom-call | flops 7247757312 | bytes 221184 | tf_op jit(solution)/shard_map/last_merge/pallas_call | solution.py:396
  269.6 11.1 %all-to-all-done.2.got = s16[4,1,64,1152]{3,2,1,0:T(8,128)(2,1)S(1)} async-done(((s16[4,1,64,1152]{3,2,1,0:T(8,128)(2,1)}), s16[4,1,64,1152]{3,2,1,0:T(8,128)(2,1)S(1)}, u32[]{:S(2)}, u32[]{:S(2)}) %all-to-all-start.2) | async-done | bytes 589856 | tf_op jit(solution)/shard_map/all_to_all | solution.py:522
  280.7 3.5 %all-to-all-start = ((s16[4,1,64,1152]{3,2,1,0:T(8,128)(2,1)}), s16[4,1,64,1152]{3,2,1,0:T(8,128)(2,1)S(1)}, u32[]{:S(2)}, u32[]{:S(2)}) async-start(s16[4,1,64,1152]{3,2,1,0:T(8,128)(2,1)} %last_merge.5), calls=%async_computation | async-start | bytes 1179648 | tf_op jit(solution)/shard_map/all_to_all | solution.py:522
  284.2 2.7 compose.3.refs_0_
  289.5 10.0 %all-to-all-done.got = s16[4,1,64,1152]{3,2,1,0:T(8,128)(2,1)S(1)} async-done(((s16[4,1,64,1152]{3,2,1,0:T(8,128)(2,1)}), s16[4,1,64,1152]{3,2,1,0:T(8,128)(2,1)S(1)}, u32[]{:S(2)}, u32[]{:S(2)}) %all-to-all-start) | async-done | bytes 589856 | tf_op jit(solution)/shard_map/all_to_all | solution.py:522
  (94 shorter events, 39.3 us)
Async XLA Ops:
  4.1 17.6 %collective-permute-start.1 = (bf16[8,48,1152]{2,1,0:T(8,128)(2,1)}, bf16[8,48,1152]{2,1,0:T(8,128)(2,1)}, u32[]{:S(2)}, u32[]{:S(2)}) collective-permute-start(bf16[8,48,1152]{2,1,0:T(8,128)(2,1)} %get-tuple-element.77), channel_id=1, source_target_pairs={{1,0},{2,1},{3,2},{4,3},{5,4},{6,5},{7,6},{8,7},{9,8},{10,9},{11,1... | collective-permute-start | bytes 2654216 | tf_op jit(solution)/shard_map/ppermute | solution.py:485
  5.4 6.2 %copy-start.5 = (f32[4]{0:T(128)S(1)}, f32[4]{0:T(128)}, u32[]{:S(2)}) copy-start(f32[4]{0:T(128)} %constant.54) | copy-start | bytes 52
  5.4 6.5 %copy-start.4 = (f32[2]{0:T(128)S(1)}, f32[2]{0:T(128)}, u32[]{:S(2)}) copy-start(f32[2]{0:T(128)} %param.8) | copy-start | bytes 28
  6.9 14.9 %collective-permute-start = (bf16[8,48,1152]{2,1,0:T(8,128)(2,1)}, bf16[8,48,1152]{2,1,0:T(8,128)(2,1)}, u32[]{:S(2)}, u32[]{:S(2)}) collective-permute-start(bf16[8,48,1152]{2,1,0:T(8,128)(2,1)} %get-tuple-element.80), channel_id=1, source_target_pairs={{0,1},{1,2},{2,3},{3,4},{4,5},{5,6},{6,7},{7,8},{8,9},{9,10},{10,1... | collective-permute-start | bytes 2654216 | tf_op jit(solution)/shard_map/ppermute | solution.py:485
  21.7 61.8 %collective-permute-start.2 = (bf16[8,48,1152]{2,1,0:T(8,128)(2,1)}, bf16[8,48,1152]{2,1,0:T(8,128)(2,1)S(1)}, u32[]{:S(2)}, u32[]{:S(2)}) collective-permute-start(bf16[8,48,1152]{2,1,0:T(8,128)(2,1)} %get-tuple-element.40), channel_id=1, source_target_pairs={{0,1},{1,2},{2,3},{3,4},{4,5},{5,6},{6,7},{7,8},{8,9},{9,10},{10,1... | collective-permute-start | bytes 2654216 | tf_op jit(solution)/shard_map/ppermute | solution.py:485
  32.7 50.9 %collective-permute-start.3 = (bf16[8,48,1152]{2,1,0:T(8,128)(2,1)S(1)}, bf16[8,48,1152]{2,1,0:T(8,128)(2,1)S(1)}, u32[]{:S(2)}, u32[]{:S(2)}) collective-permute-start(bf16[8,48,1152]{2,1,0:T(8,128)(2,1)S(1)} %get-tuple-element.41), channel_id=1, source_target_pairs={{1,0},{2,1},{3,2},{4,3},{5,4},{6,5},{7,6},{8,7},{9,8},{10,9},{11,1... | collective-permute-start | bytes 2654216 | tf_op jit(solution)/shard_map/ppermute | solution.py:485
  80.5 55.3 %collective-permute-start.6 = (s16[4,208,1152]{2,1,0:T(8,128)(2,1)}, s16[4,208,1152]{2,1,0:T(8,128)(2,1)S(1)}, u32[]{:S(2)}, u32[]{:S(2)}) collective-permute-start(s16[4,208,1152]{2,1,0:T(8,128)(2,1)} %get-tuple-element.38), channel_id=1, source_target_pairs={{0,1},{1,0},{2,3},{3,2},{4,5},{5,4},{6,7},{7,6},{8,9},{9,8},{10,11... | collective-permute-start | bytes 5750792 | tf_op jit(solution)/shard_map/ppermute | solution.py:488
  83.6 52.2 %collective-permute-start.4 = (bf16[8,48,1152]{2,1,0:T(8,128)(2,1)S(1)}, bf16[8,48,1152]{2,1,0:T(8,128)(2,1)S(1)}, u32[]{:S(2)}, u32[]{:S(2)}) collective-permute-start(bf16[8,48,1152]{2,1,0:T(8,128)(2,1)S(1)} %get-tuple-element.43), channel_id=1, source_target_pairs={{0,1},{1,2},{2,3},{3,4},{4,5},{5,6},{6,7},{7,8},{8,9},{9,10},{10,1... | collective-permute-start | bytes 2654216 | tf_op jit(solution)/shard_map/ppermute | solution.py:485
  85.6 50.2 %collective-permute-start.5 = (bf16[8,48,1152]{2,1,0:T(8,128)(2,1)S(1)}, bf16[8,48,1152]{2,1,0:T(8,128)(2,1)S(1)}, u32[]{:S(2)}, u32[]{:S(2)}) collective-permute-start(bf16[8,48,1152]{2,1,0:T(8,128)(2,1)S(1)} %get-tuple-element.44), channel_id=1, source_target_pairs={{1,0},{2,1},{3,2},{4,3},{5,4},{6,5},{7,6},{8,7},{9,8},{10,9},{11,1... | collective-permute-start | bytes 2654216 | tf_op jit(solution)/shard_map/ppermute | solution.py:485
  133.5 11.4 %collective-permute-start.7 = (s16[4,208,1152]{2,1,0:T(8,128)(2,1)}, s16[4,208,1152]{2,1,0:T(8,128)(2,1)S(1)}, u32[]{:S(2)}, u32[]{:S(2)}) collective-permute-start(s16[4,208,1152]{2,1,0:T(8,128)(2,1)} %get-tuple-element.42), channel_id=1, source_target_pairs={{0,1},{1,0},{2,3},{3,2},{4,5},{5,4},{6,7},{7,6},{8,9},{9,8},{10,11... | collective-permute-start | bytes 5750792 | tf_op jit(solution)/shard_map/ppermute | solution.py:488
  135.8 7.4 %copy-start.12 = (bf16[8,48,1152]{2,1,0:T(8,128)(2,1)}, bf16[8,48,1152]{2,1,0:T(8,128)(2,1)S(1)}, u32[]{:S(2)}) copy-start(bf16[8,48,1152]{2,1,0:T(8,128)(2,1)S(1)} %collective-permute-done.4.before) | copy-start | bytes 2654212
  135.8 7.4 %copy-start.13 = (bf16[8,48,1152]{2,1,0:T(8,128)(2,1)}, bf16[8,48,1152]{2,1,0:T(8,128)(2,1)S(1)}, u32[]{:S(2)}) copy-start(bf16[8,48,1152]{2,1,0:T(8,128)(2,1)S(1)} %collective-permute-done.5.after) | copy-start | bytes 2654212
  143.2 56.0 %collective-permute-start.8 = (s16[2,208,1152]{2,1,0:T(8,128)(2,1)}, s16[2,208,1152]{2,1,0:T(8,128)(2,1)S(1)}, u32[]{:S(2)}, u32[]{:S(2)}) collective-permute-start(s16[2,208,1152]{2,1,0:T(8,128)(2,1)} %get-tuple-element.47), channel_id=1, source_target_pairs={{0,2},{1,3},{2,0},{3,1},{4,6},{5,7},{6,4},{7,5},{8,10},{9,11},{10,... | collective-permute-start | bytes 2875400 | tf_op jit(solution)/shard_map/ppermute | solution.py:488
  152.2 47.0 %collective-permute-start.9 = (s16[2,208,1152]{2,1,0:T(8,128)(2,1)}, s16[2,208,1152]{2,1,0:T(8,128)(2,1)S(1)}, u32[]{:S(2)}, u32[]{:S(2)}) collective-permute-start(s16[2,208,1152]{2,1,0:T(8,128)(2,1)} %get-tuple-element.50), channel_id=1, source_target_pairs={{0,2},{1,3},{2,0},{3,1},{4,6},{5,7},{6,4},{7,5},{8,10},{9,11},{10,... | collective-permute-start | bytes 2875400 | tf_op jit(solution)/shard_map/ppermute | solution.py:488
  199.1 11.0 %collective-permute-start.10 = (s16[4,208,1152]{2,1,0:T(8,128)(2,1)}, s16[4,208,1152]{2,1,0:T(8,128)(2,1)S(1)}, u32[]{:S(2)}, u32[]{:S(2)}) collective-permute-start(s16[4,208,1152]{2,1,0:T(8,128)(2,1)} %get-tuple-element.52), channel_id=1, source_target_pairs={{0,1},{1,0},{2,3},{3,2},{4,5},{5,4},{6,7},{7,6},{8,9},{9,8},{10,11... | collective-permute-start | bytes 5750792 | tf_op jit(solution)/shard_map/ppermute | solution.py:488
  204.1 5.6 %copy-start.17 = (s16[1,208,1152]{2,1,0:T(8,128)(2,1)S(1)}, s16[1,208,1152]{2,1,0:T(8,128)(2,1)}, u32[]{:S(2)}) copy-start(s16[1,208,1152]{2,1,0:T(8,128)(2,1)} %get-tuple-element.55) | copy-start | bytes 1437700
  208.1 28.1 %collective-permute-start.12 = (s16[1,208,1152]{2,1,0:T(8,128)(2,1)}, s16[1,208,1152]{2,1,0:T(8,128)(2,1)S(1)}, u32[]{:S(2)}, u32[]{:S(2)}) collective-permute-start(s16[1,208,1152]{2,1,0:T(8,128)(2,1)} %get-tuple-element.58), channel_id=1, source_target_pairs={{0,4},{1,5},{2,6},{3,7},{4,0},{5,1},{6,2},{7,3},{8,12},{9,13},{10,... | collective-permute-start | bytes 1437704 | tf_op jit(solution)/shard_map/ppermute | solution.py:488
  209.7 22.2 %collective-permute-start.11 = (s16[1,208,1152]{2,1,0:T(8,128)(2,1)S(1)}, s16[1,208,1152]{2,1,0:T(8,128)(2,1)S(1)}, u32[]{:S(2)}, u32[]{:S(2)}) collective-permute-start(s16[1,208,1152]{2,1,0:T(8,128)(2,1)S(1)} %copy-done.17), channel_id=1, source_target_pairs={{0,4},{1,5},{2,6},{3,7},{4,0},{5,1},{6,2},{7,3},{8,12},{9,13},{10,... | collective-permute-start | bytes 1437704 | tf_op jit(solution)/shard_map/ppermute | solution.py:488
  217.5 28.6 %collective-permute-start.13 = (s16[2,208,1152]{2,1,0:T(8,128)(2,1)}, s16[2,208,1152]{2,1,0:T(8,128)(2,1)S(1)}, u32[]{:S(2)}, u32[]{:S(2)}) collective-permute-start(s16[2,208,1152]{2,1,0:T(8,128)(2,1)} %get-tuple-element.61), channel_id=1, source_target_pairs={{0,2},{1,3},{2,0},{3,1},{4,6},{5,7},{6,4},{7,5},{8,10},{9,11},{10,... | collective-permute-start | bytes 2875400 | tf_op jit(solution)/shard_map/ppermute | solution.py:488
  240.4 21.5 %all-to-all-start.1 = ((s16[4,1,64,1152]{3,2,1,0:T(8,128)(2,1)}), s16[4,1,64,1152]{3,2,1,0:T(8,128)(2,1)S(1)}, u32[]{:S(2)}, u32[]{:S(2)}) async-start(s16[4,1,64,1152]{3,2,1,0:T(8,128)(2,1)} %last_merge.4), calls=%async_computation.1 | async-start | bytes 1179648 | tf_op jit(solution)/shard_map/all_to_all | solution.py:522
  250.9 14.4 %collective-permute-start.14 = (s16[1,208,1152]{2,1,0:T(8,128)(2,1)}, s16[1,208,1152]{2,1,0:T(8,128)(2,1)S(1)}, u32[]{:S(2)}, u32[]{:S(2)}) collective-permute-start(s16[1,208,1152]{2,1,0:T(8,128)(2,1)} %get-tuple-element.68), channel_id=1, source_target_pairs={{0,4},{1,5},{2,6},{3,7},{4,0},{5,1},{6,2},{7,3},{8,12},{9,13},{10,... | collective-permute-start | bytes 1437704 | tf_op jit(solution)/shard_map/ppermute | solution.py:488
  261.9 7.7 %copy-start = (s16[4,1,64,1152]{3,2,1,0:T(8,128)(2,1)}, s16[4,1,64,1152]{3,2,1,0:T(8,128)(2,1)S(1)}, u32[]{:S(2)}) copy-start(s16[4,1,64,1152]{3,2,1,0:T(8,128)(2,1)S(1)} %all-to-all-done.1.got) | copy-start | bytes 1769476
  261.9 18.8 %all-to-all-start.2 = ((s16[4,1,64,1152]{3,2,1,0:T(8,128)(2,1)}), s16[4,1,64,1152]{3,2,1,0:T(8,128)(2,1)S(1)}, u32[]{:S(2)}, u32[]{:S(2)}) async-start(s16[4,1,64,1152]{3,2,1,0:T(8,128)(2,1)} %last_merge.3), calls=%async_computation.2 | async-start | bytes 1179648 | tf_op jit(solution)/shard_map/all_to_all | solution.py:522
  280.7 18.8 %all-to-all-start = ((s16[4,1,64,1152]{3,2,1,0:T(8,128)(2,1)}), s16[4,1,64,1152]{3,2,1,0:T(8,128)(2,1)S(1)}, u32[]{:S(2)}, u32[]{:S(2)}) async-start(s16[4,1,64,1152]{3,2,1,0:T(8,128)(2,1)} %last_merge.5), calls=%async_computation | async-start | bytes 1179648 | tf_op jit(solution)/shard_map/all_to_all | solution.py:522
  (15 other events, 34.9 us)

commit v5 on v4

--- a/solution.py
+++ b/solution.py
@@ -9,6 +9,7 @@
 from jax.sharding import PartitionSpec as P
 
 LANES = 128
+HALF = LANES // 2
 CODES = 32700.0
 VMEM_LIMIT = 56 * 1024 * 1024
 
@@ -70,7 +71,7 @@
     lax.fori_loop(0, strips // together, step, 0)
 
 
-def render_kernel(ctl, light, table, slope, row_band, column_band, main, above, below, before, after, send, keep, cells, image, stage, ends, *, groups, units, unit, block, rows, offset, total):
+def render_kernel(ctl, light, table, slope, row_band, column_band, main, above, below, before, after, send, keep, cells, halves, image, stage, ends, *, groups, units, unit, block, rows, offset, total):
     i = pl.program_id(0)
     half = (groups // 2) * units
     rest = lax.rem(i, half)
@@ -82,12 +83,12 @@
     width = main.shape[2]
     tall = padded_rows(unit)
     aligned = block == unit
-    inner = slice(LANES, LANES + width)
+    inner = slice(HALF, HALF + width)
 
     @pl.when(i == 0)
     def _():
-        cells[:, :, 0:LANES] = jnp.zeros((layers, tall + 32, LANES), jnp.bfloat16)
-        cells[:, :, LANES + width:] = jnp.zeros((layers, tall + 32, LANES), jnp.bfloat16)
+        halves[:, :, 0:LANES] = jnp.zeros((layers, tall, LANES), jnp.bfloat16)
+        halves[:, :, width:] = jnp.zeros((layers, tall, LANES), jnp.bfloat16)
 
     def load_layer(layer, carry):
         up = above[layer].astype(jnp.float32)
@@ -95,9 +96,9 @@
         up = jnp.where(start > 0, up, 0.0)
         down = jnp.where(start + unit < total, down, 0.0)
         if aligned:
-            cells[layer, 0:16, inner] = up.astype(jnp.bfloat16)
-            cells[layer, 16:16 + unit, inner] = main[layer]
-            cells[layer, 16 + unit:32 + unit, inner] = down.astype(jnp.bfloat16)
+            cells[layer, 0:16, :] = up.astype(jnp.bfloat16)
+            cells[layer, 16:16 + unit, :] = main[layer]
+            cells[layer, 16 + unit:32 + unit, :] = down.astype(jnp.bfloat16)
         else:
             shift = pl.multiple_of(lax.rem(start, block), 8)
             stage[0:block, :] = main[layer].astype(jnp.float32)
@@ -109,7 +110,8 @@
             stage[16:16 + unit, :] = body
             stage[16 + unit:24 + unit, :] = down
             stage[24 + unit:tall + 32, :] = jnp.zeros((tall + 8 - unit, width), jnp.float32)
-            cells[layer, :, inner] = stage[0:tall + 32, :].astype(jnp.bfloat16)
+            cells[layer, :, :] = stage[0:tall + 32, :].astype(jnp.bfloat16)
+        halves[layer, :, inner] = cells[layer, 16:16 + tall, :]
         return carry
 
     lax.fori_loop(0, layers, load_layer, 0)
@@ -125,8 +127,7 @@
     def strip(c, carry):
         at = pl.multiple_of(c * LANES, LANES)
         cols = pl.ds(at, LANES)
-        shifted = pl.ds(pl.multiple_of(at + LANES, LANES), LANES)
-        window = pl.ds(at, 3 * LANES)
+        window = pl.ds(at, 2 * LANES)
         spans = [slice(r, r + step) for r in range(0, tall, step)]
         inside = [slice(16 + r, 16 + r + step) for r in range(0, tall, step)]
         if aligned:
@@ -135,18 +136,21 @@
         else:
             low = [ends[0, s, cols] for s in spans]
             far = [ends[1, s, cols] for s in spans]
-        here = [cells[0, s, shifted].astype(jnp.float32) for s in inside]
+        here = [cells[0, s, cols].astype(jnp.float32) for s in inside]
         clear = [None] * len(spans)
         colour = [None] * len(spans)
         for first in range(0, layers, 2):
             pair = range(first, min(first + 2, layers))
-            slope_y = [jnp.dot(row_band[...], cells[l, :, shifted], preferred_element_type=jnp.float32) for l in pair]
-            slope_z = [jnp.dot(cells[l, 16:16 + tall, window], column_band[...], preferred_element_type=jnp.float32) for l in pair]
+            count = len(pair)
+            both = jnp.concatenate([cells[l, :, cols] for l in pair], axis=1) if count > 1 else cells[first, :, cols]
+            slope_y = jnp.dot(row_band[...], both, preferred_element_type=jnp.float32)
+            wide = halves[first:first + count, :, window].reshape(count * tall, 2 * LANES)
+            slope_z = jnp.dot(wide, column_band[...], preferred_element_type=jnp.float32)
             for n, s in enumerate(spans):
                 parts, picks, shades, tilts = [], [], [], []
                 for m, layer in enumerate(pair):
                     if layer + 1 < layers:
-                        high = cells[layer + 1, inside[n], shifted].astype(jnp.float32)
+                        high = cells[layer + 1, inside[n], cols].astype(jnp.float32)
                     else:
                         high = far[n]
                     position = jnp.clip(here[n] * 2.5 + 7.5, 0.0, 15.0)
@@ -156,8 +160,8 @@
                     tilts.append([lookup(slopes[k], index) for k in range(4)])
                     picks.append(choose(bins, whole))
                     gx = high - low[n]
-                    gy = slope_y[m][s]
-                    gz = slope_z[m][s]
+                    gy = slope_y[s, m * LANES:(m + 1) * LANES]
+                    gz = slope_z[m * tall + s.start:m * tall + s.stop]
                     facing = jnp.abs(gx * lx + gy * ly + gz * lz)
                     square = gx * gx + gy * gy + gz * gz
                     shades.append(0.045 + facing * lax.rsqrt(jnp.maximum(square, 4.0)))
@@ -220,40 +224,40 @@
     return over(front, back)
 
 
-def merge_kernel(ctl, mine, got, send, keep, *, groups, units, unit):
-    i = pl.program_id(0)
+def merge_kernel(ctl, mine, got, *sends, units, unit):
+    turn = pl.program_id(0) // units
     width = mine.shape[3]
-    sending = i < (groups // 2) * units
-
-    @pl.when(sending)
-    def _():
-        def put(at):
-            cols = pl.ds(at, LANES)
-            put_codes(send, get_unit(ctl, mine, got, cols, unit), cols, unit)
-
-        each_strip(width, put)
-
-    @pl.when(jnp.logical_not(sending))
-    def _():
-        def put(at):
-            cols = pl.ds(at, LANES)
-            merged = get_unit(ctl, mine, got, cols, unit)
-            for k in range(4):
-                keep[0, k, :, cols] = merged[k]
-
-        each_strip(width, put)
-
-
-def last_merge_kernel(ctl, mine, got, send, image, *, unit, blocks):
-    width = mine.shape[3]
-
-    def put(at):
-        cols = pl.ds(at, LANES)
-        merged = get_unit(ctl, mine, got, cols, unit)
-        for k in range(4):
-            image[k, :, cols] = merged[k]
-
-    each_strip(width, put)
+    for k, send in enumerate(sends):
+        @pl.when(turn == k)
+        def _(send=send):
+            def put(at):
+                cols = pl.ds(at, LANES)
+                put_codes(send, get_unit(ctl, mine, got, cols, unit), cols, unit)
+
+            each_strip(width, put)
+
+
+def gather_kernel(ctl, *refs, unit, blocks):
+    parts, send, image = refs[:-2], refs[-2], refs[-1]
+    width = image.shape[2]
+    for me in range(len(parts)):
+        @pl.when(ctl[0] == me)
+        def _(me=me):
+            def put(at):
+                cols = pl.ds(at, LANES)
+                total = None
+                for j in range(len(parts)):
+                    got = parts[me ^ j]
+                    part = decode(
+                        [got[0, k * unit:(k + 1) * unit, cols] for k in range(4)],
+                        got[0, 4 * unit:4 * unit + 16, cols],
+                    )
+                    total = part if total is None else over(total, part)
+                for k in range(4):
+                    image[k, :, cols] = total[k]
+
+            each_strip(width, put)
+
     part = width // blocks
     for b in range(blocks):
         wide = jnp.concatenate([image[k, :, b * part:(b + 1) * part] for k in range(4)], axis=1)
@@ -312,7 +316,7 @@
     block = math.lcm(unit, 16)
     tall = padded_rows(unit)
     row_band = band((tall, tall + 32), 1, 16)
-    column_band = band((3 * LANES, LANES), 0, LANES)
+    column_band = band((2 * LANES, LANES), 0, HALF)
     half = (groups // 2) * units
     index = unit_index(groups, units, 0)
 
@@ -344,7 +348,7 @@
                 pl.BlockSpec(table.shape, lambda i, ctl: (0, 0)),
                 pl.BlockSpec(slope.shape, lambda i, ctl: (0, 0)),
                 pl.BlockSpec((tall, tall + 32), lambda i, ctl: (0, 0)),
-                pl.BlockSpec((3 * LANES, LANES), lambda i, ctl: (0, 0)),
+                pl.BlockSpec((2 * LANES, LANES), lambda i, ctl: (0, 0)),
                 pl.BlockSpec((layers, block, width), main_at),
                 pl.BlockSpec((layers, 16, width), above_at),
                 pl.BlockSpec((layers, 16, width), below_at),
@@ -353,7 +357,8 @@
             ],
             out_specs=specs,
             scratch_shapes=[
-                pltpu.VMEM((layers, tall + 32, width + 2 * LANES), jnp.bfloat16),
+                pltpu.VMEM((layers, tall + 32, width), jnp.bfloat16),
+                pltpu.VMEM((layers, tall, width + LANES), jnp.bfloat16),
                 pltpu.VMEM((4, tall, width), jnp.float32),
                 pltpu.VMEM((max(block, tall + 32), width) if block != unit else (8, LANES), jnp.float32),
                 pltpu.VMEM((2, tall, width) if block != unit else (1, 8, LANES), jnp.float32),
@@ -366,50 +371,53 @@
     )(ctl, light, table, slope, row_band, column_band, field, field, field, before, after)
 
 
-def merge(ctl, mine, got, *, groups, units, unit):
+def merge(ctl, mine, got, *, places, units, unit):
     width = mine.shape[3]
-    half = (groups // 2) * units
-    index = unit_index(groups, units, 0)
-    shapes, specs = split_outputs(groups, units, unit, width)
-    cells = 4 * 2 * half * unit * width
+    cells = 4 * places * units * unit * width
+
+    def index(i, ctl):
+        return (ctl[0] ^ (i // units)) * units + lax.rem(i, units)
+
+    def spec(k):
+        return pl.BlockSpec(
+            (1, 4 * unit + 16, width), lambda i, ctl: (jnp.clip(i - k * units, 0, units - 1), 0, 0)
+        )
+
     return pl.pallas_call(
-        functools.partial(merge_kernel, groups=groups, units=units, unit=unit),
+        functools.partial(merge_kernel, units=units, unit=unit),
         grid_spec=pltpu.PrefetchScalarGridSpec(
             num_scalar_prefetch=1,
-            grid=(2 * half,),
+            grid=(places * units,),
             in_specs=[
                 pl.BlockSpec((1, 4, unit, width), lambda i, ctl: (index(i, ctl), 0, 0, 0)),
                 pl.BlockSpec((1, 4 * unit + 16, width), lambda i, ctl: (index(i, ctl), 0, 0)),
             ],
-            out_specs=specs,
+            out_specs=[spec(k) for k in range(places)],
         ),
-        out_shape=shapes,
+        out_shape=[jax.ShapeDtypeStruct((units, 4 * unit + 16, width), jnp.int16)] * places,
         compiler_params=params(),
         cost_estimate=pl.CostEstimate(flops=32768 * cells, bytes_accessed=cells, transcendentals=0),
         name="merge",
     )(ctl, mine, got)
 
 
-def last_merge(ctl, mine, got, *, units, unit, blocks):
-    width = mine.shape[3]
+def gather_parts(ctl, parts, *, units, unit, blocks):
+    width = parts[0].shape[2]
     cells = 4 * units * unit * width
     return pl.pallas_call(
-        functools.partial(last_merge_kernel, unit=unit, blocks=blocks),
+        functools.partial(gather_kernel, unit=unit, blocks=blocks),
         grid_spec=pltpu.PrefetchScalarGridSpec(
             num_scalar_prefetch=1,
             grid=(units,),
-            in_specs=[
-                pl.BlockSpec((1, 4, unit, width), lambda i, ctl: (i, 0, 0, 0)),
-                pl.BlockSpec((1, 4 * unit + 16, width), lambda i, ctl: (i, 0, 0)),
-            ],
+            in_specs=[pl.BlockSpec((1, 4 * unit + 16, width), lambda i, ctl: (i, 0, 0))] * len(parts),
             out_specs=pl.BlockSpec((blocks, 1, unit + 16, 4 * width // blocks), lambda i, ctl: (0, i, 0, 0)),
             scratch_shapes=[pltpu.VMEM((4, unit, width), jnp.float32)],
         ),
         out_shape=jax.ShapeDtypeStruct((blocks, units, unit + 16, 4 * width // blocks), jnp.int16),
         compiler_params=params(),
-        cost_estimate=pl.CostEstimate(flops=32768 * cells, bytes_accessed=cells, transcendentals=0),
-        name="last_merge",
-    )(ctl, mine, got)
+        cost_estimate=pl.CostEstimate(flops=131072 * cells, bytes_accessed=cells, transcendentals=0),
+        name="gather_parts",
+    )(ctl, *parts)
 
 
 def compose(got, so_far, *, unit, first, rows):
@@ -445,7 +453,7 @@
     layers, total, width = field.shape
     rows = total // tiles
     unit = unit_rows(rows)
-    levels = tiles.bit_length() - 1
+    places = tiles // 2
 
     table = jnp.take(transfer, bin_order, axis=1)
     table = table * jnp.array([[1.0], [1.0], [1.0], [0.01]], jnp.float32)
@@ -462,13 +470,12 @@
     )
 
     tile = lax.axis_index("tile")
-    bits = [((tile >> b) & 1).astype(jnp.int32) for b in range(levels)]
-    controls = [jnp.stack([bits[min(b, levels - 1)], bits[max(b - 1, 0)]]) for b in range(levels + 1)]
+    core, place = (tile & 1).astype(jnp.int32), (tile >> 1).astype(jnp.int32)
+    render_control = jnp.stack([core, core])
+    merge_control = jnp.stack([place, core])
     up = [(i, i + 1) for i in range(devices - 1)]
     down = [(j, i) for i, j in up]
     both = ("depth", "tile")
-    front = field[0].reshape(tiles, rows, width)
-    back = field[layers - 1].reshape(tiles, rows, width)
 
     sizes = chunk_units(rows // unit)
     count = len(sizes)
@@ -476,16 +483,16 @@
     halos = []
     for n, units in enumerate(sizes):
         def cut(layer):
-            part = layer[:, starts[n]:starts[n] + units * unit]
+            part = field.reshape(layers, tiles, rows, width)[layer:layer + 1, :, starts[n]:starts[n] + units * unit]
             return part.reshape(tiles * units, unit, width)
 
-        ends = (cut(back), cut(front))
+        ends = (cut(layers - 1), cut(0))
         if n > 0:
             ends, _ = lax.optimization_barrier((ends, halos[n - 1]))
         halos.append((lax.ppermute(ends[0], both, up), lax.ppermute(ends[1], both, down)))
 
-    def exchange(send, level):
-        return lax.ppermute(send, "tile", [(i, i ^ (1 << level)) for i in range(tiles)])
+    def exchange(send, distance):
+        return lax.ppermute(send, "tile", [(i, i ^ distance) for i in range(tiles)])
 
     chain = []
     waits = []
@@ -501,42 +508,31 @@
     def start_chunk(n):
         before, after = halos[n]
         send, keep = render(
-            after_last(controls[0]), light, table, slope, field, before, after,
+            after_last(render_control), light, table, slope, field, before, after,
             groups=tiles, units=sizes[n], unit=unit, rows=rows, offset=starts[n],
         )
         chain.append(send)
-        state[n] = (keep, exchange(send, 0))
-
-    def merge_chunk(n, level):
+        state[n] = (keep, exchange(send, 1))
+
+    def merge_chunk(n):
         keep, got = state[n]
-        send, keep = merge(
-            after_last(controls[level]), keep, got, groups=tiles >> level, units=sizes[n], unit=unit
-        )
-        chain.append(send)
-        state[n] = (keep, exchange(send, level))
+        sends = merge(after_last(merge_control), keep, got, places=places, units=sizes[n], unit=unit)
+        chain.append(sends[-1])
+        state[n] = [sends[0]] + [exchange(sends[k], 2 * k) for k in range(1, places)]
 
     def block_chunk(n):
-        keep, got = state[n]
-        send = last_merge(after_last(controls[levels]), keep, got, units=sizes[n], unit=unit, blocks=blocks)
+        send = gather_parts(after_last(merge_control), state[n], units=sizes[n], unit=unit, blocks=blocks)
         chain.append(send)
         state[n] = lax.all_to_all(send, "depth", split_axis=0, concat_axis=0, tiled=True)
 
-    def turn(step):
-        n, level = step
-        return (level + 1.5 if n == count - 1 else level, n)
-
     last = count - 1
-    for n, level in sorted([(n, level) for n in range(count) for level in range(levels + 1)], key=turn):
+    steps = [(n, level) for n in range(count) for level in range(3)]
+    for n, level in sorted(steps, key=lambda step: (step[1] + 1.5 * (step[0] == last), step[0])):
         if n == 0 and level == 1 and count > 1:
             waits.extend(halos[last])
         if n == 0 and level == 2:
-            waits.extend(state[k][1] for k in range(last))
-        if level == 0:
-            start_chunk(n)
-        elif level < levels:
-            merge_chunk(n, level)
-        else:
-            block_chunk(n)
+            waits.extend(part for k in range(last) for part in state[k])
+        (start_chunk, merge_chunk, block_chunk)[level](n)
     final = None
     for n in range(count):
         final = compose(state[n], final, unit=unit, first=starts[n] // unit, rows=rows)

time: 304 us -> 287 us (0.944)
  Pallas kernels: 188 us -> 174 us
  starting transfers between devices: 45.3 us -> 53.7 us
  waiting for transfers between devices: 44.1 us -> 37.8 us
  local copies, waits for them, and re-layouts: 17.5 us -> 13.6 us
    all_to_all x3, waiting for transfers between devices: 31.3 us -> 15.3 us  [block_chunk(): lax.all_to_all(send, 'depth', split_axis=0, concat_axis=0, tiled=True)]
    pallas_call x9 -> x6, Pallas kernels: 40.4 us -> 30.7 us  [the longest x3 18.6 us: merge(): pl.pallas_call(functools.partial(merge_kernel, units=units, unit=unit), g...]
    ppermute x9 -> x12, waiting for transfers between devices: 12.9 us -> 22.5 us  [exchange(): return lax.ppermute(send, 'tile', [(i, i ^ distance) for i in range(tiles)])]
    slice x3 -> x0, local copies, waits for them, and re-layouts: 5.52 us -> none  [the longest x1 2.96 us: per_device(): front = field[0].reshape(tiles, rows, width)]
    pallas_call x3, Pallas kernels: 140 us -> 135 us  [render(): pl.pallas_call(kernel, grid_spec=pltpu.PrefetchScalarGridSpec(num_scalar_...]
    reshape x0 -> x1, local copies, waits for them, and re-layouts: none -> 4.22 us  [cut(): return part.reshape(tiles * units, unit, width)]
    ppermute x9 -> x12, starting transfers between devices: 11.9 us -> 16 us  [exchange(): return lax.ppermute(send, 'tile', [(i, i ^ distance) for i in range(tiles)])]
    unnamed x43 -> x47, local copies, waits for them, and re-layouts: 9.02 us -> 6.43 us
  transfers between devices with their start and end apart: 18 -> 21, of which waited for: 4 -> 5; matrix products, arithmetic and copies ran while one was open for 3% -> 2% of each run, Pallas kernels for 61% -> 60%
where the time goes in v5:
time: 287 us; the launch traced here: 286 us
  Pallas kernels  174 us (61%)
  starting transfers between devices  53.7 us (19%)
  waiting for transfers between devices  37.8 us (13%)
  local copies, waits for them, and re-layouts  13.6 us (5%)
  other arithmetic  3.47 us (1%)
  between operations  3.12 us (1%)
    pallas_call x3, Pallas kernels, render(): pl.pallas_call(kernel, grid_spec=pltpu.PrefetchScalarGridSpec(num_scalar_...  135 us
    ppermute x12, waiting for transfers between devices, exchange(): return lax.ppermute(send, 'tile', [(i, i ^ distance) for i in range(tiles)])  22.5 us
    ppermute x3, starting transfers between devices, per_device(): lax.ppermute(ends[0], both, up)  19.9 us
    pallas_call x3, Pallas kernels, merge(): pl.pallas_call(functools.partial(merge_kernel, units=units, unit=unit), g...  18.6 us
    ppermute x12, starting transfers between devices, exchange(): return lax.ppermute(send, 'tile', [(i, i ^ distance) for i in range(tiles)])  16 us
    all_to_all x3, waiting for transfers between devices, block_chunk(): lax.all_to_all(send, 'depth', split_axis=0, concat_axis=0, tiled=True)  15.3 us
    all_to_all x3, starting transfers between devices, block_chunk(): lax.all_to_all(send, 'depth', split_axis=0, concat_axis=0, tiled=True)  13.9 us
    pallas_call x3, Pallas kernels, gather_parts(): pl.pallas_call(functools.partial(gather_kernel, unit=unit, blocks=blocks)...  12.1 us
  transfers between devices with their start and end apart: 21, of which 5 were waited for; matrix products, arithmetic and copies ran while one was open for 2% of the time, Pallas kernels for 60%

profile of v5, /device:TPU:0, one launch (start us, length us, event | category | flops | bytes accessed | tf_op | source)
XLA Modules:
  0.0 285.7 jit_solution(3065394465765648425)
XLA Ops:
  0.0 4.2 %slice_bitcast_fusion = (bf16[8,48,1152]{2,1,0:T(8,128)(2,1)S(1)}, bf16[8,48,1152]{2,1,0:T(8,128)(2,1)S(1)}, bf16[8,48,1152]{2,1,0:T(8,128)(2,1)S(1)}, bf16[8,48...) fusion(bf16[6,8,144,1152]{3,2,1,0:T(8,128)(2,1)} %bitcast.20), kind=kLoop, calls=%fused_computation.2 | loop fusion | bytes 10616832 | tf_op jit(solution)/shard_map/reshape | solution.py:487
  5.5 4.1 %collective-permute-start = (bf16[8,48,1152]{2,1,0:T(8,128)(2,1)}, bf16[8,48,1152]{2,1,0:T(8,128)(2,1)}, u32[]{:S(2)}, u32[]{:S(2)}) collective-permute-start(bf16[8,48,1152]{2,1,0:T(8,128)(2,1)} %get-tuple-element.72), channel_id=1, source_target_pairs={{0,1},{1,2},{2,3},{3,4},{4,5},{5,6},{6,7},{7,8},{8,9},{9,10},{10,1... | collective-permute-start | bytes 2654216 | tf_op jit(solution)/shard_map/ppermute | solution.py:492
  19.0 13.8 %collective-permute-start.2 = (bf16[8,48,1152]{2,1,0:T(8,128)(2,1)}, bf16[8,48,1152]{2,1,0:T(8,128)(2,1)S(1)}, u32[]{:S(2)}, u32[]{:S(2)}) collective-permute-start(bf16[8,48,1152]{2,1,0:T(8,128)(2,1)} %get-tuple-element.37), channel_id=1, source_target_pairs={{0,1},{1,2},{2,3},{3,4},{4,5},{5,6},{6,7},{7,8},{8,9},{9,10},{10,1... | collective-permute-start | bytes 2654216 | tf_op jit(solution)/shard_map/ppermute | solution.py:492
  34.1 45.1 %render.3 = (s16[4,208,1152]{2,1,0:T(8,128)(2,1)}, f32[4,4,48,1152]{3,2,1,0:T(8,128)}) custom-call(s32[2]{0:T(128)} %pad_add_fusion.1.ctl, f32[3]{0:T(128)} %maximum_multiply_fusion.light, bf16[128,256]{1,0:T(8,128)(2,1)} %convert_element_type.34.table, f32[8,128]{1,0:T(8,128)} %pad.16.slope, bf16[48,80]{1,0:T(8,128)(2,1)} %select_convert_fusion.1.row_band, ...), custom_call_target="tpu_custom_call" | custom-call | flops 43486543872 | bytes 15925248 | tf_op jit(solution)/shard_map/render/pallas_call | solution.py:341
  79.2 3.1 %collective-permute-start.6 = (s16[4,208,1152]{2,1,0:T(8,128)(2,1)}, s16[4,208,1152]{2,1,0:T(8,128)(2,1)S(1)}, u32[]{:S(2)}, u32[]{:S(2)}) collective-permute-start(s16[4,208,1152]{2,1,0:T(8,128)(2,1)} %get-tuple-element.35), channel_id=1, source_target_pairs={{0,1},{1,0},{2,3},{3,2},{4,5},{5,4},{6,7},{7,6},{8,9},{9,8},{10,11... | collective-permute-start | bytes 5750792 | tf_op jit(solution)/shard_map/ppermute | solution.py:495
  85.6 45.1 %render.4 = (s16[4,208,1152]{2,1,0:T(8,128)(2,1)}, f32[4,4,48,1152]{3,2,1,0:T(8,128)}) custom-call(s32[2]{0:T(128)} %pad_add_fusion.1.ctl, f32[3]{0:T(128)} %maximum_multiply_fusion.light, bf16[128,256]{1,0:T(8,128)(2,1)} %convert_element_type.34.table, f32[8,128]{1,0:T(8,128)} %pad.16.slope, bf16[48,80]{1,0:T(8,128)(2,1)} %select_convert_fusion.1.row_band, ...), custom_call_target="tpu_custom_call" | custom-call | flops 43486543872 | bytes 15925248 | tf_op jit(solution)/shard_map/render/pallas_call | solution.py:341
  134.3 6.2 %merge.3 = (s16[1,208,1152]{2,1,0:T(8,128)(2,1)}, s16[1,208,1152]{2,1,0:T(8,128)(2,1)}, s16[1,208,1152]{2,1,0:T(8,128)(2,1)}, s16[1,208,1152]{2,1,0:T(8,128)(2,1)}) custom-call(s32[2]{0:T(128)} %pad_add_fusion.ctl, f32[4,4,48,1152]{3,2,1,0:T(8,128)} %get-tuple-element.43.mine, s16[4,208,1152]{2,1,0:T(8,128)(2,1)} %copy-done.6), custom_call_target="tpu_custom_call" | custom-call | flops 28991029248 | bytes 884736 | tf_op jit(solution)/shard_map/merge/pallas_call | solution.py:386
  145.4 6.2 %merge.4 = (s16[1,208,1152]{2,1,0:T(8,128)(2,1)}, s16[1,208,1152]{2,1,0:T(8,128)(2,1)}, s16[1,208,1152]{2,1,0:T(8,128)(2,1)}, s16[1,208,1152]{2,1,0:T(8,128)(2,1)}) custom-call(s32[2]{0:T(128)} %pad_add_fusion.ctl, f32[4,4,48,1152]{3,2,1,0:T(8,128)} %get-tuple-element.46.mine, s16[4,208,1152]{2,1,0:T(8,128)(2,1)} %copy-done.8), custom_call_target="tpu_custom_call" | custom-call | flops 28991029248 | bytes 884736 | tf_op jit(solution)/shard_map/merge/pallas_call | solution.py:386
  154.6 11.3 %collective-permute-done.8.refs_1_ = s16[1,208,1152]{2,1,0:T(8,128)(2,1)S(1)} collective-permute-done((s16[1,208,1152]{2,1,0:T(8,128)(2,1)}, s16[1,208,1152]{2,1,0:T(8,128)(2,1)S(1)}, u32[]{:S(2)}, u32[]{:S(2)}) %collective-permute-start.8) | collective-permute-done | bytes 479264 | tf_op jit(solution)/shard_map/ppermute | solution.py:495
  166.4 45.1 %render.5 = (s16[4,208,1152]{2,1,0:T(8,128)(2,1)}, f32[4,4,48,1152]{3,2,1,0:T(8,128)}) custom-call(s32[2]{0:T(128)} %pad_add_fusion.1.ctl, f32[3]{0:T(128)} %maximum_multiply_fusion.light, bf16[128,256]{1,0:T(8,128)(2,1)} %convert_element_type.34.table, f32[8,128]{1,0:T(8,128)} %pad.16.slope, bf16[48,80]{1,0:T(8,128)(2,1)} %select_convert_fusion.1.row_band, ...), custom_call_target="tpu_custom_call" | custom-call | flops 43486543872 | bytes 15925248 | tf_op jit(solution)/shard_map/render/pallas_call | solution.py:341
  212.6 4.0 %gather_parts.3 = s16[4,1,64,1152]{3,2,1,0:T(8,128)(2,1)} custom-call(s32[2]{0:T(128)} %pad_add_fusion.ctl, s16[1,208,1152]{2,1,0:T(8,128)(2,1)} %get-tuple-element.50.refs_0_, s16[1,208,1152]{2,1,0:T(8,128)(2,1)} %copy-done.14, s16[1,208,1152]{2,1,0:T(8,128)(2,1)} %copy-done.15, s16[1,208,1152]{2,1,0:T(8,128)(2,1)} %copy-done.13), custom_call_target="tpu_custom_call" | custom-call | flops 28991029248 | bytes 221184 | tf_op jit(solution)/shard_map/gather_parts/pallas_call | solution.py:407
  216.6 4.0 %gather_parts.4 = s16[4,1,64,1152]{3,2,1,0:T(8,128)(2,1)} custom-call(s32[2]{0:T(128)} %pad_add_fusion.ctl, s16[1,208,1152]{2,1,0:T(8,128)(2,1)} %get-tuple-element.53.refs_0_, s16[1,208,1152]{2,1,0:T(8,128)(2,1)} %copy-done.17, s16[1,208,1152]{2,1,0:T(8,128)(2,1)} %copy-done.18, s16[1,208,1152]{2,1,0:T(8,128)(2,1)} %copy-done.16), custom_call_target="tpu_custom_call" | custom-call | flops 28991029248 | bytes 221184 | tf_op jit(solution)/shard_map/gather_parts/pallas_call | solution.py:407
  220.5 5.6 %all-to-all-start.1 = ((s16[4,1,64,1152]{3,2,1,0:T(8,128)(2,1)}), s16[4,1,64,1152]{3,2,1,0:T(8,128)(2,1)S(1)}, u32[]{:S(2)}, u32[]{:S(2)}) async-start(s16[4,1,64,1152]{3,2,1,0:T(8,128)(2,1)} %gather_parts.4), calls=%async_computation.1 | async-start | bytes 1179648 | tf_op jit(solution)/shard_map/all_to_all | solution.py:526
  227.4 6.2 %merge.5 = (s16[1,208,1152]{2,1,0:T(8,128)(2,1)}, s16[1,208,1152]{2,1,0:T(8,128)(2,1)}, s16[1,208,1152]{2,1,0:T(8,128)(2,1)}, s16[1,208,1152]{2,1,0:T(8,128)(2,1)}) custom-call(s32[2]{0:T(128)} %pad_add_fusion.ctl, f32[4,4,48,1152]{3,2,1,0:T(8,128)} %get-tuple-element.59.mine, s16[4,208,1152]{2,1,0:T(8,128)(2,1)} %copy-done.7), custom_call_target="tpu_custom_call" | custom-call | flops 28991029248 | bytes 884736 | tf_op jit(solution)/shard_map/merge/pallas_call | solution.py:386
  234.4 2.6 collective-permute-start.17
  237.1 5.5 %all-to-all-done.1.got = s16[4,1,64,1152]{3,2,1,0:T(8,128)(2,1)S(1)} async-done(((s16[4,1,64,1152]{3,2,1,0:T(8,128)(2,1)}), s16[4,1,64,1152]{3,2,1,0:T(8,128)(2,1)S(1)}, u32[]{:S(2)}, u32[]{:S(2)}) %all-to-all-start.1) | async-done | bytes 589856 | tf_op jit(solution)/shard_map/all_to_all | solution.py:526
  242.6 3.5 %all-to-all-start.2 = ((s16[4,1,64,1152]{3,2,1,0:T(8,128)(2,1)}), s16[4,1,64,1152]{3,2,1,0:T(8,128)(2,1)S(1)}, u32[]{:S(2)}, u32[]{:S(2)}) async-start(s16[4,1,64,1152]{3,2,1,0:T(8,128)(2,1)} %gather_parts.3), calls=%async_computation.2 | async-start | bytes 1179648 | tf_op jit(solution)/shard_map/all_to_all | solution.py:526
  247.6 9.7 %collective-permute-done.17.refs_3_ = s16[1,208,1152]{2,1,0:T(8,128)(2,1)S(1)} collective-permute-done((s16[1,208,1152]{2,1,0:T(8,128)(2,1)}, s16[1,208,1152]{2,1,0:T(8,128)(2,1)S(1)}, u32[]{:S(2)}, u32[]{:S(2)}) %collective-permute-start.17) | collective-permute-done | bytes 479264 | tf_op jit(solution)/shard_map/ppermute | solution.py:495
  258.1 4.2 %gather_parts.5 = s16[4,1,64,1152]{3,2,1,0:T(8,128)(2,1)} custom-call(s32[2]{0:T(128)} %pad_add_fusion.ctl, s16[1,208,1152]{2,1,0:T(8,128)(2,1)} %get-tuple-element.62.refs_0_, s16[1,208,1152]{2,1,0:T(8,128)(2,1)} %copy-done.19, s16[1,208,1152]{2,1,0:T(8,128)(2,1)} %copy-done.20, s16[1,208,1152]{2,1,0:T(8,128)(2,1)} %copy-done.21), custom_call_target="tpu_custom_call" | custom-call | flops 28991029248 | bytes 221184 | tf_op jit(solution)/shard_map/gather_parts/pallas_call | solution.py:407
  262.3 4.8 %all-to-all-start = ((s16[4,1,64,1152]{3,2,1,0:T(8,128)(2,1)}), s16[4,1,64,1152]{3,2,1,0:T(8,128)(2,1)S(1)}, u32[]{:S(2)}, u32[]{:S(2)}) async-start(s16[4,1,64,1152]{3,2,1,0:T(8,128)(2,1)} %gather_parts.5), calls=%async_computation | async-start | bytes 1179648 | tf_op jit(solution)/shard_map/all_to_all | solution.py:526
  267.1 2.7 compose.3.refs_0_
  269.8 2.7 compose.4.refs_0_
  272.4 9.7 %all-to-all-done.got = s16[4,1,64,1152]{3,2,1,0:T(8,128)(2,1)S(1)} async-done(((s16[4,1,64,1152]{3,2,1,0:T(8,128)(2,1)}), s16[4,1,64,1152]{3,2,1,0:T(8,128)(2,1)S(1)}, u32[]{:S(2)}, u32[]{:S(2)}) %all-to-all-start) | async-done | bytes 589856 | tf_op jit(solution)/shard_map/all_to_all | solution.py:526
  283.0 2.7 compose.5
  (97 shorter events, 30.6 us)
Async XLA Ops:
  0.0 10.6 %copy-start.4 = (f32[2]{0:T(128)S(1)}, f32[2]{0:T(128)}, u32[]{:S(2)}) copy-start(f32[2]{0:T(128)} %param.8) | copy-start | bytes 28
  4.2 14.7 %collective-permute-start.1 = (bf16[8,48,1152]{2,1,0:T(8,128)(2,1)}, bf16[8,48,1152]{2,1,0:T(8,128)(2,1)}, u32[]{:S(2)}, u32[]{:S(2)}) collective-permute-start(bf16[8,48,1152]{2,1,0:T(8,128)(2,1)} %get-tuple-element.71), channel_id=1, source_target_pairs={{1,0},{2,1},{3,2},{4,3},{5,4},{6,5},{7,6},{8,7},{9,8},{10,9},{11,1... | collective-permute-start | bytes 2654216 | tf_op jit(solution)/shard_map/ppermute | solution.py:492
  5.5 13.5 %collective-permute-start = (bf16[8,48,1152]{2,1,0:T(8,128)(2,1)}, bf16[8,48,1152]{2,1,0:T(8,128)(2,1)}, u32[]{:S(2)}, u32[]{:S(2)}) collective-permute-start(bf16[8,48,1152]{2,1,0:T(8,128)(2,1)} %get-tuple-element.72), channel_id=1, source_target_pairs={{0,1},{1,2},{2,3},{3,4},{4,5},{5,6},{6,7},{7,8},{8,9},{9,10},{10,1... | collective-permute-start | bytes 2654216 | tf_op jit(solution)/shard_map/ppermute | solution.py:492
  19.0 63.3 %collective-permute-start.2 = (bf16[8,48,1152]{2,1,0:T(8,128)(2,1)}, bf16[8,48,1152]{2,1,0:T(8,128)(2,1)S(1)}, u32[]{:S(2)}, u32[]{:S(2)}) collective-permute-start(bf16[8,48,1152]{2,1,0:T(8,128)(2,1)} %get-tuple-element.37), channel_id=1, source_target_pairs={{0,1},{1,2},{2,3},{3,4},{4,5},{5,6},{6,7},{7,8},{8,9},{9,10},{10,1... | collective-permute-start | bytes 2654216 | tf_op jit(solution)/shard_map/ppermute | solution.py:492
  32.8 49.5 %collective-permute-start.3 = (bf16[8,48,1152]{2,1,0:T(8,128)(2,1)S(1)}, bf16[8,48,1152]{2,1,0:T(8,128)(2,1)S(1)}, u32[]{:S(2)}, u32[]{:S(2)}) collective-permute-start(bf16[8,48,1152]{2,1,0:T(8,128)(2,1)S(1)} %get-tuple-element.38), channel_id=1, source_target_pairs={{1,0},{2,1},{3,2},{4,3},{5,4},{6,5},{7,6},{8,7},{9,8},{10,9},{11,1... | collective-permute-start | bytes 2654216 | tf_op jit(solution)/shard_map/ppermute | solution.py:492
  79.2 53.9 %collective-permute-start.6 = (s16[4,208,1152]{2,1,0:T(8,128)(2,1)}, s16[4,208,1152]{2,1,0:T(8,128)(2,1)S(1)}, u32[]{:S(2)}, u32[]{:S(2)}) collective-permute-start(s16[4,208,1152]{2,1,0:T(8,128)(2,1)} %get-tuple-element.35), channel_id=1, source_target_pairs={{0,1},{1,0},{2,3},{3,2},{4,5},{5,4},{6,7},{7,6},{8,9},{9,8},{10,11... | collective-permute-start | bytes 5750792 | tf_op jit(solution)/shard_map/ppermute | solution.py:495
  82.3 50.8 %collective-permute-start.4 = (bf16[8,48,1152]{2,1,0:T(8,128)(2,1)S(1)}, bf16[8,48,1152]{2,1,0:T(8,128)(2,1)S(1)}, u32[]{:S(2)}, u32[]{:S(2)}) collective-permute-start(bf16[8,48,1152]{2,1,0:T(8,128)(2,1)S(1)} %get-tuple-element.40), channel_id=1, source_target_pairs={{0,1},{1,2},{2,3},{3,4},{4,5},{5,6},{6,7},{7,8},{8,9},{9,10},{10,1... | collective-permute-start | bytes 2654216 | tf_op jit(solution)/shard_map/ppermute | solution.py:492
  84.2 48.8 %collective-permute-start.5 = (bf16[8,48,1152]{2,1,0:T(8,128)(2,1)S(1)}, bf16[8,48,1152]{2,1,0:T(8,128)(2,1)S(1)}, u32[]{:S(2)}, u32[]{:S(2)}) collective-permute-start(bf16[8,48,1152]{2,1,0:T(8,128)(2,1)S(1)} %get-tuple-element.41), channel_id=1, source_target_pairs={{1,0},{2,1},{3,2},{4,3},{5,4},{6,5},{7,6},{8,7},{9,8},{10,9},{11,1... | collective-permute-start | bytes 2654216 | tf_op jit(solution)/shard_map/ppermute | solution.py:492
  130.7 13.4 %collective-permute-start.7 = (s16[4,208,1152]{2,1,0:T(8,128)(2,1)}, s16[4,208,1152]{2,1,0:T(8,128)(2,1)S(1)}, u32[]{:S(2)}, u32[]{:S(2)}) collective-permute-start(s16[4,208,1152]{2,1,0:T(8,128)(2,1)} %get-tuple-element.39), channel_id=1, source_target_pairs={{0,1},{1,0},{2,3},{3,2},{4,5},{5,4},{6,7},{7,6},{8,9},{9,8},{10,11... | collective-permute-start | bytes 5750792 | tf_op jit(solution)/shard_map/ppermute | solution.py:495
  140.6 71.1 %collective-permute-start.10 = (s16[1,208,1152]{2,1,0:T(8,128)(2,1)}, s16[1,208,1152]{2,1,0:T(8,128)(2,1)S(1)}, u32[]{:S(2)}, u32[]{:S(2)}) collective-permute-start(s16[1,208,1152]{2,1,0:T(8,128)(2,1)} %get-tuple-element.44), channel_id=1, source_target_pairs={{0,6},{1,7},{2,4},{3,5},{4,2},{5,3},{6,0},{7,1},{8,14},{9,15},{10,... | collective-permute-start | bytes 1437704 | tf_op jit(solution)/shard_map/ppermute | solution.py:495
  142.9 23.0 %collective-permute-start.8 = (s16[1,208,1152]{2,1,0:T(8,128)(2,1)}, s16[1,208,1152]{2,1,0:T(8,128)(2,1)S(1)}, u32[]{:S(2)}, u32[]{:S(2)}) collective-permute-start(s16[1,208,1152]{2,1,0:T(8,128)(2,1)} %get-tuple-element.51), channel_id=1, source_target_pairs={{0,2},{1,3},{2,0},{3,1},{4,6},{5,7},{6,4},{7,5},{8,10},{9,11},{10,... | collective-permute-start | bytes 1437704 | tf_op jit(solution)/shard_map/ppermute | solution.py:495
  143.7 67.9 %collective-permute-start.9 = (s16[1,208,1152]{2,1,0:T(8,128)(2,1)}, s16[1,208,1152]{2,1,0:T(8,128)(2,1)S(1)}, u32[]{:S(2)}, u32[]{:S(2)}) collective-permute-start(s16[1,208,1152]{2,1,0:T(8,128)(2,1)} %get-tuple-element.52), channel_id=1, source_target_pairs={{0,4},{1,5},{2,6},{3,7},{4,0},{5,1},{6,2},{7,3},{8,12},{9,13},{10,... | collective-permute-start | bytes 1437704 | tf_op jit(solution)/shard_map/ppermute | solution.py:495
  151.6 60.1 %collective-permute-start.13 = (s16[1,208,1152]{2,1,0:T(8,128)(2,1)}, s16[1,208,1152]{2,1,0:T(8,128)(2,1)S(1)}, u32[]{:S(2)}, u32[]{:S(2)}) collective-permute-start(s16[1,208,1152]{2,1,0:T(8,128)(2,1)} %get-tuple-element.47), channel_id=1, source_target_pairs={{0,6},{1,7},{2,4},{3,5},{4,2},{5,3},{6,0},{7,1},{8,14},{9,15},{10,... | collective-permute-start | bytes 1437704 | tf_op jit(solution)/shard_map/ppermute | solution.py:495
  153.9 57.8 %collective-permute-start.11 = (s16[1,208,1152]{2,1,0:T(8,128)(2,1)}, s16[1,208,1152]{2,1,0:T(8,128)(2,1)S(1)}, u32[]{:S(2)}, u32[]{:S(2)}) collective-permute-start(s16[1,208,1152]{2,1,0:T(8,128)(2,1)} %get-tuple-element.54), channel_id=1, source_target_pairs={{0,2},{1,3},{2,0},{3,1},{4,6},{5,7},{6,4},{7,5},{8,10},{9,11},{10,... | collective-permute-start | bytes 1437704 | tf_op jit(solution)/shard_map/ppermute | solution.py:495
  166.0 45.6 %copy-start.14 = (s16[1,208,1152]{2,1,0:T(8,128)(2,1)}, s16[1,208,1152]{2,1,0:T(8,128)(2,1)S(1)}, u32[]{:S(2)}) copy-start(s16[1,208,1152]{2,1,0:T(8,128)(2,1)S(1)} %collective-permute-done.8.refs_1_) | copy-start | bytes 1437700
  166.0 45.7 %collective-permute-start.12 = (s16[1,208,1152]{2,1,0:T(8,128)(2,1)}, s16[1,208,1152]{2,1,0:T(8,128)(2,1)S(1)}, u32[]{:S(2)}, u32[]{:S(2)}) collective-permute-start(s16[1,208,1152]{2,1,0:T(8,128)(2,1)} %get-tuple-element.55), channel_id=1, source_target_pairs={{0,4},{1,5},{2,6},{3,7},{4,0},{5,1},{6,2},{7,3},{8,12},{9,13},{10,... | collective-permute-start | bytes 1437704 | tf_op jit(solution)/shard_map/ppermute | solution.py:495
  211.6 14.5 %collective-permute-start.14 = (s16[4,208,1152]{2,1,0:T(8,128)(2,1)}, s16[4,208,1152]{2,1,0:T(8,128)(2,1)S(1)}, u32[]{:S(2)}, u32[]{:S(2)}) collective-permute-start(s16[4,208,1152]{2,1,0:T(8,128)(2,1)} %get-tuple-element.49), channel_id=1, source_target_pairs={{0,1},{1,0},{2,3},{3,2},{4,5},{5,4},{6,7},{7,6},{8,9},{9,8},{10,11... | collective-permute-start | bytes 5750792 | tf_op jit(solution)/shard_map/ppermute | solution.py:495
  220.5 22.1 %all-to-all-start.1 = ((s16[4,1,64,1152]{3,2,1,0:T(8,128)(2,1)}), s16[4,1,64,1152]{3,2,1,0:T(8,128)(2,1)S(1)}, u32[]{:S(2)}, u32[]{:S(2)}) async-start(s16[4,1,64,1152]{3,2,1,0:T(8,128)(2,1)} %gather_parts.4), calls=%async_computation.1 | async-start | bytes 1179648 | tf_op jit(solution)/shard_map/all_to_all | solution.py:526
  233.6 14.0 %collective-permute-start.15 = (s16[1,208,1152]{2,1,0:T(8,128)(2,1)}, s16[1,208,1152]{2,1,0:T(8,128)(2,1)S(1)}, u32[]{:S(2)}, u32[]{:S(2)}) collective-permute-start(s16[1,208,1152]{2,1,0:T(8,128)(2,1)} %get-tuple-element.63), channel_id=1, source_target_pairs={{0,2},{1,3},{2,0},{3,1},{4,6},{5,7},{6,4},{7,5},{8,10},{9,11},{10,... | collective-permute-start | bytes 1437704 | tf_op jit(solution)/shard_map/ppermute | solution.py:495
  233.6 14.0 %collective-permute-start.16 = (s16[1,208,1152]{2,1,0:T(8,128)(2,1)}, s16[1,208,1152]{2,1,0:T(8,128)(2,1)S(1)}, u32[]{:S(2)}, u32[]{:S(2)}) collective-permute-start(s16[1,208,1152]{2,1,0:T(8,128)(2,1)} %get-tuple-element.64), channel_id=1, source_target_pairs={{0,4},{1,5},{2,6},{3,7},{4,0},{5,1},{6,2},{7,3},{8,12},{9,13},{10,... | collective-permute-start | bytes 1437704 | tf_op jit(solution)/shard_map/ppermute | solution.py:495
  234.4 22.9 %collective-permute-start.17 = (s16[1,208,1152]{2,1,0:T(8,128)(2,1)}, s16[1,208,1152]{2,1,0:T(8,128)(2,1)S(1)}, u32[]{:S(2)}, u32[]{:S(2)}) collective-permute-start(s16[1,208,1152]{2,1,0:T(8,128)(2,1)} %get-tuple-element.60), channel_id=1, source_target_pairs={{0,6},{1,7},{2,4},{3,5},{4,2},{5,3},{6,0},{7,1},{8,14},{9,15},{10,... | collective-permute-start | bytes 1437704 | tf_op jit(solution)/shard_map/ppermute | solution.py:495
  242.6 19.7 %copy-start = (s16[4,1,64,1152]{3,2,1,0:T(8,128)(2,1)}, s16[4,1,64,1152]{3,2,1,0:T(8,128)(2,1)S(1)}, u32[]{:S(2)}) copy-start(s16[4,1,64,1152]{3,2,1,0:T(8,128)(2,1)S(1)} %all-to-all-done.1.got) | copy-start | bytes 1769476
  242.6 19.7 %all-to-all-start.2 = ((s16[4,1,64,1152]{3,2,1,0:T(8,128)(2,1)}), s16[4,1,64,1152]{3,2,1,0:T(8,128)(2,1)S(1)}, u32[]{:S(2)}, u32[]{:S(2)}) async-start(s16[4,1,64,1152]{3,2,1,0:T(8,128)(2,1)} %gather_parts.3), calls=%async_computation.2 | async-start | bytes 1179648 | tf_op jit(solution)/shard_map/all_to_all | solution.py:526
  262.3 19.9 %all-to-all-start = ((s16[4,1,64,1152]{3,2,1,0:T(8,128)(2,1)}), s16[4,1,64,1152]{3,2,1,0:T(8,128)(2,1)S(1)}, u32[]{:S(2)}, u32[]{:S(2)}) async-start(s16[4,1,64,1152]{3,2,1,0:T(8,128)(2,1)} %gather_parts.5), calls=%async_computation | async-start | bytes 1179648 | tf_op jit(solution)/shard_map/all_to_all | solution.py:526
  (20 other events, 97.2 us)

commit v6 on v5

--- a/solution.py
+++ b/solution.py
@@ -9,7 +9,6 @@
 from jax.sharding import PartitionSpec as P
 
 LANES = 128
-HALF = LANES // 2
 CODES = 32700.0
 VMEM_LIMIT = 56 * 1024 * 1024
 
@@ -71,7 +70,7 @@
     lax.fori_loop(0, strips // together, step, 0)
 
 
-def render_kernel(ctl, light, table, slope, row_band, column_band, main, above, below, before, after, send, keep, cells, halves, image, stage, ends, *, groups, units, unit, block, rows, offset, total):
+def render_kernel(ctl, light, table, slope, row_bands, column_bands, main, above, below, before, after, send, keep, cells, slopes_y, slopes_z, image, stage, ends, *, groups, units, unit, block, rows, offset, total):
     i = pl.program_id(0)
     half = (groups // 2) * units
     rest = lax.rem(i, half)
@@ -83,89 +82,91 @@
     width = main.shape[2]
     tall = padded_rows(unit)
     aligned = block == unit
-    inner = slice(HALF, HALF + width)
-
-    @pl.when(i == 0)
-    def _():
-        halves[:, :, 0:LANES] = jnp.zeros((layers, tall, LANES), jnp.bfloat16)
-        halves[:, :, width:] = jnp.zeros((layers, tall, LANES), jnp.bfloat16)
 
     def load_layer(layer, carry):
+        shift = pl.multiple_of(lax.rem(start, block), 8)
+        stage[0:block, :] = main[layer].astype(jnp.float32)
+        body = stage[pl.ds(shift, unit), :]
         up = above[layer].astype(jnp.float32)
         down = below[layer].astype(jnp.float32)
-        up = jnp.where(start > 0, up, 0.0)
-        down = jnp.where(start + unit < total, down, 0.0)
-        if aligned:
-            cells[layer, 0:16, :] = up.astype(jnp.bfloat16)
-            cells[layer, 16:16 + unit, :] = main[layer]
-            cells[layer, 16 + unit:32 + unit, :] = down.astype(jnp.bfloat16)
-        else:
-            shift = pl.multiple_of(lax.rem(start, block), 8)
-            stage[0:block, :] = main[layer].astype(jnp.float32)
-            body = stage[pl.ds(shift, unit), :]
-            up = jnp.where(lax.rem(start, 16) == 0, up[8:16], up[0:8])
-            down = jnp.where(lax.rem(start + unit, 16) == 0, down[0:8], down[8:16])
-            stage[0:8, :] = jnp.zeros((8, width), jnp.float32)
-            stage[8:16, :] = up
-            stage[16:16 + unit, :] = body
-            stage[16 + unit:24 + unit, :] = down
-            stage[24 + unit:tall + 32, :] = jnp.zeros((tall + 8 - unit, width), jnp.float32)
-            cells[layer, :, :] = stage[0:tall + 32, :].astype(jnp.bfloat16)
-        halves[layer, :, inner] = cells[layer, 16:16 + tall, :]
+        up = jnp.where(lax.rem(start, 16) == 0, up[8:16], up[0:8])
+        down = jnp.where(lax.rem(start + unit, 16) == 0, down[0:8], down[8:16])
+        stage[0:8, :] = jnp.zeros((8, width), jnp.float32)
+        stage[8:16, :] = up
+        stage[16:16 + unit, :] = body
+        stage[16 + unit:24 + unit, :] = down
+        stage[24 + unit:tall + 32, :] = jnp.zeros((tall + 8 - unit, width), jnp.float32)
+        cells[layer, :, :] = stage[0:tall + 32, :].astype(jnp.bfloat16)
         return carry
 
-    lax.fori_loop(0, layers, load_layer, 0)
     if not aligned:
+        lax.fori_loop(0, layers, load_layer, 0)
         ends[0, 0:unit, :] = before[0].astype(jnp.float32)
         ends[1, 0:unit, :] = after[0].astype(jnp.float32)
+
+    def own(first, count, s, cols):
+        if aligned:
+            return main[first:first + count, s, cols]
+        return cells[first:first + count, 16 + s.start:16 + s.stop, cols]
+
+    def tower(layer, cols):
+        if aligned:
+            return jnp.concatenate([above[layer, :, cols], main[layer, :, cols], below[layer, :, cols]], axis=0)
+        return cells[layer, :, cols]
+
+    def end(which, s, cols):
+        if aligned:
+            return (before, after)[which][0, s, cols].astype(jnp.float32)
+        return ends[which, s, cols]
 
     lx, ly, lz = light[0], light[1], light[2]
     step = 16
     bins = table.shape[1] // step
-    slopes = [jnp.broadcast_to(slope[k:k + 1, :], (step, LANES)) for k in range(4)]
+    tilts_of = [jnp.broadcast_to(slope[k:k + 1, :], (step, LANES)) for k in range(4)]
+    row_kind = jnp.where(start == 0, 1, 0) + jnp.where(start + unit == total, 2, 0)
 
     def strip(c, carry):
         at = pl.multiple_of(c * LANES, LANES)
         cols = pl.ds(at, LANES)
-        window = pl.ds(at, 2 * LANES)
-        spans = [slice(r, r + step) for r in range(0, tall, step)]
-        inside = [slice(16 + r, 16 + r + step) for r in range(0, tall, step)]
-        if aligned:
-            low = [before[0, s, cols].astype(jnp.float32) for s in spans]
-            far = [after[0, s, cols].astype(jnp.float32) for s in spans]
-        else:
-            low = [ends[0, s, cols] for s in spans]
-            far = [ends[1, s, cols] for s in spans]
-        here = [cells[0, s, cols].astype(jnp.float32) for s in inside]
-        clear = [None] * len(spans)
-        colour = [None] * len(spans)
+        window = pl.ds(pl.multiple_of(jnp.clip(at - LANES, 0, width - 3 * LANES), LANES), 3 * LANES)
+        column_kind = jnp.where(at == 0, 0, jnp.where(at == width - LANES, 2, 1))
         for first in range(0, layers, 2):
-            pair = range(first, min(first + 2, layers))
-            count = len(pair)
-            both = jnp.concatenate([cells[l, :, cols] for l in pair], axis=1) if count > 1 else cells[first, :, cols]
-            slope_y = jnp.dot(row_band[...], both, preferred_element_type=jnp.float32)
-            wide = halves[first:first + count, :, window].reshape(count * tall, 2 * LANES)
-            slope_z = jnp.dot(wide, column_band[...], preferred_element_type=jnp.float32)
-            for n, s in enumerate(spans):
+            count = min(2, layers - first)
+            towers = [tower(first + m, cols) for m in range(count)]
+            both = jnp.concatenate(towers, axis=1) if count > 1 else towers[0]
+            found = jnp.dot(row_bands[row_kind], both, preferred_element_type=jnp.float32)
+            wide = own(first, count, slice(0, tall), window).reshape(count * tall, 3 * LANES)
+            across = jnp.dot(wide, column_bands[column_kind], preferred_element_type=jnp.float32)
+            for m in range(count):
+                slopes_y[first + m] = found[:, m * LANES:(m + 1) * LANES]
+                slopes_z[first + m] = across[m * tall:(m + 1) * tall]
+
+        for r in range(0, tall, step):
+            s = slice(r, r + step)
+            low = end(0, s, cols)
+            here = own(0, 1, s, cols)[0].astype(jnp.float32)
+            clear, colour = None, None
+            for first in range(0, layers, 2):
+                pair = range(first, min(first + 2, layers))
                 parts, picks, shades, tilts = [], [], [], []
-                for m, layer in enumerate(pair):
+                for layer in pair:
                     if layer + 1 < layers:
-                        high = cells[layer + 1, inside[n], cols].astype(jnp.float32)
+                        high = own(layer + 1, 1, s, cols)[0].astype(jnp.float32)
                     else:
-                        high = far[n]
-                    position = jnp.clip(here[n] * 2.5 + 7.5, 0.0, 15.0)
+                        high = end(1, s, cols)
+                    position = jnp.clip(here * 2.5 + 7.5, 0.0, 15.0)
                     index = position.astype(jnp.int32)
                     whole = index.astype(jnp.float32)
                     parts.append(position - whole)
-                    tilts.append([lookup(slopes[k], index) for k in range(4)])
+                    tilts.append([lookup(tilts_of[k], index) for k in range(4)])
                     picks.append(choose(bins, whole))
-                    gx = high - low[n]
-                    gy = slope_y[s, m * LANES:(m + 1) * LANES]
-                    gz = slope_z[m * tall + s.start:m * tall + s.stop]
+                    gx = high - low
+                    gy = slopes_y[layer, s, :]
+                    gz = slopes_z[layer, s, :]
                     facing = jnp.abs(gx * lx + gy * ly + gz * lz)
                     square = gx * gx + gy * gy + gz * gz
                     shades.append(0.045 + facing * lax.rsqrt(jnp.maximum(square, 4.0)))
-                    low[n], here[n] = here[n], high
+                    low, here = here, high
                 pick = jnp.concatenate(picks, axis=1) if len(picks) > 1 else picks[0]
                 found = jnp.dot(table[...], pick, preferred_element_type=jnp.float32)
                 for m, layer in enumerate(pair):
@@ -176,29 +177,23 @@
                         + parts[m] * tilts[m][k]
                         for k in range(4)
                     ]
-                    shade = shades[m]
                     if layer == 0:
-                        colour[n] = [tf[k] * shade for k in range(3)]
-                        clear[n] = 1.0 - tf[3]
+                        colour = [tf[k] * shades[m] for k in range(3)]
+                        clear = 1.0 - tf[3]
                     else:
-                        seen = shade * clear[n]
-                        colour[n] = [colour[n][k] + tf[k] * seen for k in range(3)]
-                        clear[n] = clear[n] - clear[n] * tf[3]
-        for n, s in enumerate(spans):
+                        seen = shades[m] * clear
+                        colour = [colour[k] + tf[k] * seen for k in range(3)]
+                        clear = clear - clear * tf[3]
             for k in range(3):
-                image[k, s, cols] = colour[n][k]
-            image[3, s, cols] = 1.0 - clear[n]
+                image[k, s, cols] = colour[k]
+            image[3, s, cols] = 1.0 - clear
         return carry
 
     lax.fori_loop(0, width // LANES, strip, 0)
 
     @pl.when(sending)
     def _():
-        def put(at):
-            cols = pl.ds(at, LANES)
-            put_codes(send, [image[k, 0:unit, cols] for k in range(4)], cols, unit)
-
-        each_strip(width, put)
+        send[0] = image[:, 0:unit, :]
 
     @pl.when(jnp.logical_not(sending))
     def _():
@@ -212,11 +207,8 @@
     send[0, 4 * unit:4 * unit + 16, cols] = row
 
 
-def get_unit(ctl, mine, got, cols, unit):
-    theirs = decode(
-        [got[0, k * unit:(k + 1) * unit, cols] for k in range(4)],
-        got[0, 4 * unit:4 * unit + 16, cols],
-    )
+def get_unit(ctl, mine, got, cols):
+    theirs = [got[0, k, :, cols] for k in range(4)]
     ours = [mine[0, k, :, cols] for k in range(4)]
     behind = ctl[1] == 1
     front = [jnp.where(behind, t, o) for t, o in zip(theirs, ours)]
@@ -232,7 +224,7 @@
         def _(send=send):
             def put(at):
                 cols = pl.ds(at, LANES)
-                put_codes(send, get_unit(ctl, mine, got, cols, unit), cols, unit)
+                put_codes(send, get_unit(ctl, mine, got, cols), cols, unit)
 
             each_strip(width, put)
 
@@ -296,11 +288,11 @@
 def split_outputs(groups, units, unit, width):
     half = (groups // 2) * units
     shapes = [
-        jax.ShapeDtypeStruct((half, 4 * unit + 16, width), jnp.int16),
+        jax.ShapeDtypeStruct((half, 4, unit, width), jnp.float32),
         jax.ShapeDtypeStruct((half, 4, unit, width), jnp.float32),
     ]
     specs = [
-        pl.BlockSpec((1, 4 * unit + 16, width), lambda i, ctl: (jnp.minimum(i, half - 1), 0, 0)),
+        pl.BlockSpec((1, 4, unit, width), lambda i, ctl: (jnp.minimum(i, half - 1), 0, 0, 0)),
         pl.BlockSpec((1, 4, unit, width), lambda i, ctl: (jnp.maximum(i - half, 0), 0, 0, 0)),
     ]
     return shapes, specs
@@ -316,7 +308,13 @@
     block = math.lcm(unit, 16)
     tall = padded_rows(unit)
     row_band = band((tall, tall + 32), 1, 16)
-    column_band = band((2 * LANES, LANES), 0, HALF)
+    place = lax.broadcasted_iota(jnp.int32, (tall, tall + 32), 1)
+    top, bottom = place >= 16, place < 16 + unit
+    row_bands = jnp.stack([
+        jnp.where(jnp.logical_and(jnp.logical_or(top, kind % 2 == 0), jnp.logical_or(bottom, kind < 2)), row_band, 0)
+        for kind in range(4)
+    ])
+    column_bands = jnp.stack([band((3 * LANES, LANES), 0, k * LANES) for k in range(3)])
     half = (groups // 2) * units
     index = unit_index(groups, units, 0)
 
@@ -347,8 +345,8 @@
                 pl.BlockSpec(memory_space=pltpu.SMEM),
                 pl.BlockSpec(table.shape, lambda i, ctl: (0, 0)),
                 pl.BlockSpec(slope.shape, lambda i, ctl: (0, 0)),
-                pl.BlockSpec((tall, tall + 32), lambda i, ctl: (0, 0)),
-                pl.BlockSpec((2 * LANES, LANES), lambda i, ctl: (0, 0)),
+                pl.BlockSpec((4, tall, tall + 32), lambda i, ctl: (0, 0, 0)),
+                pl.BlockSpec((3, 3 * LANES, LANES), lambda i, ctl: (0, 0, 0)),
                 pl.BlockSpec((layers, block, width), main_at),
                 pl.BlockSpec((layers, 16, width), above_at),
                 pl.BlockSpec((layers, 16, width), below_at),
@@ -357,8 +355,9 @@
             ],
             out_specs=specs,
             scratch_shapes=[
-                pltpu.VMEM((layers, tall + 32, width), jnp.bfloat16),
-                pltpu.VMEM((layers, tall, width + LANES), jnp.bfloat16),
+                pltpu.VMEM((layers, tall + 32, width) if block != unit else (1, 16, LANES), jnp.bfloat16),
+                pltpu.VMEM((layers, tall, LANES), jnp.float32),
+                pltpu.VMEM((layers, tall, LANES), jnp.float32),
                 pltpu.VMEM((4, tall, width), jnp.float32),
                 pltpu.VMEM((max(block, tall + 32), width) if block != unit else (8, LANES), jnp.float32),
                 pltpu.VMEM((2, tall, width) if block != unit else (1, 8, LANES), jnp.float32),
@@ -368,7 +367,7 @@
         compiler_params=params(),
         cost_estimate=pl.CostEstimate(flops=16384 * cells, bytes_accessed=6 * cells, transcendentals=cells),
         name="render",
-    )(ctl, light, table, slope, row_band, column_band, field, field, field, before, after)
+    )(ctl, light, table, slope, row_bands, column_bands, field, field, field, before, after)
 
 
 def merge(ctl, mine, got, *, places, units, unit):
@@ -390,7 +389,7 @@
             grid=(places * units,),
             in_specs=[
                 pl.BlockSpec((1, 4, unit, width), lambda i, ctl: (index(i, ctl), 0, 0, 0)),
-                pl.BlockSpec((1, 4 * unit + 16, width), lambda i, ctl: (index(i, ctl), 0, 0)),
+                pl.BlockSpec((1, 4, unit, width), lambda i, ctl: (index(i, ctl), 0, 0, 0)),
             ],
             out_specs=[spec(k) for k in range(places)],
         ),

time: 287 us -> 270 us (0.941)
  Pallas kernels: 174 us -> 159 us
  local copies, waits for them, and re-layouts: 13.6 us -> 9.67 us
    pallas_call x3, Pallas kernels: 135 us -> 121 us  [render(): pl.pallas_call(kernel, grid_spec=pltpu.PrefetchScalarGridSpec(num_scalar_...]
    unnamed x47 -> x41, local copies, waits for them, and re-layouts: 6.43 us -> 2.51 us
  transfers between devices with their start and end apart: 21 -> 21, of which waited for: 5 -> 6; matrix products, arithmetic and copies ran while one was open for 2% -> 2% of each run, Pallas kernels for 60% -> 58%
where the time goes in v6:
time: 270 us; the launch traced here: 269 us
  Pallas kernels  159 us (59%)
  starting transfers between devices  53.4 us (20%)
  waiting for transfers between devices  39.9 us (15%)
  local copies, waits for them, and re-layouts  9.67 us (4%)
  other arithmetic  3.66 us (1%)
  between operations  2.87 us (1%)
    pallas_call x3, Pallas kernels, render(): pl.pallas_call(kernel, grid_spec=pltpu.PrefetchScalarGridSpec(num_scalar_...  121 us
    ppermute x12, waiting for transfers between devices, exchange(): return lax.ppermute(send, 'tile', [(i, i ^ distance) for i in range(tiles)])  22.4 us
    ppermute x3, starting transfers between devices, per_device(): lax.ppermute(ends[0], both, up)  20.5 us
    pallas_call x3, Pallas kernels, merge(): pl.pallas_call(functools.partial(merge_kernel, units=units, unit=unit), g...  18.8 us
    all_to_all x3, waiting for transfers between devices, block_chunk(): lax.all_to_all(send, 'depth', split_axis=0, concat_axis=0, tiled=True)  17.4 us
    ppermute x12, starting transfers between devices, exchange(): return lax.ppermute(send, 'tile', [(i, i ^ distance) for i in range(tiles)])  16 us
    all_to_all x3, starting transfers between devices, block_chunk(): lax.all_to_all(send, 'depth', split_axis=0, concat_axis=0, tiled=True)  13 us
    pallas_call x3, Pallas kernels, gather_parts(): pl.pallas_call(functools.partial(gather_kernel, unit=unit, blocks=blocks)...  11.9 us
  transfers between devices with their start and end apart: 21, of which 6 were waited for; matrix products, arithmetic and copies ran while one was open for 2% of the time, Pallas kernels for 58%

profile of v6, /device:TPU:0, one launch (start us, length us, event | category | flops | bytes accessed | tf_op | source)
XLA Modules:
  0.0 268.7 jit_solution(1265499462226417615)
XLA Ops:
  0.0 4.2 %slice_bitcast_fusion = (bf16[8,48,1152]{2,1,0:T(8,128)(2,1)S(1)}, bf16[8,48,1152]{2,1,0:T(8,128)(2,1)S(1)}, bf16[8,48,1152]{2,1,0:T(8,128)(2,1)S(1)}, bf16[8,48...) fusion(bf16[6,8,144,1152]{3,2,1,0:T(8,128)(2,1)} %bitcast.20), kind=kLoop, calls=%fused_computation.2 | loop fusion | bytes 10616832 | tf_op jit(solution)/shard_map/reshape | solution.py:486
  5.5 4.0 %collective-permute-start = (bf16[8,48,1152]{2,1,0:T(8,128)(2,1)}, bf16[8,48,1152]{2,1,0:T(8,128)(2,1)}, u32[]{:S(2)}, u32[]{:S(2)}) collective-permute-start(bf16[8,48,1152]{2,1,0:T(8,128)(2,1)} %get-tuple-element.72), channel_id=1, source_target_pairs={{0,1},{1,2},{2,3},{3,4},{4,5},{5,6},{6,7},{7,8},{8,9},{9,10},{10,1... | collective-permute-start | bytes 2654216 | tf_op jit(solution)/shard_map/ppermute | solution.py:491
  18.3 14.5 %collective-permute-start.2 = (bf16[8,48,1152]{2,1,0:T(8,128)(2,1)}, bf16[8,48,1152]{2,1,0:T(8,128)(2,1)S(1)}, u32[]{:S(2)}, u32[]{:S(2)}) collective-permute-start(bf16[8,48,1152]{2,1,0:T(8,128)(2,1)} %get-tuple-element.37), channel_id=1, source_target_pairs={{0,1},{1,2},{2,3},{3,4},{4,5},{5,6},{6,7},{7,8},{8,9},{9,10},{10,1... | collective-permute-start | bytes 2654216 | tf_op jit(solution)/shard_map/ppermute | solution.py:491
  34.1 40.2 %render.3 = (f32[4,4,48,1152]{3,2,1,0:T(8,128)}, f32[4,4,48,1152]{3,2,1,0:T(8,128)}) custom-call(s32[2]{0:T(128)} %pad_add_fusion.1.ctl, f32[3]{0:T(128)} %maximum_multiply_fusion.light, bf16[128,256]{1,0:T(8,128)(2,1)} %convert_element_type.95.table, f32[8,128]{1,0:T(8,128)} %pad.23.slope, bf16[4,48,80]{2,1,0:T(8,128)(2,1)} %pad_maximum_fusion.1.row_bands, ...), custom_call_target="tpu_custom_call" | custom-call | flops 43486543872 | bytes 15925248 | tf_op jit(solution)/shard_map/render/pallas_call | solution.py:339
  74.3 3.1 %collective-permute-start.6 = (f32[4,4,48,1152]{3,2,1,0:T(8,128)}, f32[4,4,48,1152]{3,2,1,0:T(8,128)}, u32[]{:S(2)}, u32[]{:S(2)}) collective-permute-start(f32[4,4,48,1152]{3,2,1,0:T(8,128)} %get-tuple-element.35), channel_id=1, source_target_pairs={{0,1},{1,0},{2,3},{3,2},{4,5},{5,4},{6,7},{7,6},{8,9},{9,8},{10,11... | collective-permute-start | bytes 10616840 | tf_op jit(solution)/shard_map/ppermute | solution.py:494
  80.7 40.2 %render.4 = (f32[4,4,48,1152]{3,2,1,0:T(8,128)}, f32[4,4,48,1152]{3,2,1,0:T(8,128)}) custom-call(s32[2]{0:T(128)} %pad_add_fusion.1.ctl, f32[3]{0:T(128)} %maximum_multiply_fusion.light, bf16[128,256]{1,0:T(8,128)(2,1)} %convert_element_type.95.table, f32[8,128]{1,0:T(8,128)} %pad.23.slope, bf16[4,48,80]{2,1,0:T(8,128)(2,1)} %pad_maximum_fusion.1.row_bands, ...), custom_call_target="tpu_custom_call" | custom-call | flops 43486543872 | bytes 15925248 | tf_op jit(solution)/shard_map/render/pallas_call | solution.py:339
  123.8 6.3 %merge.3 = (s16[1,208,1152]{2,1,0:T(8,128)(2,1)}, s16[1,208,1152]{2,1,0:T(8,128)(2,1)}, s16[1,208,1152]{2,1,0:T(8,128)(2,1)}, s16[1,208,1152]{2,1,0:T(8,128)(2,1)}) custom-call(s32[2]{0:T(128)} %pad_add_fusion.ctl, f32[4,4,48,1152]{3,2,1,0:T(8,128)} %get-tuple-element.43.mine, f32[4,4,48,1152]{3,2,1,0:T(8,128)} %collective-permute-done.6.got), custom_call_target="tpu_custom_call" | custom-call | flops 28991029248 | bytes 884736 | tf_op jit(solution)/shard_map/merge/pallas_call | solution.py:385
  133.7 6.3 %merge.4 = (s16[1,208,1152]{2,1,0:T(8,128)(2,1)}, s16[1,208,1152]{2,1,0:T(8,128)(2,1)}, s16[1,208,1152]{2,1,0:T(8,128)(2,1)}, s16[1,208,1152]{2,1,0:T(8,128)(2,1)}) custom-call(s32[2]{0:T(128)} %pad_add_fusion.ctl, f32[4,4,48,1152]{3,2,1,0:T(8,128)} %get-tuple-element.46.mine, f32[4,4,48,1152]{3,2,1,0:T(8,128)} %collective-permute-done.7.got), custom_call_target="tpu_custom_call" | custom-call | flops 28991029248 | bytes 884736 | tf_op jit(solution)/shard_map/merge/pallas_call | solution.py:385
  143.0 12.5 %collective-permute-done.8.refs_1_ = s16[1,208,1152]{2,1,0:T(8,128)(2,1)S(1)} collective-permute-done((s16[1,208,1152]{2,1,0:T(8,128)(2,1)}, s16[1,208,1152]{2,1,0:T(8,128)(2,1)S(1)}, u32[]{:S(2)}, u32[]{:S(2)}) %collective-permute-start.8) | collective-permute-done | bytes 479264 | tf_op jit(solution)/shard_map/ppermute | solution.py:494
  156.0 40.1 %render.5 = (f32[4,4,48,1152]{3,2,1,0:T(8,128)}, f32[4,4,48,1152]{3,2,1,0:T(8,128)}) custom-call(s32[2]{0:T(128)} %pad_add_fusion.1.ctl, f32[3]{0:T(128)} %maximum_multiply_fusion.light, bf16[128,256]{1,0:T(8,128)(2,1)} %convert_element_type.95.table, f32[8,128]{1,0:T(8,128)} %pad.23.slope, bf16[4,48,80]{2,1,0:T(8,128)(2,1)} %pad_maximum_fusion.1.row_bands, ...), custom_call_target="tpu_custom_call" | custom-call | flops 43486543872 | bytes 15925248 | tf_op jit(solution)/shard_map/render/pallas_call | solution.py:339
  197.1 3.9 %gather_parts.3 = s16[4,1,64,1152]{3,2,1,0:T(8,128)(2,1)} custom-call(s32[2]{0:T(128)} %pad_add_fusion.ctl, s16[1,208,1152]{2,1,0:T(8,128)(2,1)} %get-tuple-element.50.refs_0_, s16[1,208,1152]{2,1,0:T(8,128)(2,1)} %copy-done.11, s16[1,208,1152]{2,1,0:T(8,128)(2,1)} %copy-done.12, s16[1,208,1152]{2,1,0:T(8,128)(2,1)} %copy-done.10), custom_call_target="tpu_custom_call" | custom-call | flops 28991029248 | bytes 221184 | tf_op jit(solution)/shard_map/gather_parts/pallas_call | solution.py:406
  201.0 4.0 %gather_parts.4 = s16[4,1,64,1152]{3,2,1,0:T(8,128)(2,1)} custom-call(s32[2]{0:T(128)} %pad_add_fusion.ctl, s16[1,208,1152]{2,1,0:T(8,128)(2,1)} %get-tuple-element.53.refs_0_, s16[1,208,1152]{2,1,0:T(8,128)(2,1)} %copy-done.14, s16[1,208,1152]{2,1,0:T(8,128)(2,1)} %copy-done.15, s16[1,208,1152]{2,1,0:T(8,128)(2,1)} %copy-done.13), custom_call_target="tpu_custom_call" | custom-call | flops 28991029248 | bytes 221184 | tf_op jit(solution)/shard_map/gather_parts/pallas_call | solution.py:406
  205.0 5.6 %all-to-all-start.1 = ((s16[4,1,64,1152]{3,2,1,0:T(8,128)(2,1)}), s16[4,1,64,1152]{3,2,1,0:T(8,128)(2,1)S(1)}, u32[]{:S(2)}, u32[]{:S(2)}) async-start(s16[4,1,64,1152]{3,2,1,0:T(8,128)(2,1)} %gather_parts.4), calls=%async_computation.1 | async-start | bytes 1179648 | tf_op jit(solution)/shard_map/all_to_all | solution.py:525
  210.6 6.2 %merge.5 = (s16[1,208,1152]{2,1,0:T(8,128)(2,1)}, s16[1,208,1152]{2,1,0:T(8,128)(2,1)}, s16[1,208,1152]{2,1,0:T(8,128)(2,1)}, s16[1,208,1152]{2,1,0:T(8,128)(2,1)}) custom-call(s32[2]{0:T(128)} %pad_add_fusion.ctl, f32[4,4,48,1152]{3,2,1,0:T(8,128)} %get-tuple-element.59.mine, f32[4,4,48,1152]{3,2,1,0:T(8,128)} %collective-permute-done.14.got), custom_call_target="tpu_custom_call" | custom-call | flops 28991029248 | bytes 884736 | tf_op jit(solution)/shard_map/merge/pallas_call | solution.py:385
  217.7 2.7 collective-permute-start.17
  220.3 6.8 %all-to-all-done.1.got = s16[4,1,64,1152]{3,2,1,0:T(8,128)(2,1)S(1)} async-done(((s16[4,1,64,1152]{3,2,1,0:T(8,128)(2,1)}), s16[4,1,64,1152]{3,2,1,0:T(8,128)(2,1)S(1)}, u32[]{:S(2)}, u32[]{:S(2)}) %all-to-all-start.1) | async-done | bytes 589856 | tf_op jit(solution)/shard_map/all_to_all | solution.py:525
  227.1 3.5 %all-to-all-start.2 = ((s16[4,1,64,1152]{3,2,1,0:T(8,128)(2,1)}), s16[4,1,64,1152]{3,2,1,0:T(8,128)(2,1)S(1)}, u32[]{:S(2)}, u32[]{:S(2)}) async-start(s16[4,1,64,1152]{3,2,1,0:T(8,128)(2,1)} %gather_parts.3), calls=%async_computation.2 | async-start | bytes 1179648 | tf_op jit(solution)/shard_map/all_to_all | solution.py:525
  230.9 9.7 %collective-permute-done.17.refs_3_ = s16[1,208,1152]{2,1,0:T(8,128)(2,1)S(1)} collective-permute-done((s16[1,208,1152]{2,1,0:T(8,128)(2,1)}, s16[1,208,1152]{2,1,0:T(8,128)(2,1)S(1)}, u32[]{:S(2)}, u32[]{:S(2)}) %collective-permute-start.17) | collective-permute-done | bytes 479264 | tf_op jit(solution)/shard_map/ppermute | solution.py:494
  241.3 4.0 %gather_parts.5 = s16[4,1,64,1152]{3,2,1,0:T(8,128)(2,1)} custom-call(s32[2]{0:T(128)} %pad_add_fusion.ctl, s16[1,208,1152]{2,1,0:T(8,128)(2,1)} %get-tuple-element.62.refs_0_, s16[1,208,1152]{2,1,0:T(8,128)(2,1)} %copy-done.16, s16[1,208,1152]{2,1,0:T(8,128)(2,1)} %copy-done.17, s16[1,208,1152]{2,1,0:T(8,128)(2,1)} %copy-done.18), custom_call_target="tpu_custom_call" | custom-call | flops 28991029248 | bytes 221184 | tf_op jit(solution)/shard_map/gather_parts/pallas_call | solution.py:406
  246.2 3.9 %all-to-all-start = ((s16[4,1,64,1152]{3,2,1,0:T(8,128)(2,1)}), s16[4,1,64,1152]{3,2,1,0:T(8,128)(2,1)S(1)}, u32[]{:S(2)}, u32[]{:S(2)}) async-start(s16[4,1,64,1152]{3,2,1,0:T(8,128)(2,1)} %gather_parts.5), calls=%async_computation | async-start | bytes 1179648 | tf_op jit(solution)/shard_map/all_to_all | solution.py:525
  250.2 2.7 compose.3.refs_0_
  252.8 2.7 compose.4.refs_0_
  255.5 9.7 %all-to-all-done.got = s16[4,1,64,1152]{3,2,1,0:T(8,128)(2,1)S(1)} async-done(((s16[4,1,64,1152]{3,2,1,0:T(8,128)(2,1)}), s16[4,1,64,1152]{3,2,1,0:T(8,128)(2,1)S(1)}, u32[]{:S(2)}, u32[]{:S(2)}) %all-to-all-start) | async-done | bytes 589856 | tf_op jit(solution)/shard_map/all_to_all | solution.py:525
  266.1 2.7 compose.5
  (99 shorter events, 26.4 us)
Async XLA Ops:
  0.0 13.5 %copy-start.5 = (f32[4]{0:T(128)S(1)}, f32[4]{0:T(128)}, u32[]{:S(2)}) copy-start(f32[4]{0:T(128)} %constant.60) | copy-start | bytes 52
  4.2 14.0 %collective-permute-start.1 = (bf16[8,48,1152]{2,1,0:T(8,128)(2,1)}, bf16[8,48,1152]{2,1,0:T(8,128)(2,1)}, u32[]{:S(2)}, u32[]{:S(2)}) collective-permute-start(bf16[8,48,1152]{2,1,0:T(8,128)(2,1)} %get-tuple-element.71), channel_id=1, source_target_pairs={{1,0},{2,1},{3,2},{4,3},{5,4},{6,5},{7,6},{8,7},{9,8},{10,9},{11,1... | collective-permute-start | bytes 2654216 | tf_op jit(solution)/shard_map/ppermute | solution.py:491
  5.5 12.7 %collective-permute-start = (bf16[8,48,1152]{2,1,0:T(8,128)(2,1)}, bf16[8,48,1152]{2,1,0:T(8,128)(2,1)}, u32[]{:S(2)}, u32[]{:S(2)}) collective-permute-start(bf16[8,48,1152]{2,1,0:T(8,128)(2,1)} %get-tuple-element.72), channel_id=1, source_target_pairs={{0,1},{1,2},{2,3},{3,4},{4,5},{5,6},{6,7},{7,8},{8,9},{9,10},{10,1... | collective-permute-start | bytes 2654216 | tf_op jit(solution)/shard_map/ppermute | solution.py:491
  18.3 59.1 %collective-permute-start.2 = (bf16[8,48,1152]{2,1,0:T(8,128)(2,1)}, bf16[8,48,1152]{2,1,0:T(8,128)(2,1)S(1)}, u32[]{:S(2)}, u32[]{:S(2)}) collective-permute-start(bf16[8,48,1152]{2,1,0:T(8,128)(2,1)} %get-tuple-element.37), channel_id=1, source_target_pairs={{0,1},{1,2},{2,3},{3,4},{4,5},{5,6},{6,7},{7,8},{8,9},{9,10},{10,1... | collective-permute-start | bytes 2654216 | tf_op jit(solution)/shard_map/ppermute | solution.py:491
  32.8 44.6 %collective-permute-start.3 = (bf16[8,48,1152]{2,1,0:T(8,128)(2,1)S(1)}, bf16[8,48,1152]{2,1,0:T(8,128)(2,1)S(1)}, u32[]{:S(2)}, u32[]{:S(2)}) collective-permute-start(bf16[8,48,1152]{2,1,0:T(8,128)(2,1)S(1)} %get-tuple-element.38), channel_id=1, source_target_pairs={{1,0},{2,1},{3,2},{4,3},{5,4},{6,5},{7,6},{8,7},{9,8},{10,9},{11,1... | collective-permute-start | bytes 2654216 | tf_op jit(solution)/shard_map/ppermute | solution.py:491
  74.3 49.5 %collective-permute-start.6 = (f32[4,4,48,1152]{3,2,1,0:T(8,128)}, f32[4,4,48,1152]{3,2,1,0:T(8,128)}, u32[]{:S(2)}, u32[]{:S(2)}) collective-permute-start(f32[4,4,48,1152]{3,2,1,0:T(8,128)} %get-tuple-element.35), channel_id=1, source_target_pairs={{0,1},{1,0},{2,3},{3,2},{4,5},{5,4},{6,7},{7,6},{8,9},{9,8},{10,11... | collective-permute-start | bytes 10616840 | tf_op jit(solution)/shard_map/ppermute | solution.py:494
  77.4 46.4 %collective-permute-start.4 = (bf16[8,48,1152]{2,1,0:T(8,128)(2,1)S(1)}, bf16[8,48,1152]{2,1,0:T(8,128)(2,1)S(1)}, u32[]{:S(2)}, u32[]{:S(2)}) collective-permute-start(bf16[8,48,1152]{2,1,0:T(8,128)(2,1)S(1)} %get-tuple-element.40), channel_id=1, source_target_pairs={{0,1},{1,2},{2,3},{3,4},{4,5},{5,6},{6,7},{7,8},{8,9},{9,10},{10,1... | collective-permute-start | bytes 2654216 | tf_op jit(solution)/shard_map/ppermute | solution.py:491
  79.4 44.4 %collective-permute-start.5 = (bf16[8,48,1152]{2,1,0:T(8,128)(2,1)S(1)}, bf16[8,48,1152]{2,1,0:T(8,128)(2,1)S(1)}, u32[]{:S(2)}, u32[]{:S(2)}) collective-permute-start(bf16[8,48,1152]{2,1,0:T(8,128)(2,1)S(1)} %get-tuple-element.41), channel_id=1, source_target_pairs={{1,0},{2,1},{3,2},{4,3},{5,4},{6,5},{7,6},{8,7},{9,8},{10,9},{11,1... | collective-permute-start | bytes 2654216 | tf_op jit(solution)/shard_map/ppermute | solution.py:491
  120.9 12.8 %collective-permute-start.7 = (f32[4,4,48,1152]{3,2,1,0:T(8,128)}, f32[4,4,48,1152]{3,2,1,0:T(8,128)}, u32[]{:S(2)}, u32[]{:S(2)}) collective-permute-start(f32[4,4,48,1152]{3,2,1,0:T(8,128)} %get-tuple-element.39), channel_id=1, source_target_pairs={{0,1},{1,0},{2,3},{3,2},{4,5},{5,4},{6,7},{7,6},{8,9},{9,8},{10,11... | collective-permute-start | bytes 10616840 | tf_op jit(solution)/shard_map/ppermute | solution.py:494
  130.1 66.1 %collective-permute-start.10 = (s16[1,208,1152]{2,1,0:T(8,128)(2,1)}, s16[1,208,1152]{2,1,0:T(8,128)(2,1)S(1)}, u32[]{:S(2)}, u32[]{:S(2)}) collective-permute-start(s16[1,208,1152]{2,1,0:T(8,128)(2,1)} %get-tuple-element.44), channel_id=1, source_target_pairs={{0,6},{1,7},{2,4},{3,5},{4,2},{5,3},{6,0},{7,1},{8,14},{9,15},{10,... | collective-permute-start | bytes 1437704 | tf_op jit(solution)/shard_map/ppermute | solution.py:494
  132.5 23.0 %collective-permute-start.8 = (s16[1,208,1152]{2,1,0:T(8,128)(2,1)}, s16[1,208,1152]{2,1,0:T(8,128)(2,1)S(1)}, u32[]{:S(2)}, u32[]{:S(2)}) collective-permute-start(s16[1,208,1152]{2,1,0:T(8,128)(2,1)} %get-tuple-element.51), channel_id=1, source_target_pairs={{0,2},{1,3},{2,0},{3,1},{4,6},{5,7},{6,4},{7,5},{8,10},{9,11},{10,... | collective-permute-start | bytes 1437704 | tf_op jit(solution)/shard_map/ppermute | solution.py:494
  133.3 62.9 %collective-permute-start.9 = (s16[1,208,1152]{2,1,0:T(8,128)(2,1)}, s16[1,208,1152]{2,1,0:T(8,128)(2,1)S(1)}, u32[]{:S(2)}, u32[]{:S(2)}) collective-permute-start(s16[1,208,1152]{2,1,0:T(8,128)(2,1)} %get-tuple-element.52), channel_id=1, source_target_pairs={{0,4},{1,5},{2,6},{3,7},{4,0},{5,1},{6,2},{7,3},{8,12},{9,13},{10,... | collective-permute-start | bytes 1437704 | tf_op jit(solution)/shard_map/ppermute | solution.py:494
  140.0 56.3 %collective-permute-start.13 = (s16[1,208,1152]{2,1,0:T(8,128)(2,1)}, s16[1,208,1152]{2,1,0:T(8,128)(2,1)S(1)}, u32[]{:S(2)}, u32[]{:S(2)}) collective-permute-start(s16[1,208,1152]{2,1,0:T(8,128)(2,1)} %get-tuple-element.47), channel_id=1, source_target_pairs={{0,6},{1,7},{2,4},{3,5},{4,2},{5,3},{6,0},{7,1},{8,14},{9,15},{10,... | collective-permute-start | bytes 1437704 | tf_op jit(solution)/shard_map/ppermute | solution.py:494
  142.3 54.0 %collective-permute-start.11 = (s16[1,208,1152]{2,1,0:T(8,128)(2,1)}, s16[1,208,1152]{2,1,0:T(8,128)(2,1)S(1)}, u32[]{:S(2)}, u32[]{:S(2)}) collective-permute-start(s16[1,208,1152]{2,1,0:T(8,128)(2,1)} %get-tuple-element.54), channel_id=1, source_target_pairs={{0,2},{1,3},{2,0},{3,1},{4,6},{5,7},{6,4},{7,5},{8,10},{9,11},{10,... | collective-permute-start | bytes 1437704 | tf_op jit(solution)/shard_map/ppermute | solution.py:494
  155.5 40.6 %copy-start.11 = (s16[1,208,1152]{2,1,0:T(8,128)(2,1)}, s16[1,208,1152]{2,1,0:T(8,128)(2,1)S(1)}, u32[]{:S(2)}) copy-start(s16[1,208,1152]{2,1,0:T(8,128)(2,1)S(1)} %collective-permute-done.8.refs_1_) | copy-start | bytes 1437700
  155.5 40.8 %collective-permute-start.12 = (s16[1,208,1152]{2,1,0:T(8,128)(2,1)}, s16[1,208,1152]{2,1,0:T(8,128)(2,1)S(1)}, u32[]{:S(2)}, u32[]{:S(2)}) collective-permute-start(s16[1,208,1152]{2,1,0:T(8,128)(2,1)} %get-tuple-element.55), channel_id=1, source_target_pairs={{0,4},{1,5},{2,6},{3,7},{4,0},{5,1},{6,2},{7,3},{8,12},{9,13},{10,... | collective-permute-start | bytes 1437704 | tf_op jit(solution)/shard_map/ppermute | solution.py:494
  196.2 14.4 %collective-permute-start.14 = (f32[4,4,48,1152]{3,2,1,0:T(8,128)}, f32[4,4,48,1152]{3,2,1,0:T(8,128)}, u32[]{:S(2)}, u32[]{:S(2)}) collective-permute-start(f32[4,4,48,1152]{3,2,1,0:T(8,128)} %get-tuple-element.49), channel_id=1, source_target_pairs={{0,1},{1,0},{2,3},{3,2},{4,5},{5,4},{6,7},{7,6},{8,9},{9,8},{10,11... | collective-permute-start | bytes 10616840 | tf_op jit(solution)/shard_map/ppermute | solution.py:494
  205.0 22.1 %all-to-all-start.1 = ((s16[4,1,64,1152]{3,2,1,0:T(8,128)(2,1)}), s16[4,1,64,1152]{3,2,1,0:T(8,128)(2,1)S(1)}, u32[]{:S(2)}, u32[]{:S(2)}) async-start(s16[4,1,64,1152]{3,2,1,0:T(8,128)(2,1)} %gather_parts.4), calls=%async_computation.1 | async-start | bytes 1179648 | tf_op jit(solution)/shard_map/all_to_all | solution.py:525
  216.9 14.0 %collective-permute-start.15 = (s16[1,208,1152]{2,1,0:T(8,128)(2,1)}, s16[1,208,1152]{2,1,0:T(8,128)(2,1)S(1)}, u32[]{:S(2)}, u32[]{:S(2)}) collective-permute-start(s16[1,208,1152]{2,1,0:T(8,128)(2,1)} %get-tuple-element.63), channel_id=1, source_target_pairs={{0,2},{1,3},{2,0},{3,1},{4,6},{5,7},{6,4},{7,5},{8,10},{9,11},{10,... | collective-permute-start | bytes 1437704 | tf_op jit(solution)/shard_map/ppermute | solution.py:494
  216.9 14.0 %collective-permute-start.16 = (s16[1,208,1152]{2,1,0:T(8,128)(2,1)}, s16[1,208,1152]{2,1,0:T(8,128)(2,1)S(1)}, u32[]{:S(2)}, u32[]{:S(2)}) collective-permute-start(s16[1,208,1152]{2,1,0:T(8,128)(2,1)} %get-tuple-element.64), channel_id=1, source_target_pairs={{0,4},{1,5},{2,6},{3,7},{4,0},{5,1},{6,2},{7,3},{8,12},{9,13},{10,... | collective-permute-start | bytes 1437704 | tf_op jit(solution)/shard_map/ppermute | solution.py:494
  217.7 22.9 %collective-permute-start.17 = (s16[1,208,1152]{2,1,0:T(8,128)(2,1)}, s16[1,208,1152]{2,1,0:T(8,128)(2,1)S(1)}, u32[]{:S(2)}, u32[]{:S(2)}) collective-permute-start(s16[1,208,1152]{2,1,0:T(8,128)(2,1)} %get-tuple-element.60), channel_id=1, source_target_pairs={{0,6},{1,7},{2,4},{3,5},{4,2},{5,3},{6,0},{7,1},{8,14},{9,15},{10,... | collective-permute-start | bytes 1437704 | tf_op jit(solution)/shard_map/ppermute | solution.py:494
  227.1 18.2 %copy-start = (s16[4,1,64,1152]{3,2,1,0:T(8,128)(2,1)}, s16[4,1,64,1152]{3,2,1,0:T(8,128)(2,1)S(1)}, u32[]{:S(2)}) copy-start(s16[4,1,64,1152]{3,2,1,0:T(8,128)(2,1)S(1)} %all-to-all-done.1.got) | copy-start | bytes 1769476
  227.1 19.1 %all-to-all-start.2 = ((s16[4,1,64,1152]{3,2,1,0:T(8,128)(2,1)}), s16[4,1,64,1152]{3,2,1,0:T(8,128)(2,1)S(1)}, u32[]{:S(2)}, u32[]{:S(2)}) async-start(s16[4,1,64,1152]{3,2,1,0:T(8,128)(2,1)} %gather_parts.3), calls=%async_computation.2 | async-start | bytes 1179648 | tf_op jit(solution)/shard_map/all_to_all | solution.py:525
  246.2 19.0 %all-to-all-start = ((s16[4,1,64,1152]{3,2,1,0:T(8,128)(2,1)}), s16[4,1,64,1152]{3,2,1,0:T(8,128)(2,1)S(1)}, u32[]{:S(2)}, u32[]{:S(2)}) async-start(s16[4,1,64,1152]{3,2,1,0:T(8,128)(2,1)} %gather_parts.5), calls=%async_computation | async-start | bytes 1179648 | tf_op jit(solution)/shard_map/all_to_all | solution.py:525
  (17 other events, 91.9 us)

commit v7 on v6

--- a/solution.py
+++ b/solution.py
@@ -48,12 +48,6 @@
     )
 
 
-def choose(bins, whole):
-    place = whole.astype(jnp.bfloat16)
-    one, zero = jnp.ones_like(place), jnp.zeros_like(place)
-    return jnp.concatenate([jnp.where(place == k, one, zero) for k in range(bins)], axis=0)
-
-
 def padded_rows(unit):
     return -(-unit // 16) * 16
 
@@ -70,7 +64,7 @@
     lax.fori_loop(0, strips // together, step, 0)
 
 
-def render_kernel(ctl, light, table, slope, row_bands, column_bands, main, above, below, before, after, send, keep, cells, slopes_y, slopes_z, image, stage, ends, *, groups, units, unit, block, rows, offset, total):
+def render_kernel(ctl, light, table, row_bands, column_bands, main, above, below, before, after, send, keep, cells, slopes_y, slopes_z, image, stage, ends, *, groups, units, unit, block, rows, offset, total):
     i = pl.program_id(0)
     half = (groups // 2) * units
     rest = lax.rem(i, half)
@@ -121,8 +115,7 @@
 
     lx, ly, lz = light[0], light[1], light[2]
     step = 16
-    bins = table.shape[1] // step
-    tilts_of = [jnp.broadcast_to(slope[k:k + 1, :], (step, LANES)) for k in range(4)]
+    tables = [jnp.broadcast_to(table[k:k + 1, :], (step, LANES)) for k in range(8)]
     row_kind = jnp.where(start == 0, 1, 0) + jnp.where(start + unit == total, 2, 0)
 
     def strip(c, carry):
@@ -146,44 +139,26 @@
             low = end(0, s, cols)
             here = own(0, 1, s, cols)[0].astype(jnp.float32)
             clear, colour = None, None
-            for first in range(0, layers, 2):
-                pair = range(first, min(first + 2, layers))
-                parts, picks, shades, tilts = [], [], [], []
-                for layer in pair:
-                    if layer + 1 < layers:
-                        high = own(layer + 1, 1, s, cols)[0].astype(jnp.float32)
-                    else:
-                        high = end(1, s, cols)
-                    position = jnp.clip(here * 2.5 + 7.5, 0.0, 15.0)
-                    index = position.astype(jnp.int32)
-                    whole = index.astype(jnp.float32)
-                    parts.append(position - whole)
-                    tilts.append([lookup(tilts_of[k], index) for k in range(4)])
-                    picks.append(choose(bins, whole))
-                    gx = high - low
-                    gy = slopes_y[layer, s, :]
-                    gz = slopes_z[layer, s, :]
-                    facing = jnp.abs(gx * lx + gy * ly + gz * lz)
-                    square = gx * gx + gy * gy + gz * gz
-                    shades.append(0.045 + facing * lax.rsqrt(jnp.maximum(square, 4.0)))
-                    low, here = here, high
-                pick = jnp.concatenate(picks, axis=1) if len(picks) > 1 else picks[0]
-                found = jnp.dot(table[...], pick, preferred_element_type=jnp.float32)
-                for m, layer in enumerate(pair):
-                    lanes = slice(m * LANES, (m + 1) * LANES)
-                    tf = [
-                        found[k * step:(k + 1) * step, lanes]
-                        + found[(4 + k) * step:(5 + k) * step, lanes]
-                        + parts[m] * tilts[m][k]
-                        for k in range(4)
-                    ]
-                    if layer == 0:
-                        colour = [tf[k] * shades[m] for k in range(3)]
-                        clear = 1.0 - tf[3]
-                    else:
-                        seen = shades[m] * clear
-                        colour = [colour[k] + tf[k] * seen for k in range(3)]
-                        clear = clear - clear * tf[3]
+            for layer in range(layers):
+                high = own(layer + 1, 1, s, cols)[0].astype(jnp.float32) if layer + 1 < layers else end(1, s, cols)
+                position = jnp.clip(here * 2.5 + 7.5, 0.0, 15.0)
+                index = position.astype(jnp.int32)
+                part = position - index.astype(jnp.float32)
+                tf = [lookup(tables[k], index) + part * lookup(tables[4 + k], index) for k in range(4)]
+                gx = high - low
+                gy = slopes_y[layer, s, :]
+                gz = slopes_z[layer, s, :]
+                facing = jnp.abs(gx * lx + gy * ly + gz * lz)
+                square = gx * gx + gy * gy + gz * gz
+                shade = 0.045 + facing * lax.rsqrt(jnp.maximum(square, 4.0))
+                low, here = here, high
+                if layer == 0:
+                    colour = [tf[k] * shade for k in range(3)]
+                    clear = 1.0 - tf[3]
+                else:
+                    seen = shade * clear
+                    colour = [colour[k] + tf[k] * seen for k in range(3)]
+                    clear = clear - clear * tf[3]
             for k in range(3):
                 image[k, s, cols] = colour[k]
             image[3, s, cols] = 1.0 - clear
@@ -200,14 +175,7 @@
         keep[0] = image[:, 0:unit, :]
 
 
-def put_codes(send, values, cols, unit):
-    codes, row = encode(values)
-    for k in range(4):
-        send[0, k * unit:(k + 1) * unit, cols] = codes[k]
-    send[0, 4 * unit:4 * unit + 16, cols] = row
-
-
-def get_unit(ctl, mine, got, cols):
+def merge_pair(ctl, mine, got, cols):
     theirs = [got[0, k, :, cols] for k in range(4)]
     ours = [mine[0, k, :, cols] for k in range(4)]
     behind = ctl[1] == 1
@@ -216,17 +184,42 @@
     return over(front, back)
 
 
-def merge_kernel(ctl, mine, got, *sends, units, unit):
-    turn = pl.program_id(0) // units
-    width = mine.shape[3]
+def merge_kernel(ctl, *refs, members, places, unit):
+    inputs, sends = refs[:2 * members], refs[2 * members:2 * members + places]
+    image, tops = refs[2 * members + places:]
+    turn = pl.program_id(0)
+    width = image.shape[2]
+
+    for n in range(members):
+        @pl.when(lax.rem(turn, members) == n)
+        def _(n=n):
+            def put(at):
+                cols = pl.ds(at, LANES)
+                merged = merge_pair(ctl, inputs[2 * n], inputs[2 * n + 1], cols)
+                for k in range(4):
+                    image[k, :, cols] = merged[k]
+                top = functools.reduce(jnp.maximum, merged)
+                tops[0:8, cols] = jnp.max(top.reshape(unit // 8, 8, LANES), axis=0)
+
+            each_strip(width, put)
+
+    top = jnp.max(tops[0:8, :], axis=0, keepdims=True)
+    exponent = jnp.ceil(jnp.log2(jnp.maximum(top, 1e-30)))
+    tops[0:8, :] = jnp.broadcast_to(jnp.exp2(-exponent) * CODES, (8, width))
+    row = jnp.broadcast_to(exponent, (16, width)).astype(jnp.int32).astype(jnp.int16)
+
     for k, send in enumerate(sends):
-        @pl.when(turn == k)
+        @pl.when(turn // members == k)
         def _(send=send):
             def put(at):
                 cols = pl.ds(at, LANES)
-                put_codes(send, get_unit(ctl, mine, got, cols), cols, unit)
+                factor = tops[0:1, cols]
+                for k in range(4):
+                    codes = (image[k, :, cols] * factor + 0.5).astype(jnp.int32).astype(jnp.int16)
+                    send[0, k * unit:(k + 1) * unit, cols] = codes
 
             each_strip(width, put)
+            send[0, 4 * unit:4 * unit + 16, :] = row
 
 
 def gather_kernel(ctl, *refs, unit, blocks):
@@ -303,7 +296,7 @@
     return jnp.where(place == 1, 1.0, jnp.where(place == -1, -1.0, 0.0)).astype(jnp.bfloat16)
 
 
-def render(ctl, light, table, slope, field, before, after, *, groups, units, unit, rows, offset):
+def render(ctl, light, table, field, before, after, *, groups, units, unit, rows, offset, halo_at):
     layers, total, width = field.shape
     block = math.lcm(unit, 16)
     tall = padded_rows(unit)
@@ -344,14 +337,13 @@
             in_specs=[
                 pl.BlockSpec(memory_space=pltpu.SMEM),
                 pl.BlockSpec(table.shape, lambda i, ctl: (0, 0)),
-                pl.BlockSpec(slope.shape, lambda i, ctl: (0, 0)),
                 pl.BlockSpec((4, tall, tall + 32), lambda i, ctl: (0, 0, 0)),
                 pl.BlockSpec((3, 3 * LANES, LANES), lambda i, ctl: (0, 0, 0)),
                 pl.BlockSpec((layers, block, width), main_at),
                 pl.BlockSpec((layers, 16, width), above_at),
                 pl.BlockSpec((layers, 16, width), below_at),
-                pl.BlockSpec((1, unit, width), lambda i, ctl: (index(i, ctl), 0, 0)),
-                pl.BlockSpec((1, unit, width), lambda i, ctl: (index(i, ctl), 0, 0)),
+                pl.BlockSpec((1, unit, width), lambda i, ctl: (index(i, ctl), halo_at, 0)),
+                pl.BlockSpec((1, unit, width), lambda i, ctl: (index(i, ctl), halo_at, 0)),
             ],
             out_specs=specs,
             scratch_shapes=[
@@ -367,37 +359,34 @@
         compiler_params=params(),
         cost_estimate=pl.CostEstimate(flops=16384 * cells, bytes_accessed=6 * cells, transcendentals=cells),
         name="render",
-    )(ctl, light, table, slope, row_bands, column_bands, field, field, field, before, after)
-
-
-def merge(ctl, mine, got, *, places, units, unit):
-    width = mine.shape[3]
-    cells = 4 * places * units * unit * width
-
-    def index(i, ctl):
-        return (ctl[0] ^ (i // units)) * units + lax.rem(i, units)
+    )(ctl, light, table, row_bands, column_bands, field, field, field, before, after)
+
+
+def merge(ctl, pairs, *, places, unit):
+    members = len(pairs)
+    width = pairs[0][0].shape[3]
+    cells = 4 * places * members * unit * width
 
     def spec(k):
         return pl.BlockSpec(
-            (1, 4 * unit + 16, width), lambda i, ctl: (jnp.clip(i - k * units, 0, units - 1), 0, 0)
+            (1, 4 * unit + 16, width), lambda i, ctl: (jnp.clip(i - k * members, 0, members - 1), 0, 0)
         )
 
     return pl.pallas_call(
-        functools.partial(merge_kernel, units=units, unit=unit),
+        functools.partial(merge_kernel, members=members, places=places, unit=unit),
         grid_spec=pltpu.PrefetchScalarGridSpec(
             num_scalar_prefetch=1,
-            grid=(places * units,),
-            in_specs=[
-                pl.BlockSpec((1, 4, unit, width), lambda i, ctl: (index(i, ctl), 0, 0, 0)),
-                pl.BlockSpec((1, 4, unit, width), lambda i, ctl: (index(i, ctl), 0, 0, 0)),
-            ],
+            grid=(places * members,),
+            in_specs=[pl.BlockSpec((1, 4, unit, width), lambda i, ctl: (ctl[0] ^ (i // members), 0, 0, 0))]
+            * (2 * members),
             out_specs=[spec(k) for k in range(places)],
+            scratch_shapes=[pltpu.VMEM((4, unit, width), jnp.float32), pltpu.VMEM((8, width), jnp.float32)],
         ),
-        out_shape=[jax.ShapeDtypeStruct((units, 4 * unit + 16, width), jnp.int16)] * places,
+        out_shape=[jax.ShapeDtypeStruct((members, 4 * unit + 16, width), jnp.int16)] * places,
         compiler_params=params(),
         cost_estimate=pl.CostEstimate(flops=32768 * cells, bytes_accessed=cells, transcendentals=0),
         name="merge",
-    )(ctl, mine, got)
+    )(ctl, *[array for pair in pairs for array in pair])
 
 
 def gather_parts(ctl, parts, *, units, unit, blocks):
@@ -441,10 +430,6 @@
     )(*operands)
 
 
-def chunk_units(units):
-    return [1] * units
-
-
 def per_device(field, transfer, bin_order, light_angles):
     tiles = lax.axis_size("tile")
     blocks = lax.axis_size("depth")
@@ -458,11 +443,7 @@
     table = table * jnp.array([[1.0], [1.0], [1.0], [0.01]], jnp.float32)
     bins = table.shape[1]
     slope = jnp.concatenate([table[:, 1:] - table[:, :-1], jnp.zeros_like(table[:, :1])], axis=1)
-    slope = jnp.pad(slope, ((0, 4), (0, LANES - bins)))
-    coarse = lax.reduce_precision(table, exponent_bits=8, mantissa_bits=7)
-    table = jnp.concatenate([coarse, table - coarse], axis=0)
-    spread = jnp.eye(16, dtype=jnp.float32)
-    table = (table[:, None, :, None] * spread[None, :, None, :]).reshape(8 * 16, bins * 16).astype(jnp.bfloat16)
+    table = jnp.pad(jnp.concatenate([table, slope], axis=0), ((0, 0), (0, LANES - bins)))
     azimuth, polar = light_angles[0], light_angles[1]
     light = 0.105 * jnp.stack(
         [jnp.cos(azimuth) * jnp.sin(polar), jnp.sin(azimuth) * jnp.sin(polar), jnp.cos(polar)]
@@ -476,19 +457,20 @@
     down = [(j, i) for i, j in up]
     both = ("depth", "tile")
 
-    sizes = chunk_units(rows // unit)
-    count = len(sizes)
-    starts = [sum(sizes[:n]) * unit for n in range(count)]
+    count = rows // unit
+    starts = [n * unit for n in range(count)]
+
+    def cut(layer, first, stop):
+        part = field.reshape(layers, tiles, rows, width)[layer:layer + 1, :, first * unit:stop * unit]
+        return part.reshape(tiles, (stop - first) * unit, width)
+
     halos = []
-    for n, units in enumerate(sizes):
-        def cut(layer):
-            part = field.reshape(layers, tiles, rows, width)[layer:layer + 1, :, starts[n]:starts[n] + units * unit]
-            return part.reshape(tiles * units, unit, width)
-
-        ends = (cut(layers - 1), cut(0))
-        if n > 0:
-            ends, _ = lax.optimization_barrier((ends, halos[n - 1]))
-        halos.append((lax.ppermute(ends[0], both, up), lax.ppermute(ends[1], both, down)))
+    for first, stop in [(0, 1), (1, count)][:count]:
+        ends = (cut(layers - 1, first, stop), cut(0, first, stop))
+        if halos:
+            ends, _ = lax.optimization_barrier((ends, halos[0][:2]))
+        pair = (lax.ppermute(ends[0], both, up), lax.ppermute(ends[1], both, down))
+        halos += [pair + (n - first,) for n in range(first, stop)]
 
     def exchange(send, distance):
         return lax.ppermute(send, "tile", [(i, i ^ distance) for i in range(tiles)])
@@ -505,36 +487,41 @@
     state = [None] * count
 
     def start_chunk(n):
-        before, after = halos[n]
+        before, after, at = halos[n]
         send, keep = render(
-            after_last(render_control), light, table, slope, field, before, after,
-            groups=tiles, units=sizes[n], unit=unit, rows=rows, offset=starts[n],
+            after_last(render_control), light, table, field, before, after,
+            groups=tiles, units=1, unit=unit, rows=rows, offset=starts[n], halo_at=at,
         )
         chain.append(send)
         state[n] = (keep, exchange(send, 1))
 
-    def merge_chunk(n):
-        keep, got = state[n]
-        sends = merge(after_last(merge_control), keep, got, places=places, units=sizes[n], unit=unit)
+    def merge_group(members):
+        sends = merge(after_last(merge_control), [state[n] for n in members], places=places, unit=unit)
         chain.append(sends[-1])
-        state[n] = [sends[0]] + [exchange(sends[k], 2 * k) for k in range(1, places)]
-
-    def block_chunk(n):
-        send = gather_parts(after_last(merge_control), state[n], units=sizes[n], unit=unit, blocks=blocks)
+        return [sends[0]] + [exchange(sends[k], 2 * k) for k in range(1, places)]
+
+    def block_group(members, parts):
+        send = gather_parts(after_last(merge_control), parts, units=len(members), unit=unit, blocks=blocks)
         chain.append(send)
-        state[n] = lax.all_to_all(send, "depth", split_axis=0, concat_axis=0, tiled=True)
-
-    last = count - 1
-    steps = [(n, level) for n in range(count) for level in range(3)]
-    for n, level in sorted(steps, key=lambda step: (step[1] + 1.5 * (step[0] == last), step[0])):
-        if n == 0 and level == 1 and count > 1:
-            waits.extend(halos[last])
-        if n == 0 and level == 2:
-            waits.extend(part for k in range(last) for part in state[k])
-        (start_chunk, merge_chunk, block_chunk)[level](n)
+        return lax.all_to_all(send, "depth", split_axis=0, concat_axis=0, tiled=True)
+
+    early, late = list(range(count - 1)), [count - 1]
+    results = []
+    if early:
+        for n in early:
+            start_chunk(n)
+        early_parts = merge_group(early)
+        start_chunk(count - 1)
+        waits.extend(early_parts)
+        results.append(block_group(early, early_parts))
+    else:
+        start_chunk(count - 1)
+    results.append(block_group(late, merge_group(late)))
     final = None
-    for n in range(count):
-        final = compose(state[n], final, unit=unit, first=starts[n] // unit, rows=rows)
+    done = 0
+    for result in results:
+        final = compose(result, final, unit=unit, first=done, rows=rows)
+        done += result.shape[1]
     return final
 
 

time: 270 us -> 304 us (1.13)
  Pallas kernels: 159 us -> 207 us
  starting transfers between devices: 53.4 us -> 36.9 us
    pallas_call x3, Pallas kernels: 121 us -> 172 us  [render(): pl.pallas_call(kernel, grid_spec=pltpu.PrefetchScalarGridSpec(num_scalar_...]
    ppermute x12 -> x9, starting transfers between devices: 16 us -> 9.04 us  [exchange(): return lax.ppermute(send, 'tile', [(i, i ^ distance) for i in range(tiles)])]
    all_to_all x3 -> x2, starting transfers between devices: 13 us -> 7.33 us  [block_group(): lax.all_to_all(send, 'depth', split_axis=0, concat_axis=0, tiled=True)]
    ppermute x6 -> x4, starting transfers between devices: 24.4 us -> 20.5 us  [per_device(): pair = (lax.ppermute(ends[0], both, up), lax.ppermute(ends[1], both, down))]
    pallas_call x3 -> x2, Pallas kernels: 11.9 us -> 9.06 us  [gather_parts(): pl.pallas_call(functools.partial(gather_kernel, unit=unit, blocks=blocks)...]
    pallas_call x3 -> x2, Pallas kernels: 8 us -> 6.26 us  [compose(): pl.pallas_call(functools.partial(compose_kernel, unit=unit, blocks=blocks...]
    ppermute x12 -> x9, waiting for transfers between devices: 22.4 us -> 23.9 us  [exchange(): return lax.ppermute(send, 'tile', [(i, i ^ distance) for i in range(tiles)])]
    pallas_call x3 -> x2, Pallas kernels: 18.8 us -> 19.6 us  [merge(): pl.pallas_call(functools.partial(merge_kernel, members=members, places=pl...]
  transfers between devices with their start and end apart: 21 -> 15, of which waited for: 6 -> 5; matrix products, arithmetic and copies ran while one was open for 2% -> 3% of each run, Pallas kernels for 58% -> 61%
where the time goes in v7:
time: 304 us; the launch traced here: 303 us
  Pallas kernels  207 us (68%)
  waiting for transfers between devices  41.2 us (14%)
  starting transfers between devices  36.9 us (12%)
  local copies, waits for them, and re-layouts  11 us (4%)
  other arithmetic  3.52 us (1%)
  between operations  3.11 us (1%)
    pallas_call x3, Pallas kernels, render(): pl.pallas_call(kernel, grid_spec=pltpu.PrefetchScalarGridSpec(num_scalar_...  172 us
    ppermute x9, waiting for transfers between devices, exchange(): return lax.ppermute(send, 'tile', [(i, i ^ distance) for i in range(tiles)])  23.9 us
    ppermute x4, starting transfers between devices, per_device(): pair = (lax.ppermute(ends[0], both, up), lax.ppermute(ends[1], both, down))  20.5 us
    pallas_call x2, Pallas kernels, merge(): pl.pallas_call(functools.partial(merge_kernel, members=members, places=pl...  19.6 us
    all_to_all x2, waiting for transfers between devices, block_group(): lax.all_to_all(send, 'depth', split_axis=0, concat_axis=0, tiled=True)  17.3 us
    pallas_call x2, Pallas kernels, gather_parts(): pl.pallas_call(functools.partial(gather_kernel, unit=unit, blocks=blocks)...  9.06 us
    ppermute x9, starting transfers between devices, exchange(): return lax.ppermute(send, 'tile', [(i, i ^ distance) for i in range(tiles)])  9.04 us
    all_to_all x2, starting transfers between devices, block_group(): lax.all_to_all(send, 'depth', split_axis=0, concat_axis=0, tiled=True)  7.33 us
  transfers between devices with their start and end apart: 15, of which 5 were waited for; matrix products, arithmetic and copies ran while one was open for 3% of the time, Pallas kernels for 61%

profile of v7, /device:TPU:0, one launch (start us, length us, event | category | flops | bytes accessed | tf_op | source)
XLA Modules:
  0.0 302.9 jit_solution(18139755520067489814)
XLA Ops:
  0.0 1.6 slice_bitcast_fusion.2
  2.9 4.0 %collective-permute-start = (bf16[8,48,1152]{2,1,0:T(8,128)(2,1)S(1)}, bf16[8,48,1152]{2,1,0:T(8,128)(2,1)}, u32[]{:S(2)}, u32[]{:S(2)}) collective-permute-start(bf16[8,48,1152]{2,1,0:T(8,128)(2,1)S(1)} %get-tuple-element.52), channel_id=1, source_target_pairs={{0,1},{1,2},{2,3},{3,4},{4,5},{5,6},{6,7},{7,8},{8,9},{9,10},{10,1... | collective-permute-start | bytes 2654216 | tf_op jit(solution)/shard_map/ppermute | solution.py:472
  14.7 2.3 slice_bitcast_fusion
  17.0 14.0 %collective-permute-start.2 = (bf16[8,96,1152]{2,1,0:T(8,128)(2,1)S(1)}, bf16[8,96,1152]{2,1,0:T(8,128)(2,1)}, u32[]{:S(2)}, u32[]{:S(2)}) collective-permute-start(bf16[8,96,1152]{2,1,0:T(8,128)(2,1)S(1)} %get-tuple-element.29), channel_id=1, source_target_pairs={{0,1},{1,2},{2,3},{3,4},{4,5},{5,6},{6,7},{7,8},{8,9},{9,10},{10,1... | collective-permute-start | bytes 5308424 | tf_op jit(solution)/shard_map/ppermute | solution.py:472
  32.3 57.5 %render.3 = (f32[4,4,48,1152]{3,2,1,0:T(8,128)}, f32[4,4,48,1152]{3,2,1,0:T(8,128)}) custom-call(s32[2]{0:T(128)} %pad_add_fusion.1.ctl, f32[3]{0:T(128)} %maximum_multiply_fusion.light, f32[8,128]{1,0:T(8,128)} %pad.5.table, bf16[4,48,80]{2,1,0:T(8,128)(2,1)} %pad_maximum_fusion.1.row_bands, bf16[3,384,128]{2,1,0:T(8,128)(2,1)} %pad_maximum_fusion.column_bands, ...), custom_call_target="tpu_custom_call" | custom-call | flops 43486543872 | bytes 15925248 | tf_op jit(solution)/shard_map/render/pallas_call | solution.py:332
  89.8 2.0 collective-permute-start.4
  91.8 57.4 %render.4 = (f32[4,4,48,1152]{3,2,1,0:T(8,128)}, f32[4,4,48,1152]{3,2,1,0:T(8,128)}) custom-call(s32[2]{0:T(128)} %pad_add_fusion.1.ctl, f32[3]{0:T(128)} %maximum_multiply_fusion.light, f32[8,128]{1,0:T(8,128)} %pad.5.table, bf16[4,48,80]{2,1,0:T(8,128)(2,1)} %pad_maximum_fusion.1.row_bands, bf16[3,384,128]{2,1,0:T(8,128)(2,1)} %pad_maximum_fusion.column_bands, ...), custom_call_target="tpu_custom_call" | custom-call | flops 43486543872 | bytes 15925248 | tf_op jit(solution)/shard_map/render/pallas_call | solution.py:332
  149.9 5.9 %collective-permute-done.5.refs_3_ = f32[4,4,48,1152]{3,2,1,0:T(8,128)} collective-permute-done((f32[4,4,48,1152]{3,2,1,0:T(8,128)}, f32[4,4,48,1152]{3,2,1,0:T(8,128)}, u32[]{:S(2)}, u32[]{:S(2)}) %collective-permute-start.5) | collective-permute-done | bytes 3538976 | tf_op jit(solution)/shard_map/ppermute | solution.py:476
  155.8 13.0 %merge.2 = (s16[2,208,1152]{2,1,0:T(8,128)(2,1)}, s16[2,208,1152]{2,1,0:T(8,128)(2,1)}, s16[2,208,1152]{2,1,0:T(8,128)(2,1)}, s16[2,208,1152]{2,1,0:T(8,128)(2,1)}) custom-call(s32[2]{0:T(128)} %pad_add_fusion.ctl, f32[4,4,48,1152]{3,2,1,0:T(8,128)} %get-tuple-element.33.refs_0_, f32[4,4,48,1152]{3,2,1,0:T(8,128)} %copy-done.5, ...), custom_call_target="tpu_custom_call" | custom-call | flops 57982058496 | bytes 1769472 | tf_op jit(solution)/shard_map/merge/pallas_call | solution.py:375
  172.3 57.4 %render.5 = (f32[4,4,48,1152]{3,2,1,0:T(8,128)}, f32[4,4,48,1152]{3,2,1,0:T(8,128)}) custom-call(s32[2]{0:T(128)} %pad_add_fusion.1.ctl, f32[3]{0:T(128)} %maximum_multiply_fusion.light, f32[8,128]{1,0:T(8,128)} %pad.5.table, bf16[4,48,80]{2,1,0:T(8,128)(2,1)} %pad_maximum_fusion.1.row_bands, bf16[3,384,128]{2,1,0:T(8,128)(2,1)} %pad_maximum_fusion.column_bands, ...), custom_call_target="tpu_custom_call" | custom-call | flops 43486543872 | bytes 15925248 | tf_op jit(solution)/shard_map/render/pallas_call | solution.py:332
  231.4 5.1 %gather_parts.2 = s16[4,2,64,1152]{3,2,1,0:T(8,128)(2,1)} custom-call(s32[2]{0:T(128)} %pad_add_fusion.ctl, s16[2,208,1152]{2,1,0:T(8,128)(2,1)} %get-tuple-element.38.refs_0_, s16[2,208,1152]{2,1,0:T(8,128)(2,1)} %copy-done.8, s16[2,208,1152]{2,1,0:T(8,128)(2,1)} %copy-done.9, s16[2,208,1152]{2,1,0:T(8,128)(2,1)} %copy-done.7), custom_call_target="tpu_custom_call" | custom-call | flops 57982058496 | bytes 442368 | tf_op jit(solution)/shard_map/gather_parts/pallas_call | solution.py:395
  236.5 1.8 copy-done.6
  238.3 6.5 %merge.3 = (s16[1,208,1152]{2,1,0:T(8,128)(2,1)}, s16[1,208,1152]{2,1,0:T(8,128)(2,1)}, s16[1,208,1152]{2,1,0:T(8,128)(2,1)}, s16[1,208,1152]{2,1,0:T(8,128)(2,1)}) custom-call(s32[2]{0:T(128)} %pad_add_fusion.ctl, f32[4,4,48,1152]{3,2,1,0:T(8,128)} %get-tuple-element.43.refs_0_, f32[4,4,48,1152]{3,2,1,0:T(8,128)} %copy-done.6), custom_call_target="tpu_custom_call" | custom-call | flops 28991029248 | bytes 884736 | tf_op jit(solution)/shard_map/merge/pallas_call | solution.py:375
  244.8 1.8 collective-permute-start.10
  246.6 1.7 collective-permute-start.12
  248.3 3.9 %all-to-all-start.1 = ((s16[4,2,64,1152]{3,2,1,0:T(8,128)(2,1)}), s16[4,2,64,1152]{3,2,1,0:T(8,128)(2,1)S(1)}, u32[]{:S(2)}, u32[]{:S(2)}) async-start(s16[4,2,64,1152]{3,2,1,0:T(8,128)(2,1)} %gather_parts.2), calls=%async_computation.1 | async-start | bytes 2359296 | tf_op jit(solution)/shard_map/all_to_all | solution.py:506
  252.1 6.6 %collective-permute-done.10.refs_1_ = s16[1,208,1152]{2,1,0:T(8,128)(2,1)S(1)} collective-permute-done((s16[1,208,1152]{2,1,0:T(8,128)(2,1)}, s16[1,208,1152]{2,1,0:T(8,128)(2,1)S(1)}, u32[]{:S(2)}, u32[]{:S(2)}) %collective-permute-start.10) | collective-permute-done | bytes 479264 | tf_op jit(solution)/shard_map/ppermute | solution.py:476
  258.8 11.4 %collective-permute-done.11.refs_2_ = s16[1,208,1152]{2,1,0:T(8,128)(2,1)S(1)} collective-permute-done((s16[1,208,1152]{2,1,0:T(8,128)(2,1)}, s16[1,208,1152]{2,1,0:T(8,128)(2,1)S(1)}, u32[]{:S(2)}, u32[]{:S(2)}) %collective-permute-start.11) | collective-permute-done | bytes 479264 | tf_op jit(solution)/shard_map/ppermute | solution.py:476
  271.1 4.0 %gather_parts.3 = s16[4,1,64,1152]{3,2,1,0:T(8,128)(2,1)} custom-call(s32[2]{0:T(128)} %pad_add_fusion.ctl, s16[1,208,1152]{2,1,0:T(8,128)(2,1)} %get-tuple-element.46.refs_0_, s16[1,208,1152]{2,1,0:T(8,128)(2,1)} %copy-done.11, s16[1,208,1152]{2,1,0:T(8,128)(2,1)} %copy-done.12, s16[1,208,1152]{2,1,0:T(8,128)(2,1)} %copy-done.13), custom_call_target="tpu_custom_call" | custom-call | flops 28991029248 | bytes 221184 | tf_op jit(solution)/shard_map/gather_parts/pallas_call | solution.py:395
  275.1 5.5 %all-to-all-done.1.got = s16[4,2,64,1152]{3,2,1,0:T(8,128)(2,1)S(1)} async-done(((s16[4,2,64,1152]{3,2,1,0:T(8,128)(2,1)}), s16[4,2,64,1152]{3,2,1,0:T(8,128)(2,1)S(1)}, u32[]{:S(2)}, u32[]{:S(2)}) %all-to-all-start.1) | async-done | bytes 1179680 | tf_op jit(solution)/shard_map/all_to_all | solution.py:506
  280.6 3.5 %all-to-all-start = ((s16[4,1,64,1152]{3,2,1,0:T(8,128)(2,1)}), s16[4,1,64,1152]{3,2,1,0:T(8,128)(2,1)S(1)}, u32[]{:S(2)}, u32[]{:S(2)}) async-start(s16[4,1,64,1152]{3,2,1,0:T(8,128)(2,1)} %gather_parts.3), calls=%async_computation | async-start | bytes 1179648 | tf_op jit(solution)/shard_map/all_to_all | solution.py:506
  284.1 3.6 %compose.2.refs_0_ = f32[4,144,288]{2,1,0:T(8,128)} custom-call(s16[4,2,64,1152]{3,2,1,0:T(8,128)(2,1)} %copy-done), custom_call_target="tpu_custom_call" | custom-call | flops 14495514624 | bytes 442368 | tf_op jit(solution)/shard_map/compose/pallas_call | solution.py:420
  287.7 11.8 %all-to-all-done.got = s16[4,1,64,1152]{3,2,1,0:T(8,128)(2,1)S(1)} async-done(((s16[4,1,64,1152]{3,2,1,0:T(8,128)(2,1)}), s16[4,1,64,1152]{3,2,1,0:T(8,128)(2,1)S(1)}, u32[]{:S(2)}, u32[]{:S(2)}) %all-to-all-start) | async-done | bytes 589856 | tf_op jit(solution)/shard_map/all_to_all | solution.py:506
  300.2 2.7 compose.3
  (71 shorter events, 14.9 us)
Async XLA Ops:
  0.0 11.9 %copy-start.4 = (f32[4]{0:T(128)S(1)}, f32[4]{0:T(128)}, u32[]{:S(2)}) copy-start(f32[4]{0:T(128)} %constant.60) | copy-start | bytes 52
  0.0 6.9 %copy-start.14 = (s32[16]{0:T(128)S(1)}, s32[16]{0:T(128)}, u32[]{:S(2)}) copy-start(s32[16]{0:T(128)} %param.7) | copy-start | bytes 196
  0.0 7.0 %copy-start.3 = (f32[2]{0:T(128)S(1)}, f32[2]{0:T(128)}, u32[]{:S(2)}) copy-start(f32[2]{0:T(128)} %param.8) | copy-start | bytes 28
  0.0 11.2 %copy-start.2 = (f32[4,16]{1,0:T(4,128)S(1)}, f32[4,16]{1,0:T(4,128)}, u32[]{:S(2)}) copy-start(f32[4,16]{1,0:T(4,128)} %param.6) | copy-start | bytes 772
  1.6 15.4 %collective-permute-start.1 = (bf16[8,48,1152]{2,1,0:T(8,128)(2,1)S(1)}, bf16[8,48,1152]{2,1,0:T(8,128)(2,1)S(1)}, u32[]{:S(2)}, u32[]{:S(2)}) collective-permute-start(bf16[8,48,1152]{2,1,0:T(8,128)(2,1)S(1)} %get-tuple-element.51), channel_id=1, source_target_pairs={{1,0},{2,1},{3,2},{4,3},{5,4},{6,5},{7,6},{8,7},{9,8},{10,9},{11,1... | collective-permute-start | bytes 2654216 | tf_op jit(solution)/shard_map/ppermute | solution.py:472
  2.9 14.1 %collective-permute-start = (bf16[8,48,1152]{2,1,0:T(8,128)(2,1)S(1)}, bf16[8,48,1152]{2,1,0:T(8,128)(2,1)}, u32[]{:S(2)}, u32[]{:S(2)}) collective-permute-start(bf16[8,48,1152]{2,1,0:T(8,128)(2,1)S(1)} %get-tuple-element.52), channel_id=1, source_target_pairs={{0,1},{1,2},{2,3},{3,4},{4,5},{5,6},{6,7},{7,8},{8,9},{9,10},{10,1... | collective-permute-start | bytes 2654216 | tf_op jit(solution)/shard_map/ppermute | solution.py:472
  17.0 15.3 %copy-start.10 = (bf16[8,48,1152]{2,1,0:T(8,128)(2,1)}, bf16[8,48,1152]{2,1,0:T(8,128)(2,1)S(1)}, u32[]{:S(2)}) copy-start(bf16[8,48,1152]{2,1,0:T(8,128)(2,1)S(1)} %collective-permute-done.1.after) | copy-start | bytes 2654212
  17.0 74.8 %collective-permute-start.2 = (bf16[8,96,1152]{2,1,0:T(8,128)(2,1)S(1)}, bf16[8,96,1152]{2,1,0:T(8,128)(2,1)}, u32[]{:S(2)}, u32[]{:S(2)}) collective-permute-start(bf16[8,96,1152]{2,1,0:T(8,128)(2,1)S(1)} %get-tuple-element.29), channel_id=1, source_target_pairs={{0,1},{1,2},{2,3},{3,4},{4,5},{5,6},{6,7},{7,8},{8,9},{9,10},{10,1... | collective-permute-start | bytes 5308424 | tf_op jit(solution)/shard_map/ppermute | solution.py:472
  31.0 60.8 %collective-permute-start.3 = (bf16[8,96,1152]{2,1,0:T(8,128)(2,1)S(1)}, bf16[8,96,1152]{2,1,0:T(8,128)(2,1)}, u32[]{:S(2)}, u32[]{:S(2)}) collective-permute-start(bf16[8,96,1152]{2,1,0:T(8,128)(2,1)S(1)} %get-tuple-element.30), channel_id=1, source_target_pairs={{1,0},{2,1},{3,2},{4,3},{5,4},{6,5},{7,6},{8,7},{9,8},{10,9},{11,1... | collective-permute-start | bytes 5308424 | tf_op jit(solution)/shard_map/ppermute | solution.py:472
  89.8 60.1 %collective-permute-start.4 = (f32[4,4,48,1152]{3,2,1,0:T(8,128)}, f32[4,4,48,1152]{3,2,1,0:T(8,128)S(1)}, u32[]{:S(2)}, u32[]{:S(2)}) collective-permute-start(f32[4,4,48,1152]{3,2,1,0:T(8,128)} %get-tuple-element.27), channel_id=1, source_target_pairs={{0,1},{1,0},{2,3},{3,2},{4,5},{5,4},{6,7},{7,6},{8,9},{9,8},{10,11... | collective-permute-start | bytes 10616840 | tf_op jit(solution)/shard_map/ppermute | solution.py:476
  149.2 6.6 %collective-permute-start.5 = (f32[4,4,48,1152]{3,2,1,0:T(8,128)}, f32[4,4,48,1152]{3,2,1,0:T(8,128)}, u32[]{:S(2)}, u32[]{:S(2)}) collective-permute-start(f32[4,4,48,1152]{3,2,1,0:T(8,128)} %get-tuple-element.31), channel_id=1, source_target_pairs={{0,1},{1,0},{2,3},{3,2},{4,5},{5,4},{6,7},{7,6},{8,9},{9,8},{10,11... | collective-permute-start | bytes 10616840 | tf_op jit(solution)/shard_map/ppermute | solution.py:476
  149.9 5.9 %copy-start.5 = (f32[4,4,48,1152]{3,2,1,0:T(8,128)}, f32[4,4,48,1152]{3,2,1,0:T(8,128)S(1)}, u32[]{:S(2)}) copy-start(f32[4,4,48,1152]{3,2,1,0:T(8,128)S(1)} %collective-permute-done.4.refs_1_) | copy-start | bytes 10616836
  168.8 61.0 %collective-permute-start.8 = (s16[2,208,1152]{2,1,0:T(8,128)(2,1)}, s16[2,208,1152]{2,1,0:T(8,128)(2,1)S(1)}, u32[]{:S(2)}, u32[]{:S(2)}) collective-permute-start(s16[2,208,1152]{2,1,0:T(8,128)(2,1)} %get-tuple-element.35), channel_id=1, source_target_pairs={{0,6},{1,7},{2,4},{3,5},{4,2},{5,3},{6,0},{7,1},{8,14},{9,15},{10,... | collective-permute-start | bytes 2875400 | tf_op jit(solution)/shard_map/ppermute | solution.py:476
  169.7 60.1 %collective-permute-start.6 = (s16[2,208,1152]{2,1,0:T(8,128)(2,1)}, s16[2,208,1152]{2,1,0:T(8,128)(2,1)S(1)}, u32[]{:S(2)}, u32[]{:S(2)}) collective-permute-start(s16[2,208,1152]{2,1,0:T(8,128)(2,1)} %get-tuple-element.39), channel_id=1, source_target_pairs={{0,2},{1,3},{2,0},{3,1},{4,6},{5,7},{6,4},{7,5},{8,10},{9,11},{10,... | collective-permute-start | bytes 2875400 | tf_op jit(solution)/shard_map/ppermute | solution.py:476
  171.1 58.7 %collective-permute-start.7 = (s16[2,208,1152]{2,1,0:T(8,128)(2,1)}, s16[2,208,1152]{2,1,0:T(8,128)(2,1)S(1)}, u32[]{:S(2)}, u32[]{:S(2)}) collective-permute-start(s16[2,208,1152]{2,1,0:T(8,128)(2,1)} %get-tuple-element.40), channel_id=1, source_target_pairs={{0,4},{1,5},{2,6},{3,7},{4,0},{5,1},{6,2},{7,3},{8,12},{9,13},{10,... | collective-permute-start | bytes 2875400 | tf_op jit(solution)/shard_map/ppermute | solution.py:476
  229.8 6.7 %collective-permute-start.9 = (f32[4,4,48,1152]{3,2,1,0:T(8,128)}, f32[4,4,48,1152]{3,2,1,0:T(8,128)S(1)}, u32[]{:S(2)}, u32[]{:S(2)}) collective-permute-start(f32[4,4,48,1152]{3,2,1,0:T(8,128)} %get-tuple-element.37), channel_id=1, source_target_pairs={{0,1},{1,0},{2,3},{3,2},{4,5},{5,4},{6,7},{7,6},{8,9},{9,8},{10,11... | collective-permute-start | bytes 10616840 | tf_op jit(solution)/shard_map/ppermute | solution.py:476
  236.5 1.8 copy-start.6
  244.8 14.0 %collective-permute-start.10 = (s16[1,208,1152]{2,1,0:T(8,128)(2,1)}, s16[1,208,1152]{2,1,0:T(8,128)(2,1)S(1)}, u32[]{:S(2)}, u32[]{:S(2)}) collective-permute-start(s16[1,208,1152]{2,1,0:T(8,128)(2,1)} %get-tuple-element.47), channel_id=1, source_target_pairs={{0,2},{1,3},{2,0},{3,1},{4,6},{5,7},{6,4},{7,5},{8,10},{9,11},{10,... | collective-permute-start | bytes 1437704 | tf_op jit(solution)/shard_map/ppermute | solution.py:476
  246.6 23.6 %collective-permute-start.11 = (s16[1,208,1152]{2,1,0:T(8,128)(2,1)}, s16[1,208,1152]{2,1,0:T(8,128)(2,1)S(1)}, u32[]{:S(2)}, u32[]{:S(2)}) collective-permute-start(s16[1,208,1152]{2,1,0:T(8,128)(2,1)} %get-tuple-element.48), channel_id=1, source_target_pairs={{0,4},{1,5},{2,6},{3,7},{4,0},{5,1},{6,2},{7,3},{8,12},{9,13},{10,... | collective-permute-start | bytes 1437704 | tf_op jit(solution)/shard_map/ppermute | solution.py:476
  246.6 23.6 %collective-permute-start.12 = (s16[1,208,1152]{2,1,0:T(8,128)(2,1)}, s16[1,208,1152]{2,1,0:T(8,128)(2,1)S(1)}, u32[]{:S(2)}, u32[]{:S(2)}) collective-permute-start(s16[1,208,1152]{2,1,0:T(8,128)(2,1)} %get-tuple-element.44), channel_id=1, source_target_pairs={{0,6},{1,7},{2,4},{3,5},{4,2},{5,3},{6,0},{7,1},{8,14},{9,15},{10,... | collective-permute-start | bytes 1437704 | tf_op jit(solution)/shard_map/ppermute | solution.py:476
  248.3 32.3 %all-to-all-start.1 = ((s16[4,2,64,1152]{3,2,1,0:T(8,128)(2,1)}), s16[4,2,64,1152]{3,2,1,0:T(8,128)(2,1)S(1)}, u32[]{:S(2)}, u32[]{:S(2)}) async-start(s16[4,2,64,1152]{3,2,1,0:T(8,128)(2,1)} %gather_parts.2), calls=%async_computation.1 | async-start | bytes 2359296 | tf_op jit(solution)/shard_map/all_to_all | solution.py:506
  258.8 11.4 %copy-start.11 = (s16[1,208,1152]{2,1,0:T(8,128)(2,1)}, s16[1,208,1152]{2,1,0:T(8,128)(2,1)S(1)}, u32[]{:S(2)}) copy-start(s16[1,208,1152]{2,1,0:T(8,128)(2,1)S(1)} %collective-permute-done.10.refs_1_) | copy-start | bytes 1437700
  280.6 3.5 %copy-start = (s16[4,2,64,1152]{3,2,1,0:T(8,128)(2,1)}, s16[4,2,64,1152]{3,2,1,0:T(8,128)(2,1)S(1)}, u32[]{:S(2)}) copy-start(s16[4,2,64,1152]{3,2,1,0:T(8,128)(2,1)S(1)} %all-to-all-done.1.got) | copy-start | bytes 3538948
  280.6 18.8 %all-to-all-start = ((s16[4,1,64,1152]{3,2,1,0:T(8,128)(2,1)}), s16[4,1,64,1152]{3,2,1,0:T(8,128)(2,1)S(1)}, u32[]{:S(2)}, u32[]{:S(2)}) async-start(s16[4,1,64,1152]{3,2,1,0:T(8,128)(2,1)} %gather_parts.3), calls=%async_computation | async-start | bytes 1179648 | tf_op jit(solution)/shard_map/all_to_all | solution.py:506
  (6 other events, 6.4 us)

commit v8 on v7

--- a/solution.py
+++ b/solution.py
@@ -10,6 +10,7 @@
 
 LANES = 128
 CODES = 32700.0
+ON_MATRIX = 6
 VMEM_LIMIT = 56 * 1024 * 1024
 
 
@@ -17,20 +18,22 @@
     return 48 if rows % 48 == 0 else rows
 
 
-def encode(values):
-    top = functools.reduce(jnp.maximum, values)
-    top = jnp.max(top, axis=0, keepdims=True)
-    exponent = jnp.ceil(jnp.log2(jnp.maximum(top, 1e-30)))
-    factor = jnp.exp2(-exponent) * CODES
-    codes = [(v * factor + 0.5).astype(jnp.int32).astype(jnp.int16) for v in values]
-    row = jnp.broadcast_to(exponent, (16, exponent.shape[1]))
-    return codes, row.astype(jnp.int32).astype(jnp.int16)
-
-
-def decode(codes, row):
-    exponent = row.astype(jnp.int32).astype(jnp.float32)[0:1]
-    scale = jnp.exp2(exponent) * (1.0 / CODES)
-    return [c.astype(jnp.int32).astype(jnp.float32) * scale for c in codes]
+def exponent_of(top):
+    return jnp.ceil(jnp.log2(jnp.maximum(top, 1e-30)))
+
+
+def pack(low, high, factor):
+    low = (low * factor + 0.5).astype(jnp.int32)
+    high = (high * factor + 0.5).astype(jnp.int32)
+    return low | (high << 16)
+
+
+def unpack(word, scale):
+    return (word & 0xFFFF).astype(jnp.float32) * scale, (word >> 16).astype(jnp.float32) * scale
+
+
+def scale_of(row):
+    return jnp.exp2(row.astype(jnp.float32)) * (1.0 / CODES)
 
 
 def over(front, back):
@@ -48,6 +51,12 @@
     )
 
 
+def choose(bins, whole):
+    place = whole.astype(jnp.bfloat16)
+    one, zero = jnp.ones_like(place), jnp.zeros_like(place)
+    return jnp.concatenate([jnp.where(place == k, one, zero) for k in range(bins)], axis=0)
+
+
 def padded_rows(unit):
     return -(-unit // 16) * 16
 
@@ -64,7 +73,7 @@
     lax.fori_loop(0, strips // together, step, 0)
 
 
-def render_kernel(ctl, light, table, row_bands, column_bands, main, above, below, before, after, send, keep, cells, slopes_y, slopes_z, image, stage, ends, *, groups, units, unit, block, rows, offset, total):
+def render_kernel(ctl, light, table, slope, row_bands, column_bands, main, above, below, before, after, send, keep, cells, slopes_y, slopes_z, image, stage, ends, *, groups, units, unit, block, rows, offset, total):
     i = pl.program_id(0)
     half = (groups // 2) * units
     rest = lax.rem(i, half)
@@ -115,7 +124,9 @@
 
     lx, ly, lz = light[0], light[1], light[2]
     step = 16
-    tables = [jnp.broadcast_to(table[k:k + 1, :], (step, LANES)) for k in range(8)]
+    bins = table.shape[1] // step
+    rows_found = table.shape[0] // (2 * step)
+    tilts_of = [jnp.broadcast_to(slope[k:k + 1, :], (step, LANES)) for k in range(rows_found - 4, 4)]
     row_kind = jnp.where(start == 0, 1, 0) + jnp.where(start + unit == total, 2, 0)
 
     def strip(c, carry):
@@ -139,26 +150,45 @@
             low = end(0, s, cols)
             here = own(0, 1, s, cols)[0].astype(jnp.float32)
             clear, colour = None, None
-            for layer in range(layers):
-                high = own(layer + 1, 1, s, cols)[0].astype(jnp.float32) if layer + 1 < layers else end(1, s, cols)
-                position = jnp.clip(here * 2.5 + 7.5, 0.0, 15.0)
-                index = position.astype(jnp.int32)
-                part = position - index.astype(jnp.float32)
-                tf = [lookup(tables[k], index) + part * lookup(tables[4 + k], index) for k in range(4)]
-                gx = high - low
-                gy = slopes_y[layer, s, :]
-                gz = slopes_z[layer, s, :]
-                facing = jnp.abs(gx * lx + gy * ly + gz * lz)
-                square = gx * gx + gy * gy + gz * gz
-                shade = 0.045 + facing * lax.rsqrt(jnp.maximum(square, 4.0))
-                low, here = here, high
-                if layer == 0:
-                    colour = [tf[k] * shade for k in range(3)]
-                    clear = 1.0 - tf[3]
-                else:
-                    seen = shade * clear
-                    colour = [colour[k] + tf[k] * seen for k in range(3)]
-                    clear = clear - clear * tf[3]
+            for first in range(0, layers, 2):
+                pair = range(first, min(first + 2, layers))
+                parts, picks, shades, tilts = [], [], [], []
+                for layer in pair:
+                    if layer + 1 < layers:
+                        high = own(layer + 1, 1, s, cols)[0].astype(jnp.float32)
+                    else:
+                        high = end(1, s, cols)
+                    position = jnp.clip(here * 2.5 + 7.5, 0.0, 15.0)
+                    index = position.astype(jnp.int32)
+                    whole = index.astype(jnp.float32)
+                    parts.append(position - whole)
+                    tilts.append([lookup(tilt, index) for tilt in tilts_of])
+                    picks.append(choose(bins, whole))
+                    gx = high - low
+                    gy = slopes_y[layer, s, :]
+                    gz = slopes_z[layer, s, :]
+                    facing = jnp.abs(gx * lx + gy * ly + gz * lz)
+                    square = gx * gx + gy * gy + gz * gz
+                    shades.append(0.045 + facing * lax.rsqrt(jnp.maximum(square, 4.0)))
+                    low, here = here, high
+                pick = jnp.concatenate(picks, axis=1) if len(picks) > 1 else picks[0]
+                found = jnp.dot(table[...], pick, preferred_element_type=jnp.float32)
+                for m, layer in enumerate(pair):
+                    lanes = slice(m * LANES, (m + 1) * LANES)
+                    half_rows = rows_found * step
+                    looked = [
+                        found[k * step:(k + 1) * step, lanes]
+                        + found[half_rows + k * step:half_rows + (k + 1) * step, lanes]
+                        for k in range(rows_found)
+                    ] + tilts[m]
+                    tf = [looked[k] + parts[m] * looked[4 + k] for k in range(4)]
+                    if layer == 0:
+                        colour = [tf[k] * shades[m] for k in range(3)]
+                        clear = 1.0 - tf[3]
+                    else:
+                        seen = shades[m] * clear
+                        colour = [colour[k] + tf[k] * seen for k in range(3)]
+                        clear = clear - clear * tf[3]
             for k in range(3):
                 image[k, s, cols] = colour[k]
             image[3, s, cols] = 1.0 - clear
@@ -203,10 +233,9 @@
 
             each_strip(width, put)
 
-    top = jnp.max(tops[0:8, :], axis=0, keepdims=True)
-    exponent = jnp.ceil(jnp.log2(jnp.maximum(top, 1e-30)))
+    exponent = exponent_of(jnp.max(tops[0:8, :], axis=0, keepdims=True))
     tops[0:8, :] = jnp.broadcast_to(jnp.exp2(-exponent) * CODES, (8, width))
-    row = jnp.broadcast_to(exponent, (16, width)).astype(jnp.int32).astype(jnp.int16)
+    row = jnp.broadcast_to(exponent, (8, width)).astype(jnp.int32)
 
     for k, send in enumerate(sends):
         @pl.when(turn // members == k)
@@ -214,12 +243,11 @@
             def put(at):
                 cols = pl.ds(at, LANES)
                 factor = tops[0:1, cols]
-                for k in range(4):
-                    codes = (image[k, :, cols] * factor + 0.5).astype(jnp.int32).astype(jnp.int16)
-                    send[0, k * unit:(k + 1) * unit, cols] = codes
+                for k in range(2):
+                    send[0, k * unit:(k + 1) * unit, cols] = pack(image[2 * k, :, cols], image[2 * k + 1, :, cols], factor)
 
             each_strip(width, put)
-            send[0, 4 * unit:4 * unit + 16, :] = row
+            send[0, 2 * unit:2 * unit + 8, :] = row
 
 
 def gather_kernel(ctl, *refs, unit, blocks):
@@ -233,10 +261,10 @@
                 total = None
                 for j in range(len(parts)):
                     got = parts[me ^ j]
-                    part = decode(
-                        [got[0, k * unit:(k + 1) * unit, cols] for k in range(4)],
-                        got[0, 4 * unit:4 * unit + 16, cols],
-                    )
+                    scale = scale_of(got[0, 2 * unit:2 * unit + 1, cols])
+                    part = []
+                    for k in range(2):
+                        part += unpack(got[0, k * unit:(k + 1) * unit, cols], scale)
                     total = part if total is None else over(total, part)
                 for k in range(4):
                     image[k, :, cols] = total[k]
@@ -244,19 +272,23 @@
             each_strip(width, put)
 
     part = width // blocks
+    half = unit // 2
     for b in range(blocks):
         wide = jnp.concatenate([image[k, :, b * part:(b + 1) * part] for k in range(4)], axis=1)
-        codes, row = encode([wide])
-        send[b, 0, 0:unit, :] = codes[0]
-        send[b, 0, unit:unit + 16, :] = row
+        exponent = exponent_of(jnp.max(wide, axis=0, keepdims=True))
+        factor = jnp.exp2(-exponent) * CODES
+        send[b, 0, 8:8 + half, :] = pack(wide[:half], wide[half:], factor)
+        send[b, 0, 0:8, :] = jnp.broadcast_to(exponent, (8, 4 * part)).astype(jnp.int32)
 
 
 def compose_kernel(got, *refs, unit, blocks):
     out = refs[-1]
     part = out.shape[2]
+    half = unit // 2
     total = None
     for b in range(blocks):
-        wide = decode([got[b, 0, 0:unit, :]], got[b, 0, unit:unit + 16, :])[0]
+        scale = scale_of(got[b, 0, 0:1, :])
+        wide = jnp.concatenate(unpack(got[b, 0, 8:8 + half, :], scale), axis=0)
         layer = [wide[:, k * part:(k + 1) * part] for k in range(4)]
         total = layer if total is None else over(total, layer)
     for k in range(4):
@@ -296,7 +328,7 @@
     return jnp.where(place == 1, 1.0, jnp.where(place == -1, -1.0, 0.0)).astype(jnp.bfloat16)
 
 
-def render(ctl, light, table, field, before, after, *, groups, units, unit, rows, offset, halo_at):
+def render(ctl, light, table, slope, field, before, after, *, groups, units, unit, rows, offset, halo_at):
     layers, total, width = field.shape
     block = math.lcm(unit, 16)
     tall = padded_rows(unit)
@@ -337,6 +369,7 @@
             in_specs=[
                 pl.BlockSpec(memory_space=pltpu.SMEM),
                 pl.BlockSpec(table.shape, lambda i, ctl: (0, 0)),
+                pl.BlockSpec(slope.shape, lambda i, ctl: (0, 0)),
                 pl.BlockSpec((4, tall, tall + 32), lambda i, ctl: (0, 0, 0)),
                 pl.BlockSpec((3, 3 * LANES, LANES), lambda i, ctl: (0, 0, 0)),
                 pl.BlockSpec((layers, block, width), main_at),
@@ -359,7 +392,7 @@
         compiler_params=params(),
         cost_estimate=pl.CostEstimate(flops=16384 * cells, bytes_accessed=6 * cells, transcendentals=cells),
         name="render",
-    )(ctl, light, table, row_bands, column_bands, field, field, field, before, after)
+    )(ctl, light, table, slope, row_bands, column_bands, field, field, field, before, after)
 
 
 def merge(ctl, pairs, *, places, unit):
@@ -369,7 +402,7 @@
 
     def spec(k):
         return pl.BlockSpec(
-            (1, 4 * unit + 16, width), lambda i, ctl: (jnp.clip(i - k * members, 0, members - 1), 0, 0)
+            (1, 2 * unit + 8, width), lambda i, ctl: (jnp.clip(i - k * members, 0, members - 1), 0, 0)
         )
 
     return pl.pallas_call(
@@ -382,7 +415,7 @@
             out_specs=[spec(k) for k in range(places)],
             scratch_shapes=[pltpu.VMEM((4, unit, width), jnp.float32), pltpu.VMEM((8, width), jnp.float32)],
         ),
-        out_shape=[jax.ShapeDtypeStruct((members, 4 * unit + 16, width), jnp.int16)] * places,
+        out_shape=[jax.ShapeDtypeStruct((members, 2 * unit + 8, width), jnp.int32)] * places,
         compiler_params=params(),
         cost_estimate=pl.CostEstimate(flops=32768 * cells, bytes_accessed=cells, transcendentals=0),
         name="merge",
@@ -397,11 +430,11 @@
         grid_spec=pltpu.PrefetchScalarGridSpec(
             num_scalar_prefetch=1,
             grid=(units,),
-            in_specs=[pl.BlockSpec((1, 4 * unit + 16, width), lambda i, ctl: (i, 0, 0))] * len(parts),
-            out_specs=pl.BlockSpec((blocks, 1, unit + 16, 4 * width // blocks), lambda i, ctl: (0, i, 0, 0)),
+            in_specs=[pl.BlockSpec((1, 2 * unit + 8, width), lambda i, ctl: (i, 0, 0))] * len(parts),
+            out_specs=pl.BlockSpec((blocks, 1, unit // 2 + 8, 4 * width // blocks), lambda i, ctl: (0, i, 0, 0)),
             scratch_shapes=[pltpu.VMEM((4, unit, width), jnp.float32)],
         ),
-        out_shape=jax.ShapeDtypeStruct((blocks, units, unit + 16, 4 * width // blocks), jnp.int16),
+        out_shape=jax.ShapeDtypeStruct((blocks, units, unit // 2 + 8, 4 * width // blocks), jnp.int32),
         compiler_params=params(),
         cost_estimate=pl.CostEstimate(flops=131072 * cells, bytes_accessed=cells, transcendentals=0),
         name="gather_parts",
@@ -413,7 +446,7 @@
     part = got.shape[3] // 4
     cells = 4 * units * unit * part * blocks
     operands = [got]
-    in_specs = [pl.BlockSpec((blocks, 1, unit + 16, 4 * part), lambda i: (0, i, 0, 0))]
+    in_specs = [pl.BlockSpec((blocks, 1, unit // 2 + 8, 4 * part), lambda i: (0, i, 0, 0))]
     if so_far is not None:
         operands.append(so_far)
         in_specs.append(pl.BlockSpec(memory_space=pl.ANY))
@@ -443,7 +476,13 @@
     table = table * jnp.array([[1.0], [1.0], [1.0], [0.01]], jnp.float32)
     bins = table.shape[1]
     slope = jnp.concatenate([table[:, 1:] - table[:, :-1], jnp.zeros_like(table[:, :1])], axis=1)
-    table = jnp.pad(jnp.concatenate([table, slope], axis=0), ((0, 0), (0, LANES - bins)))
+    table = jnp.concatenate([table, slope[:ON_MATRIX - 4]], axis=0)
+    slope = jnp.pad(slope, ((0, 4), (0, LANES - bins)))
+    coarse = lax.reduce_precision(table, exponent_bits=8, mantissa_bits=7)
+    table = jnp.concatenate([coarse, table - coarse], axis=0)
+    spread = jnp.eye(16, dtype=jnp.float32)
+    table = (table[:, None, :, None] * spread[None, :, None, :]).reshape(2 * ON_MATRIX * 16, bins * 16)
+    table = table.astype(jnp.bfloat16)
     azimuth, polar = light_angles[0], light_angles[1]
     light = 0.105 * jnp.stack(
         [jnp.cos(azimuth) * jnp.sin(polar), jnp.sin(azimuth) * jnp.sin(polar), jnp.cos(polar)]
@@ -489,7 +528,7 @@
     def start_chunk(n):
         before, after, at = halos[n]
         send, keep = render(
-            after_last(render_control), light, table, field, before, after,
+            after_last(render_control), light, table, slope, field, before, after,
             groups=tiles, units=1, unit=unit, rows=rows, offset=starts[n], halo_at=at,
         )
         chain.append(send)

time: 304 us -> 260 us (0.86)
  Pallas kernels: 207 us -> 163 us
    pallas_call x3, Pallas kernels: 172 us -> 128 us  [render(): pl.pallas_call(kernel, grid_spec=pltpu.PrefetchScalarGridSpec(num_scalar_...]
  transfers between devices with their start and end apart: 15 -> 15, of which waited for: 5 -> 5; matrix products, arithmetic and copies ran while one was open for 3% -> 4% of each run, Pallas kernels for 61% -> 55%
where the time goes in v8:
time: 260 us; the launch traced here: 259 us
  Pallas kernels  163 us (63%)
  waiting for transfers between devices  41.1 us (16%)
  starting transfers between devices  35.4 us (14%)
  local copies, waits for them, and re-layouts  12.3 us (5%)
  other arithmetic  3.69 us (1%)
  between operations  3.11 us (1%)
    pallas_call x3, Pallas kernels, render(): pl.pallas_call(kernel, grid_spec=pltpu.PrefetchScalarGridSpec(num_scalar_...  128 us
    ppermute x9, waiting for transfers between devices, exchange(): return lax.ppermute(send, 'tile', [(i, i ^ distance) for i in range(tiles)])  23.9 us
    pallas_call x2, Pallas kernels, merge(): pl.pallas_call(functools.partial(merge_kernel, members=members, places=pl...  19.4 us
    ppermute x4, starting transfers between devices, per_device(): pair = (lax.ppermute(ends[0], both, up), lax.ppermute(ends[1], both, down))  19 us
    all_to_all x2, waiting for transfers between devices, block_group(): lax.all_to_all(send, 'depth', split_axis=0, concat_axis=0, tiled=True)  17.2 us
    pallas_call x2, Pallas kernels, gather_parts(): pl.pallas_call(functools.partial(gather_kernel, unit=unit, blocks=blocks)...  9.19 us
    ppermute x9, starting transfers between devices, exchange(): return lax.ppermute(send, 'tile', [(i, i ^ distance) for i in range(tiles)])  9.03 us
    all_to_all x2, starting transfers between devices, block_group(): lax.all_to_all(send, 'depth', split_axis=0, concat_axis=0, tiled=True)  7.34 us
  transfers between devices with their start and end apart: 15, of which 5 were waited for; matrix products, arithmetic and copies ran while one was open for 4% of the time, Pallas kernels for 55%

profile of v8, /device:TPU:0, one launch (start us, length us, event | category | flops | bytes accessed | tf_op | source)
XLA Modules:
  0.0 258.8 jit_solution(12222978186957793961)
XLA Ops:
  0.0 1.6 slice_bitcast_fusion.2
  2.9 4.0 %collective-permute-start = (bf16[8,48,1152]{2,1,0:T(8,128)(2,1)S(1)}, bf16[8,48,1152]{2,1,0:T(8,128)(2,1)}, u32[]{:S(2)}, u32[]{:S(2)}) collective-permute-start(bf16[8,48,1152]{2,1,0:T(8,128)(2,1)S(1)} %get-tuple-element.52), channel_id=1, source_target_pairs={{0,1},{1,2},{2,3},{3,4},{4,5},{5,6},{6,7},{7,8},{8,9},{9,10},{10,1... | collective-permute-start | bytes 2654216 | tf_op jit(solution)/shard_map/ppermute | solution.py:511
  16.3 2.3 slice_bitcast_fusion
  18.6 12.5 %collective-permute-start.2 = (bf16[8,96,1152]{2,1,0:T(8,128)(2,1)S(1)}, bf16[8,96,1152]{2,1,0:T(8,128)(2,1)}, u32[]{:S(2)}, u32[]{:S(2)}) collective-permute-start(bf16[8,96,1152]{2,1,0:T(8,128)(2,1)S(1)} %get-tuple-element.29), channel_id=1, source_target_pairs={{0,1},{1,2},{2,3},{3,4},{4,5},{5,6},{6,7},{7,8},{8,9},{9,10},{10,1... | collective-permute-start | bytes 5308424 | tf_op jit(solution)/shard_map/ppermute | solution.py:511
  32.3 42.7 %render.3 = (f32[4,4,48,1152]{3,2,1,0:T(8,128)}, f32[4,4,48,1152]{3,2,1,0:T(8,128)}) custom-call(s32[2]{0:T(128)} %pad_add_fusion.1.ctl, f32[3]{0:T(128)} %maximum_multiply_fusion.light, bf16[192,256]{1,0:T(8,128)(2,1)} %convert_element_type.95.table, f32[8,128]{1,0:T(8,128)} %pad.5.slope, bf16[4,48,80]{2,1,0:T(8,128)(2,1)} %pad_maximum_fusion.1.row_bands, ...), custom_call_target="tpu_custom_call" | custom-call | flops 43486543872 | bytes 15925248 | tf_op jit(solution)/shard_map/render/pallas_call | solution.py:364
  75.0 2.0 collective-permute-start.4
  77.0 42.9 %render.4 = (f32[4,4,48,1152]{3,2,1,0:T(8,128)}, f32[4,4,48,1152]{3,2,1,0:T(8,128)}) custom-call(s32[2]{0:T(128)} %pad_add_fusion.1.ctl, f32[3]{0:T(128)} %maximum_multiply_fusion.light, bf16[192,256]{1,0:T(8,128)(2,1)} %convert_element_type.95.table, f32[8,128]{1,0:T(8,128)} %pad.5.slope, bf16[4,48,80]{2,1,0:T(8,128)(2,1)} %pad_maximum_fusion.1.row_bands, ...), custom_call_target="tpu_custom_call" | custom-call | flops 43486543872 | bytes 15925248 | tf_op jit(solution)/shard_map/render/pallas_call | solution.py:364
  120.5 5.9 %collective-permute-done.5.refs_3_ = f32[4,4,48,1152]{3,2,1,0:T(8,128)} collective-permute-done((f32[4,4,48,1152]{3,2,1,0:T(8,128)}, f32[4,4,48,1152]{3,2,1,0:T(8,128)}, u32[]{:S(2)}, u32[]{:S(2)}) %collective-permute-start.5) | collective-permute-done | bytes 3538976 | tf_op jit(solution)/shard_map/ppermute | solution.py:515
  126.5 12.9 %merge.2 = (s32[2,104,1152]{2,1,0:T(8,128)}, s32[2,104,1152]{2,1,0:T(8,128)}, s32[2,104,1152]{2,1,0:T(8,128)}, s32[2,104,1152]{2,1,0:T(8,128)}) custom-call(s32[2]{0:T(128)} %pad_add_fusion.ctl, f32[4,4,48,1152]{3,2,1,0:T(8,128)} %get-tuple-element.33.refs_0_, f32[4,4,48,1152]{3,2,1,0:T(8,128)} %copy-done.5, f32[4,4,48,1152]{3,2,1,0:T(8,128)} %get-tuple-element.34.refs_2_, ...), custom_call_target="tpu_custom_call" | custom-call | flops 57982058496 | bytes 1769472 | tf_op jit(solution)/shard_map/merge/pallas_call | solution.py:408
  142.8 42.8 %render.5 = (f32[4,4,48,1152]{3,2,1,0:T(8,128)}, f32[4,4,48,1152]{3,2,1,0:T(8,128)}) custom-call(s32[2]{0:T(128)} %pad_add_fusion.1.ctl, f32[3]{0:T(128)} %maximum_multiply_fusion.light, bf16[192,256]{1,0:T(8,128)(2,1)} %convert_element_type.95.table, f32[8,128]{1,0:T(8,128)} %pad.5.slope, bf16[4,48,80]{2,1,0:T(8,128)(2,1)} %pad_maximum_fusion.1.row_bands, ...), custom_call_target="tpu_custom_call" | custom-call | flops 43486543872 | bytes 15925248 | tf_op jit(solution)/shard_map/render/pallas_call | solution.py:364
  187.3 5.2 %gather_parts.2 = s32[4,2,32,1152]{3,2,1,0:T(8,128)} custom-call(s32[2]{0:T(128)} %pad_add_fusion.ctl, s32[2,104,1152]{2,1,0:T(8,128)} %get-tuple-element.38.refs_0_, s32[2,104,1152]{2,1,0:T(8,128)} %copy-done.8, s32[2,104,1152]{2,1,0:T(8,128)} %copy-done.9, s32[2,104,1152]{2,1,0:T(8,128)} %copy-done.7), custom_call_target="tpu_custom_call" | custom-call | flops 57982058496 | bytes 442368 | tf_op jit(solution)/shard_map/gather_parts/pallas_call | solution.py:428
  192.5 1.8 copy-done.6
  194.3 6.5 %merge.3 = (s32[1,104,1152]{2,1,0:T(8,128)}, s32[1,104,1152]{2,1,0:T(8,128)}, s32[1,104,1152]{2,1,0:T(8,128)}, s32[1,104,1152]{2,1,0:T(8,128)}) custom-call(s32[2]{0:T(128)} %pad_add_fusion.ctl, f32[4,4,48,1152]{3,2,1,0:T(8,128)} %get-tuple-element.43.refs_0_, f32[4,4,48,1152]{3,2,1,0:T(8,128)} %copy-done.6), custom_call_target="tpu_custom_call" | custom-call | flops 28991029248 | bytes 884736 | tf_op jit(solution)/shard_map/merge/pallas_call | solution.py:408
  200.7 1.8 collective-permute-start.10
  202.5 1.7 collective-permute-start.12
  204.2 3.9 %all-to-all-start.1 = ((s32[4,2,32,1152]{3,2,1,0:T(8,128)}), s32[4,2,32,1152]{3,2,1,0:T(8,128)S(1)}, u32[]{:S(2)}, u32[]{:S(2)}) async-start(s32[4,2,32,1152]{3,2,1,0:T(8,128)} %gather_parts.2), calls=%async_computation.1 | async-start | bytes 2359296 | tf_op jit(solution)/shard_map/all_to_all | solution.py:545
  208.1 6.6 %collective-permute-done.10.refs_1_ = s32[1,104,1152]{2,1,0:T(8,128)S(1)} collective-permute-done((s32[1,104,1152]{2,1,0:T(8,128)}, s32[1,104,1152]{2,1,0:T(8,128)S(1)}, u32[]{:S(2)}, u32[]{:S(2)}) %collective-permute-start.10) | collective-permute-done | bytes 479264 | tf_op jit(solution)/shard_map/ppermute | solution.py:515
  214.7 11.4 %collective-permute-done.11.refs_2_ = s32[1,104,1152]{2,1,0:T(8,128)S(1)} collective-permute-done((s32[1,104,1152]{2,1,0:T(8,128)}, s32[1,104,1152]{2,1,0:T(8,128)S(1)}, u32[]{:S(2)}, u32[]{:S(2)}) %collective-permute-start.11) | collective-permute-done | bytes 479264 | tf_op jit(solution)/shard_map/ppermute | solution.py:515
  227.0 4.0 %gather_parts.3 = s32[4,1,32,1152]{3,2,1,0:T(8,128)} custom-call(s32[2]{0:T(128)} %pad_add_fusion.ctl, s32[1,104,1152]{2,1,0:T(8,128)} %get-tuple-element.46.refs_0_, s32[1,104,1152]{2,1,0:T(8,128)} %copy-done.10, s32[1,104,1152]{2,1,0:T(8,128)} %copy-done.11, s32[1,104,1152]{2,1,0:T(8,128)} %copy-done.12), custom_call_target="tpu_custom_call" | custom-call | flops 28991029248 | bytes 221184 | tf_op jit(solution)/shard_map/gather_parts/pallas_call | solution.py:428
  231.0 5.5 %all-to-all-done.1.got = s32[4,2,32,1152]{3,2,1,0:T(8,128)S(1)} async-done(((s32[4,2,32,1152]{3,2,1,0:T(8,128)}), s32[4,2,32,1152]{3,2,1,0:T(8,128)S(1)}, u32[]{:S(2)}, u32[]{:S(2)}) %all-to-all-start.1) | async-done | bytes 1179680 | tf_op jit(solution)/shard_map/all_to_all | solution.py:545
  236.5 3.5 %all-to-all-start = ((s32[4,1,32,1152]{3,2,1,0:T(8,128)}), s32[4,1,32,1152]{3,2,1,0:T(8,128)S(1)}, u32[]{:S(2)}, u32[]{:S(2)}) async-start(s32[4,1,32,1152]{3,2,1,0:T(8,128)} %gather_parts.3), calls=%async_computation | async-start | bytes 1179648 | tf_op jit(solution)/shard_map/all_to_all | solution.py:545
  240.0 3.6 %compose.2.refs_0_ = f32[4,144,288]{2,1,0:T(8,128)} custom-call(s32[4,2,32,1152]{3,2,1,0:T(8,128)} %copy-done), custom_call_target="tpu_custom_call" | custom-call | flops 14495514624 | bytes 442368 | tf_op jit(solution)/shard_map/compose/pallas_call | solution.py:453
  243.6 11.8 %all-to-all-done.got = s32[4,1,32,1152]{3,2,1,0:T(8,128)S(1)} async-done(((s32[4,1,32,1152]{3,2,1,0:T(8,128)}), s32[4,1,32,1152]{3,2,1,0:T(8,128)S(1)}, u32[]{:S(2)}, u32[]{:S(2)}) %all-to-all-start) | async-done | bytes 589856 | tf_op jit(solution)/shard_map/all_to_all | solution.py:545
  256.2 2.7 %compose.3 = f32[4,144,288]{2,1,0:T(8,128)} custom-call(s32[4,1,32,1152]{3,2,1,0:T(8,128)} %copy-done.1, f32[4,144,288]{2,1,0:T(8,128)} %compose.2.refs_0_), custom_call_target="tpu_custom_call", output_to_operand_aliasing={{}: (1, {})} | custom-call | flops 7247757312 | bytes 221184 | tf_op jit(solution)/shard_map/compose/pallas_call | solution.py:453
  (75 shorter events, 16.4 us)
Async XLA Ops:
  0.0 11.9 %copy-start.4 = (f32[4]{0:T(128)S(1)}, f32[4]{0:T(128)}, u32[]{:S(2)}) copy-start(f32[4]{0:T(128)} %constant.60) | copy-start | bytes 52
  0.0 6.9 %copy-start.13 = (s32[16]{0:T(128)S(1)}, s32[16]{0:T(128)}, u32[]{:S(2)}) copy-start(s32[16]{0:T(128)} %param.7) | copy-start | bytes 196
  0.0 7.0 %copy-start.3 = (f32[2]{0:T(128)S(1)}, f32[2]{0:T(128)}, u32[]{:S(2)}) copy-start(f32[2]{0:T(128)} %param.8) | copy-start | bytes 28
  0.0 11.2 %copy-start.2 = (f32[4,16]{1,0:T(4,128)S(1)}, f32[4,16]{1,0:T(4,128)}, u32[]{:S(2)}) copy-start(f32[4,16]{1,0:T(4,128)} %param.6) | copy-start | bytes 772
  1.6 16.9 %collective-permute-start.1 = (bf16[8,48,1152]{2,1,0:T(8,128)(2,1)S(1)}, bf16[8,48,1152]{2,1,0:T(8,128)(2,1)}, u32[]{:S(2)}, u32[]{:S(2)}) collective-permute-start(bf16[8,48,1152]{2,1,0:T(8,128)(2,1)S(1)} %get-tuple-element.51), channel_id=1, source_target_pairs={{1,0},{2,1},{3,2},{4,3},{5,4},{6,5},{7,6},{8,7},{9,8},{10,9},{11,1... | collective-permute-start | bytes 2654216 | tf_op jit(solution)/shard_map/ppermute | solution.py:511
  2.9 15.6 %collective-permute-start = (bf16[8,48,1152]{2,1,0:T(8,128)(2,1)S(1)}, bf16[8,48,1152]{2,1,0:T(8,128)(2,1)}, u32[]{:S(2)}, u32[]{:S(2)}) collective-permute-start(bf16[8,48,1152]{2,1,0:T(8,128)(2,1)S(1)} %get-tuple-element.52), channel_id=1, source_target_pairs={{0,1},{1,2},{2,3},{3,4},{4,5},{5,6},{6,7},{7,8},{8,9},{9,10},{10,1... | collective-permute-start | bytes 2654216 | tf_op jit(solution)/shard_map/ppermute | solution.py:511
  18.6 58.5 %collective-permute-start.2 = (bf16[8,96,1152]{2,1,0:T(8,128)(2,1)S(1)}, bf16[8,96,1152]{2,1,0:T(8,128)(2,1)}, u32[]{:S(2)}, u32[]{:S(2)}) collective-permute-start(bf16[8,96,1152]{2,1,0:T(8,128)(2,1)S(1)} %get-tuple-element.29), channel_id=1, source_target_pairs={{0,1},{1,2},{2,3},{3,4},{4,5},{5,6},{6,7},{7,8},{8,9},{9,10},{10,1... | collective-permute-start | bytes 5308424 | tf_op jit(solution)/shard_map/ppermute | solution.py:511
  31.0 46.0 %collective-permute-start.3 = (bf16[8,96,1152]{2,1,0:T(8,128)(2,1)S(1)}, bf16[8,96,1152]{2,1,0:T(8,128)(2,1)}, u32[]{:S(2)}, u32[]{:S(2)}) collective-permute-start(bf16[8,96,1152]{2,1,0:T(8,128)(2,1)S(1)} %get-tuple-element.30), channel_id=1, source_target_pairs={{1,0},{2,1},{3,2},{4,3},{5,4},{6,5},{7,6},{8,7},{9,8},{10,9},{11,1... | collective-permute-start | bytes 5308424 | tf_op jit(solution)/shard_map/ppermute | solution.py:511
  75.0 45.5 %collective-permute-start.4 = (f32[4,4,48,1152]{3,2,1,0:T(8,128)}, f32[4,4,48,1152]{3,2,1,0:T(8,128)S(1)}, u32[]{:S(2)}, u32[]{:S(2)}) collective-permute-start(f32[4,4,48,1152]{3,2,1,0:T(8,128)} %get-tuple-element.27), channel_id=1, source_target_pairs={{0,1},{1,0},{2,3},{3,2},{4,5},{5,4},{6,7},{7,6},{8,9},{9,8},{10,11... | collective-permute-start | bytes 10616840 | tf_op jit(solution)/shard_map/ppermute | solution.py:515
  119.9 6.6 %collective-permute-start.5 = (f32[4,4,48,1152]{3,2,1,0:T(8,128)}, f32[4,4,48,1152]{3,2,1,0:T(8,128)}, u32[]{:S(2)}, u32[]{:S(2)}) collective-permute-start(f32[4,4,48,1152]{3,2,1,0:T(8,128)} %get-tuple-element.31), channel_id=1, source_target_pairs={{0,1},{1,0},{2,3},{3,2},{4,5},{5,4},{6,7},{7,6},{8,9},{9,8},{10,11... | collective-permute-start | bytes 10616840 | tf_op jit(solution)/shard_map/ppermute | solution.py:515
  120.5 5.9 %copy-start.5 = (f32[4,4,48,1152]{3,2,1,0:T(8,128)}, f32[4,4,48,1152]{3,2,1,0:T(8,128)S(1)}, u32[]{:S(2)}) copy-start(f32[4,4,48,1152]{3,2,1,0:T(8,128)S(1)} %collective-permute-done.4.refs_1_) | copy-start | bytes 10616836
  139.4 46.4 %collective-permute-start.8 = (s32[2,104,1152]{2,1,0:T(8,128)}, s32[2,104,1152]{2,1,0:T(8,128)S(1)}, u32[]{:S(2)}, u32[]{:S(2)}) collective-permute-start(s32[2,104,1152]{2,1,0:T(8,128)} %get-tuple-element.35), channel_id=1, source_target_pairs={{0,6},{1,7},{2,4},{3,5},{4,2},{5,3},{6,0},{7,1},{8,14},{9,15},{10,... | collective-permute-start | bytes 2875400 | tf_op jit(solution)/shard_map/ppermute | solution.py:515
  140.2 45.5 %collective-permute-start.6 = (s32[2,104,1152]{2,1,0:T(8,128)}, s32[2,104,1152]{2,1,0:T(8,128)S(1)}, u32[]{:S(2)}, u32[]{:S(2)}) collective-permute-start(s32[2,104,1152]{2,1,0:T(8,128)} %get-tuple-element.39), channel_id=1, source_target_pairs={{0,2},{1,3},{2,0},{3,1},{4,6},{5,7},{6,4},{7,5},{8,10},{9,11},{10,... | collective-permute-start | bytes 2875400 | tf_op jit(solution)/shard_map/ppermute | solution.py:515
  141.6 44.1 %collective-permute-start.7 = (s32[2,104,1152]{2,1,0:T(8,128)}, s32[2,104,1152]{2,1,0:T(8,128)S(1)}, u32[]{:S(2)}, u32[]{:S(2)}) collective-permute-start(s32[2,104,1152]{2,1,0:T(8,128)} %get-tuple-element.40), channel_id=1, source_target_pairs={{0,4},{1,5},{2,6},{3,7},{4,0},{5,1},{6,2},{7,3},{8,12},{9,13},{10,... | collective-permute-start | bytes 2875400 | tf_op jit(solution)/shard_map/ppermute | solution.py:515
  185.7 6.8 %collective-permute-start.9 = (f32[4,4,48,1152]{3,2,1,0:T(8,128)}, f32[4,4,48,1152]{3,2,1,0:T(8,128)S(1)}, u32[]{:S(2)}, u32[]{:S(2)}) collective-permute-start(f32[4,4,48,1152]{3,2,1,0:T(8,128)} %get-tuple-element.37), channel_id=1, source_target_pairs={{0,1},{1,0},{2,3},{3,2},{4,5},{5,4},{6,7},{7,6},{8,9},{9,8},{10,11... | collective-permute-start | bytes 10616840 | tf_op jit(solution)/shard_map/ppermute | solution.py:515
  185.7 1.6 copy-start.7
  192.5 1.8 copy-start.6
  200.7 14.0 %collective-permute-start.10 = (s32[1,104,1152]{2,1,0:T(8,128)}, s32[1,104,1152]{2,1,0:T(8,128)S(1)}, u32[]{:S(2)}, u32[]{:S(2)}) collective-permute-start(s32[1,104,1152]{2,1,0:T(8,128)} %get-tuple-element.47), channel_id=1, source_target_pairs={{0,2},{1,3},{2,0},{3,1},{4,6},{5,7},{6,4},{7,5},{8,10},{9,11},{10,... | collective-permute-start | bytes 1437704 | tf_op jit(solution)/shard_map/ppermute | solution.py:515
  202.5 23.6 %collective-permute-start.11 = (s32[1,104,1152]{2,1,0:T(8,128)}, s32[1,104,1152]{2,1,0:T(8,128)S(1)}, u32[]{:S(2)}, u32[]{:S(2)}) collective-permute-start(s32[1,104,1152]{2,1,0:T(8,128)} %get-tuple-element.48), channel_id=1, source_target_pairs={{0,4},{1,5},{2,6},{3,7},{4,0},{5,1},{6,2},{7,3},{8,12},{9,13},{10,... | collective-permute-start | bytes 1437704 | tf_op jit(solution)/shard_map/ppermute | solution.py:515
  202.5 23.6 %collective-permute-start.12 = (s32[1,104,1152]{2,1,0:T(8,128)}, s32[1,104,1152]{2,1,0:T(8,128)S(1)}, u32[]{:S(2)}, u32[]{:S(2)}) collective-permute-start(s32[1,104,1152]{2,1,0:T(8,128)} %get-tuple-element.44), channel_id=1, source_target_pairs={{0,6},{1,7},{2,4},{3,5},{4,2},{5,3},{6,0},{7,1},{8,14},{9,15},{10,... | collective-permute-start | bytes 1437704 | tf_op jit(solution)/shard_map/ppermute | solution.py:515
  204.2 32.3 %all-to-all-start.1 = ((s32[4,2,32,1152]{3,2,1,0:T(8,128)}), s32[4,2,32,1152]{3,2,1,0:T(8,128)S(1)}, u32[]{:S(2)}, u32[]{:S(2)}) async-start(s32[4,2,32,1152]{3,2,1,0:T(8,128)} %gather_parts.2), calls=%async_computation.1 | async-start | bytes 2359296 | tf_op jit(solution)/shard_map/all_to_all | solution.py:545
  214.7 11.4 %copy-start.10 = (s32[1,104,1152]{2,1,0:T(8,128)}, s32[1,104,1152]{2,1,0:T(8,128)S(1)}, u32[]{:S(2)}) copy-start(s32[1,104,1152]{2,1,0:T(8,128)S(1)} %collective-permute-done.10.refs_1_) | copy-start | bytes 1437700
  236.5 3.5 %copy-start = (s32[4,2,32,1152]{3,2,1,0:T(8,128)}, s32[4,2,32,1152]{3,2,1,0:T(8,128)S(1)}, u32[]{:S(2)}) copy-start(s32[4,2,32,1152]{3,2,1,0:T(8,128)S(1)} %all-to-all-done.1.got) | copy-start | bytes 3538948
  236.5 18.8 %all-to-all-start = ((s32[4,1,32,1152]{3,2,1,0:T(8,128)}), s32[4,1,32,1152]{3,2,1,0:T(8,128)S(1)}, u32[]{:S(2)}, u32[]{:S(2)}) async-start(s32[4,1,32,1152]{3,2,1,0:T(8,128)} %gather_parts.3), calls=%async_computation | async-start | bytes 1179648 | tf_op jit(solution)/shard_map/all_to_all | solution.py:545
  (5 other events, 4.9 us)

commit v9 on v8

--- a/solution.py
+++ b/solution.py
@@ -10,7 +10,7 @@
 
 LANES = 128
 CODES = 32700.0
-ON_MATRIX = 6
+ON_MATRIX = 4
 VMEM_LIMIT = 56 * 1024 * 1024
 
 
@@ -51,10 +51,24 @@
     )
 
 
-def choose(bins, whole):
-    place = whole.astype(jnp.bfloat16)
-    one, zero = jnp.ones_like(place), jnp.zeros_like(place)
-    return jnp.concatenate([jnp.where(place == k, one, zero) for k in range(bins)], axis=0)
+def one_hot(x, levels):
+    rows = []
+    for j in range(levels):
+        if j == 0:
+            row = 1 - x
+        elif j == levels - 1:
+            row = x - (levels - 2)
+        else:
+            row = jnp.minimum(x if j == 1 else x - (j - 1), (j + 1) - x)
+        rows.append(jnp.maximum(row, 0))
+    return rows
+
+
+def choose(bins, index, whole):
+    high = (index >> 2).astype(jnp.float32)
+    low = (whole - 4.0 * high).astype(jnp.bfloat16)
+    highs, lows = one_hot(high.astype(jnp.bfloat16), bins // 4), one_hot(low, 4)
+    return jnp.concatenate([h * l for h in highs for l in lows], axis=0)
 
 
 def padded_rows(unit):
@@ -163,7 +177,7 @@
                     whole = index.astype(jnp.float32)
                     parts.append(position - whole)
                     tilts.append([lookup(tilt, index) for tilt in tilts_of])
-                    picks.append(choose(bins, whole))
+                    picks.append(choose(bins, index, whole))
                     gx = high - low
                     gy = slopes_y[layer, s, :]
                     gz = slopes_z[layer, s, :]

time: 260 us -> 259 us (level)
    unnamed x29 -> x31, local copies, waits for them, and re-layouts: 5.23 us -> 5.24 us
  transfers between devices with their start and end apart: 15 -> 15, of which waited for: 5 -> 5; matrix products, arithmetic and copies ran while one was open for 4% -> 3% of each run, Pallas kernels for 55% -> 54%
where the time goes in v9:
time: 259 us; the launch traced here: 258 us
  Pallas kernels  162 us (63%)
  waiting for transfers between devices  41.1 us (16%)
  starting transfers between devices  35.8 us (14%)
  local copies, waits for them, and re-layouts  12 us (5%)
  other arithmetic  3.7 us (1%)
  between operations  3.01 us (1%)
    pallas_call x3, Pallas kernels, render(): pl.pallas_call(kernel, grid_spec=pltpu.PrefetchScalarGridSpec(num_scalar_...  127 us
    ppermute x9, waiting for transfers between devices, exchange(): return lax.ppermute(send, 'tile', [(i, i ^ distance) for i in range(tiles)])  23.9 us
    ppermute x4, starting transfers between devices, per_device(): pair = (lax.ppermute(ends[0], both, up), lax.ppermute(ends[1], both, down))  19.4 us
    pallas_call x2, Pallas kernels, merge(): pl.pallas_call(functools.partial(merge_kernel, members=members, places=pl...  19.3 us
    all_to_all x2, waiting for transfers between devices, block_group(): lax.all_to_all(send, 'depth', split_axis=0, concat_axis=0, tiled=True)  17.2 us
    pallas_call x2, Pallas kernels, gather_parts(): pl.pallas_call(functools.partial(gather_kernel, unit=unit, blocks=blocks)...  9.2 us
    ppermute x9, starting transfers between devices, exchange(): return lax.ppermute(send, 'tile', [(i, i ^ distance) for i in range(tiles)])  9.05 us
    all_to_all x2, starting transfers between devices, block_group(): lax.all_to_all(send, 'depth', split_axis=0, concat_axis=0, tiled=True)  7.33 us
  transfers between devices with their start and end apart: 15, of which 5 were waited for; matrix products, arithmetic and copies ran while one was open for 3% of the time, Pallas kernels for 54%

profile of v9, /device:TPU:0, one launch (start us, length us, event | category | flops | bytes accessed | tf_op | source)
XLA Modules:
  0.0 257.8 jit_solution(14711881412080474475)
XLA Ops:
  0.0 1.6 slice_bitcast_fusion.2
  2.9 4.0 %collective-permute-start = (bf16[8,48,1152]{2,1,0:T(8,128)(2,1)S(1)}, bf16[8,48,1152]{2,1,0:T(8,128)(2,1)}, u32[]{:S(2)}, u32[]{:S(2)}) collective-permute-start(bf16[8,48,1152]{2,1,0:T(8,128)(2,1)S(1)} %get-tuple-element.54), channel_id=1, source_target_pairs={{0,1},{1,2},{2,3},{3,4},{4,5},{5,6},{6,7},{7,8},{8,9},{9,10},{10,1... | collective-permute-start | bytes 2654216 | tf_op jit(solution)/shard_map/ppermute | solution.py:525
  15.8 2.3 slice_bitcast_fusion
  18.1 12.9 %collective-permute-start.2 = (bf16[8,96,1152]{2,1,0:T(8,128)(2,1)S(1)}, bf16[8,96,1152]{2,1,0:T(8,128)(2,1)}, u32[]{:S(2)}, u32[]{:S(2)}) collective-permute-start(bf16[8,96,1152]{2,1,0:T(8,128)(2,1)S(1)} %get-tuple-element.29), channel_id=1, source_target_pairs={{0,1},{1,2},{2,3},{3,4},{4,5},{5,6},{6,7},{7,8},{8,9},{9,10},{10,1... | collective-permute-start | bytes 5308424 | tf_op jit(solution)/shard_map/ppermute | solution.py:525
  32.3 42.5 %render.3 = (f32[4,4,48,1152]{3,2,1,0:T(8,128)}, f32[4,4,48,1152]{3,2,1,0:T(8,128)}) custom-call(s32[2]{0:T(128)} %pad_add_fusion.1.ctl, f32[3]{0:T(128)} %maximum_multiply_fusion.light, bf16[128,256]{1,0:T(8,128)(2,1)} %convert_element_type.95.table, f32[8,128]{1,0:T(8,128)} %pad.23.slope, bf16[4,48,80]{2,1,0:T(8,128)(2,1)} %pad_maximum_fusion.1.row_bands, ...), custom_call_target="tpu_custom_call" | custom-call | flops 43486543872 | bytes 15925248 | tf_op jit(solution)/shard_map/render/pallas_call | solution.py:378
  74.8 2.0 collective-permute-start.4
  76.9 42.4 %render.4 = (f32[4,4,48,1152]{3,2,1,0:T(8,128)}, f32[4,4,48,1152]{3,2,1,0:T(8,128)}) custom-call(s32[2]{0:T(128)} %pad_add_fusion.1.ctl, f32[3]{0:T(128)} %maximum_multiply_fusion.light, bf16[128,256]{1,0:T(8,128)(2,1)} %convert_element_type.95.table, f32[8,128]{1,0:T(8,128)} %pad.23.slope, bf16[4,48,80]{2,1,0:T(8,128)(2,1)} %pad_maximum_fusion.1.row_bands, ...), custom_call_target="tpu_custom_call" | custom-call | flops 43486543872 | bytes 15925248 | tf_op jit(solution)/shard_map/render/pallas_call | solution.py:378
  120.0 5.9 %collective-permute-done.5.refs_3_ = f32[4,4,48,1152]{3,2,1,0:T(8,128)} collective-permute-done((f32[4,4,48,1152]{3,2,1,0:T(8,128)}, f32[4,4,48,1152]{3,2,1,0:T(8,128)}, u32[]{:S(2)}, u32[]{:S(2)}) %collective-permute-start.5) | collective-permute-done | bytes 3538976 | tf_op jit(solution)/shard_map/ppermute | solution.py:529
  125.8 12.9 %merge.2 = (s32[2,104,1152]{2,1,0:T(8,128)}, s32[2,104,1152]{2,1,0:T(8,128)}, s32[2,104,1152]{2,1,0:T(8,128)}, s32[2,104,1152]{2,1,0:T(8,128)}) custom-call(s32[2]{0:T(128)} %pad_add_fusion.ctl, f32[4,4,48,1152]{3,2,1,0:T(8,128)} %get-tuple-element.33.refs_0_, f32[4,4,48,1152]{3,2,1,0:T(8,128)} %copy-done.5, f32[4,4,48,1152]{3,2,1,0:T(8,128)} %get-tuple-element.34.refs_2_, ...), custom_call_target="tpu_custom_call" | custom-call | flops 57982058496 | bytes 1769472 | tf_op jit(solution)/shard_map/merge/pallas_call | solution.py:422
  142.2 42.5 %render.5 = (f32[4,4,48,1152]{3,2,1,0:T(8,128)}, f32[4,4,48,1152]{3,2,1,0:T(8,128)}) custom-call(s32[2]{0:T(128)} %pad_add_fusion.1.ctl, f32[3]{0:T(128)} %maximum_multiply_fusion.light, bf16[128,256]{1,0:T(8,128)(2,1)} %convert_element_type.95.table, f32[8,128]{1,0:T(8,128)} %pad.23.slope, bf16[4,48,80]{2,1,0:T(8,128)(2,1)} %pad_maximum_fusion.1.row_bands, ...), custom_call_target="tpu_custom_call" | custom-call | flops 43486543872 | bytes 15925248 | tf_op jit(solution)/shard_map/render/pallas_call | solution.py:378
  186.3 5.2 %gather_parts.2 = s32[4,2,32,1152]{3,2,1,0:T(8,128)} custom-call(s32[2]{0:T(128)} %pad_add_fusion.ctl, s32[2,104,1152]{2,1,0:T(8,128)} %get-tuple-element.38.refs_0_, s32[2,104,1152]{2,1,0:T(8,128)} %copy-done.8, s32[2,104,1152]{2,1,0:T(8,128)} %copy-done.9, s32[2,104,1152]{2,1,0:T(8,128)} %copy-done.7), custom_call_target="tpu_custom_call" | custom-call | flops 57982058496 | bytes 442368 | tf_op jit(solution)/shard_map/gather_parts/pallas_call | solution.py:442
  191.5 1.8 copy-done.6
  193.2 6.4 %merge.3 = (s32[1,104,1152]{2,1,0:T(8,128)}, s32[1,104,1152]{2,1,0:T(8,128)}, s32[1,104,1152]{2,1,0:T(8,128)}, s32[1,104,1152]{2,1,0:T(8,128)}) custom-call(s32[2]{0:T(128)} %pad_add_fusion.ctl, f32[4,4,48,1152]{3,2,1,0:T(8,128)} %get-tuple-element.43.refs_0_, f32[4,4,48,1152]{3,2,1,0:T(8,128)} %copy-done.6), custom_call_target="tpu_custom_call" | custom-call | flops 28991029248 | bytes 884736 | tf_op jit(solution)/shard_map/merge/pallas_call | solution.py:422
  199.7 1.8 collective-permute-start.10
  201.5 1.7 collective-permute-start.12
  203.2 3.9 %all-to-all-start.1 = ((s32[4,2,32,1152]{3,2,1,0:T(8,128)}), s32[4,2,32,1152]{3,2,1,0:T(8,128)S(1)}, u32[]{:S(2)}, u32[]{:S(2)}) async-start(s32[4,2,32,1152]{3,2,1,0:T(8,128)} %gather_parts.2), calls=%async_computation.1 | async-start | bytes 2359296 | tf_op jit(solution)/shard_map/all_to_all | solution.py:559
  207.0 6.6 %collective-permute-done.10.refs_1_ = s32[1,104,1152]{2,1,0:T(8,128)S(1)} collective-permute-done((s32[1,104,1152]{2,1,0:T(8,128)}, s32[1,104,1152]{2,1,0:T(8,128)S(1)}, u32[]{:S(2)}, u32[]{:S(2)}) %collective-permute-start.10) | collective-permute-done | bytes 479264 | tf_op jit(solution)/shard_map/ppermute | solution.py:529
  213.7 11.4 %collective-permute-done.11.refs_2_ = s32[1,104,1152]{2,1,0:T(8,128)S(1)} collective-permute-done((s32[1,104,1152]{2,1,0:T(8,128)}, s32[1,104,1152]{2,1,0:T(8,128)S(1)}, u32[]{:S(2)}, u32[]{:S(2)}) %collective-permute-start.11) | collective-permute-done | bytes 479264 | tf_op jit(solution)/shard_map/ppermute | solution.py:529
  226.0 4.0 %gather_parts.3 = s32[4,1,32,1152]{3,2,1,0:T(8,128)} custom-call(s32[2]{0:T(128)} %pad_add_fusion.ctl, s32[1,104,1152]{2,1,0:T(8,128)} %get-tuple-element.46.refs_0_, s32[1,104,1152]{2,1,0:T(8,128)} %copy-done.11, s32[1,104,1152]{2,1,0:T(8,128)} %copy-done.12, s32[1,104,1152]{2,1,0:T(8,128)} %copy-done.13), custom_call_target="tpu_custom_call" | custom-call | flops 28991029248 | bytes 221184 | tf_op jit(solution)/shard_map/gather_parts/pallas_call | solution.py:442
  230.0 5.5 %all-to-all-done.1.got = s32[4,2,32,1152]{3,2,1,0:T(8,128)S(1)} async-done(((s32[4,2,32,1152]{3,2,1,0:T(8,128)}), s32[4,2,32,1152]{3,2,1,0:T(8,128)S(1)}, u32[]{:S(2)}, u32[]{:S(2)}) %all-to-all-start.1) | async-done | bytes 1179680 | tf_op jit(solution)/shard_map/all_to_all | solution.py:559
  235.5 3.5 %all-to-all-start = ((s32[4,1,32,1152]{3,2,1,0:T(8,128)}), s32[4,1,32,1152]{3,2,1,0:T(8,128)S(1)}, u32[]{:S(2)}, u32[]{:S(2)}) async-start(s32[4,1,32,1152]{3,2,1,0:T(8,128)} %gather_parts.3), calls=%async_computation | async-start | bytes 1179648 | tf_op jit(solution)/shard_map/all_to_all | solution.py:559
  239.0 3.6 %compose.2.refs_0_ = f32[4,144,288]{2,1,0:T(8,128)} custom-call(s32[4,2,32,1152]{3,2,1,0:T(8,128)} %copy-done), custom_call_target="tpu_custom_call" | custom-call | flops 14495514624 | bytes 442368 | tf_op jit(solution)/shard_map/compose/pallas_call | solution.py:467
  242.6 11.8 %all-to-all-done.got = s32[4,1,32,1152]{3,2,1,0:T(8,128)S(1)} async-done(((s32[4,1,32,1152]{3,2,1,0:T(8,128)}), s32[4,1,32,1152]{3,2,1,0:T(8,128)S(1)}, u32[]{:S(2)}, u32[]{:S(2)}) %all-to-all-start) | async-done | bytes 589856 | tf_op jit(solution)/shard_map/all_to_all | solution.py:559
  255.2 2.7 %compose.3 = f32[4,144,288]{2,1,0:T(8,128)} custom-call(s32[4,1,32,1152]{3,2,1,0:T(8,128)} %copy-done.1, f32[4,144,288]{2,1,0:T(8,128)} %compose.2.refs_0_), custom_call_target="tpu_custom_call", output_to_operand_aliasing={{}: (1, {})} | custom-call | flops 7247757312 | bytes 221184 | tf_op jit(solution)/shard_map/compose/pallas_call | solution.py:467
  (75 shorter events, 16.2 us)
Async XLA Ops:
  0.0 11.1 %copy-start.4 = (f32[4]{0:T(128)S(1)}, f32[4]{0:T(128)}, u32[]{:S(2)}) copy-start(f32[4]{0:T(128)} %constant.60) | copy-start | bytes 52
  0.0 6.9 %copy-start.14 = (s32[16]{0:T(128)S(1)}, s32[16]{0:T(128)}, u32[]{:S(2)}) copy-start(s32[16]{0:T(128)} %param.7) | copy-start | bytes 196
  0.0 7.0 %copy-start.3 = (f32[2]{0:T(128)S(1)}, f32[2]{0:T(128)}, u32[]{:S(2)}) copy-start(f32[2]{0:T(128)} %param.8) | copy-start | bytes 28
  0.0 10.3 %copy-start.2 = (f32[4,16]{1,0:T(4,128)S(1)}, f32[4,16]{1,0:T(4,128)}, u32[]{:S(2)}) copy-start(f32[4,16]{1,0:T(4,128)} %param.6) | copy-start | bytes 772
  1.6 16.5 %collective-permute-start.1 = (bf16[8,48,1152]{2,1,0:T(8,128)(2,1)S(1)}, bf16[8,48,1152]{2,1,0:T(8,128)(2,1)S(1)}, u32[]{:S(2)}, u32[]{:S(2)}) collective-permute-start(bf16[8,48,1152]{2,1,0:T(8,128)(2,1)S(1)} %get-tuple-element.53), channel_id=1, source_target_pairs={{1,0},{2,1},{3,2},{4,3},{5,4},{6,5},{7,6},{8,7},{9,8},{10,9},{11,1... | collective-permute-start | bytes 2654216 | tf_op jit(solution)/shard_map/ppermute | solution.py:525
  2.9 15.2 %collective-permute-start = (bf16[8,48,1152]{2,1,0:T(8,128)(2,1)S(1)}, bf16[8,48,1152]{2,1,0:T(8,128)(2,1)}, u32[]{:S(2)}, u32[]{:S(2)}) collective-permute-start(bf16[8,48,1152]{2,1,0:T(8,128)(2,1)S(1)} %get-tuple-element.54), channel_id=1, source_target_pairs={{0,1},{1,2},{2,3},{3,4},{4,5},{5,6},{6,7},{7,8},{8,9},{9,10},{10,1... | collective-permute-start | bytes 2654216 | tf_op jit(solution)/shard_map/ppermute | solution.py:525
  18.1 14.2 %copy-start.10 = (bf16[8,48,1152]{2,1,0:T(8,128)(2,1)}, bf16[8,48,1152]{2,1,0:T(8,128)(2,1)S(1)}, u32[]{:S(2)}) copy-start(bf16[8,48,1152]{2,1,0:T(8,128)(2,1)S(1)} %collective-permute-done.1.after) | copy-start | bytes 2654212
  18.1 58.7 %collective-permute-start.2 = (bf16[8,96,1152]{2,1,0:T(8,128)(2,1)S(1)}, bf16[8,96,1152]{2,1,0:T(8,128)(2,1)}, u32[]{:S(2)}, u32[]{:S(2)}) collective-permute-start(bf16[8,96,1152]{2,1,0:T(8,128)(2,1)S(1)} %get-tuple-element.29), channel_id=1, source_target_pairs={{0,1},{1,2},{2,3},{3,4},{4,5},{5,6},{6,7},{7,8},{8,9},{9,10},{10,1... | collective-permute-start | bytes 5308424 | tf_op jit(solution)/shard_map/ppermute | solution.py:525
  31.0 45.8 %collective-permute-start.3 = (bf16[8,96,1152]{2,1,0:T(8,128)(2,1)S(1)}, bf16[8,96,1152]{2,1,0:T(8,128)(2,1)}, u32[]{:S(2)}, u32[]{:S(2)}) collective-permute-start(bf16[8,96,1152]{2,1,0:T(8,128)(2,1)S(1)} %get-tuple-element.30), channel_id=1, source_target_pairs={{1,0},{2,1},{3,2},{4,3},{5,4},{6,5},{7,6},{8,7},{9,8},{10,9},{11,1... | collective-permute-start | bytes 5308424 | tf_op jit(solution)/shard_map/ppermute | solution.py:525
  74.8 45.1 %collective-permute-start.4 = (f32[4,4,48,1152]{3,2,1,0:T(8,128)}, f32[4,4,48,1152]{3,2,1,0:T(8,128)S(1)}, u32[]{:S(2)}, u32[]{:S(2)}) collective-permute-start(f32[4,4,48,1152]{3,2,1,0:T(8,128)} %get-tuple-element.27), channel_id=1, source_target_pairs={{0,1},{1,0},{2,3},{3,2},{4,5},{5,4},{6,7},{7,6},{8,9},{9,8},{10,11... | collective-permute-start | bytes 10616840 | tf_op jit(solution)/shard_map/ppermute | solution.py:529
  119.3 6.6 %collective-permute-start.5 = (f32[4,4,48,1152]{3,2,1,0:T(8,128)}, f32[4,4,48,1152]{3,2,1,0:T(8,128)}, u32[]{:S(2)}, u32[]{:S(2)}) collective-permute-start(f32[4,4,48,1152]{3,2,1,0:T(8,128)} %get-tuple-element.31), channel_id=1, source_target_pairs={{0,1},{1,0},{2,3},{3,2},{4,5},{5,4},{6,7},{7,6},{8,9},{9,8},{10,11... | collective-permute-start | bytes 10616840 | tf_op jit(solution)/shard_map/ppermute | solution.py:529
  120.0 5.9 %copy-start.5 = (f32[4,4,48,1152]{3,2,1,0:T(8,128)}, f32[4,4,48,1152]{3,2,1,0:T(8,128)S(1)}, u32[]{:S(2)}) copy-start(f32[4,4,48,1152]{3,2,1,0:T(8,128)S(1)} %collective-permute-done.4.refs_1_) | copy-start | bytes 10616836
  138.7 46.0 %collective-permute-start.8 = (s32[2,104,1152]{2,1,0:T(8,128)}, s32[2,104,1152]{2,1,0:T(8,128)S(1)}, u32[]{:S(2)}, u32[]{:S(2)}) collective-permute-start(s32[2,104,1152]{2,1,0:T(8,128)} %get-tuple-element.35), channel_id=1, source_target_pairs={{0,6},{1,7},{2,4},{3,5},{4,2},{5,3},{6,0},{7,1},{8,14},{9,15},{10,... | collective-permute-start | bytes 2875400 | tf_op jit(solution)/shard_map/ppermute | solution.py:529
  139.5 45.1 %collective-permute-start.6 = (s32[2,104,1152]{2,1,0:T(8,128)}, s32[2,104,1152]{2,1,0:T(8,128)S(1)}, u32[]{:S(2)}, u32[]{:S(2)}) collective-permute-start(s32[2,104,1152]{2,1,0:T(8,128)} %get-tuple-element.39), channel_id=1, source_target_pairs={{0,2},{1,3},{2,0},{3,1},{4,6},{5,7},{6,4},{7,5},{8,10},{9,11},{10,... | collective-permute-start | bytes 2875400 | tf_op jit(solution)/shard_map/ppermute | solution.py:529
  141.0 43.7 %collective-permute-start.7 = (s32[2,104,1152]{2,1,0:T(8,128)}, s32[2,104,1152]{2,1,0:T(8,128)S(1)}, u32[]{:S(2)}, u32[]{:S(2)}) collective-permute-start(s32[2,104,1152]{2,1,0:T(8,128)} %get-tuple-element.40), channel_id=1, source_target_pairs={{0,4},{1,5},{2,6},{3,7},{4,0},{5,1},{6,2},{7,3},{8,12},{9,13},{10,... | collective-permute-start | bytes 2875400 | tf_op jit(solution)/shard_map/ppermute | solution.py:529
  184.7 6.8 %collective-permute-start.9 = (f32[4,4,48,1152]{3,2,1,0:T(8,128)}, f32[4,4,48,1152]{3,2,1,0:T(8,128)S(1)}, u32[]{:S(2)}, u32[]{:S(2)}) collective-permute-start(f32[4,4,48,1152]{3,2,1,0:T(8,128)} %get-tuple-element.37), channel_id=1, source_target_pairs={{0,1},{1,0},{2,3},{3,2},{4,5},{5,4},{6,7},{7,6},{8,9},{9,8},{10,11... | collective-permute-start | bytes 10616840 | tf_op jit(solution)/shard_map/ppermute | solution.py:529
  191.5 1.8 copy-start.6
  199.7 14.0 %collective-permute-start.10 = (s32[1,104,1152]{2,1,0:T(8,128)}, s32[1,104,1152]{2,1,0:T(8,128)S(1)}, u32[]{:S(2)}, u32[]{:S(2)}) collective-permute-start(s32[1,104,1152]{2,1,0:T(8,128)} %get-tuple-element.47), channel_id=1, source_target_pairs={{0,2},{1,3},{2,0},{3,1},{4,6},{5,7},{6,4},{7,5},{8,10},{9,11},{10,... | collective-permute-start | bytes 1437704 | tf_op jit(solution)/shard_map/ppermute | solution.py:529
  201.5 23.6 %collective-permute-start.11 = (s32[1,104,1152]{2,1,0:T(8,128)}, s32[1,104,1152]{2,1,0:T(8,128)S(1)}, u32[]{:S(2)}, u32[]{:S(2)}) collective-permute-start(s32[1,104,1152]{2,1,0:T(8,128)} %get-tuple-element.48), channel_id=1, source_target_pairs={{0,4},{1,5},{2,6},{3,7},{4,0},{5,1},{6,2},{7,3},{8,12},{9,13},{10,... | collective-permute-start | bytes 1437704 | tf_op jit(solution)/shard_map/ppermute | solution.py:529
  201.5 23.6 %collective-permute-start.12 = (s32[1,104,1152]{2,1,0:T(8,128)}, s32[1,104,1152]{2,1,0:T(8,128)S(1)}, u32[]{:S(2)}, u32[]{:S(2)}) collective-permute-start(s32[1,104,1152]{2,1,0:T(8,128)} %get-tuple-element.44), channel_id=1, source_target_pairs={{0,6},{1,7},{2,4},{3,5},{4,2},{5,3},{6,0},{7,1},{8,14},{9,15},{10,... | collective-permute-start | bytes 1437704 | tf_op jit(solution)/shard_map/ppermute | solution.py:529
  203.2 32.3 %all-to-all-start.1 = ((s32[4,2,32,1152]{3,2,1,0:T(8,128)}), s32[4,2,32,1152]{3,2,1,0:T(8,128)S(1)}, u32[]{:S(2)}, u32[]{:S(2)}) async-start(s32[4,2,32,1152]{3,2,1,0:T(8,128)} %gather_parts.2), calls=%async_computation.1 | async-start | bytes 2359296 | tf_op jit(solution)/shard_map/all_to_all | solution.py:559
  213.7 11.4 %copy-start.11 = (s32[1,104,1152]{2,1,0:T(8,128)}, s32[1,104,1152]{2,1,0:T(8,128)S(1)}, u32[]{:S(2)}) copy-start(s32[1,104,1152]{2,1,0:T(8,128)S(1)} %collective-permute-done.10.refs_1_) | copy-start | bytes 1437700
  235.5 3.5 %copy-start = (s32[4,2,32,1152]{3,2,1,0:T(8,128)}, s32[4,2,32,1152]{3,2,1,0:T(8,128)S(1)}, u32[]{:S(2)}) copy-start(s32[4,2,32,1152]{3,2,1,0:T(8,128)S(1)} %all-to-all-done.1.got) | copy-start | bytes 3538948
  235.5 18.8 %all-to-all-start = ((s32[4,1,32,1152]{3,2,1,0:T(8,128)}), s32[4,1,32,1152]{3,2,1,0:T(8,128)S(1)}, u32[]{:S(2)}, u32[]{:S(2)}) async-start(s32[4,1,32,1152]{3,2,1,0:T(8,128)} %gather_parts.3), calls=%async_computation | async-start | bytes 1179648 | tf_op jit(solution)/shard_map/all_to_all | solution.py:559
  (6 other events, 6.4 us)

commit v10 on v8

--- a/solution.py
+++ b/solution.py
@@ -10,7 +10,7 @@
 
 LANES = 128
 CODES = 32700.0
-ON_MATRIX = 6
+ON_MATRIX = 4
 VMEM_LIMIT = 56 * 1024 * 1024
 
 
@@ -124,8 +124,8 @@
 
     lx, ly, lz = light[0], light[1], light[2]
     step = 16
-    bins = table.shape[1] // step
-    rows_found = table.shape[0] // (2 * step)
+    bins = table.shape[1] // (2 * step)
+    rows_found = table.shape[0] // step
     tilts_of = [jnp.broadcast_to(slope[k:k + 1, :], (step, LANES)) for k in range(rows_found - 4, 4)]
     row_kind = jnp.where(start == 0, 1, 0) + jnp.where(start + unit == total, 2, 0)
 
@@ -172,15 +172,10 @@
                     shades.append(0.045 + facing * lax.rsqrt(jnp.maximum(square, 4.0)))
                     low, here = here, high
                 pick = jnp.concatenate(picks, axis=1) if len(picks) > 1 else picks[0]
-                found = jnp.dot(table[...], pick, preferred_element_type=jnp.float32)
+                found = jnp.dot(table[...], jnp.concatenate([pick, pick], axis=0), preferred_element_type=jnp.float32)
                 for m, layer in enumerate(pair):
                     lanes = slice(m * LANES, (m + 1) * LANES)
-                    half_rows = rows_found * step
-                    looked = [
-                        found[k * step:(k + 1) * step, lanes]
-                        + found[half_rows + k * step:half_rows + (k + 1) * step, lanes]
-                        for k in range(rows_found)
-                    ] + tilts[m]
+                    looked = [found[k * step:(k + 1) * step, lanes] for k in range(rows_found)] + tilts[m]
                     tf = [looked[k] + parts[m] * looked[4 + k] for k in range(4)]
                     if layer == 0:
                         colour = [tf[k] * shades[m] for k in range(3)]
@@ -479,9 +474,9 @@
     table = jnp.concatenate([table, slope[:ON_MATRIX - 4]], axis=0)
     slope = jnp.pad(slope, ((0, 4), (0, LANES - bins)))
     coarse = lax.reduce_precision(table, exponent_bits=8, mantissa_bits=7)
-    table = jnp.concatenate([coarse, table - coarse], axis=0)
+    table = jnp.concatenate([coarse, table - coarse], axis=1)
     spread = jnp.eye(16, dtype=jnp.float32)
-    table = (table[:, None, :, None] * spread[None, :, None, :]).reshape(2 * ON_MATRIX * 16, bins * 16)
+    table = (table[:, None, :, None] * spread[None, :, None, :]).reshape(ON_MATRIX * 16, 2 * bins * 16)
     table = table.astype(jnp.bfloat16)
     azimuth, polar = light_angles[0], light_angles[1]
     light = 0.105 * jnp.stack(

time: 260 us -> 272 us (1.046)
  Pallas kernels: 163 us -> 176 us
    pallas_call x3, Pallas kernels: 128 us -> 141 us  [render(): pl.pallas_call(kernel, grid_spec=pltpu.PrefetchScalarGridSpec(num_scalar_...]
  transfers between devices with their start and end apart: 15 -> 15, of which waited for: 5 -> 5; matrix products, arithmetic and copies ran while one was open for 4% -> 3% of each run, Pallas kernels for 55% -> 57%
where the time goes in v10:
time: 272 us; the launch traced here: 271 us
  Pallas kernels  176 us (65%)
  waiting for transfers between devices  41.1 us (15%)
  starting transfers between devices  35.5 us (13%)
  local copies, waits for them, and re-layouts  12.3 us (5%)
  other arithmetic  3.77 us (1%)
  between operations  3 us (1%)
    pallas_call x3, Pallas kernels, render(): pl.pallas_call(kernel, grid_spec=pltpu.PrefetchScalarGridSpec(num_scalar_...  141 us
    ppermute x9, waiting for transfers between devices, exchange(): return lax.ppermute(send, 'tile', [(i, i ^ distance) for i in range(tiles)])  23.9 us
    pallas_call x2, Pallas kernels, merge(): pl.pallas_call(functools.partial(merge_kernel, members=members, places=pl...  19.3 us
    ppermute x4, starting transfers between devices, per_device(): pair = (lax.ppermute(ends[0], both, up), lax.ppermute(ends[1], both, down))  19.1 us
    all_to_all x2, waiting for transfers between devices, block_group(): lax.all_to_all(send, 'depth', split_axis=0, concat_axis=0, tiled=True)  17.2 us
    pallas_call x2, Pallas kernels, gather_parts(): pl.pallas_call(functools.partial(gather_kernel, unit=unit, blocks=blocks)...  9.2 us
    ppermute x9, starting transfers between devices, exchange(): return lax.ppermute(send, 'tile', [(i, i ^ distance) for i in range(tiles)])  9.04 us
    all_to_all x2, starting transfers between devices, block_group(): lax.all_to_all(send, 'depth', split_axis=0, concat_axis=0, tiled=True)  7.33 us
  transfers between devices with their start and end apart: 15, of which 5 were waited for; matrix products, arithmetic and copies ran while one was open for 3% of the time, Pallas kernels for 57%

profile of v10, /device:TPU:0, one launch (start us, length us, event | category | flops | bytes accessed | tf_op | source)
XLA Modules:
  0.0 271.3 jit_solution(16434416103998531231)
XLA Ops:
  0.0 1.6 slice_bitcast_fusion.2
  2.9 4.0 %collective-permute-start = (bf16[8,48,1152]{2,1,0:T(8,128)(2,1)S(1)}, bf16[8,48,1152]{2,1,0:T(8,128)(2,1)}, u32[]{:S(2)}, u32[]{:S(2)}) collective-permute-start(bf16[8,48,1152]{2,1,0:T(8,128)(2,1)S(1)} %get-tuple-element.54), channel_id=1, source_target_pairs={{0,1},{1,2},{2,3},{3,4},{4,5},{5,6},{6,7},{7,8},{8,9},{9,10},{10,1... | collective-permute-start | bytes 2654216 | tf_op jit(solution)/shard_map/ppermute | solution.py:506
  16.2 2.3 slice_bitcast_fusion
  18.5 12.5 %collective-permute-start.2 = (bf16[8,96,1152]{2,1,0:T(8,128)(2,1)S(1)}, bf16[8,96,1152]{2,1,0:T(8,128)(2,1)}, u32[]{:S(2)}, u32[]{:S(2)}) collective-permute-start(bf16[8,96,1152]{2,1,0:T(8,128)(2,1)S(1)} %get-tuple-element.29), channel_id=1, source_target_pairs={{0,1},{1,2},{2,3},{3,4},{4,5},{5,6},{6,7},{7,8},{8,9},{9,10},{10,1... | collective-permute-start | bytes 5308424 | tf_op jit(solution)/shard_map/ppermute | solution.py:506
  32.3 47.0 %render.3 = (f32[4,4,48,1152]{3,2,1,0:T(8,128)}, f32[4,4,48,1152]{3,2,1,0:T(8,128)}) custom-call(s32[2]{0:T(128)} %pad_add_fusion.1.ctl, f32[3]{0:T(128)} %maximum_multiply_fusion.light, bf16[64,512]{1,0:T(8,128)(2,1)} %convert_element_type.95.table, f32[8,128]{1,0:T(8,128)} %pad.23.slope, bf16[4,48,80]{2,1,0:T(8,128)(2,1)} %pad_maximum_fusion.1.row_bands, ...), custom_call_target="tpu_custom_call" | custom-call | flops 43486543872 | bytes 15925248 | tf_op jit(solution)/shard_map/render/pallas_call | solution.py:359
  79.4 2.0 collective-permute-start.4
  81.4 46.9 %render.4 = (f32[4,4,48,1152]{3,2,1,0:T(8,128)}, f32[4,4,48,1152]{3,2,1,0:T(8,128)}) custom-call(s32[2]{0:T(128)} %pad_add_fusion.1.ctl, f32[3]{0:T(128)} %maximum_multiply_fusion.light, bf16[64,512]{1,0:T(8,128)(2,1)} %convert_element_type.95.table, f32[8,128]{1,0:T(8,128)} %pad.23.slope, bf16[4,48,80]{2,1,0:T(8,128)(2,1)} %pad_maximum_fusion.1.row_bands, ...), custom_call_target="tpu_custom_call" | custom-call | flops 43486543872 | bytes 15925248 | tf_op jit(solution)/shard_map/render/pallas_call | solution.py:359
  129.0 5.9 %collective-permute-done.5.refs_3_ = f32[4,4,48,1152]{3,2,1,0:T(8,128)} collective-permute-done((f32[4,4,48,1152]{3,2,1,0:T(8,128)}, f32[4,4,48,1152]{3,2,1,0:T(8,128)}, u32[]{:S(2)}, u32[]{:S(2)}) %collective-permute-start.5) | collective-permute-done | bytes 3538976 | tf_op jit(solution)/shard_map/ppermute | solution.py:510
  134.9 12.9 %merge.2 = (s32[2,104,1152]{2,1,0:T(8,128)}, s32[2,104,1152]{2,1,0:T(8,128)}, s32[2,104,1152]{2,1,0:T(8,128)}, s32[2,104,1152]{2,1,0:T(8,128)}) custom-call(s32[2]{0:T(128)} %pad_add_fusion.ctl, f32[4,4,48,1152]{3,2,1,0:T(8,128)} %get-tuple-element.33.refs_0_, f32[4,4,48,1152]{3,2,1,0:T(8,128)} %copy-done.5, f32[4,4,48,1152]{3,2,1,0:T(8,128)} %get-tuple-element.34.refs_2_, ...), custom_call_target="tpu_custom_call" | custom-call | flops 57982058496 | bytes 1769472 | tf_op jit(solution)/shard_map/merge/pallas_call | solution.py:403
  151.2 46.9 %render.5 = (f32[4,4,48,1152]{3,2,1,0:T(8,128)}, f32[4,4,48,1152]{3,2,1,0:T(8,128)}) custom-call(s32[2]{0:T(128)} %pad_add_fusion.1.ctl, f32[3]{0:T(128)} %maximum_multiply_fusion.light, bf16[64,512]{1,0:T(8,128)(2,1)} %convert_element_type.95.table, f32[8,128]{1,0:T(8,128)} %pad.23.slope, bf16[4,48,80]{2,1,0:T(8,128)(2,1)} %pad_maximum_fusion.1.row_bands, ...), custom_call_target="tpu_custom_call" | custom-call | flops 43486543872 | bytes 15925248 | tf_op jit(solution)/shard_map/render/pallas_call | solution.py:359
  199.7 5.2 %gather_parts.2 = s32[4,2,32,1152]{3,2,1,0:T(8,128)} custom-call(s32[2]{0:T(128)} %pad_add_fusion.ctl, s32[2,104,1152]{2,1,0:T(8,128)} %get-tuple-element.38.refs_0_, s32[2,104,1152]{2,1,0:T(8,128)} %copy-done.8, s32[2,104,1152]{2,1,0:T(8,128)} %copy-done.9, s32[2,104,1152]{2,1,0:T(8,128)} %copy-done.7), custom_call_target="tpu_custom_call" | custom-call | flops 57982058496 | bytes 442368 | tf_op jit(solution)/shard_map/gather_parts/pallas_call | solution.py:423
  204.9 1.8 copy-done.6
  206.7 6.4 %merge.3 = (s32[1,104,1152]{2,1,0:T(8,128)}, s32[1,104,1152]{2,1,0:T(8,128)}, s32[1,104,1152]{2,1,0:T(8,128)}, s32[1,104,1152]{2,1,0:T(8,128)}) custom-call(s32[2]{0:T(128)} %pad_add_fusion.ctl, f32[4,4,48,1152]{3,2,1,0:T(8,128)} %get-tuple-element.43.refs_0_, f32[4,4,48,1152]{3,2,1,0:T(8,128)} %copy-done.6), custom_call_target="tpu_custom_call" | custom-call | flops 28991029248 | bytes 884736 | tf_op jit(solution)/shard_map/merge/pallas_call | solution.py:403
  213.2 1.8 collective-permute-start.10
  214.9 1.7 collective-permute-start.12
  216.6 3.9 %all-to-all-start.1 = ((s32[4,2,32,1152]{3,2,1,0:T(8,128)}), s32[4,2,32,1152]{3,2,1,0:T(8,128)S(1)}, u32[]{:S(2)}, u32[]{:S(2)}) async-start(s32[4,2,32,1152]{3,2,1,0:T(8,128)} %gather_parts.2), calls=%async_computation.1 | async-start | bytes 2359296 | tf_op jit(solution)/shard_map/all_to_all | solution.py:540
  220.5 6.6 %collective-permute-done.10.refs_1_ = s32[1,104,1152]{2,1,0:T(8,128)S(1)} collective-permute-done((s32[1,104,1152]{2,1,0:T(8,128)}, s32[1,104,1152]{2,1,0:T(8,128)S(1)}, u32[]{:S(2)}, u32[]{:S(2)}) %collective-permute-start.10) | collective-permute-done | bytes 479264 | tf_op jit(solution)/shard_map/ppermute | solution.py:510
  227.1 11.3 %collective-permute-done.11.refs_2_ = s32[1,104,1152]{2,1,0:T(8,128)S(1)} collective-permute-done((s32[1,104,1152]{2,1,0:T(8,128)}, s32[1,104,1152]{2,1,0:T(8,128)S(1)}, u32[]{:S(2)}, u32[]{:S(2)}) %collective-permute-start.11) | collective-permute-done | bytes 479264 | tf_op jit(solution)/shard_map/ppermute | solution.py:510
  239.4 4.0 %gather_parts.3 = s32[4,1,32,1152]{3,2,1,0:T(8,128)} custom-call(s32[2]{0:T(128)} %pad_add_fusion.ctl, s32[1,104,1152]{2,1,0:T(8,128)} %get-tuple-element.46.refs_0_, s32[1,104,1152]{2,1,0:T(8,128)} %copy-done.11, s32[1,104,1152]{2,1,0:T(8,128)} %copy-done.12, s32[1,104,1152]{2,1,0:T(8,128)} %copy-done.13), custom_call_target="tpu_custom_call" | custom-call | flops 28991029248 | bytes 221184 | tf_op jit(solution)/shard_map/gather_parts/pallas_call | solution.py:423
  243.4 5.5 %all-to-all-done.1.got = s32[4,2,32,1152]{3,2,1,0:T(8,128)S(1)} async-done(((s32[4,2,32,1152]{3,2,1,0:T(8,128)}), s32[4,2,32,1152]{3,2,1,0:T(8,128)S(1)}, u32[]{:S(2)}, u32[]{:S(2)}) %all-to-all-start.1) | async-done | bytes 1179680 | tf_op jit(solution)/shard_map/all_to_all | solution.py:540
  248.9 3.5 %all-to-all-start = ((s32[4,1,32,1152]{3,2,1,0:T(8,128)}), s32[4,1,32,1152]{3,2,1,0:T(8,128)S(1)}, u32[]{:S(2)}, u32[]{:S(2)}) async-start(s32[4,1,32,1152]{3,2,1,0:T(8,128)} %gather_parts.3), calls=%async_computation | async-start | bytes 1179648 | tf_op jit(solution)/shard_map/all_to_all | solution.py:540
  252.4 3.6 %compose.2.refs_0_ = f32[4,144,288]{2,1,0:T(8,128)} custom-call(s32[4,2,32,1152]{3,2,1,0:T(8,128)} %copy-done), custom_call_target="tpu_custom_call" | custom-call | flops 14495514624 | bytes 442368 | tf_op jit(solution)/shard_map/compose/pallas_call | solution.py:448
  256.0 11.8 %all-to-all-done.got = s32[4,1,32,1152]{3,2,1,0:T(8,128)S(1)} async-done(((s32[4,1,32,1152]{3,2,1,0:T(8,128)}), s32[4,1,32,1152]{3,2,1,0:T(8,128)S(1)}, u32[]{:S(2)}, u32[]{:S(2)}) %all-to-all-start) | async-done | bytes 589856 | tf_op jit(solution)/shard_map/all_to_all | solution.py:540
  268.6 2.7 compose.3
  (75 shorter events, 16.5 us)
Async XLA Ops:
  0.0 11.1 %copy-start.4 = (f32[4]{0:T(128)S(1)}, f32[4]{0:T(128)}, u32[]{:S(2)}) copy-start(f32[4]{0:T(128)} %constant.60) | copy-start | bytes 52
  0.0 6.9 %copy-start.14 = (s32[16]{0:T(128)S(1)}, s32[16]{0:T(128)}, u32[]{:S(2)}) copy-start(s32[16]{0:T(128)} %param.7) | copy-start | bytes 196
  0.0 7.0 %copy-start.3 = (f32[2]{0:T(128)S(1)}, f32[2]{0:T(128)}, u32[]{:S(2)}) copy-start(f32[2]{0:T(128)} %param.8) | copy-start | bytes 28
  0.0 10.3 %copy-start.2 = (f32[4,16]{1,0:T(4,128)S(1)}, f32[4,16]{1,0:T(4,128)}, u32[]{:S(2)}) copy-start(f32[4,16]{1,0:T(4,128)} %param.6) | copy-start | bytes 772
  1.6 16.8 %collective-permute-start.1 = (bf16[8,48,1152]{2,1,0:T(8,128)(2,1)S(1)}, bf16[8,48,1152]{2,1,0:T(8,128)(2,1)S(1)}, u32[]{:S(2)}, u32[]{:S(2)}) collective-permute-start(bf16[8,48,1152]{2,1,0:T(8,128)(2,1)S(1)} %get-tuple-element.53), channel_id=1, source_target_pairs={{1,0},{2,1},{3,2},{4,3},{5,4},{6,5},{7,6},{8,7},{9,8},{10,9},{11,1... | collective-permute-start | bytes 2654216 | tf_op jit(solution)/shard_map/ppermute | solution.py:506
  2.9 15.5 %collective-permute-start = (bf16[8,48,1152]{2,1,0:T(8,128)(2,1)S(1)}, bf16[8,48,1152]{2,1,0:T(8,128)(2,1)}, u32[]{:S(2)}, u32[]{:S(2)}) collective-permute-start(bf16[8,48,1152]{2,1,0:T(8,128)(2,1)S(1)} %get-tuple-element.54), channel_id=1, source_target_pairs={{0,1},{1,2},{2,3},{3,4},{4,5},{5,6},{6,7},{7,8},{8,9},{9,10},{10,1... | collective-permute-start | bytes 2654216 | tf_op jit(solution)/shard_map/ppermute | solution.py:506
  18.5 13.8 %copy-start.10 = (bf16[8,48,1152]{2,1,0:T(8,128)(2,1)}, bf16[8,48,1152]{2,1,0:T(8,128)(2,1)S(1)}, u32[]{:S(2)}) copy-start(bf16[8,48,1152]{2,1,0:T(8,128)(2,1)S(1)} %collective-permute-done.1.after) | copy-start | bytes 2654212
  18.5 62.9 %collective-permute-start.2 = (bf16[8,96,1152]{2,1,0:T(8,128)(2,1)S(1)}, bf16[8,96,1152]{2,1,0:T(8,128)(2,1)}, u32[]{:S(2)}, u32[]{:S(2)}) collective-permute-start(bf16[8,96,1152]{2,1,0:T(8,128)(2,1)S(1)} %get-tuple-element.29), channel_id=1, source_target_pairs={{0,1},{1,2},{2,3},{3,4},{4,5},{5,6},{6,7},{7,8},{8,9},{9,10},{10,1... | collective-permute-start | bytes 5308424 | tf_op jit(solution)/shard_map/ppermute | solution.py:506
  31.0 50.4 %collective-permute-start.3 = (bf16[8,96,1152]{2,1,0:T(8,128)(2,1)S(1)}, bf16[8,96,1152]{2,1,0:T(8,128)(2,1)}, u32[]{:S(2)}, u32[]{:S(2)}) collective-permute-start(bf16[8,96,1152]{2,1,0:T(8,128)(2,1)S(1)} %get-tuple-element.30), channel_id=1, source_target_pairs={{1,0},{2,1},{3,2},{4,3},{5,4},{6,5},{7,6},{8,7},{9,8},{10,9},{11,1... | collective-permute-start | bytes 5308424 | tf_op jit(solution)/shard_map/ppermute | solution.py:506
  79.4 49.6 %collective-permute-start.4 = (f32[4,4,48,1152]{3,2,1,0:T(8,128)}, f32[4,4,48,1152]{3,2,1,0:T(8,128)S(1)}, u32[]{:S(2)}, u32[]{:S(2)}) collective-permute-start(f32[4,4,48,1152]{3,2,1,0:T(8,128)} %get-tuple-element.27), channel_id=1, source_target_pairs={{0,1},{1,0},{2,3},{3,2},{4,5},{5,4},{6,7},{7,6},{8,9},{9,8},{10,11... | collective-permute-start | bytes 10616840 | tf_op jit(solution)/shard_map/ppermute | solution.py:510
  128.3 6.6 %collective-permute-start.5 = (f32[4,4,48,1152]{3,2,1,0:T(8,128)}, f32[4,4,48,1152]{3,2,1,0:T(8,128)}, u32[]{:S(2)}, u32[]{:S(2)}) collective-permute-start(f32[4,4,48,1152]{3,2,1,0:T(8,128)} %get-tuple-element.31), channel_id=1, source_target_pairs={{0,1},{1,0},{2,3},{3,2},{4,5},{5,4},{6,7},{7,6},{8,9},{9,8},{10,11... | collective-permute-start | bytes 10616840 | tf_op jit(solution)/shard_map/ppermute | solution.py:510
  129.0 5.9 %copy-start.5 = (f32[4,4,48,1152]{3,2,1,0:T(8,128)}, f32[4,4,48,1152]{3,2,1,0:T(8,128)S(1)}, u32[]{:S(2)}) copy-start(f32[4,4,48,1152]{3,2,1,0:T(8,128)S(1)} %collective-permute-done.4.refs_1_) | copy-start | bytes 10616836
  147.7 50.4 %collective-permute-start.8 = (s32[2,104,1152]{2,1,0:T(8,128)}, s32[2,104,1152]{2,1,0:T(8,128)S(1)}, u32[]{:S(2)}, u32[]{:S(2)}) collective-permute-start(s32[2,104,1152]{2,1,0:T(8,128)} %get-tuple-element.35), channel_id=1, source_target_pairs={{0,6},{1,7},{2,4},{3,5},{4,2},{5,3},{6,0},{7,1},{8,14},{9,15},{10,... | collective-permute-start | bytes 2875400 | tf_op jit(solution)/shard_map/ppermute | solution.py:510
  148.5 49.6 %collective-permute-start.6 = (s32[2,104,1152]{2,1,0:T(8,128)}, s32[2,104,1152]{2,1,0:T(8,128)S(1)}, u32[]{:S(2)}, u32[]{:S(2)}) collective-permute-start(s32[2,104,1152]{2,1,0:T(8,128)} %get-tuple-element.39), channel_id=1, source_target_pairs={{0,2},{1,3},{2,0},{3,1},{4,6},{5,7},{6,4},{7,5},{8,10},{9,11},{10,... | collective-permute-start | bytes 2875400 | tf_op jit(solution)/shard_map/ppermute | solution.py:510
  150.0 48.1 %collective-permute-start.7 = (s32[2,104,1152]{2,1,0:T(8,128)}, s32[2,104,1152]{2,1,0:T(8,128)S(1)}, u32[]{:S(2)}, u32[]{:S(2)}) collective-permute-start(s32[2,104,1152]{2,1,0:T(8,128)} %get-tuple-element.40), channel_id=1, source_target_pairs={{0,4},{1,5},{2,6},{3,7},{4,0},{5,1},{6,2},{7,3},{8,12},{9,13},{10,... | collective-permute-start | bytes 2875400 | tf_op jit(solution)/shard_map/ppermute | solution.py:510
  198.1 6.8 %collective-permute-start.9 = (f32[4,4,48,1152]{3,2,1,0:T(8,128)}, f32[4,4,48,1152]{3,2,1,0:T(8,128)S(1)}, u32[]{:S(2)}, u32[]{:S(2)}) collective-permute-start(f32[4,4,48,1152]{3,2,1,0:T(8,128)} %get-tuple-element.37), channel_id=1, source_target_pairs={{0,1},{1,0},{2,3},{3,2},{4,5},{5,4},{6,7},{7,6},{8,9},{9,8},{10,11... | collective-permute-start | bytes 10616840 | tf_op jit(solution)/shard_map/ppermute | solution.py:510
  204.9 1.8 copy-start.6
  213.2 14.0 %collective-permute-start.10 = (s32[1,104,1152]{2,1,0:T(8,128)}, s32[1,104,1152]{2,1,0:T(8,128)S(1)}, u32[]{:S(2)}, u32[]{:S(2)}) collective-permute-start(s32[1,104,1152]{2,1,0:T(8,128)} %get-tuple-element.47), channel_id=1, source_target_pairs={{0,2},{1,3},{2,0},{3,1},{4,6},{5,7},{6,4},{7,5},{8,10},{9,11},{10,... | collective-permute-start | bytes 1437704 | tf_op jit(solution)/shard_map/ppermute | solution.py:510
  214.9 23.6 %collective-permute-start.11 = (s32[1,104,1152]{2,1,0:T(8,128)}, s32[1,104,1152]{2,1,0:T(8,128)S(1)}, u32[]{:S(2)}, u32[]{:S(2)}) collective-permute-start(s32[1,104,1152]{2,1,0:T(8,128)} %get-tuple-element.48), channel_id=1, source_target_pairs={{0,4},{1,5},{2,6},{3,7},{4,0},{5,1},{6,2},{7,3},{8,12},{9,13},{10,... | collective-permute-start | bytes 1437704 | tf_op jit(solution)/shard_map/ppermute | solution.py:510
  214.9 23.6 %collective-permute-start.12 = (s32[1,104,1152]{2,1,0:T(8,128)}, s32[1,104,1152]{2,1,0:T(8,128)S(1)}, u32[]{:S(2)}, u32[]{:S(2)}) collective-permute-start(s32[1,104,1152]{2,1,0:T(8,128)} %get-tuple-element.44), channel_id=1, source_target_pairs={{0,6},{1,7},{2,4},{3,5},{4,2},{5,3},{6,0},{7,1},{8,14},{9,15},{10,... | collective-permute-start | bytes 1437704 | tf_op jit(solution)/shard_map/ppermute | solution.py:510
  216.6 32.3 %all-to-all-start.1 = ((s32[4,2,32,1152]{3,2,1,0:T(8,128)}), s32[4,2,32,1152]{3,2,1,0:T(8,128)S(1)}, u32[]{:S(2)}, u32[]{:S(2)}) async-start(s32[4,2,32,1152]{3,2,1,0:T(8,128)} %gather_parts.2), calls=%async_computation.1 | async-start | bytes 2359296 | tf_op jit(solution)/shard_map/all_to_all | solution.py:540
  227.1 11.4 %copy-start.11 = (s32[1,104,1152]{2,1,0:T(8,128)}, s32[1,104,1152]{2,1,0:T(8,128)S(1)}, u32[]{:S(2)}) copy-start(s32[1,104,1152]{2,1,0:T(8,128)S(1)} %collective-permute-done.10.refs_1_) | copy-start | bytes 1437700
  248.9 3.5 %copy-start = (s32[4,2,32,1152]{3,2,1,0:T(8,128)}, s32[4,2,32,1152]{3,2,1,0:T(8,128)S(1)}, u32[]{:S(2)}) copy-start(s32[4,2,32,1152]{3,2,1,0:T(8,128)S(1)} %all-to-all-done.1.got) | copy-start | bytes 3538948
  248.9 18.8 %all-to-all-start = ((s32[4,1,32,1152]{3,2,1,0:T(8,128)}), s32[4,1,32,1152]{3,2,1,0:T(8,128)S(1)}, u32[]{:S(2)}, u32[]{:S(2)}) async-start(s32[4,1,32,1152]{3,2,1,0:T(8,128)} %gather_parts.3), calls=%async_computation | async-start | bytes 1179648 | tf_op jit(solution)/shard_map/all_to_all | solution.py:540
  (6 other events, 6.4 us)

commit v11 on v8

--- a/solution.py
+++ b/solution.py
@@ -10,7 +10,7 @@
 
 LANES = 128
 CODES = 32700.0
-ON_MATRIX = 6
+ON_MATRIX = 4
 VMEM_LIMIT = 56 * 1024 * 1024
 
 
@@ -134,16 +134,17 @@
         cols = pl.ds(at, LANES)
         window = pl.ds(pl.multiple_of(jnp.clip(at - LANES, 0, width - 3 * LANES), LANES), 3 * LANES)
         column_kind = jnp.where(at == 0, 0, jnp.where(at == width - LANES, 2, 1))
+        wide = own(0, layers, slice(0, tall), window).reshape(layers * tall, 3 * LANES)
+        across = jnp.dot(wide, column_bands[column_kind], preferred_element_type=jnp.float32)
+        for layer in range(layers):
+            slopes_z[layer] = across[layer * tall:(layer + 1) * tall]
         for first in range(0, layers, 2):
             count = min(2, layers - first)
             towers = [tower(first + m, cols) for m in range(count)]
             both = jnp.concatenate(towers, axis=1) if count > 1 else towers[0]
             found = jnp.dot(row_bands[row_kind], both, preferred_element_type=jnp.float32)
-            wide = own(first, count, slice(0, tall), window).reshape(count * tall, 3 * LANES)
-            across = jnp.dot(wide, column_bands[column_kind], preferred_element_type=jnp.float32)
             for m in range(count):
                 slopes_y[first + m] = found[:, m * LANES:(m + 1) * LANES]
-                slopes_z[first + m] = across[m * tall:(m + 1) * tall]
 
         for r in range(0, tall, step):
             s = slice(r, r + step)

time: 260 us -> 252 us (0.969)
  Pallas kernels: 163 us -> 155 us
    pallas_call x3, Pallas kernels: 128 us -> 120 us  [render(): pl.pallas_call(kernel, grid_spec=pltpu.PrefetchScalarGridSpec(num_scalar_...]
    unnamed x29 -> x31, local copies, waits for them, and re-layouts: 5.23 us -> 4.93 us
  transfers between devices with their start and end apart: 15 -> 15, of which waited for: 5 -> 7; matrix products, arithmetic and copies ran while one was open for 4% -> 4% of each run, Pallas kernels for 55% -> 53%
where the time goes in v11:
time: 252 us; the launch traced here: 251 us
  Pallas kernels  155 us (62%)
  waiting for transfers between devices  41.5 us (16%)
  starting transfers between devices  36.8 us (15%)
  local copies, waits for them, and re-layouts  11.7 us (5%)
  other arithmetic  3.7 us (1%)
  between operations  2.97 us (1%)
    pallas_call x3, Pallas kernels, render(): pl.pallas_call(kernel, grid_spec=pltpu.PrefetchScalarGridSpec(num_scalar_...  120 us
    ppermute x9, waiting for transfers between devices, exchange(): return lax.ppermute(send, 'tile', [(i, i ^ distance) for i in range(tiles)])  24.1 us
    ppermute x4, starting transfers between devices, per_device(): pair = (lax.ppermute(ends[0], both, up), lax.ppermute(ends[1], both, down))  19.4 us
    pallas_call x2, Pallas kernels, merge(): pl.pallas_call(functools.partial(merge_kernel, members=members, places=pl...  19.3 us
    all_to_all x2, waiting for transfers between devices, block_group(): lax.all_to_all(send, 'depth', split_axis=0, concat_axis=0, tiled=True)  17.4 us
    pallas_call x2, Pallas kernels, gather_parts(): pl.pallas_call(functools.partial(gather_kernel, unit=unit, blocks=blocks)...  9.2 us
    ppermute x9, starting transfers between devices, exchange(): return lax.ppermute(send, 'tile', [(i, i ^ distance) for i in range(tiles)])  9.06 us
    all_to_all x2, starting transfers between devices, block_group(): lax.all_to_all(send, 'depth', split_axis=0, concat_axis=0, tiled=True)  8.29 us
  transfers between devices with their start and end apart: 15, of which 7 were waited for; matrix products, arithmetic and copies ran while one was open for 4% of the time, Pallas kernels for 53%

profile of v11, /device:TPU:0, one launch (start us, length us, event | category | flops | bytes accessed | tf_op | source)
XLA Modules:
  0.0 251.5 jit_solution(2198030097819063022)
XLA Ops:
  0.0 1.6 slice_bitcast_fusion.2
  2.9 4.0 %collective-permute-start = (bf16[8,48,1152]{2,1,0:T(8,128)(2,1)S(1)}, bf16[8,48,1152]{2,1,0:T(8,128)(2,1)}, u32[]{:S(2)}, u32[]{:S(2)}) collective-permute-start(bf16[8,48,1152]{2,1,0:T(8,128)(2,1)S(1)} %get-tuple-element.54), channel_id=1, source_target_pairs={{0,1},{1,2},{2,3},{3,4},{4,5},{5,6},{6,7},{7,8},{8,9},{9,10},{10,1... | collective-permute-start | bytes 2654216 | tf_op jit(solution)/shard_map/ppermute | solution.py:512
  15.8 2.3 slice_bitcast_fusion
  18.1 12.9 %collective-permute-start.2 = (bf16[8,96,1152]{2,1,0:T(8,128)(2,1)S(1)}, bf16[8,96,1152]{2,1,0:T(8,128)(2,1)}, u32[]{:S(2)}, u32[]{:S(2)}) collective-permute-start(bf16[8,96,1152]{2,1,0:T(8,128)(2,1)S(1)} %get-tuple-element.29), channel_id=1, source_target_pairs={{0,1},{1,2},{2,3},{3,4},{4,5},{5,6},{6,7},{7,8},{8,9},{9,10},{10,1... | collective-permute-start | bytes 5308424 | tf_op jit(solution)/shard_map/ppermute | solution.py:512
  32.3 40.0 %render.3 = (f32[4,4,48,1152]{3,2,1,0:T(8,128)}, f32[4,4,48,1152]{3,2,1,0:T(8,128)}) custom-call(s32[2]{0:T(128)} %pad_add_fusion.1.ctl, f32[3]{0:T(128)} %maximum_multiply_fusion.light, bf16[128,256]{1,0:T(8,128)(2,1)} %convert_element_type.95.table, f32[8,128]{1,0:T(8,128)} %pad.23.slope, bf16[4,48,80]{2,1,0:T(8,128)(2,1)} %pad_maximum_fusion.1.row_bands, ...), custom_call_target="tpu_custom_call" | custom-call | flops 43486543872 | bytes 15925248 | tf_op jit(solution)/shard_map/render/pallas_call | solution.py:365
  72.3 2.0 collective-permute-start.4
  74.3 40.0 %render.4 = (f32[4,4,48,1152]{3,2,1,0:T(8,128)}, f32[4,4,48,1152]{3,2,1,0:T(8,128)}) custom-call(s32[2]{0:T(128)} %pad_add_fusion.1.ctl, f32[3]{0:T(128)} %maximum_multiply_fusion.light, bf16[128,256]{1,0:T(8,128)(2,1)} %convert_element_type.95.table, f32[8,128]{1,0:T(8,128)} %pad.23.slope, bf16[4,48,80]{2,1,0:T(8,128)(2,1)} %pad_maximum_fusion.1.row_bands, ...), custom_call_target="tpu_custom_call" | custom-call | flops 43486543872 | bytes 15925248 | tf_op jit(solution)/shard_map/render/pallas_call | solution.py:365
  115.0 5.9 %collective-permute-done.5.refs_3_ = f32[4,4,48,1152]{3,2,1,0:T(8,128)} collective-permute-done((f32[4,4,48,1152]{3,2,1,0:T(8,128)}, f32[4,4,48,1152]{3,2,1,0:T(8,128)}, u32[]{:S(2)}, u32[]{:S(2)}) %collective-permute-start.5) | collective-permute-done | bytes 3538976 | tf_op jit(solution)/shard_map/ppermute | solution.py:516
  120.9 12.9 %merge.2 = (s32[2,104,1152]{2,1,0:T(8,128)}, s32[2,104,1152]{2,1,0:T(8,128)}, s32[2,104,1152]{2,1,0:T(8,128)}, s32[2,104,1152]{2,1,0:T(8,128)}) custom-call(s32[2]{0:T(128)} %pad_add_fusion.ctl, f32[4,4,48,1152]{3,2,1,0:T(8,128)} %get-tuple-element.33.refs_0_, f32[4,4,48,1152]{3,2,1,0:T(8,128)} %copy-done.5, f32[4,4,48,1152]{3,2,1,0:T(8,128)} %get-tuple-element.34.refs_2_, ...), custom_call_target="tpu_custom_call" | custom-call | flops 57982058496 | bytes 1769472 | tf_op jit(solution)/shard_map/merge/pallas_call | solution.py:409
  134.6 1.5 collective-permute-start.6
  137.3 40.0 %render.5 = (f32[4,4,48,1152]{3,2,1,0:T(8,128)}, f32[4,4,48,1152]{3,2,1,0:T(8,128)}) custom-call(s32[2]{0:T(128)} %pad_add_fusion.1.ctl, f32[3]{0:T(128)} %maximum_multiply_fusion.light, bf16[128,256]{1,0:T(8,128)(2,1)} %convert_element_type.95.table, f32[8,128]{1,0:T(8,128)} %pad.23.slope, bf16[4,48,80]{2,1,0:T(8,128)(2,1)} %pad_maximum_fusion.1.row_bands, ...), custom_call_target="tpu_custom_call" | custom-call | flops 43486543872 | bytes 15925248 | tf_op jit(solution)/shard_map/render/pallas_call | solution.py:365
  180.0 5.2 %gather_parts.2 = s32[4,2,32,1152]{3,2,1,0:T(8,128)} custom-call(s32[2]{0:T(128)} %pad_add_fusion.ctl, s32[2,104,1152]{2,1,0:T(8,128)} %get-tuple-element.38.refs_0_, s32[2,104,1152]{2,1,0:T(8,128)} %copy-done.8, s32[2,104,1152]{2,1,0:T(8,128)} %copy-done.9, s32[2,104,1152]{2,1,0:T(8,128)} %copy-done.7), custom_call_target="tpu_custom_call" | custom-call | flops 57982058496 | bytes 442368 | tf_op jit(solution)/shard_map/gather_parts/pallas_call | solution.py:429
  185.1 1.8 copy-done.6
  186.9 6.4 %merge.3 = (s32[1,104,1152]{2,1,0:T(8,128)}, s32[1,104,1152]{2,1,0:T(8,128)}, s32[1,104,1152]{2,1,0:T(8,128)}, s32[1,104,1152]{2,1,0:T(8,128)}) custom-call(s32[2]{0:T(128)} %pad_add_fusion.ctl, f32[4,4,48,1152]{3,2,1,0:T(8,128)} %get-tuple-element.43.refs_0_, f32[4,4,48,1152]{3,2,1,0:T(8,128)} %copy-done.6), custom_call_target="tpu_custom_call" | custom-call | flops 28991029248 | bytes 884736 | tf_op jit(solution)/shard_map/merge/pallas_call | solution.py:409
  193.4 2.0 collective-permute-start.10
  196.9 4.8 %all-to-all-start.1 = ((s32[4,2,32,1152]{3,2,1,0:T(8,128)}), s32[4,2,32,1152]{3,2,1,0:T(8,128)S(1)}, u32[]{:S(2)}, u32[]{:S(2)}) async-start(s32[4,2,32,1152]{3,2,1,0:T(8,128)} %gather_parts.2), calls=%async_computation.1 | async-start | bytes 2359296 | tf_op jit(solution)/shard_map/all_to_all | solution.py:546
  201.7 5.7 %collective-permute-done.10.refs_1_ = s32[1,104,1152]{2,1,0:T(8,128)S(1)} collective-permute-done((s32[1,104,1152]{2,1,0:T(8,128)}, s32[1,104,1152]{2,1,0:T(8,128)S(1)}, u32[]{:S(2)}, u32[]{:S(2)}) %collective-permute-start.10) | collective-permute-done | bytes 479264 | tf_op jit(solution)/shard_map/ppermute | solution.py:516
  207.4 11.1 %collective-permute-done.11.refs_2_ = s32[1,104,1152]{2,1,0:T(8,128)S(1)} collective-permute-done((s32[1,104,1152]{2,1,0:T(8,128)}, s32[1,104,1152]{2,1,0:T(8,128)S(1)}, u32[]{:S(2)}, u32[]{:S(2)}) %collective-permute-start.11) | collective-permute-done | bytes 479264 | tf_op jit(solution)/shard_map/ppermute | solution.py:516
  219.4 4.0 %gather_parts.3 = s32[4,1,32,1152]{3,2,1,0:T(8,128)} custom-call(s32[2]{0:T(128)} %pad_add_fusion.ctl, s32[1,104,1152]{2,1,0:T(8,128)} %get-tuple-element.46.refs_0_, s32[1,104,1152]{2,1,0:T(8,128)} %copy-done.11, s32[1,104,1152]{2,1,0:T(8,128)} %copy-done.12, s32[1,104,1152]{2,1,0:T(8,128)} %copy-done.13), custom_call_target="tpu_custom_call" | custom-call | flops 28991029248 | bytes 221184 | tf_op jit(solution)/shard_map/gather_parts/pallas_call | solution.py:429
  223.4 5.7 %all-to-all-done.1.got = s32[4,2,32,1152]{3,2,1,0:T(8,128)S(1)} async-done(((s32[4,2,32,1152]{3,2,1,0:T(8,128)}), s32[4,2,32,1152]{3,2,1,0:T(8,128)S(1)}, u32[]{:S(2)}, u32[]{:S(2)}) %all-to-all-start.1) | async-done | bytes 1179680 | tf_op jit(solution)/shard_map/all_to_all | solution.py:546
  229.1 3.5 %all-to-all-start = ((s32[4,1,32,1152]{3,2,1,0:T(8,128)}), s32[4,1,32,1152]{3,2,1,0:T(8,128)S(1)}, u32[]{:S(2)}, u32[]{:S(2)}) async-start(s32[4,1,32,1152]{3,2,1,0:T(8,128)} %gather_parts.3), calls=%async_computation | async-start | bytes 1179648 | tf_op jit(solution)/shard_map/all_to_all | solution.py:546
  232.6 3.6 %compose.2.refs_0_ = f32[4,144,288]{2,1,0:T(8,128)} custom-call(s32[4,2,32,1152]{3,2,1,0:T(8,128)} %copy-done), custom_call_target="tpu_custom_call" | custom-call | flops 14495514624 | bytes 442368 | tf_op jit(solution)/shard_map/compose/pallas_call | solution.py:454
  236.2 11.8 %all-to-all-done.got = s32[4,1,32,1152]{3,2,1,0:T(8,128)S(1)} async-done(((s32[4,1,32,1152]{3,2,1,0:T(8,128)}), s32[4,1,32,1152]{3,2,1,0:T(8,128)S(1)}, u32[]{:S(2)}, u32[]{:S(2)}) %all-to-all-start) | async-done | bytes 589856 | tf_op jit(solution)/shard_map/all_to_all | solution.py:546
  248.8 2.7 %compose.3 = f32[4,144,288]{2,1,0:T(8,128)} custom-call(s32[4,1,32,1152]{3,2,1,0:T(8,128)} %copy-done.1, f32[4,144,288]{2,1,0:T(8,128)} %compose.2.refs_0_), custom_call_target="tpu_custom_call", output_to_operand_aliasing={{}: (1, {})} | custom-call | flops 7247757312 | bytes 221184 | tf_op jit(solution)/shard_map/compose/pallas_call | solution.py:454
  (75 shorter events, 17.3 us)
Async XLA Ops:
  0.0 11.1 %copy-start.4 = (f32[4]{0:T(128)S(1)}, f32[4]{0:T(128)}, u32[]{:S(2)}) copy-start(f32[4]{0:T(128)} %constant.60) | copy-start | bytes 52
  0.0 6.9 %copy-start.14 = (s32[16]{0:T(128)S(1)}, s32[16]{0:T(128)}, u32[]{:S(2)}) copy-start(s32[16]{0:T(128)} %param.7) | copy-start | bytes 196
  0.0 7.0 %copy-start.3 = (f32[2]{0:T(128)S(1)}, f32[2]{0:T(128)}, u32[]{:S(2)}) copy-start(f32[2]{0:T(128)} %param.8) | copy-start | bytes 28
  0.0 10.3 %copy-start.2 = (f32[4,16]{1,0:T(4,128)S(1)}, f32[4,16]{1,0:T(4,128)}, u32[]{:S(2)}) copy-start(f32[4,16]{1,0:T(4,128)} %param.6) | copy-start | bytes 772
  1.6 16.5 %collective-permute-start.1 = (bf16[8,48,1152]{2,1,0:T(8,128)(2,1)S(1)}, bf16[8,48,1152]{2,1,0:T(8,128)(2,1)S(1)}, u32[]{:S(2)}, u32[]{:S(2)}) collective-permute-start(bf16[8,48,1152]{2,1,0:T(8,128)(2,1)S(1)} %get-tuple-element.53), channel_id=1, source_target_pairs={{1,0},{2,1},{3,2},{4,3},{5,4},{6,5},{7,6},{8,7},{9,8},{10,9},{11,1... | collective-permute-start | bytes 2654216 | tf_op jit(solution)/shard_map/ppermute | solution.py:512
  2.9 15.2 %collective-permute-start = (bf16[8,48,1152]{2,1,0:T(8,128)(2,1)S(1)}, bf16[8,48,1152]{2,1,0:T(8,128)(2,1)}, u32[]{:S(2)}, u32[]{:S(2)}) collective-permute-start(bf16[8,48,1152]{2,1,0:T(8,128)(2,1)S(1)} %get-tuple-element.54), channel_id=1, source_target_pairs={{0,1},{1,2},{2,3},{3,4},{4,5},{5,6},{6,7},{7,8},{8,9},{9,10},{10,1... | collective-permute-start | bytes 2654216 | tf_op jit(solution)/shard_map/ppermute | solution.py:512
  18.1 14.2 %copy-start.10 = (bf16[8,48,1152]{2,1,0:T(8,128)(2,1)}, bf16[8,48,1152]{2,1,0:T(8,128)(2,1)S(1)}, u32[]{:S(2)}) copy-start(bf16[8,48,1152]{2,1,0:T(8,128)(2,1)S(1)} %collective-permute-done.1.after) | copy-start | bytes 2654212
  18.1 56.2 %collective-permute-start.2 = (bf16[8,96,1152]{2,1,0:T(8,128)(2,1)S(1)}, bf16[8,96,1152]{2,1,0:T(8,128)(2,1)}, u32[]{:S(2)}, u32[]{:S(2)}) collective-permute-start(bf16[8,96,1152]{2,1,0:T(8,128)(2,1)S(1)} %get-tuple-element.29), channel_id=1, source_target_pairs={{0,1},{1,2},{2,3},{3,4},{4,5},{5,6},{6,7},{7,8},{8,9},{9,10},{10,1... | collective-permute-start | bytes 5308424 | tf_op jit(solution)/shard_map/ppermute | solution.py:512
  31.0 43.3 %collective-permute-start.3 = (bf16[8,96,1152]{2,1,0:T(8,128)(2,1)S(1)}, bf16[8,96,1152]{2,1,0:T(8,128)(2,1)}, u32[]{:S(2)}, u32[]{:S(2)}) collective-permute-start(bf16[8,96,1152]{2,1,0:T(8,128)(2,1)S(1)} %get-tuple-element.30), channel_id=1, source_target_pairs={{1,0},{2,1},{3,2},{4,3},{5,4},{6,5},{7,6},{8,7},{9,8},{10,9},{11,1... | collective-permute-start | bytes 5308424 | tf_op jit(solution)/shard_map/ppermute | solution.py:512
  72.3 42.7 %collective-permute-start.4 = (f32[4,4,48,1152]{3,2,1,0:T(8,128)}, f32[4,4,48,1152]{3,2,1,0:T(8,128)S(1)}, u32[]{:S(2)}, u32[]{:S(2)}) collective-permute-start(f32[4,4,48,1152]{3,2,1,0:T(8,128)} %get-tuple-element.27), channel_id=1, source_target_pairs={{0,1},{1,0},{2,3},{3,2},{4,5},{5,4},{6,7},{7,6},{8,9},{9,8},{10,11... | collective-permute-start | bytes 10616840 | tf_op jit(solution)/shard_map/ppermute | solution.py:516
  114.3 6.6 %collective-permute-start.5 = (f32[4,4,48,1152]{3,2,1,0:T(8,128)}, f32[4,4,48,1152]{3,2,1,0:T(8,128)}, u32[]{:S(2)}, u32[]{:S(2)}) collective-permute-start(f32[4,4,48,1152]{3,2,1,0:T(8,128)} %get-tuple-element.31), channel_id=1, source_target_pairs={{0,1},{1,0},{2,3},{3,2},{4,5},{5,4},{6,7},{7,6},{8,9},{9,8},{10,11... | collective-permute-start | bytes 10616840 | tf_op jit(solution)/shard_map/ppermute | solution.py:516
  115.0 5.9 %copy-start.5 = (f32[4,4,48,1152]{3,2,1,0:T(8,128)}, f32[4,4,48,1152]{3,2,1,0:T(8,128)S(1)}, u32[]{:S(2)}) copy-start(f32[4,4,48,1152]{3,2,1,0:T(8,128)S(1)} %collective-permute-done.4.refs_1_) | copy-start | bytes 10616836
  133.8 44.9 %collective-permute-start.8 = (s32[2,104,1152]{2,1,0:T(8,128)}, s32[2,104,1152]{2,1,0:T(8,128)S(1)}, u32[]{:S(2)}, u32[]{:S(2)}) collective-permute-start(s32[2,104,1152]{2,1,0:T(8,128)} %get-tuple-element.35), channel_id=1, source_target_pairs={{0,6},{1,7},{2,4},{3,5},{4,2},{5,3},{6,0},{7,1},{8,14},{9,15},{10,... | collective-permute-start | bytes 2875400 | tf_op jit(solution)/shard_map/ppermute | solution.py:516
  134.6 43.7 %collective-permute-start.6 = (s32[2,104,1152]{2,1,0:T(8,128)}, s32[2,104,1152]{2,1,0:T(8,128)S(1)}, u32[]{:S(2)}, u32[]{:S(2)}) collective-permute-start(s32[2,104,1152]{2,1,0:T(8,128)} %get-tuple-element.39), channel_id=1, source_target_pairs={{0,2},{1,3},{2,0},{3,1},{4,6},{5,7},{6,4},{7,5},{8,10},{9,11},{10,... | collective-permute-start | bytes 2875400 | tf_op jit(solution)/shard_map/ppermute | solution.py:516
  136.1 42.6 %collective-permute-start.7 = (s32[2,104,1152]{2,1,0:T(8,128)}, s32[2,104,1152]{2,1,0:T(8,128)S(1)}, u32[]{:S(2)}, u32[]{:S(2)}) collective-permute-start(s32[2,104,1152]{2,1,0:T(8,128)} %get-tuple-element.40), channel_id=1, source_target_pairs={{0,4},{1,5},{2,6},{3,7},{4,0},{5,1},{6,2},{7,3},{8,12},{9,13},{10,... | collective-permute-start | bytes 2875400 | tf_op jit(solution)/shard_map/ppermute | solution.py:516
  177.3 7.9 %collective-permute-start.9 = (f32[4,4,48,1152]{3,2,1,0:T(8,128)}, f32[4,4,48,1152]{3,2,1,0:T(8,128)S(1)}, u32[]{:S(2)}, u32[]{:S(2)}) collective-permute-start(f32[4,4,48,1152]{3,2,1,0:T(8,128)} %get-tuple-element.37), channel_id=1, source_target_pairs={{0,1},{1,0},{2,3},{3,2},{4,5},{5,4},{6,7},{7,6},{8,9},{9,8},{10,11... | collective-permute-start | bytes 10616840 | tf_op jit(solution)/shard_map/ppermute | solution.py:516
  185.1 1.8 copy-start.6
  193.4 14.0 %collective-permute-start.10 = (s32[1,104,1152]{2,1,0:T(8,128)}, s32[1,104,1152]{2,1,0:T(8,128)S(1)}, u32[]{:S(2)}, u32[]{:S(2)}) collective-permute-start(s32[1,104,1152]{2,1,0:T(8,128)} %get-tuple-element.47), channel_id=1, source_target_pairs={{0,2},{1,3},{2,0},{3,1},{4,6},{5,7},{6,4},{7,5},{8,10},{9,11},{10,... | collective-permute-start | bytes 1437704 | tf_op jit(solution)/shard_map/ppermute | solution.py:516
  195.4 23.1 %collective-permute-start.11 = (s32[1,104,1152]{2,1,0:T(8,128)}, s32[1,104,1152]{2,1,0:T(8,128)S(1)}, u32[]{:S(2)}, u32[]{:S(2)}) collective-permute-start(s32[1,104,1152]{2,1,0:T(8,128)} %get-tuple-element.48), channel_id=1, source_target_pairs={{0,4},{1,5},{2,6},{3,7},{4,0},{5,1},{6,2},{7,3},{8,12},{9,13},{10,... | collective-permute-start | bytes 1437704 | tf_op jit(solution)/shard_map/ppermute | solution.py:516
  196.3 22.2 %collective-permute-start.12 = (s32[1,104,1152]{2,1,0:T(8,128)}, s32[1,104,1152]{2,1,0:T(8,128)S(1)}, u32[]{:S(2)}, u32[]{:S(2)}) collective-permute-start(s32[1,104,1152]{2,1,0:T(8,128)} %get-tuple-element.44), channel_id=1, source_target_pairs={{0,6},{1,7},{2,4},{3,5},{4,2},{5,3},{6,0},{7,1},{8,14},{9,15},{10,... | collective-permute-start | bytes 1437704 | tf_op jit(solution)/shard_map/ppermute | solution.py:516
  196.9 32.2 %all-to-all-start.1 = ((s32[4,2,32,1152]{3,2,1,0:T(8,128)}), s32[4,2,32,1152]{3,2,1,0:T(8,128)S(1)}, u32[]{:S(2)}, u32[]{:S(2)}) async-start(s32[4,2,32,1152]{3,2,1,0:T(8,128)} %gather_parts.2), calls=%async_computation.1 | async-start | bytes 2359296 | tf_op jit(solution)/shard_map/all_to_all | solution.py:546
  207.4 11.1 %copy-start.11 = (s32[1,104,1152]{2,1,0:T(8,128)}, s32[1,104,1152]{2,1,0:T(8,128)S(1)}, u32[]{:S(2)}) copy-start(s32[1,104,1152]{2,1,0:T(8,128)S(1)} %collective-permute-done.10.refs_1_) | copy-start | bytes 1437700
  229.1 3.5 %copy-start = (s32[4,2,32,1152]{3,2,1,0:T(8,128)}, s32[4,2,32,1152]{3,2,1,0:T(8,128)S(1)}, u32[]{:S(2)}) copy-start(s32[4,2,32,1152]{3,2,1,0:T(8,128)S(1)} %all-to-all-done.1.got) | copy-start | bytes 3538948
  229.1 18.8 %all-to-all-start = ((s32[4,1,32,1152]{3,2,1,0:T(8,128)}), s32[4,1,32,1152]{3,2,1,0:T(8,128)S(1)}, u32[]{:S(2)}, u32[]{:S(2)}) async-start(s32[4,1,32,1152]{3,2,1,0:T(8,128)} %gather_parts.3), calls=%async_computation | async-start | bytes 1179648 | tf_op jit(solution)/shard_map/all_to_all | solution.py:546
  (6 other events, 5.8 us)

commit v12 on v11

--- a/solution.py
+++ b/solution.py
@@ -215,31 +215,26 @@
     return over(front, back)
 
 
-def merge_kernel(ctl, *refs, members, places, unit):
-    inputs, sends = refs[:2 * members], refs[2 * members:2 * members + places]
-    image, tops = refs[2 * members + places:]
+def merge_kernel(ctl, mine, got, *refs, places, unit):
+    sends, (image, tops) = refs[-2 - places:-2], refs[-2:]
     turn = pl.program_id(0)
     width = image.shape[2]
 
-    for n in range(members):
-        @pl.when(lax.rem(turn, members) == n)
-        def _(n=n):
-            def put(at):
-                cols = pl.ds(at, LANES)
-                merged = merge_pair(ctl, inputs[2 * n], inputs[2 * n + 1], cols)
-                for k in range(4):
-                    image[k, :, cols] = merged[k]
-                top = functools.reduce(jnp.maximum, merged)
-                tops[0:8, cols] = jnp.max(top.reshape(unit // 8, 8, LANES), axis=0)
-
-            each_strip(width, put)
-
+    def merge_strip(at):
+        cols = pl.ds(at, LANES)
+        merged = merge_pair(ctl, mine, got, cols)
+        for k in range(4):
+            image[k, :, cols] = merged[k]
+        top = functools.reduce(jnp.maximum, merged)
+        tops[0:8, cols] = jnp.max(top.reshape(unit // 8, 8, LANES), axis=0)
+
+    each_strip(width, merge_strip)
     exponent = exponent_of(jnp.max(tops[0:8, :], axis=0, keepdims=True))
     tops[0:8, :] = jnp.broadcast_to(jnp.exp2(-exponent) * CODES, (8, width))
     row = jnp.broadcast_to(exponent, (8, width)).astype(jnp.int32)
 
     for k, send in enumerate(sends):
-        @pl.when(turn // members == k)
+        @pl.when(turn == k)
         def _(send=send):
             def put(at):
                 cols = pl.ds(at, LANES)
@@ -396,31 +391,25 @@
     )(ctl, light, table, slope, row_bands, column_bands, field, field, field, before, after)
 
 
-def merge(ctl, pairs, *, places, unit):
-    members = len(pairs)
-    width = pairs[0][0].shape[3]
-    cells = 4 * places * members * unit * width
-
-    def spec(k):
-        return pl.BlockSpec(
-            (1, 2 * unit + 8, width), lambda i, ctl: (jnp.clip(i - k * members, 0, members - 1), 0, 0)
-        )
-
+def merge(ctl, mine, got, so_far, *, at, members, places, unit):
+    width = mine.shape[3]
+    cells = 4 * places * unit * width
+    image = pl.BlockSpec((1, 4, unit, width), lambda i, ctl: (ctl[0] ^ i, 0, 0, 0))
     return pl.pallas_call(
-        functools.partial(merge_kernel, members=members, places=places, unit=unit),
+        functools.partial(merge_kernel, places=places, unit=unit),
         grid_spec=pltpu.PrefetchScalarGridSpec(
             num_scalar_prefetch=1,
-            grid=(places * members,),
-            in_specs=[pl.BlockSpec((1, 4, unit, width), lambda i, ctl: (ctl[0] ^ (i // members), 0, 0, 0))]
-            * (2 * members),
-            out_specs=[spec(k) for k in range(places)],
+            grid=(places,),
+            in_specs=[image, image] + [pl.BlockSpec(memory_space=pl.ANY)] * len(so_far),
+            out_specs=[pl.BlockSpec((1, 2 * unit + 8, width), lambda i, ctl: (at, 0, 0))] * places,
             scratch_shapes=[pltpu.VMEM((4, unit, width), jnp.float32), pltpu.VMEM((8, width), jnp.float32)],
         ),
         out_shape=[jax.ShapeDtypeStruct((members, 2 * unit + 8, width), jnp.int32)] * places,
+        input_output_aliases={3 + k: k for k in range(len(so_far))},
         compiler_params=params(),
         cost_estimate=pl.CostEstimate(flops=32768 * cells, bytes_accessed=cells, transcendentals=0),
         name="merge",
-    )(ctl, *[array for pair in pairs for array in pair])
+    )(ctl, mine, got, *so_far)
 
 
 def gather_parts(ctl, parts, *, units, unit, blocks):
@@ -536,8 +525,13 @@
         state[n] = (keep, exchange(send, 1))
 
     def merge_group(members):
-        sends = merge(after_last(merge_control), [state[n] for n in members], places=places, unit=unit)
-        chain.append(sends[-1])
+        sends = []
+        for at, n in enumerate(members):
+            mine, got = state[n]
+            sends = merge(
+                after_last(merge_control), mine, got, sends, at=at, members=len(members), places=places, unit=unit
+            )
+            chain.append(sends[-1])
         return [sends[0]] + [exchange(sends[k], 2 * k) for k in range(1, places)]
 
     def block_group(members, parts):

time: 252 us -> 248 us (0.984)
  waiting for transfers between devices: 41.5 us -> 35.8 us
    ppermute x9, waiting for transfers between devices: 24.1 us -> 18.5 us  [exchange(): return lax.ppermute(send, 'tile', [(i, i ^ distance) for i in range(tiles)])]
    pallas_call x2 -> x3, Pallas kernels: 19.3 us -> 19.3 us  [merge(): pl.pallas_call(functools.partial(merge_kernel, places=places, unit=unit),...]
  transfers between devices with their start and end apart: 15 -> 15, of which waited for: 7 -> 6; matrix products, arithmetic and copies ran while one was open for 4% -> 4% of each run, Pallas kernels for 53% -> 56%
where the time goes in v12:
time: 248 us; the launch traced here: 247 us
  Pallas kernels  155 us (62%)
  starting transfers between devices  36.3 us (15%)
  waiting for transfers between devices  35.8 us (14%)
  local copies, waits for them, and re-layouts  13.5 us (5%)
  other arithmetic  3.77 us (2%)
  between operations  3.09 us (1%)
    pallas_call x3, Pallas kernels, render(): pl.pallas_call(kernel, grid_spec=pltpu.PrefetchScalarGridSpec(num_scalar_...  120 us
    pallas_call x3, Pallas kernels, merge(): pl.pallas_call(functools.partial(merge_kernel, places=places, unit=unit),...  19.3 us
    ppermute x4, starting transfers between devices, per_device(): pair = (lax.ppermute(ends[0], both, up), lax.ppermute(ends[1], both, down))  19.2 us
    ppermute x9, waiting for transfers between devices, exchange(): return lax.ppermute(send, 'tile', [(i, i ^ distance) for i in range(tiles)])  18.5 us
    all_to_all x2, waiting for transfers between devices, block_group(): lax.all_to_all(send, 'depth', split_axis=0, concat_axis=0, tiled=True)  17.3 us
    pallas_call x2, Pallas kernels, gather_parts(): pl.pallas_call(functools.partial(gather_kernel, unit=unit, blocks=blocks)...  9.18 us
    ppermute x9, starting transfers between devices, exchange(): return lax.ppermute(send, 'tile', [(i, i ^ distance) for i in range(tiles)])  9.13 us
    all_to_all x2, starting transfers between devices, block_group(): lax.all_to_all(send, 'depth', split_axis=0, concat_axis=0, tiled=True)  7.92 us
  transfers between devices with their start and end apart: 15, of which 6 were waited for; matrix products, arithmetic and copies ran while one was open for 4% of the time, Pallas kernels for 56%

profile of v12, /device:TPU:0, one launch (start us, length us, event | category | flops | bytes accessed | tf_op | source)
XLA Modules:
  0.0 247.2 jit_solution(5109173641328210491)
XLA Ops:
  0.0 1.6 slice_bitcast_fusion.2
  2.9 4.0 %collective-permute-start = (bf16[8,48,1152]{2,1,0:T(8,128)(2,1)S(1)}, bf16[8,48,1152]{2,1,0:T(8,128)(2,1)}, u32[]{:S(2)}, u32[]{:S(2)}) collective-permute-start(bf16[8,48,1152]{2,1,0:T(8,128)(2,1)S(1)} %get-tuple-element.64), channel_id=1, source_target_pairs={{0,1},{1,2},{2,3},{3,4},{4,5},{5,6},{6,7},{7,8},{8,9},{9,10},{10,1... | collective-permute-start | bytes 2654216 | tf_op jit(solution)/shard_map/ppermute | solution.py:501
  16.0 2.3 slice_bitcast_fusion
  18.3 12.7 %collective-permute-start.2 = (bf16[8,96,1152]{2,1,0:T(8,128)(2,1)S(1)}, bf16[8,96,1152]{2,1,0:T(8,128)(2,1)}, u32[]{:S(2)}, u32[]{:S(2)}) collective-permute-start(bf16[8,96,1152]{2,1,0:T(8,128)(2,1)S(1)} %get-tuple-element.34), channel_id=1, source_target_pairs={{0,1},{1,2},{2,3},{3,4},{4,5},{5,6},{6,7},{7,8},{8,9},{9,10},{10,1... | collective-permute-start | bytes 5308424 | tf_op jit(solution)/shard_map/ppermute | solution.py:501
  32.3 40.0 %render.3 = (f32[4,4,48,1152]{3,2,1,0:T(8,128)}, f32[4,4,48,1152]{3,2,1,0:T(8,128)}) custom-call(s32[2]{0:T(128)} %pad_add_fusion.1.ctl, f32[3]{0:T(128)} %maximum_multiply_fusion.light, bf16[128,256]{1,0:T(8,128)(2,1)} %convert_element_type.95.table, f32[8,128]{1,0:T(8,128)} %pad.23.slope, bf16[4,48,80]{2,1,0:T(8,128)(2,1)} %pad_maximum_fusion.1.row_bands, ...), custom_call_target="tpu_custom_call" | custom-call | flops 43486543872 | bytes 15925248 | tf_op jit(solution)/shard_map/render/pallas_call | solution.py:360
  72.3 2.0 collective-permute-start.4
  74.4 40.0 %render.4 = (f32[4,4,48,1152]{3,2,1,0:T(8,128)}, f32[4,4,48,1152]{3,2,1,0:T(8,128)}) custom-call(s32[2]{0:T(128)} %pad_add_fusion.1.ctl, f32[3]{0:T(128)} %maximum_multiply_fusion.light, bf16[128,256]{1,0:T(8,128)(2,1)} %convert_element_type.95.table, f32[8,128]{1,0:T(8,128)} %pad.23.slope, bf16[4,48,80]{2,1,0:T(8,128)(2,1)} %pad_maximum_fusion.1.row_bands, ...), custom_call_target="tpu_custom_call" | custom-call | flops 43486543872 | bytes 15925248 | tf_op jit(solution)/shard_map/render/pallas_call | solution.py:360
  115.1 1.8 copy-done.5
  116.8 6.4 %merge.3 = (s32[2,104,1152]{2,1,0:T(8,128)}, s32[2,104,1152]{2,1,0:T(8,128)}, s32[2,104,1152]{2,1,0:T(8,128)}, s32[2,104,1152]{2,1,0:T(8,128)}) custom-call(s32[2]{0:T(128)} %pad_add_fusion.ctl, f32[4,4,48,1152]{3,2,1,0:T(8,128)} %get-tuple-element.38.mine, f32[4,4,48,1152]{3,2,1,0:T(8,128)} %copy-done.5), custom_call_target="tpu_custom_call" | custom-call | flops 28991029248 | bytes 884736 | tf_op jit(solution)/shard_map/merge/pallas_call | solution.py:398
  123.3 6.4 %merge.4 = (s32[2,104,1152]{2,1,0:T(8,128)}, s32[2,104,1152]{2,1,0:T(8,128)}, s32[2,104,1152]{2,1,0:T(8,128)}, s32[2,104,1152]{2,1,0:T(8,128)}) custom-call(s32[2]{0:T(128)} %pad_add_fusion.ctl, f32[4,4,48,1152]{3,2,1,0:T(8,128)} %get-tuple-element.41.mine, ...), custom_call_target="tpu_custom_call", output_to_operand_aliasing={{0}: (3, {}), {1}: (4, {}), {2}: (5, {}), {3}: (6, {})} | custom-call | flops 28991029248 | bytes 884736 | tf_op jit(solution)/shard_map/merge/pallas_call | solution.py:398
  133.3 40.0 %render.5 = (f32[4,4,48,1152]{3,2,1,0:T(8,128)}, f32[4,4,48,1152]{3,2,1,0:T(8,128)}) custom-call(s32[2]{0:T(128)} %pad_add_fusion.1.ctl, f32[3]{0:T(128)} %maximum_multiply_fusion.light, bf16[128,256]{1,0:T(8,128)(2,1)} %convert_element_type.95.table, f32[8,128]{1,0:T(8,128)} %pad.23.slope, bf16[4,48,80]{2,1,0:T(8,128)(2,1)} %pad_maximum_fusion.1.row_bands, ...), custom_call_target="tpu_custom_call" | custom-call | flops 43486543872 | bytes 15925248 | tf_op jit(solution)/shard_map/render/pallas_call | solution.py:360
  176.2 5.2 %gather_parts.2 = s32[4,2,32,1152]{3,2,1,0:T(8,128)} custom-call(s32[2]{0:T(128)} %pad_add_fusion.ctl, s32[2,104,1152]{2,1,0:T(8,128)} %get-tuple-element.48.refs_0_, s32[2,104,1152]{2,1,0:T(8,128)} %copy-done.8, s32[2,104,1152]{2,1,0:T(8,128)} %copy-done.9, s32[2,104,1152]{2,1,0:T(8,128)} %copy-done.7), custom_call_target="tpu_custom_call" | custom-call | flops 57982058496 | bytes 442368 | tf_op jit(solution)/shard_map/gather_parts/pallas_call | solution.py:418
  181.4 1.8 copy-done.6
  183.2 6.4 %merge.5 = (s32[1,104,1152]{2,1,0:T(8,128)}, s32[1,104,1152]{2,1,0:T(8,128)}, s32[1,104,1152]{2,1,0:T(8,128)}, s32[1,104,1152]{2,1,0:T(8,128)}) custom-call(s32[2]{0:T(128)} %pad_add_fusion.ctl, f32[4,4,48,1152]{3,2,1,0:T(8,128)} %get-tuple-element.53.mine, f32[4,4,48,1152]{3,2,1,0:T(8,128)} %copy-done.6), custom_call_target="tpu_custom_call" | custom-call | flops 28991029248 | bytes 884736 | tf_op jit(solution)/shard_map/merge/pallas_call | solution.py:398
  189.6 1.7 collective-permute-start.10
  193.1 4.4 %all-to-all-start.1 = ((s32[4,2,32,1152]{3,2,1,0:T(8,128)}), s32[4,2,32,1152]{3,2,1,0:T(8,128)S(1)}, u32[]{:S(2)}, u32[]{:S(2)}) async-start(s32[4,2,32,1152]{3,2,1,0:T(8,128)} %gather_parts.2), calls=%async_computation.1 | async-start | bytes 2359296 | tf_op jit(solution)/shard_map/all_to_all | solution.py:540
  197.5 6.1 %collective-permute-done.10.refs_1_ = s32[1,104,1152]{2,1,0:T(8,128)S(1)} collective-permute-done((s32[1,104,1152]{2,1,0:T(8,128)}, s32[1,104,1152]{2,1,0:T(8,128)S(1)}, u32[]{:S(2)}, u32[]{:S(2)}) %collective-permute-start.10) | collective-permute-done | bytes 479264 | tf_op jit(solution)/shard_map/ppermute | solution.py:505
  203.6 10.7 %collective-permute-done.11.refs_2_ = s32[1,104,1152]{2,1,0:T(8,128)S(1)} collective-permute-done((s32[1,104,1152]{2,1,0:T(8,128)}, s32[1,104,1152]{2,1,0:T(8,128)S(1)}, u32[]{:S(2)}, u32[]{:S(2)}) %collective-permute-start.11) | collective-permute-done | bytes 479264 | tf_op jit(solution)/shard_map/ppermute | solution.py:505
  215.3 4.0 %gather_parts.3 = s32[4,1,32,1152]{3,2,1,0:T(8,128)} custom-call(s32[2]{0:T(128)} %pad_add_fusion.ctl, s32[1,104,1152]{2,1,0:T(8,128)} %get-tuple-element.56.refs_0_, s32[1,104,1152]{2,1,0:T(8,128)} %copy-done.11, s32[1,104,1152]{2,1,0:T(8,128)} %copy-done.12, s32[1,104,1152]{2,1,0:T(8,128)} %copy-done.13), custom_call_target="tpu_custom_call" | custom-call | flops 28991029248 | bytes 221184 | tf_op jit(solution)/shard_map/gather_parts/pallas_call | solution.py:418
  219.3 5.5 %all-to-all-done.1.got = s32[4,2,32,1152]{3,2,1,0:T(8,128)S(1)} async-done(((s32[4,2,32,1152]{3,2,1,0:T(8,128)}), s32[4,2,32,1152]{3,2,1,0:T(8,128)S(1)}, u32[]{:S(2)}, u32[]{:S(2)}) %all-to-all-start.1) | async-done | bytes 1179680 | tf_op jit(solution)/shard_map/all_to_all | solution.py:540
  224.8 3.5 %all-to-all-start = ((s32[4,1,32,1152]{3,2,1,0:T(8,128)}), s32[4,1,32,1152]{3,2,1,0:T(8,128)S(1)}, u32[]{:S(2)}, u32[]{:S(2)}) async-start(s32[4,1,32,1152]{3,2,1,0:T(8,128)} %gather_parts.3), calls=%async_computation | async-start | bytes 1179648 | tf_op jit(solution)/shard_map/all_to_all | solution.py:540
  228.3 3.6 %compose.2.refs_0_ = f32[4,144,288]{2,1,0:T(8,128)} custom-call(s32[4,2,32,1152]{3,2,1,0:T(8,128)} %copy-done), custom_call_target="tpu_custom_call" | custom-call | flops 14495514624 | bytes 442368 | tf_op jit(solution)/shard_map/compose/pallas_call | solution.py:443
  231.9 11.8 %all-to-all-done.got = s32[4,1,32,1152]{3,2,1,0:T(8,128)S(1)} async-done(((s32[4,1,32,1152]{3,2,1,0:T(8,128)}), s32[4,1,32,1152]{3,2,1,0:T(8,128)S(1)}, u32[]{:S(2)}, u32[]{:S(2)}) %all-to-all-start) | async-done | bytes 589856 | tf_op jit(solution)/shard_map/all_to_all | solution.py:540
  244.5 2.7 %compose.3 = f32[4,144,288]{2,1,0:T(8,128)} custom-call(s32[4,1,32,1152]{3,2,1,0:T(8,128)} %copy-done.1, f32[4,144,288]{2,1,0:T(8,128)} %compose.2.refs_0_), custom_call_target="tpu_custom_call", output_to_operand_aliasing={{}: (1, {})} | custom-call | flops 7247757312 | bytes 221184 | tf_op jit(solution)/shard_map/compose/pallas_call | solution.py:443
  (76 shorter events, 19.6 us)
Async XLA Ops:
  0.0 11.2 %copy-start.4 = (f32[4]{0:T(128)S(1)}, f32[4]{0:T(128)}, u32[]{:S(2)}) copy-start(f32[4]{0:T(128)} %constant.60) | copy-start | bytes 52
  0.0 6.9 %copy-start.14 = (s32[16]{0:T(128)S(1)}, s32[16]{0:T(128)}, u32[]{:S(2)}) copy-start(s32[16]{0:T(128)} %param.7) | copy-start | bytes 196
  0.0 7.0 %copy-start.3 = (f32[2]{0:T(128)S(1)}, f32[2]{0:T(128)}, u32[]{:S(2)}) copy-start(f32[2]{0:T(128)} %param.8) | copy-start | bytes 28
  0.0 10.5 %copy-start.2 = (f32[4,16]{1,0:T(4,128)S(1)}, f32[4,16]{1,0:T(4,128)}, u32[]{:S(2)}) copy-start(f32[4,16]{1,0:T(4,128)} %param.6) | copy-start | bytes 772
  1.6 16.6 %collective-permute-start.1 = (bf16[8,48,1152]{2,1,0:T(8,128)(2,1)S(1)}, bf16[8,48,1152]{2,1,0:T(8,128)(2,1)S(1)}, u32[]{:S(2)}, u32[]{:S(2)}) collective-permute-start(bf16[8,48,1152]{2,1,0:T(8,128)(2,1)S(1)} %get-tuple-element.63), channel_id=1, source_target_pairs={{1,0},{2,1},{3,2},{4,3},{5,4},{6,5},{7,6},{8,7},{9,8},{10,9},{11,1... | collective-permute-start | bytes 2654216 | tf_op jit(solution)/shard_map/ppermute | solution.py:501
  2.9 15.4 %collective-permute-start = (bf16[8,48,1152]{2,1,0:T(8,128)(2,1)S(1)}, bf16[8,48,1152]{2,1,0:T(8,128)(2,1)}, u32[]{:S(2)}, u32[]{:S(2)}) collective-permute-start(bf16[8,48,1152]{2,1,0:T(8,128)(2,1)S(1)} %get-tuple-element.64), channel_id=1, source_target_pairs={{0,1},{1,2},{2,3},{3,4},{4,5},{5,6},{6,7},{7,8},{8,9},{9,10},{10,1... | collective-permute-start | bytes 2654216 | tf_op jit(solution)/shard_map/ppermute | solution.py:501
  18.3 14.0 %copy-start.10 = (bf16[8,48,1152]{2,1,0:T(8,128)(2,1)}, bf16[8,48,1152]{2,1,0:T(8,128)(2,1)S(1)}, u32[]{:S(2)}) copy-start(bf16[8,48,1152]{2,1,0:T(8,128)(2,1)S(1)} %collective-permute-done.1.after) | copy-start | bytes 2654212
  18.3 56.0 %collective-permute-start.2 = (bf16[8,96,1152]{2,1,0:T(8,128)(2,1)S(1)}, bf16[8,96,1152]{2,1,0:T(8,128)(2,1)}, u32[]{:S(2)}, u32[]{:S(2)}) collective-permute-start(bf16[8,96,1152]{2,1,0:T(8,128)(2,1)S(1)} %get-tuple-element.34), channel_id=1, source_target_pairs={{0,1},{1,2},{2,3},{3,4},{4,5},{5,6},{6,7},{7,8},{8,9},{9,10},{10,1... | collective-permute-start | bytes 5308424 | tf_op jit(solution)/shard_map/ppermute | solution.py:501
  31.0 43.3 %collective-permute-start.3 = (bf16[8,96,1152]{2,1,0:T(8,128)(2,1)S(1)}, bf16[8,96,1152]{2,1,0:T(8,128)(2,1)}, u32[]{:S(2)}, u32[]{:S(2)}) collective-permute-start(bf16[8,96,1152]{2,1,0:T(8,128)(2,1)S(1)} %get-tuple-element.35), channel_id=1, source_target_pairs={{1,0},{2,1},{3,2},{4,3},{5,4},{6,5},{7,6},{8,7},{9,8},{10,9},{11,1... | collective-permute-start | bytes 5308424 | tf_op jit(solution)/shard_map/ppermute | solution.py:501
  72.3 42.8 %collective-permute-start.4 = (f32[4,4,48,1152]{3,2,1,0:T(8,128)}, f32[4,4,48,1152]{3,2,1,0:T(8,128)S(1)}, u32[]{:S(2)}, u32[]{:S(2)}) collective-permute-start(f32[4,4,48,1152]{3,2,1,0:T(8,128)} %get-tuple-element.32), channel_id=1, source_target_pairs={{0,1},{1,0},{2,3},{3,2},{4,5},{5,4},{6,7},{7,6},{8,9},{9,8},{10,11... | collective-permute-start | bytes 10616840 | tf_op jit(solution)/shard_map/ppermute | solution.py:505
  114.4 8.9 %collective-permute-start.5 = (f32[4,4,48,1152]{3,2,1,0:T(8,128)}, f32[4,4,48,1152]{3,2,1,0:T(8,128)}, u32[]{:S(2)}, u32[]{:S(2)}) collective-permute-start(f32[4,4,48,1152]{3,2,1,0:T(8,128)} %get-tuple-element.36), channel_id=1, source_target_pairs={{0,1},{1,0},{2,3},{3,2},{4,5},{5,4},{6,7},{7,6},{8,9},{9,8},{10,11... | collective-permute-start | bytes 10616840 | tf_op jit(solution)/shard_map/ppermute | solution.py:505
  115.1 1.8 copy-start.5
  129.7 45.3 %collective-permute-start.8 = (s32[2,104,1152]{2,1,0:T(8,128)}, s32[2,104,1152]{2,1,0:T(8,128)S(1)}, u32[]{:S(2)}, u32[]{:S(2)}) collective-permute-start(s32[2,104,1152]{2,1,0:T(8,128)} %get-tuple-element.45), channel_id=1, source_target_pairs={{0,6},{1,7},{2,4},{3,5},{4,2},{5,3},{6,0},{7,1},{8,14},{9,15},{10,... | collective-permute-start | bytes 2875400 | tf_op jit(solution)/shard_map/ppermute | solution.py:505
  130.8 43.4 %collective-permute-start.6 = (s32[2,104,1152]{2,1,0:T(8,128)}, s32[2,104,1152]{2,1,0:T(8,128)S(1)}, u32[]{:S(2)}, u32[]{:S(2)}) collective-permute-start(s32[2,104,1152]{2,1,0:T(8,128)} %get-tuple-element.49), channel_id=1, source_target_pairs={{0,2},{1,3},{2,0},{3,1},{4,6},{5,7},{6,4},{7,5},{8,10},{9,11},{10,... | collective-permute-start | bytes 2875400 | tf_op jit(solution)/shard_map/ppermute | solution.py:505
  132.3 42.6 %collective-permute-start.7 = (s32[2,104,1152]{2,1,0:T(8,128)}, s32[2,104,1152]{2,1,0:T(8,128)S(1)}, u32[]{:S(2)}, u32[]{:S(2)}) collective-permute-start(s32[2,104,1152]{2,1,0:T(8,128)} %get-tuple-element.50), channel_id=1, source_target_pairs={{0,4},{1,5},{2,6},{3,7},{4,0},{5,1},{6,2},{7,3},{8,12},{9,13},{10,... | collective-permute-start | bytes 2875400 | tf_op jit(solution)/shard_map/ppermute | solution.py:505
  173.2 8.2 %collective-permute-start.9 = (f32[4,4,48,1152]{3,2,1,0:T(8,128)}, f32[4,4,48,1152]{3,2,1,0:T(8,128)S(1)}, u32[]{:S(2)}, u32[]{:S(2)}) collective-permute-start(f32[4,4,48,1152]{3,2,1,0:T(8,128)} %get-tuple-element.47), channel_id=1, source_target_pairs={{0,1},{1,0},{2,3},{3,2},{4,5},{5,4},{6,7},{7,6},{8,9},{9,8},{10,11... | collective-permute-start | bytes 10616840 | tf_op jit(solution)/shard_map/ppermute | solution.py:505
  181.4 1.8 copy-start.6
  189.6 14.0 %collective-permute-start.10 = (s32[1,104,1152]{2,1,0:T(8,128)}, s32[1,104,1152]{2,1,0:T(8,128)S(1)}, u32[]{:S(2)}, u32[]{:S(2)}) collective-permute-start(s32[1,104,1152]{2,1,0:T(8,128)} %get-tuple-element.57), channel_id=1, source_target_pairs={{0,2},{1,3},{2,0},{3,1},{4,6},{5,7},{6,4},{7,5},{8,10},{9,11},{10,... | collective-permute-start | bytes 1437704 | tf_op jit(solution)/shard_map/ppermute | solution.py:505
  191.3 23.1 %collective-permute-start.11 = (s32[1,104,1152]{2,1,0:T(8,128)}, s32[1,104,1152]{2,1,0:T(8,128)S(1)}, u32[]{:S(2)}, u32[]{:S(2)}) collective-permute-start(s32[1,104,1152]{2,1,0:T(8,128)} %get-tuple-element.58), channel_id=1, source_target_pairs={{0,4},{1,5},{2,6},{3,7},{4,0},{5,1},{6,2},{7,3},{8,12},{9,13},{10,... | collective-permute-start | bytes 1437704 | tf_op jit(solution)/shard_map/ppermute | solution.py:505
  192.2 22.2 %collective-permute-start.12 = (s32[1,104,1152]{2,1,0:T(8,128)}, s32[1,104,1152]{2,1,0:T(8,128)S(1)}, u32[]{:S(2)}, u32[]{:S(2)}) collective-permute-start(s32[1,104,1152]{2,1,0:T(8,128)} %get-tuple-element.54), channel_id=1, source_target_pairs={{0,6},{1,7},{2,4},{3,5},{4,2},{5,3},{6,0},{7,1},{8,14},{9,15},{10,... | collective-permute-start | bytes 1437704 | tf_op jit(solution)/shard_map/ppermute | solution.py:505
  193.1 31.7 %all-to-all-start.1 = ((s32[4,2,32,1152]{3,2,1,0:T(8,128)}), s32[4,2,32,1152]{3,2,1,0:T(8,128)S(1)}, u32[]{:S(2)}, u32[]{:S(2)}) async-start(s32[4,2,32,1152]{3,2,1,0:T(8,128)} %gather_parts.2), calls=%async_computation.1 | async-start | bytes 2359296 | tf_op jit(solution)/shard_map/all_to_all | solution.py:540
  203.6 10.7 %copy-start.11 = (s32[1,104,1152]{2,1,0:T(8,128)}, s32[1,104,1152]{2,1,0:T(8,128)S(1)}, u32[]{:S(2)}) copy-start(s32[1,104,1152]{2,1,0:T(8,128)S(1)} %collective-permute-done.10.refs_1_) | copy-start | bytes 1437700
  224.8 3.5 %copy-start = (s32[4,2,32,1152]{3,2,1,0:T(8,128)}, s32[4,2,32,1152]{3,2,1,0:T(8,128)S(1)}, u32[]{:S(2)}) copy-start(s32[4,2,32,1152]{3,2,1,0:T(8,128)S(1)} %all-to-all-done.1.got) | copy-start | bytes 3538948
  224.8 18.8 %all-to-all-start = ((s32[4,1,32,1152]{3,2,1,0:T(8,128)}), s32[4,1,32,1152]{3,2,1,0:T(8,128)S(1)}, u32[]{:S(2)}, u32[]{:S(2)}) async-start(s32[4,1,32,1152]{3,2,1,0:T(8,128)} %gather_parts.3), calls=%async_computation | async-start | bytes 1179648 | tf_op jit(solution)/shard_map/all_to_all | solution.py:540
  (6 other events, 5.7 us)
